TPU v7x, 32 devices: a whole 2x2x4 slice. The times are simulated.
32 devices in a mesh: lat: 8 (over y, x, core), lon: 4 (over z).
Axes of the slice: x: 2, y: 2, z: 4, core: 2. Of those that a mesh axis runs over, the one named last changes fastest.
Arguments:
- fields: bfloat16 [32, 64, 1024], P(None, 'lat', 'lon'), may hold values from -6 to 6
- cotangent: bfloat16 [32, 64, 1024], P(None, 'lat', 'lon'), may hold values from -0.0234375 to 0.0234375
- kernel_in: bfloat16 [9, 128, 32], replicated, may hold values from -0.375 to 0.375
- kernel_mid: bfloat16 [9, 128, 128], replicated, may hold values from -0.1875 to 0.1875
- kernel_out: bfloat16 [9, 32, 128], replicated, may hold values from -0.1875 to 0.1875
- patch_anchors: int32 [8, 4, 4, 2], P('lat', 'lon'), may hold values from 0 to 8
- blend_weights: int32 [4, 64, 1024], P(None, 'lat', 'lon'), may hold values from 1 to 8
- tile_counts: int32 [8, 4], P('lat', 'lon'), may hold values from 0 to 4, as said below
Outputs:
- blended: float32 [32, 64, 1024], P(None, 'lat', 'lon')
- grad_in: float32 [9, 128, 32], replicated
- grad_mid: float32 [9, 128, 128], replicated
- grad_out: float32 [9, 32, 128], replicated
Inputs may be any that keep to these rules, and one draw needn't show every extreme that they name: `tile_counts`: the counts of the tiles in lat rows i and i + 4 at the same lon sum to exactly 4; tile (1, 0) holds 4 patches and tile (5, 0) none.
All inputs are finite; a program needn't handle non-finite values.
Results may differ from a plain program's by a relative error of at most 0.005.
Values may be sent and summed in bfloat16 or wider, within the bound.
No kernel may reach another device: no remote copies, remote signals or barrier semaphores. Data moves between devices by JAX's collectives and lax.ppermute only.
A program may use at most 64 MiB of HBM per device.

v0:
```python
import jax
import jax.numpy as jnp
from jax import lax
from jax.sharding import PartitionSpec as P

MARGIN = 4
SLOTS = 4


KERNEL_TAPS = ((0, 0), (0, 1), (0, 2), (1, 0), (1, 1), (1, 2), (2, 0), (2, 1), (2, 2))


def extended_2(block, sides, width):
    for axis, dim in sides:
        count = lax.axis_size(axis)
        forward = [(i, i + 1) for i in range(count - 1)]
        forward.append((count - 1, 0))
        backward = [(target, source) for source, target in forward]
        low = lax.ppermute(
            lax.slice_in_dim(block, block.shape[dim] - width, None, axis=dim), axis, forward
        )
        high = lax.ppermute(lax.slice_in_dim(block, 0, width, axis=dim), axis, backward)
        block = jnp.concatenate([low, block, high], axis=dim)
    return block


def shifted(value, axis, steps):
    count = lax.axis_size(axis)
    pairs = [(source, (source + steps) % count) for source in range(count)]
    return lax.ppermute(value, axis, pairs)


def forward_conv(values, kernel):
    height, breadth = (values.shape[1], values.shape[2])
    padded = jnp.pad(values, ((0, 0), (1, 1), (1, 1)))
    summed = jnp.zeros((kernel.shape[1], height, breadth), jnp.float32)
    for tap_index, (tap_row, tap_col) in enumerate(KERNEL_TAPS):
        summed = summed + jnp.einsum(
            "ok,khw->ohw",
            kernel[tap_index],
            padded[:, tap_row : tap_row + height, tap_col : tap_col + breadth],
            preferred_element_type=jnp.float32,
        )
    return summed


def backward_conv(cotangent, kernel):
    height, breadth = (cotangent.shape[1], cotangent.shape[2])
    padded = jnp.pad(cotangent, ((0, 0), (1, 1), (1, 1)))
    summed = jnp.zeros((kernel.shape[2], height, breadth), jnp.float32)
    for tap_index, (tap_row, tap_col) in enumerate(KERNEL_TAPS):
        summed = summed + jnp.einsum(
            "ok,ohw->khw",
            kernel[tap_index],
            padded[:, 2 - tap_row : 2 - tap_row + height, 2 - tap_col : 2 - tap_col + breadth],
            preferred_element_type=jnp.float32,
        )
    return summed


def kernel_grad(cotangent, values):
    height, breadth = (values.shape[1], values.shape[2])
    padded = jnp.pad(values, ((0, 0), (1, 1), (1, 1)))
    pieces = [
        jnp.einsum(
            "ohw,khw->ok",
            cotangent,
            padded[:, tap_row : tap_row + height, tap_col : tap_col + breadth],
            preferred_element_type=jnp.float32,
        )
        for tap_row, tap_col in KERNEL_TAPS
    ]
    return jnp.stack(pieces)


def silu_slope(pre_act):
    sigmoid = jax.nn.sigmoid(pre_act)
    return sigmoid * (1.0 + pre_act * (1.0 - sigmoid))


def patch_pass(inputs, out_grad, kernel_in, kernel_mid, kernel_out):
    pre_one = forward_conv(inputs, kernel_in)
    hidden_one = jax.nn.silu(pre_one).astype(jnp.bfloat16)
    pre_two = forward_conv(hidden_one, kernel_mid)
    hidden_two = (hidden_one.astype(jnp.float32) + jax.nn.silu(pre_two)).astype(jnp.bfloat16)
    result = forward_conv(hidden_two, kernel_out)
    grad_two = backward_conv(out_grad, kernel_out)
    delta_two = (grad_two * silu_slope(pre_two)).astype(jnp.bfloat16)
    grad_one = grad_two + backward_conv(delta_two, kernel_mid)
    delta_one = (grad_one * silu_slope(pre_one)).astype(jnp.bfloat16)
    return (
        result,
        kernel_grad(delta_one, inputs),
        kernel_grad(delta_two, hidden_one),
        kernel_grad(out_grad, hidden_two),
    )


def run_patches(inputs, out_grads, kernel_in, kernel_mid, kernel_out):
    initial = (
        jnp.zeros(kernel_in.shape, jnp.float32),
        jnp.zeros(kernel_mid.shape, jnp.float32),
        jnp.zeros(kernel_out.shape, jnp.float32),
    )

    def step_patch(running, slot_pair):
        result, part_in, part_mid, part_out = patch_pass(
            slot_pair[0], slot_pair[1], kernel_in, kernel_mid, kernel_out
        )
        return ((running[0] + part_in, running[1] + part_mid, running[2] + part_out), result)

    return lax.scan(step_patch, initial, (inputs, out_grads))


def fold_canvas(canvas, keep_top, keep_bottom):
    extended = extended_2(canvas, (("lat", 1), ("lon", 2)), MARGIN)
    height = canvas.shape[1] - 2 * MARGIN
    breadth = canvas.shape[2] - 2 * MARGIN
    inner_rows = slice(2 * MARGIN, 2 * MARGIN + height)
    inner_cols = slice(2 * MARGIN, 2 * MARGIN + breadth)
    center_part = extended[:, inner_rows, inner_cols]
    col_left = ((0, 0), (0, 0), (0, breadth - MARGIN))
    col_right = ((0, 0), (0, 0), (breadth - MARGIN, 0))
    upper_part = (
        extended[:, :MARGIN, inner_cols]
        + jnp.pad(extended[:, :MARGIN, :MARGIN], col_left)
        + jnp.pad(extended[:, :MARGIN, -MARGIN:], col_right)
    )
    lower_part = (
        extended[:, -MARGIN:, inner_cols]
        + jnp.pad(extended[:, -MARGIN:, :MARGIN], col_left)
        + jnp.pad(extended[:, -MARGIN:, -MARGIN:], col_right)
    )
    summed = (
        center_part
        + jnp.pad(extended[:, inner_rows, :MARGIN], col_left)
        + jnp.pad(extended[:, inner_rows, -MARGIN:], col_right)
    )
    summed = summed + jnp.pad(upper_part * keep_top, ((0, 0), (0, height - MARGIN), (0, 0)))
    summed = summed + jnp.pad(lower_part * keep_bottom, ((0, 0), (height - MARGIN, 0), (0, 0)))
    return summed


def shards(
    fields, cotangent, kernel_in, kernel_mid, kernel_out, patch_anchors, blend_weights, tile_counts
):
    channels, height, breadth = (fields.shape[0], fields.shape[1], fields.shape[2])
    canvas_rows = height + 2 * MARGIN
    canvas_cols = breadth + 2 * MARGIN
    lat_size = lax.axis_size("lat")
    lat_index = lax.axis_index("lat")
    keep_top = (lat_index > 0).astype(jnp.float32)
    keep_bottom = (lat_index < lat_size - 1).astype(jnp.float32)
    slot_count = tile_counts[0, 0]
    slot_live = (jnp.arange(SLOTS) < slot_count).astype(jnp.int32)
    weights = (blend_weights * slot_live[:, None, None]).astype(jnp.float32)
    starts = patch_anchors[0, 0]

    def place_slots(per_slot):
        canvas = jnp.zeros((per_slot.shape[1], canvas_rows, canvas_cols), jnp.float32)
        for slot_index in range(SLOTS):
            corner = (jnp.int32(0), starts[slot_index, 0], starts[slot_index, 1])
            current = lax.dynamic_slice(canvas, corner, per_slot.shape[1:])
            canvas = lax.dynamic_update_slice(canvas, current + per_slot[slot_index], corner)
        return canvas

    total_weight = jnp.maximum(
        fold_canvas(place_slots(weights[:, None]), keep_top, keep_bottom), 1.0
    )
    scaled = (cotangent.astype(jnp.float32) / total_weight).astype(jnp.bfloat16)
    wide_fields, wide_scaled = (
        extended_2(fields, (("lat", 1), ("lon", 2)), MARGIN),
        extended_2(scaled, (("lat", 1), ("lon", 2)), MARGIN),
    )
    row_ids = jnp.arange(canvas_rows)[None, :, None]
    keep_rows = ((row_ids >= MARGIN) | (keep_top > 0.0)) & (
        (row_ids < height + MARGIN) | (keep_bottom > 0.0)
    )
    wide_fields = jnp.where(keep_rows, wide_fields, jnp.zeros_like(wide_fields))
    wide_scaled = jnp.where(keep_rows, wide_scaled, jnp.zeros_like(wide_scaled))
    window_list = []
    grad_list = []
    for slot_index in range(SLOTS):
        corner = (jnp.int32(0), starts[slot_index, 0], starts[slot_index, 1])
        window_list.append(lax.dynamic_slice(wide_fields, corner, (channels, height, breadth)))
        scaled_window = lax.dynamic_slice(wide_scaled, corner, (channels, height, breadth)).astype(
            jnp.float32
        )
        grad_list.append((weights[slot_index] * scaled_window).astype(jnp.bfloat16))
    inputs = jnp.stack(window_list)
    out_grads = jnp.stack(grad_list)
    half_slots = SLOTS // 2
    upper_half = (lat_index >= lat_size // 2).astype(jnp.int32)
    first_count = jnp.where(upper_half == 0, slot_count, SLOTS - slot_count)
    outgoing_inputs = jnp.where(upper_half == 0, inputs[half_slots:], inputs[:half_slots])
    outgoing_grads = jnp.where(upper_half == 0, out_grads[half_slots:], out_grads[:half_slots])
    incoming_inputs, incoming_grads = shifted(
        (outgoing_inputs, outgoing_grads), "lat", lat_size // 2
    )
    table_inputs = jnp.concatenate([inputs, incoming_inputs], axis=0)
    table_grads = jnp.concatenate([out_grads, incoming_grads], axis=0)
    position = upper_half * half_slots + jnp.arange(half_slots, dtype=jnp.int32)
    picked = jnp.where(
        position < first_count,
        jnp.where(upper_half == 0, position, position + SLOTS - half_slots),
        jnp.where(upper_half == 0, SLOTS + position - first_count, position - first_count),
    )
    picked = jnp.clip(picked, 0, SLOTS + half_slots - 1)
    totals, computed = run_patches(
        jnp.take(table_inputs, picked, axis=0),
        jnp.take(table_grads, picked, axis=0),
        kernel_in,
        kernel_mid,
        kernel_out,
    )
    returned = shifted(computed, "lat", lat_size // 2)
    ordered = jnp.where(
        upper_half == 0,
        jnp.concatenate([computed, returned], axis=0),
        jnp.concatenate([returned, computed], axis=0),
    )
    where_slot = jnp.clip(
        jnp.arange(SLOTS, dtype=jnp.int32) + upper_half * first_count, 0, SLOTS - 1
    )
    outputs = jnp.take(ordered, where_slot, axis=0)
    weighted = weights[:, None] * outputs
    numerator = fold_canvas(place_slots(weighted), keep_top, keep_bottom)
    blended = numerator / total_weight
    summed_grads = lax.psum((totals[0], totals[1], totals[2]), ("lat", "lon"))
    return (blended, summed_grads[0], summed_grads[1], summed_grads[2])


def solution(mesh):
    return jax.shard_map(
        shards,
        mesh=mesh,
        in_specs=(
            P(None, "lat", "lon"),
            P(None, "lat", "lon"),
            P(),
            P(),
            P(),
            P("lat", "lon", None, None),
            P(None, "lat", "lon"),
            P("lat", "lon"),
        ),
        out_specs=(P(None, "lat", "lon"), P(), P(), P()),
        check_vma=False,
    )
```

profile of v0, /device:TPU:0, one launch (start us, length us, event | category | flops | bytes accessed | tf_op | source)
XLA Modules:
  0.0 351.4 jit_solution(17506148137876961783)
XLA Ops:
  28.4 2.8 collective-permute-start.1
  32.6 2.2 collective-permute-start.2
  34.8 2.1 collective-permute-start.3
  36.9 1.8 collective-permute-done.2
  39.7 2.6 collective-permute-start.5
  44.2 2.2 collective-permute-start.12
  46.8 3.8 %collective-permute-start.7 = (bf16[32,16,4]{2,1,0:T(8,128)(2,1)S(1)}, bf16[32,16,4]{2,1,0:T(8,128)(2,1)S(1)}, u32[]{:S(2)}, u32[]{:S(2)}) collective-permute-start(bf16[32,16,4]{2,1,0:T(8,128)(2,1)S(1)} %get-tuple-element.248), channel_id=1, source_target_pairs={{1,0},{2,1},{3,2},{0,3},{5,4},{6,5},{7,6},{4,7},{9,8},{10,9},{11,1... | collective-permute-start | bytes 12296 | tf_op jit(solution)/shard_map/ppermute | solution.py:22
  50.6 2.7 collective-permute-done.12
  53.3 2.0 collective-permute-done.6
  60.7 6.6 %collective-permute-done.8 = bf16[2,32,8,256]{3,2,1,0:T(8,128)(2,1)S(1)} collective-permute-done((bf16[2,32,8,256]{3,2,1,0:T(8,128)(2,1)S(1)}, bf16[2,32,8,256]{3,2,1,0:T(8,128)(2,1)S(1)}, u32[]{:S(2)}, u32[]{:S(2)}) %collective-permute-start.8) | collective-permute-done | bytes 262176 | tf_op jit(solution)/shard_map/ppermute | solution.py:30
  67.9 2.9 collective-permute-done.13
  72.4 72.6 %while.19 = (s32[]{:T(128)}, f32[9,128,32]{1,2,0:T(8,128)S(1)}, f32[9,128,128]{2,1,0:T(8,128)S(1)}, f32[9,32,128]{2,1,0:T(8,128)}, f32[2,32,8,256]{3,2,1,0:T(8,1...) while((s32[]{:T(128)}, f32[9,128,32]{1,2,0:T(8,128)S(1)}, ...), condition=%wide.region_1.3_spmd.clone, body=%wide.region_0.2_spmd.clone.sunk | while | flops 2583609344 | bytes 133587216 | solution.py:112
  146.4 10.6 %collective-permute-done.14 = f32[2,32,8,256]{3,2,1,0:T(8,128)S(1)} collective-permute-done((f32[2,32,8,256]{3,2,1,0:T(8,128)}, f32[2,32,8,256]{3,2,1,0:T(8,128)S(1)}, u32[]{:S(2)}, u32[]{:S(2)}) %collective-permute-start.14) | collective-permute-done | bytes 524320 | tf_op jit(solution)/shard_map/ppermute | solution.py:30
  159.3 10.2 %dynamic_update_slice.35 = f32[32,16,264]{2,1,0:T(8,128)S(1)} dynamic-update-slice(f32[32,16,264]{2,1,0:T(8,128)S(1)} %broadcast_in_dim.59, f32[32,8,256]{2,1,0:T(8,128)S(1)} %slice_bitcast_fusion.3, s32[]{:T(128)} %constant.84.clone.1, s32[]{:T(128)S(6)} %select_n.136, s32[]{:T(128)S(6)} %select_n.137) | dynamic-update-slice | bytes 524292 | tf_op jit(solution)/shard_map/dynamic_update_slice | solution.py:164
  169.6 10.2 %dynamic_update_slice.36 = f32[32,16,264]{2,1,0:T(8,128)S(1)} dynamic-update-slice(f32[32,16,264]{2,1,0:T(8,128)S(1)} %dynamic_update_slice.35, f32[32,8,256]{2,1,0:T(8,128)S(1)} %fusion.200, s32[]{:T(128)} %constant.84.clone.1, s32[]{:T(128)S(6)} %select_n.138, s32[]{:T(128)S(6)} %select_n.139) | dynamic-update-slice | bytes 524292 | tf_op jit(solution)/shard_map/dynamic_update_slice | solution.py:164
  180.0 10.2 %dynamic_update_slice.37 = f32[32,16,264]{2,1,0:T(8,128)S(1)} dynamic-update-slice(f32[32,16,264]{2,1,0:T(8,128)S(1)} %dynamic_update_slice.36, f32[32,8,256]{2,1,0:T(8,128)S(1)} %fusion.199, s32[]{:T(128)} %constant.84.clone.1, s32[]{:T(128)S(6)} %select_n.140, s32[]{:T(128)S(6)} %select_n.141) | dynamic-update-slice | bytes 524292 | tf_op jit(solution)/shard_map/dynamic_update_slice | solution.py:164
  190.3 10.2 %dynamic_update_slice.38 = f32[32,16,264]{2,1,0:T(8,128)S(1)} dynamic-update-slice(f32[32,16,264]{2,1,0:T(8,128)S(1)} %dynamic_update_slice.37, f32[32,8,256]{2,1,0:T(8,128)S(1)} %fusion.198, s32[]{:T(128)} %constant.84.clone.1, s32[]{:T(128)S(6)} %select_n.142, s32[]{:T(128)S(6)} %select_n.143) | dynamic-update-slice | bytes 524292 | tf_op jit(solution)/shard_map/dynamic_update_slice | solution.py:164
  200.6 2.6 collective-permute-start.16
  203.2 3.3 collective-permute-done.15
  206.8 2.3 collective-permute-start.17
  210.8 10.7 %collective-permute-done.17 = f32[32,24,4]{2,1,0:T(8,128)S(1)} collective-permute-done((f32[32,24,4]{2,1,0:T(8,128)S(1)}, f32[32,24,4]{2,1,0:T(8,128)S(1)}, u32[]{:S(2)}, u32[]{:S(2)}) %collective-permute-start.17) | collective-permute-done | bytes 12320 | tf_op jit(solution)/shard_map/ppermute | solution.py:19
  222.2 8.7 %collective-permute-done.18 = f32[32,24,4]{2,1,0:T(8,128)S(1)} collective-permute-done((f32[32,24,4]{2,1,0:T(8,128)S(1)}, f32[32,24,4]{2,1,0:T(8,128)S(1)}, u32[]{:S(2)}, u32[]{:S(2)}) %collective-permute-start.18) | collective-permute-done | bytes 12320 | tf_op jit(solution)/shard_map/ppermute | solution.py:22
  233.8 106.6 %all-reduce.24.cloned.1.call-done = (f32[9,128,32]{1,2,0:T(8,128)}, f32[9,128,128]{2,1,0:T(8,128)}, f32[9,32,128]{2,1,0:T(8,128)}) async-done(((f32[9,128,32]{1,2,0:T(8,128)}, f32[9,128,128]{2,1,0:T(8,128)}, f32[9,32,128]{2,1,0:T(8,128)}), (f32[9,128,32]{1,2,0:T(8,128)}, f32[9,128,128]{2,1,0:T(8,128)}, f32[9,32,128]{2,1,0:T(8,128)})) %all-reduce.24.cloned.1.call-update) | async-done | bytes 884752 | tf_op jit(solution)/shard_map/psum | solution.py:229
  341.9 2.0 copy.284
  (307 shorter events, 101.0 us)
Async XLA Ops:
  7.2 333.2 %all-reduce.24.cloned.1.call-start = ((), (), s32[]{:S(2)}) async-start(), calls=%async_computation | async-start | bytes 1769472 | tf_op jit(solution)/shard_map/psum | solution.py:229
  8.5 10.9 %copy-start.18 = (s32[4,8,256]{2,1,0:T(8,128)S(1)}, s32[4,8,256]{2,1,0:T(8,128)}, u32[]{:S(2)}) copy-start(s32[4,8,256]{2,1,0:T(8,128)} %param.18) | copy-start | bytes 98308
  22.0 9.2 %copy-start.7 = (bf16[32,8,256]{2,1,0:T(8,128)(2,1)S(1)}, bf16[32,8,256]{2,1,0:T(8,128)(2,1)}, u32[]{:S(2)}) copy-start(bf16[32,8,256]{2,1,0:T(8,128)(2,1)} %param.12) | copy-start | bytes 393220
  28.0 4.4 %collective-permute-start = (f32[1,4,264]{2,1,0:T(4,128)S(1)}, f32[1,4,264]{2,1,0:T(4,128)S(1)}, u32[]{:S(2)}, u32[]{:S(2)}) collective-permute-start(f32[1,4,264]{2,1,0:T(4,128)S(1)} %get-tuple-element.260), channel_id=1, source_target_pairs={{0,4},{4,8},{8,12},{12,16},{16,20},{20,24},{24,28},{28,0},{1,5},{5... | collective-permute-start | bytes 12680 | tf_op jit(solution)/shard_map/ppermute | solution.py:19
  28.4 4.1 %collective-permute-start.1 = (f32[1,4,264]{2,1,0:T(4,128)S(1)}, f32[1,4,264]{2,1,0:T(4,128)S(1)}, u32[]{:S(2)}, u32[]{:S(2)}) collective-permute-start(f32[1,4,264]{2,1,0:T(4,128)S(1)} %get-tuple-element.261), channel_id=1, source_target_pairs={{4,0},{8,4},{12,8},{16,12},{20,16},{24,20},{28,24},{0,28},{5,1},{9... | collective-permute-start | bytes 12680 | tf_op jit(solution)/shard_map/ppermute | solution.py:22
  31.2 11.1 %collective-permute-start.10 = (bf16[32,4,256]{2,1,0:T(4,128)(2,1)S(1)}, bf16[32,4,256]{2,1,0:T(4,128)(2,1)S(1)}, u32[]{:S(2)}, u32[]{:S(2)}) collective-permute-start(bf16[32,4,256]{2,1,0:T(4,128)(2,1)S(1)} %get-tuple-element.250), channel_id=1, source_target_pairs={{4,0},{8,4},{12,8},{16,12},{20,16},{24,20},{28,24},{0,28},{5,1},{9... | collective-permute-start | bytes 196616 | tf_op jit(solution)/shard_map/ppermute | solution.py:22
  32.0 10.4 %collective-permute-start.9 = (bf16[32,4,256]{2,1,0:T(4,128)(2,1)S(1)}, bf16[32,4,256]{2,1,0:T(4,128)(2,1)S(1)}, u32[]{:S(2)}, u32[]{:S(2)}) collective-permute-start(bf16[32,4,256]{2,1,0:T(4,128)(2,1)S(1)} %get-tuple-element.249), channel_id=1, source_target_pairs={{0,4},{4,8},{8,12},{12,16},{16,20},{20,24},{24,28},{28,0},{1,5},{5... | collective-permute-start | bytes 196616 | tf_op jit(solution)/shard_map/ppermute | solution.py:19
  32.6 6.0 %collective-permute-start.2 = (f32[1,24,4]{2,1,0:T(8,128)S(1)}, f32[1,24,4]{2,1,0:T(8,128)S(1)}, u32[]{:S(2)}, u32[]{:S(2)}) collective-permute-start(f32[1,24,4]{2,1,0:T(8,128)S(1)} %get-tuple-element.253), channel_id=1, source_target_pairs={{0,1},{1,2},{2,3},{3,0},{4,5},{5,6},{6,7},{7,4},{8,9},{9,10},{10,1... | collective-permute-start | bytes 1160 | tf_op jit(solution)/shard_map/ppermute | solution.py:19
  34.8 4.0 %collective-permute-start.3 = (f32[1,24,4]{2,1,0:T(8,128)S(1)}, f32[1,24,4]{2,1,0:T(8,128)S(1)}, u32[]{:S(2)}, u32[]{:S(2)}) collective-permute-start(f32[1,24,4]{2,1,0:T(8,128)S(1)} %get-tuple-element.254), channel_id=1, source_target_pairs={{1,0},{2,1},{3,2},{0,3},{5,4},{6,5},{7,6},{4,7},{9,8},{10,9},{11,1... | collective-permute-start | bytes 1160 | tf_op jit(solution)/shard_map/ppermute | solution.py:22
  39.6 6.8 %collective-permute-start.4 = (bf16[32,4,256]{2,1,0:T(4,128)(2,1)S(1)}, bf16[32,4,256]{2,1,0:T(4,128)(2,1)S(1)}, u32[]{:S(2)}, u32[]{:S(2)}) collective-permute-start(bf16[32,4,256]{2,1,0:T(4,128)(2,1)S(1)} %get-tuple-element.251), channel_id=1, source_target_pairs={{0,4},{4,8},{8,12},{12,16},{16,20},{20,24},{24,28},{28,0},{1,5},{5... | collective-permute-start | bytes 196616 | tf_op jit(solution)/shard_map/ppermute | solution.py:19
  39.7 6.8 %collective-permute-start.5 = (bf16[32,4,256]{2,1,0:T(4,128)(2,1)S(1)}, bf16[32,4,256]{2,1,0:T(4,128)(2,1)S(1)}, u32[]{:S(2)}, u32[]{:S(2)}) collective-permute-start(bf16[32,4,256]{2,1,0:T(4,128)(2,1)S(1)} %get-tuple-element.252), channel_id=1, source_target_pairs={{4,0},{8,4},{12,8},{16,12},{20,16},{24,20},{28,24},{0,28},{5,1},{9... | collective-permute-start | bytes 196616 | tf_op jit(solution)/shard_map/ppermute | solution.py:22
  42.6 8.0 %collective-permute-start.11 = (bf16[32,16,4]{2,1,0:T(8,128)(2,1)S(1)}, bf16[32,16,4]{2,1,0:T(8,128)(2,1)S(1)}, u32[]{:S(2)}, u32[]{:S(2)}) collective-permute-start(bf16[32,16,4]{2,1,0:T(8,128)(2,1)S(1)} %get-tuple-element.245), channel_id=1, source_target_pairs={{0,1},{1,2},{2,3},{3,0},{4,5},{5,6},{6,7},{7,4},{8,9},{9,10},{10,1... | collective-permute-start | bytes 12296 | tf_op jit(solution)/shard_map/ppermute | solution.py:19
  44.2 9.0 %collective-permute-start.12 = (bf16[32,16,4]{2,1,0:T(8,128)(2,1)S(1)}, bf16[32,16,4]{2,1,0:T(8,128)(2,1)S(1)}, u32[]{:S(2)}, u32[]{:S(2)}) collective-permute-start(bf16[32,16,4]{2,1,0:T(8,128)(2,1)S(1)} %get-tuple-element.246), channel_id=1, source_target_pairs={{1,0},{2,1},{3,2},{0,3},{5,4},{6,5},{7,6},{4,7},{9,8},{10,9},{11,1... | collective-permute-start | bytes 12296 | tf_op jit(solution)/shard_map/ppermute | solution.py:22
  46.7 8.6 %collective-permute-start.6 = (bf16[32,16,4]{2,1,0:T(8,128)(2,1)S(1)}, bf16[32,16,4]{2,1,0:T(8,128)(2,1)S(1)}, u32[]{:S(2)}, u32[]{:S(2)}) collective-permute-start(bf16[32,16,4]{2,1,0:T(8,128)(2,1)S(1)} %get-tuple-element.247), channel_id=1, source_target_pairs={{0,1},{1,2},{2,3},{3,0},{4,5},{5,6},{6,7},{7,4},{8,9},{9,10},{10,1... | collective-permute-start | bytes 12296 | tf_op jit(solution)/shard_map/ppermute | solution.py:19
  46.8 9.4 %collective-permute-start.7 = (bf16[32,16,4]{2,1,0:T(8,128)(2,1)S(1)}, bf16[32,16,4]{2,1,0:T(8,128)(2,1)S(1)}, u32[]{:S(2)}, u32[]{:S(2)}) collective-permute-start(bf16[32,16,4]{2,1,0:T(8,128)(2,1)S(1)} %get-tuple-element.248), channel_id=1, source_target_pairs={{1,0},{2,1},{3,2},{0,3},{5,4},{6,5},{7,6},{4,7},{9,8},{10,9},{11,1... | collective-permute-start | bytes 12296 | tf_op jit(solution)/shard_map/ppermute | solution.py:22
  58.0 9.3 %collective-permute-start.8 = (bf16[2,32,8,256]{3,2,1,0:T(8,128)(2,1)S(1)}, bf16[2,32,8,256]{3,2,1,0:T(8,128)(2,1)S(1)}, u32[]{:S(2)}, u32[]{:S(2)}) collective-permute-start(bf16[2,32,8,256]{3,2,1,0:T(8,128)(2,1)S(1)} %maximum_select_fusion.3), channel_id=1, source_target_pairs={{0,16},{4,20},{8,24},{12,28},{16,0},{20,4},{24,8},{28,12},{1,17},{... | collective-permute-start | bytes 786440 | tf_op jit(solution)/shard_map/ppermute | solution.py:30
  60.0 10.8 %collective-permute-start.13 = (bf16[2,32,8,256]{3,2,1,0:T(8,128)(2,1)S(1)}, bf16[2,32,8,256]{3,2,1,0:T(8,128)(2,1)S(1)}, u32[]{:S(2)}, u32[]{:S(2)}) collective-permute-start(bf16[2,32,8,256]{3,2,1,0:T(8,128)(2,1)S(1)} %maximum_select_fusion.4), channel_id=1, source_target_pairs={{0,16},{4,20},{8,24},{12,28},{16,0},{20,4},{24,8},{28,12},{1,17},{... | collective-permute-start | bytes 786440 | tf_op jit(solution)/shard_map/ppermute | solution.py:30
  145.0 13.3 %copy-start.1 = (f32[9,128,128]{2,1,0:T(8,128)}, f32[9,128,128]{2,1,0:T(8,128)S(1)}, u32[]{:S(2)}) copy-start(f32[9,128,128]{2,1,0:T(8,128)S(1)} %get-tuple-element.135) | copy-start | bytes 1769476
  145.0 13.3 %copy-start.3 = (f32[9,128,32]{1,2,0:T(8,128)}, f32[9,128,32]{1,2,0:T(8,128)S(1)}, u32[]{:S(2)}) copy-start(f32[9,128,32]{1,2,0:T(8,128)S(1)} %get-tuple-element.134) | copy-start | bytes 442372
  145.0 12.0 %collective-permute-start.14 = (f32[2,32,8,256]{3,2,1,0:T(8,128)}, f32[2,32,8,256]{3,2,1,0:T(8,128)S(1)}, u32[]{:S(2)}, u32[]{:S(2)}) collective-permute-start(f32[2,32,8,256]{3,2,1,0:T(8,128)} %get-tuple-element.133), channel_id=1, source_target_pairs={{0,16},{4,20},{8,24},{12,28},{16,0},{20,4},{24,8},{28,12},{1,17},{... | collective-permute-start | bytes 1572872 | tf_op jit(solution)/shard_map/ppermute | solution.py:30
  200.5 6.0 %collective-permute-start.15 = (f32[32,4,264]{2,1,0:T(4,128)S(1)}, f32[32,4,264]{2,1,0:T(4,128)S(1)}, u32[]{:S(2)}, u32[]{:S(2)}) collective-permute-start(f32[32,4,264]{2,1,0:T(4,128)S(1)} %get-tuple-element.239), channel_id=1, source_target_pairs={{0,4},{4,8},{8,12},{12,16},{16,20},{20,24},{24,28},{28,0},{1,5},{5... | collective-permute-start | bytes 405512 | tf_op jit(solution)/shard_map/ppermute | solution.py:19
  200.6 6.0 %collective-permute-start.16 = (f32[32,4,264]{2,1,0:T(4,128)S(1)}, f32[32,4,264]{2,1,0:T(4,128)S(1)}, u32[]{:S(2)}, u32[]{:S(2)}) collective-permute-start(f32[32,4,264]{2,1,0:T(4,128)S(1)} %get-tuple-element.240), channel_id=1, source_target_pairs={{4,0},{8,4},{12,8},{16,12},{20,16},{24,20},{28,24},{0,28},{5,1},{9... | collective-permute-start | bytes 405512 | tf_op jit(solution)/shard_map/ppermute | solution.py:22
  206.8 14.7 %collective-permute-start.17 = (f32[32,24,4]{2,1,0:T(8,128)S(1)}, f32[32,24,4]{2,1,0:T(8,128)S(1)}, u32[]{:S(2)}, u32[]{:S(2)}) collective-permute-start(f32[32,24,4]{2,1,0:T(8,128)S(1)} %get-tuple-element.237), channel_id=1, source_target_pairs={{0,1},{1,2},{2,3},{3,0},{4,5},{5,6},{6,7},{7,4},{8,9},{9,10},{10,1... | collective-permute-start | bytes 36872 | tf_op jit(solution)/shard_map/ppermute | solution.py:19
  209.1 21.9 %collective-permute-start.18 = (f32[32,24,4]{2,1,0:T(8,128)S(1)}, f32[32,24,4]{2,1,0:T(8,128)S(1)}, u32[]{:S(2)}, u32[]{:S(2)}) collective-permute-start(f32[32,24,4]{2,1,0:T(8,128)S(1)} %get-tuple-element.238), channel_id=1, source_target_pairs={{1,0},{2,1},{3,2},{0,3},{5,4},{6,5},{7,6},{4,7},{9,8},{10,9},{11,1... | collective-permute-start | bytes 36872 | tf_op jit(solution)/shard_map/ppermute | solution.py:22
  (24 other events, 43.5 us)
Sparse Core Ops, SparseCore 0:
  209.2 131.0 all-reduce.23
where the time goes:
time: 354 us; the launch traced here: 351 us
  waiting for transfers between devices  157 us (44%)
  local copies, waits for them, and re-layouts  62.7 us (18%)
  matrix products  60.3 us (17%)
  between operations  30.5 us (9%)
  starting transfers between devices  28.8 us (8%)
  other arithmetic  10.7 us (3%)
    psum x1, waiting for transfers between devices, shards(): summed_grads = lax.psum((totals[0], totals[1], totals[2]), ('lat', 'lon'))  107 us
    dynamic_update_slice x8, local copies, waits for them, and re-layouts, place_slots(): lax.dynamic_update_slice(canvas, current + per_slot[slot_index], corner)  43.7 us
    dot_general x54, matrix products, kernel_grad(): jnp.einsum('ohw,khw->ok', cotangent, padded[:, tap_row:tap_row + height,...  25.4 us
    dot_general x54, matrix products, forward_conv(): jnp.einsum('ok,khw->ohw', kernel[tap_index], padded[:, tap_row:tap_row +...  21.3 us
    ppermute x3, waiting for transfers between devices, shifted(): return lax.ppermute(value, axis, pairs)  20.1 us
    ppermute x8, starting transfers between devices, extended_2(): lax.ppermute(lax.slice_in_dim(block, 0, width, axis=dim), axis, backward)  18.6 us
    ppermute x8, waiting for transfers between devices, extended_2(): lax.ppermute(lax.slice_in_dim(block, block.shape[dim] - width, None, axis...  18.3 us
    dot_general x36, matrix products, backward_conv(): jnp.einsum('ok,ohw->khw', kernel[tap_index], padded[:, 2 - tap_row:2 - ta...  13.6 us
  transfers between devices with their start and end apart: 20, of which 14 were waited for; matrix products, arithmetic and copies ran while one was open for 1% of the time, Pallas kernels for 0%

commit v1 on v0

v1 whole, which is shorter than its diff:
```python
import functools

import jax
import jax.numpy as jnp
from jax import lax
from jax.experimental import pallas as pl
from jax.experimental.pallas import tpu as pltpu
from jax.sharding import PartitionSpec as P

MARGIN = 4
SLOTS = 4
LANES = 128
F32 = jnp.float32
BF16 = jnp.bfloat16
VMEM_LIMIT = 48 * 1024 * 1024


def vmem():
    return pl.BlockSpec(memory_space=pltpu.VMEM)


def smem():
    return pl.BlockSpec(memory_space=pltpu.SMEM)


def lane_ids(shape):
    return lax.broadcasted_iota(jnp.int32, shape, len(shape) - 1)


def roll(value, shift, axis):
    size = value.shape[axis]
    if isinstance(shift, int):
        shift = shift % size
        if shift == 0:
            return value
    return pltpu.roll(value, shift, axis)


def pack_kernel(anchors, counts, fields, cotangent, weights, center, to_up, to_down, edges, canvas, spread):
    channels, rows, cols = fields.shape
    wide = cols + LANES
    spread[...] = jnp.zeros_like(spread)
    for slot in range(SLOTS):

        @pl.when(slot < counts[0, 0])
        def _():
            row = anchors[0, 0, slot, 0]
            col = anchors[0, 0, slot, 1]
            values = weights[slot].astype(F32)
            values = jnp.concatenate([values, jnp.zeros((rows, LANES), F32)], axis=1)
            values = jnp.concatenate([values, jnp.zeros((2 * MARGIN, wide), F32)], axis=0)
            values = roll(values, lax.rem(col + (wide - MARGIN), wide), 1)
            values = roll(values, row, 0)
            spread[...] += values

    total = spread[...]
    canvas[...] = total
    both = []
    for source in (fields, cotangent):
        both.append(jnp.swapaxes(source[...].astype(F32), 0, 1))
    tile = jnp.concatenate(both, axis=1)
    center[...] = tile.astype(BF16)
    to_up[0:MARGIN] = tile[:MARGIN].astype(BF16)
    to_down[0:MARGIN] = tile[rows - MARGIN :].astype(BF16)
    lanes = lane_ids((2 * channels, LANES))
    packed = jnp.zeros((2 * channels, LANES), F32)
    for row in range(rows):
        first = jnp.where(lanes < MARGIN, tile[row, :, :LANES], 0.0)
        last = jnp.where(lanes >= LANES - MARGIN, tile[row, :, cols - LANES :], 0.0)
        packed = packed + roll(first, MARGIN * row, 1) + roll(last, -MARGIN * row, 1)
    edges[0 : 2 * channels] = packed.astype(BF16)
    first = total[:, :LANES]
    last = total[:, cols - LANES : cols]
    margin = total[:, cols:]
    lanes = lane_ids(margin.shape)
    height = margin.shape[0]
    to_left = jnp.where(lanes < LANES // 2, first, margin)
    to_right = jnp.where(lanes < LANES // 2, margin, last)
    edges[2 * channels : 2 * channels + height] = to_left.astype(BF16)
    edges[2 * channels + height : 2 * channels + 2 * height] = to_right.astype(BF16)
    half = height // 2
    pad = jnp.zeros((2 * channels - height, cols), F32)
    for target, part in ((to_up, total[:half]), (to_down, total[half:])):
        beside = jnp.concatenate([part[:, cols:], jnp.zeros((half, cols - LANES), F32)], axis=1)
        extra = jnp.concatenate([part[:, :cols], beside, pad], axis=0)
        target[MARGIN] = extra.astype(BF16)


def dot(left, right):
    return jnp.dot(left, right, preferred_element_type=F32)


def dot_lanes(left, right):
    return lax.dot_general(left, right, (((1,), (1,)), ((), ())), preferred_element_type=F32)


def patch_kernel(
    anchors, counts, center, up, down, left, right, up_left, up_right, down_left, down_right, canvas, weights,
    w_in, w_mid, w_mid_back, w_out, w_out_back,
    grads, inner, to_up, to_down, edges, den_out,
    window, numer, x_s, d_s, h_s, z_s, slope_s, dh_s, h2_s, dz_s, y_s,
):
    rows = center.shape[0]
    channels = center.shape[1] // 2
    cols = center.shape[2]
    wide = cols + LANES
    width = w_mid.shape[0]
    full = rows * cols
    height = rows + 2 * MARGIN
    half = height // 2
    lanes = lane_ids((2 * channels, LANES))

    total = canvas[...]
    upper = up[MARGIN].astype(F32)
    lower = down[MARGIN].astype(F32)

    def stretch(block):
        return jnp.concatenate([block[:half], block[half:height, :LANES]], axis=1)

    total = total + jnp.concatenate([stretch(upper), stretch(lower)], axis=0)
    base = 2 * channels
    left_part = left[base + height : base + 2 * height].astype(F32)
    left_part = left_part + jnp.concatenate(
        [
            up_left[base + height : base + 2 * height].astype(F32)[half:],
            down_left[base + height : base + 2 * height].astype(F32)[:half],
        ],
        axis=0,
    )
    right_part = right[base : base + height].astype(F32)
    right_part = right_part + jnp.concatenate(
        [
            up_right[base : base + height].astype(F32)[half:],
            down_right[base : base + height].astype(F32)[:half],
        ],
        axis=0,
    )
    edge_lanes = lane_ids((height, LANES))
    low = edge_lanes < MARGIN
    high = edge_lanes >= LANES - MARGIN
    zero = jnp.zeros((height, LANES), F32)
    pieces = [jnp.where(low, left_part, zero)]
    for _ in range(cols // LANES - 2):
        pieces.append(zero)
    pieces.append(jnp.where(high, right_part, zero))
    pieces.append(jnp.where(high, left_part, zero) + jnp.where(low, right_part, zero))
    den = jnp.maximum(total + jnp.concatenate(pieces, axis=1), 1.0)
    den_out[...] = den[MARGIN : MARGIN + rows, :cols]
    inverse = 1.0 / den

    left_e = left[0:base].astype(F32)
    right_e = right[0:base].astype(F32)
    up_left_e = up_left[0:base].astype(F32)
    up_right_e = up_right[0:base].astype(F32)
    down_left_e = down_left[0:base].astype(F32)
    down_right_e = down_right[0:base].astype(F32)
    for row in range(height):
        if row < MARGIN:
            body, from_left, from_right, at = up[row], up_left_e, up_right_e, rows - MARGIN + row
        elif row < MARGIN + rows:
            body, from_left, from_right, at = center[row - MARGIN], left_e, right_e, row - MARGIN
        else:
            body, from_left, from_right, at = down[row - MARGIN - rows], down_left_e, down_right_e, row - MARGIN - rows
        beside = jnp.where(
            lanes < LANES // 2, roll(from_right, -MARGIN * at, 1), roll(from_left, MARGIN * at, 1)
        )
        line = jnp.concatenate([body.astype(F32), beside], axis=1)
        scaled = line[channels:] * inverse[row : row + 1]
        window[row, 0:channels] = line[:channels]
        window[row, channels : 2 * channels] = scaled.astype(BF16).astype(F32)

    numer[...] = jnp.zeros_like(numer)
    grads[...] = jnp.zeros_like(grads)
    for ref in (x_s, d_s, h_s, z_s):
        ref[:, 0:cols] = jnp.zeros((ref.shape[0], cols), BF16)
        ref[:, cols + full : 2 * cols + full] = jnp.zeros((ref.shape[0], cols), BF16)
    y_s[:, 0:cols] = jnp.zeros((y_s.shape[0], cols), F32)
    y_s[:, cols + full : 2 * cols + full] = jnp.zeros((y_s.shape[0], cols), F32)

    def before(value):
        ids = lane_ids(value.shape)
        return jnp.where(ids == 0, 0.0, roll(value, 1, 1))

    def after(value):
        ids = lane_ids(value.shape)
        return jnp.where(ids == cols - 1, 0.0, roll(value, cols - 1, 1))

    def spread(ref, value, row, flip):
        count = value.shape[0]
        at = slice((row + 1) * cols, (row + 2) * cols)
        first, last = before(value), after(value)
        if flip:
            first, last = last, first
        ref[0:count, at] = first.astype(BF16)
        ref[count : 2 * count, at] = value.astype(BF16)
        ref[2 * count : 3 * count, at] = last.astype(BF16)

    def stack(ref, row, flip):
        starts = [(row + (2 - tap if flip else tap)) * cols for tap in range(3)]
        return jnp.concatenate([ref[:, start : start + cols] for start in starts], axis=0)

    def one_patch(slot, carry):
        row0 = anchors[0, 0, slot, 0]
        col0 = anchors[0, 0, slot, 1]
        patch_weights = weights[slot].astype(F32)
        back_shift = lax.rem(wide + MARGIN - col0, wide)
        for row in range(rows):
            line = roll(window[row0 + row], back_shift, 1)[:, :cols]
            spread(x_s, line[:channels], row, False)
            grad = line[channels:] * patch_weights[row : row + 1]
            spread(d_s, grad.astype(BF16).astype(F32), row, True)
        for row in range(rows):
            at = slice(row * cols, (row + 1) * cols)
            z1 = dot(w_in[...], stack(x_s, row, False))
            sig = 0.5 * jnp.tanh(0.5 * z1) + 0.5
            h1 = (z1 * sig).astype(BF16).astype(F32)
            slope_s[:, at] = sig * (1.0 + z1 * (1.0 - sig))
            spread(h_s, h1, row, False)
        for row in range(rows):
            at = slice(row * cols, (row + 1) * cols)
            dh2 = dot(w_out_back[...], stack(d_s, row, True))
            z2 = dot(w_mid[...], stack(h_s, row, False))
            sig = 0.5 * jnp.tanh(0.5 * z2) + 0.5
            h1 = h_s[width : 2 * width, (row + 1) * cols : (row + 2) * cols].astype(F32)
            h2 = (h1 + z2 * sig).astype(BF16)
            h2_s[:, at] = h2
            dz2 = (dh2 * (sig * (1.0 + z2 * (1.0 - sig)))).astype(BF16).astype(F32)
            dh_s[:, at] = dh2
            spread(z_s, dz2, row, True)
            y_s[:, (row + 1) * cols : (row + 2) * cols] = dot(w_out[...], h2)
        for row in range(rows):
            at = slice(row * cols, (row + 1) * cols)
            dh1 = dh_s[:, at] + dot(w_mid_back[...], stack(z_s, row, True))
            dz_s[:, at] = (dh1 * slope_s[:, at]).astype(BF16)
        small = 9 * channels
        for tap in range(3):
            ahead = slice(tap * cols, tap * cols + full)
            behind = slice((2 - tap) * cols, (2 - tap) * cols + full)
            at = slice(tap * 3 * channels, (tap + 1) * 3 * channels)
            grads[at] += dot_lanes(x_s[:, ahead], dz_s[...])
            part = dot_lanes(z_s[width : 2 * width, cols : cols + full], h_s[:, ahead])
            for tap_col in range(3):
                start = small + (3 * tap + tap_col) * width
                grads[start : start + width] += part[:, tap_col * width : (tap_col + 1) * width]
            at = slice(small + 9 * width + tap * 3 * channels, small + 9 * width + (tap + 1) * 3 * channels)
            grads[at] += dot_lanes(d_s[:, behind], h2_s[...])
        for row in range(rows):
            sums = []
            for tap_col in range(3):
                terms = [
                    y_s[
                        (3 * tap + tap_col) * channels : (3 * tap + tap_col + 1) * channels,
                        (row + tap) * cols : (row + tap + 1) * cols,
                    ]
                    for tap in range(3)
                ]
                sums.append(terms[0] + terms[1] + terms[2])
            result = before(sums[0]) + sums[1] + after(sums[2])
            result = result * patch_weights[row : row + 1]
            result = jnp.concatenate([result, jnp.zeros((channels, LANES), F32)], axis=1)
            numer[row0 + row] += roll(result, lax.rem(col0 + (wide - MARGIN), wide), 1)
        return carry

    lax.fori_loop(0, counts[0, 0], one_patch, 0)

    lanes = lane_ids((channels, LANES))
    packed = jnp.zeros((channels, LANES), F32)
    for row in range(height):
        beside = numer[row, :, cols:]
        first = jnp.where(lanes < MARGIN, beside, 0.0)
        last = jnp.where(lanes >= LANES - MARGIN, beside, 0.0)
        packed = packed + roll(first, MARGIN * row, 1) + roll(last, -MARGIN * row, 1)
    edges[...] = packed
    to_up[...] = numer[0:MARGIN, :, :cols]
    inner[...] = numer[MARGIN : MARGIN + rows, :, :cols]
    to_down[...] = numer[MARGIN + rows :, :, :cols]


def fold_kernel(
    inner, up, down, left, right, up_left, up_right, down_left, down_right, den, blended
):
    rows, channels, cols = inner.shape
    lanes = lane_ids((channels, LANES))
    inverse = 1.0 / den[...]
    lines = []
    for row in range(rows):
        line = inner[row]
        from_left = jnp.where(lanes < MARGIN, roll(left[...], -MARGIN * (row + MARGIN), 1), 0.0)
        from_right = jnp.where(lanes >= LANES - MARGIN, roll(right[...], MARGIN * (row + MARGIN), 1), 0.0)
        if row < MARGIN:
            line = line + up[row]
            at = MARGIN * (row + MARGIN + rows)
            more_left, more_right = up_left, up_right
        else:
            line = line + down[row - (rows - MARGIN)]
            at = MARGIN * (row - (rows - MARGIN))
            more_left, more_right = down_left, down_right
        from_left = from_left + jnp.where(lanes < MARGIN, roll(more_left[...], -at, 1), 0.0)
        from_right = from_right + jnp.where(lanes >= LANES - MARGIN, roll(more_right[...], at, 1), 0.0)
        beside = [from_left]
        for _ in range(cols // LANES - 2):
            beside.append(jnp.zeros((channels, LANES), F32))
        beside.append(from_right)
        line = line + jnp.concatenate(beside, axis=1)
        lines.append((line * inverse[row : row + 1])[None])
    blended[...] = jnp.swapaxes(jnp.concatenate(lines, axis=0), 0, 1)


def split_kernel(summed, grad_in, grad_mid, grad_out):
    taps, width, channels = grad_in.shape
    for tap in range(taps):
        grad_in[tap] = summed[tap * channels : (tap + 1) * channels].astype(F32).T
        start = taps * channels + tap * width
        grad_mid[tap] = summed[start : start + width].astype(F32)
        start = taps * (channels + width) + tap * channels
        grad_out[tap] = summed[start : start + channels].astype(F32)


def params():
    return pltpu.CompilerParams(vmem_limit_bytes=VMEM_LIMIT)


def shift(value, lat_step, lon_step):
    lat_size, lon_size = lax.axis_size("lat"), lax.axis_size("lon")
    pairs = []
    for lat in range(lat_size):
        for lon in range(lon_size):
            if 0 <= lat + lat_step < lat_size:
                target = (lat + lat_step) * lon_size + (lon + lon_step) % lon_size
                pairs.append((lat * lon_size + lon, target))
    return lax.ppermute(value, ("lat", "lon"), pairs)


def neighbours(to_up, to_down, edges):
    up = shift(to_down, 1, 0)
    down = shift(to_up, -1, 0)
    left = shift(edges, 0, 1)
    right = shift(edges, 0, -1)
    up_left = shift(edges, 1, 1)
    down_right = shift(edges, -1, -1)
    up_right = shift(edges, 1, -1)
    down_left = shift(edges, -1, 1)
    return up, down, left, right, up_left, up_right, down_left, down_right


def reduce_all(grads):
    lat_size, lon_size = lax.axis_size("lat"), lax.axis_size("lon")
    length = grads.shape[0]
    parts = grads.astype(BF16).reshape(lat_size, length // lat_size, LANES)
    parts = lax.all_to_all(parts, "lat", 0, 0)
    mine = jnp.sum(parts.astype(F32), axis=0)
    parts = mine.reshape(lon_size, length // (lat_size * lon_size), LANES)
    parts = lax.all_to_all(parts, "lon", 0, 0)
    mine = jnp.sum(parts, axis=0).astype(BF16)
    parts = jnp.broadcast_to(mine[None], (lon_size,) + mine.shape)
    parts = lax.all_to_all(parts, "lon", 0, 0)
    mine = parts.reshape(length // lat_size, LANES)
    parts = jnp.broadcast_to(mine[None], (lat_size,) + mine.shape)
    parts = lax.all_to_all(parts, "lat", 0, 0)
    return parts.reshape(length, LANES)


def shards(
    fields, cotangent, kernel_in, kernel_mid, kernel_out, patch_anchors, blend_weights, tile_counts
):
    channels, rows, cols = fields.shape
    taps, width, _ = kernel_in.shape
    height = rows + 2 * MARGIN
    wide = cols + LANES
    full = rows * cols
    padded = full + 2 * cols
    shape = jax.ShapeDtypeStruct
    center, to_up, to_down, edges, canvas = pl.pallas_call(
        pack_kernel,
        out_shape=(
            shape((rows, 2 * channels, cols), BF16),
            shape((MARGIN + 1, 2 * channels, cols), BF16),
            shape((MARGIN + 1, 2 * channels, cols), BF16),
            shape((2 * channels + 2 * height, LANES), BF16),
            shape((height, wide), F32),
        ),
        in_specs=[smem(), smem(), vmem(), vmem(), vmem()],
        out_specs=(vmem(),) * 5,
        scratch_shapes=[pltpu.VMEM((height, wide), F32)],
        compiler_params=params(),
        name="pack",
    )(patch_anchors, tile_counts, fields, cotangent, blend_weights)
    received = neighbours(to_up, to_down, edges)

    w_in = jnp.transpose(kernel_in, (1, 0, 2)).reshape(width, taps * channels)
    w_mid = jnp.transpose(kernel_mid, (1, 0, 2)).reshape(width, taps * width)
    w_mid_back = jnp.transpose(kernel_mid, (2, 0, 1)).reshape(width, taps * width)
    w_out = kernel_out.reshape(taps * channels, width)
    w_out_back = jnp.transpose(kernel_out, (2, 0, 1)).reshape(width, taps * channels)

    length = taps * (2 * channels + width)
    unit = 8 * lax.axis_size("lat") * lax.axis_size("lon")
    length = (length + unit - 1) // unit * unit
    grads, inner, out_up, out_down, out_edges, den = pl.pallas_call(
        patch_kernel,
        out_shape=(
            shape((length, LANES), F32),
            shape((rows, channels, cols), F32),
            shape((MARGIN, channels, cols), F32),
            shape((MARGIN, channels, cols), F32),
            shape((channels, LANES), F32),
            shape((rows, cols), F32),
        ),
        in_specs=[smem(), smem()] + [vmem()] * 16,
        out_specs=(vmem(),) * 6,
        scratch_shapes=[
            pltpu.VMEM((height, 2 * channels, wide), F32),
            pltpu.VMEM((height, channels, wide), F32),
            pltpu.VMEM((3 * channels, padded), BF16),
            pltpu.VMEM((3 * channels, padded), BF16),
            pltpu.VMEM((3 * width, padded), BF16),
            pltpu.VMEM((3 * width, padded), BF16),
            pltpu.VMEM((width, full), F32),
            pltpu.VMEM((width, full), F32),
            pltpu.VMEM((width, full), BF16),
            pltpu.VMEM((width, full), BF16),
            pltpu.VMEM((taps * channels, padded), F32),
        ],
        compiler_params=params(),
        name="patches",
    )(
        patch_anchors, tile_counts, center, *received, canvas, blend_weights,
        w_in, w_mid, w_mid_back, w_out, w_out_back,
    )
    summed = reduce_all(grads)
    returned = neighbours(out_up, out_down, out_edges)
    blended = pl.pallas_call(
        fold_kernel,
        out_shape=shape((channels, rows, cols), F32),
        in_specs=[vmem()] * 10,
        out_specs=vmem(),
        compiler_params=params(),
        name="fold",
    )(inner, *returned, den)
    grad_in, grad_mid, grad_out = pl.pallas_call(
        split_kernel,
        out_shape=(
            shape((taps, width, channels), F32),
            shape((taps, width, width), F32),
            shape((taps, channels, width), F32),
        ),
        in_specs=[vmem()],
        out_specs=(vmem(),) * 3,
        compiler_params=params(),
        name="split",
    )(summed)
    return blended, grad_in, grad_mid, grad_out


def solution(mesh):
    return jax.shard_map(
        shards,
        mesh=mesh,
        in_specs=(
            P(None, "lat", "lon"),
            P(None, "lat", "lon"),
            P(),
            P(),
            P(),
            P("lat", "lon", None, None),
            P(None, "lat", "lon"),
            P("lat", "lon"),
        ),
        out_specs=(P(None, "lat", "lon"), P(), P(), P()),
        check_vma=False,
    )
```

time: 354 us -> 121 us (0.34)
  waiting for transfers between devices: 157 us -> 9.31 us
  matrix products: 60.3 us -> 0 us
  local copies, waits for them, and re-layouts: 62.7 us -> 6.2 us
  blocking collectives: 0 us -> 38.7 us
  between operations: 30.5 us -> 1.54 us
  starting transfers between devices: 28.8 us -> 48.6 us
  Pallas kernels: 0 us -> 15.2 us
  other arithmetic: 10.7 us -> 0.12 us
    psum x1 -> x0, waiting for transfers between devices: 107 us -> none  [shards(): summed_grads = lax.psum((totals[0], totals[1], totals[2]), ('lat', 'lon'))]
    dot_general x144 -> x0, matrix products: 60.3 us -> none  [the longest x54 25.4 us: kernel_grad(): jnp.einsum('ohw,khw->ok', cotangent, padded[:, tap_row:tap_row + height,...]
    dynamic_update_slice x10 -> x0, local copies, waits for them, and re-layouts: 44 us -> none  [the longest x8 43.7 us: place_slots(): lax.dynamic_update_slice(canvas, current + per_slot[slot_index], corner)]
    ppermute x19 -> x16, waiting for transfers between devices: 50.9 us -> 9.3 us  [shift(): return lax.ppermute(value, ('lat', 'lon'), pairs)]
    all_to_all x0 -> x3, blocking collectives: none -> 38.7 us  [the longest x1 22.3 us: reduce_all(): parts = lax.all_to_all(parts, 'lat', 0, 0)]
    ppermute x19 -> x16, starting transfers between devices: 28.8 us -> 45.1 us  [shift(): return lax.ppermute(value, ('lat', 'lon'), pairs)]
    pallas_call x0 -> x4, Pallas kernels: none -> 15.2 us  [the longest x1 12.2 us: shards(): pl.pallas_call(patch_kernel, out_shape=(shape((length, LANES), F32), shap...]
    while x20 -> x0, local copies, waits for them, and re-layouts: 5.22 us -> none
  transfers between devices with their start and end apart: 20 -> 17, of which waited for: 14 -> 3; matrix products, arithmetic and copies ran while one was open for 1% -> 2% of each run, Pallas kernels for 0% -> 1%
where the time goes in v1:
time: 121 us; the launch traced here: 120 us
  starting transfers between devices  48.6 us (40%)
  blocking collectives  38.7 us (32%)
  Pallas kernels  15.2 us (13%)
  waiting for transfers between devices  9.31 us (8%)
  local copies, waits for them, and re-layouts  6.2 us (5%)
  between operations  1.54 us (1%)
    ppermute x16, starting transfers between devices, shift(): return lax.ppermute(value, ('lat', 'lon'), pairs)  45.1 us
    all_to_all x1, blocking collectives, reduce_all(): parts = lax.all_to_all(parts, 'lat', 0, 0)  22.3 us
    all_to_all x2, blocking collectives, reduce_all(): parts = lax.all_to_all(parts, 'lon', 0, 0)  16.4 us
    pallas_call x1, Pallas kernels, shards(): pl.pallas_call(patch_kernel, out_shape=(shape((length, LANES), F32), shap...  12.2 us
    ppermute x16, waiting for transfers between devices, shift(): return lax.ppermute(value, ('lat', 'lon'), pairs)  9.3 us
    unnamed x17, local copies, waits for them, and re-layouts  3.78 us
    all_to_all x1, starting transfers between devices, reduce_all(): parts = lax.all_to_all(parts, 'lat', 0, 0)  3.47 us
  transfers between devices with their start and end apart: 17, of which 3 were waited for; matrix products, arithmetic and copies ran while one was open for 2% of the time, Pallas kernels for 1%

profile of v1, /device:TPU:0, one launch (start us, length us, event | category | flops | bytes accessed | tf_op | source)
XLA Modules:
  0.0 119.6 jit_solution(10738230479346578131)
XLA Ops:
  5.0 2.5 %collective-permute-start = (bf16[5,64,256]{2,1,0:T(8,128)(2,1)S(1)}, bf16[5,64,256]{2,1,0:T(8,128)(2,1)S(1)}, u32[]{:S(2)}, u32[]{:S(2)}) collective-permute-start(bf16[5,64,256]{2,1,0:T(8,128)(2,1)S(1)} %get-tuple-element.19), channel_id=1, source_target_pairs={{0,4},{1,5},{2,6},{3,7},{4,8},{5,9},{6,10},{7,11},{8,12},{9,13},{1... | collective-permute-start | bytes 491528 | tf_op jit(solution)/shard_map/ppermute | solution.py:331
  7.5 1.3 %collective-permute-start.1 = (bf16[5,64,256]{2,1,0:T(8,128)(2,1)S(1)}, bf16[5,64,256]{2,1,0:T(8,128)(2,1)S(1)}, u32[]{:S(2)}, u32[]{:S(2)}) collective-permute-start(bf16[5,64,256]{2,1,0:T(8,128)(2,1)S(1)} %get-tuple-element.20), channel_id=1, source_target_pairs={{4,0},{5,1},{6,2},{7,3},{8,4},{9,5},{10,6},{11,7},{12,8},{13,9},{1... | collective-permute-start | bytes 491528 | tf_op jit(solution)/shard_map/ppermute | solution.py:331
  8.8 1.3 %collective-permute-start.7 = (bf16[96,128]{1,0:T(8,128)(2,1)S(1)}, bf16[96,128]{1,0:T(8,128)(2,1)S(1)}, u32[]{:S(2)}, u32[]{:S(2)}) collective-permute-start(bf16[96,128]{1,0:T(8,128)(2,1)S(1)} %get-tuple-element.21), channel_id=1, source_target_pairs={{4,3},{5,0},{6,1},{7,2},{8,7},{9,4},{10,5},{11,6},{12,11},{13,8},{... | collective-permute-start | bytes 73736 | tf_op jit(solution)/shard_map/ppermute | solution.py:331
  10.1 1.3 %collective-permute-start.6 = (bf16[96,128]{1,0:T(8,128)(2,1)S(1)}, bf16[96,128]{1,0:T(8,128)(2,1)S(1)}, u32[]{:S(2)}, u32[]{:S(2)}) collective-permute-start(bf16[96,128]{1,0:T(8,128)(2,1)S(1)} %get-tuple-element.21), channel_id=1, source_target_pairs={{4,1},{5,2},{6,3},{7,0},{8,5},{9,6},{10,7},{11,4},{12,9},{13,10},{... | collective-permute-start | bytes 73736 | tf_op jit(solution)/shard_map/ppermute | solution.py:331
  11.4 9.5 %collective-permute-start.5 = (bf16[96,128]{1,0:T(8,128)(2,1)S(1)}, bf16[96,128]{1,0:T(8,128)(2,1)S(1)}, u32[]{:S(2)}, u32[]{:S(2)}) collective-permute-start(bf16[96,128]{1,0:T(8,128)(2,1)S(1)} %get-tuple-element.21), channel_id=1, source_target_pairs={{0,7},{1,4},{2,5},{3,6},{4,11},{5,8},{6,9},{7,10},{8,15},{9,12},{1... | collective-permute-start | bytes 73736 | tf_op jit(solution)/shard_map/ppermute | solution.py:331
  20.9 4.5 %collective-permute-start.4 = (bf16[96,128]{1,0:T(8,128)(2,1)S(1)}, bf16[96,128]{1,0:T(8,128)(2,1)S(1)}, u32[]{:S(2)}, u32[]{:S(2)}) collective-permute-start(bf16[96,128]{1,0:T(8,128)(2,1)S(1)} %get-tuple-element.21), channel_id=1, source_target_pairs={{0,5},{1,6},{2,7},{3,4},{4,9},{5,10},{6,11},{7,8},{8,13},{9,14},{1... | collective-permute-start | bytes 73736 | tf_op jit(solution)/shard_map/ppermute | solution.py:331
  25.5 3.2 %collective-permute-start.3 = (bf16[96,128]{1,0:T(8,128)(2,1)S(1)}, bf16[96,128]{1,0:T(8,128)(2,1)S(1)}, u32[]{:S(2)}, u32[]{:S(2)}) collective-permute-start(bf16[96,128]{1,0:T(8,128)(2,1)S(1)} %get-tuple-element.21), channel_id=1, source_target_pairs={{0,3},{1,0},{2,1},{3,2},{4,7},{5,4},{6,5},{7,6},{8,11},{9,8},{10,9... | collective-permute-start | bytes 73736 | tf_op jit(solution)/shard_map/ppermute | solution.py:331
  28.7 1.0 copy.30.w_in
  30.6 3.7 %collective-permute-done.2.left = bf16[96,128]{1,0:T(8,128)(2,1)S(1)} collective-permute-done((bf16[96,128]{1,0:T(8,128)(2,1)S(1)}, bf16[96,128]{1,0:T(8,128)(2,1)S(1)}, u32[]{:S(2)}, u32[]{:S(2)}) %collective-permute-start.2) | collective-permute-done | bytes 24608 | tf_op jit(solution)/shard_map/ppermute | solution.py:331
  34.4 12.2 %patches.1 = (f32[1792,128]{1,0:T(8,128)S(1)}, f32[8,32,256]{2,1,0:T(8,128)S(1)}, f32[4,32,256]{2,1,0:T(8,128)S(1)}, f32[4,32,256]{2,1,0:T(8,128)S(1)}, f32[32,128]{1,0:T(8,128)S(1)}, /*index=5*/f32[8,256]{1,0:T(8,128)S(1)}) custom-call(s32[1,1,4,2]{3,2,1,0:T(4,128)S(1)} %copy.29.anchors, s32[1,1]{1,0:T(1,128)S(6)} %copy.35.counts, ...), custom_call_target="tpu_custom_call" | custom-call | tf_op jit(solution)/shard_map/patches/pallas_call | solution.py:399
  46.6 22.3 %all_to_all.20 = bf16[8,224,128]{2,1,0:T(8,128)(2,1)S(1)} all-to-all(bf16[8,224,128]{2,1,0:T(8,128)(2,1)S(1)} %bitcast.20), channel_id=1, replica_groups=mesh['lat'=8,'lon'=4] {'lat'}, dimensions={0} | all-to-all | bytes 917504 | tf_op jit(solution)/shard_map/all_to_all | solution.py:350
  69.0 8.3 %all_to_all.21 = f32[4,56,128]{2,1,0:T(8,128)S(1)} all-to-all(f32[4,56,128]{2,1,0:T(8,128)S(1)} %bitcast.23), channel_id=1, replica_groups=mesh['lat'=8,'lon'=4] {'lon'}, dimensions={0} | all-to-all | bytes 229376 | tf_op jit(solution)/shard_map/all_to_all | solution.py:353
  77.3 8.1 %all_to_all.22 = bf16[4,56,128]{2,1,0:T(8,128)(2,1)S(1)} all-to-all(bf16[4,56,128]{2,1,0:T(8,128)(2,1)S(1)} %broadcast_in_dim.6), channel_id=1, replica_groups=mesh['lat'=8,'lon'=4] {'lon'}, dimensions={0} | all-to-all | bytes 114688 | tf_op jit(solution)/shard_map/all_to_all | solution.py:356
  86.2 3.5 %all-to-all-start.3 = ((bf16[8,224,128]{2,1,0:T(8,128)(2,1)}), bf16[8,224,128]{2,1,0:T(8,128)(2,1)S(1)}, u32[]{:S(2)}, u32[]{:S(2)}) async-start(bf16[8,224,128]{2,1,0:T(8,128)(2,1)} %broadcast_in_dim.15), calls=%async_computation.3 | async-start | bytes 917504 | tf_op jit(solution)/shard_map/all_to_all | solution.py:359
  89.7 2.3 %collective-permute-start.8 = (f32[4,32,256]{2,1,0:T(8,128)S(1)}, f32[4,32,256]{2,1,0:T(8,128)S(1)}, u32[]{:S(2)}, u32[]{:S(2)}) collective-permute-start(f32[4,32,256]{2,1,0:T(8,128)S(1)} %get-tuple-element.24), channel_id=1, source_target_pairs={{0,4},{1,5},{2,6},{3,7},{4,8},{5,9},{6,10},{7,11},{8,12},{9,13},{1... | collective-permute-start | bytes 393224 | tf_op jit(solution)/shard_map/ppermute | solution.py:331
  92.0 1.3 %collective-permute-start.9 = (f32[4,32,256]{2,1,0:T(8,128)S(1)}, f32[4,32,256]{2,1,0:T(8,128)S(1)}, u32[]{:S(2)}, u32[]{:S(2)}) collective-permute-start(f32[4,32,256]{2,1,0:T(8,128)S(1)} %get-tuple-element.25), channel_id=1, source_target_pairs={{4,0},{5,1},{6,2},{7,3},{8,4},{9,5},{10,6},{11,7},{12,8},{13,9},{1... | collective-permute-start | bytes 393224 | tf_op jit(solution)/shard_map/ppermute | solution.py:331
  93.3 1.3 %collective-permute-start.15 = (f32[32,128]{1,0:T(8,128)S(1)}, f32[32,128]{1,0:T(8,128)S(1)}, u32[]{:S(2)}, u32[]{:S(2)}) collective-permute-start(f32[32,128]{1,0:T(8,128)S(1)} %get-tuple-element.26), channel_id=1, source_target_pairs={{4,3},{5,0},{6,1},{7,2},{8,7},{9,4},{10,5},{11,6},{12,11},{13,8},{... | collective-permute-start | bytes 49160 | tf_op jit(solution)/shard_map/ppermute | solution.py:331
  94.6 1.3 %collective-permute-start.14 = (f32[32,128]{1,0:T(8,128)S(1)}, f32[32,128]{1,0:T(8,128)S(1)}, u32[]{:S(2)}, u32[]{:S(2)}) collective-permute-start(f32[32,128]{1,0:T(8,128)S(1)} %get-tuple-element.26), channel_id=1, source_target_pairs={{4,1},{5,2},{6,3},{7,0},{8,5},{9,6},{10,7},{11,4},{12,9},{13,10},{... | collective-permute-start | bytes 49160 | tf_op jit(solution)/shard_map/ppermute | solution.py:331
  95.9 6.1 %collective-permute-start.13 = (f32[32,128]{1,0:T(8,128)S(1)}, f32[32,128]{1,0:T(8,128)S(1)}, u32[]{:S(2)}, u32[]{:S(2)}) collective-permute-start(f32[32,128]{1,0:T(8,128)S(1)} %get-tuple-element.26), channel_id=1, source_target_pairs={{0,7},{1,4},{2,5},{3,6},{4,11},{5,8},{6,9},{7,10},{8,15},{9,12},{1... | collective-permute-start | bytes 49160 | tf_op jit(solution)/shard_map/ppermute | solution.py:331
  102.0 4.4 %collective-permute-start.12 = (f32[32,128]{1,0:T(8,128)S(1)}, f32[32,128]{1,0:T(8,128)S(1)}, u32[]{:S(2)}, u32[]{:S(2)}) collective-permute-start(f32[32,128]{1,0:T(8,128)S(1)} %get-tuple-element.26), channel_id=1, source_target_pairs={{0,5},{1,6},{2,7},{3,4},{4,9},{5,10},{6,11},{7,8},{8,13},{9,14},{1... | collective-permute-start | bytes 49160 | tf_op jit(solution)/shard_map/ppermute | solution.py:331
  106.4 4.8 %collective-permute-start.11 = (f32[32,128]{1,0:T(8,128)S(1)}, f32[32,128]{1,0:T(8,128)S(1)}, u32[]{:S(2)}, u32[]{:S(2)}) collective-permute-start(f32[32,128]{1,0:T(8,128)S(1)} %get-tuple-element.26), channel_id=1, source_target_pairs={{0,3},{1,0},{2,1},{3,2},{4,7},{5,4},{6,5},{7,6},{8,11},{9,8},{10,9... | collective-permute-start | bytes 49160 | tf_op jit(solution)/shard_map/ppermute | solution.py:331
  111.2 1.4 %collective-permute-done.11.right = f32[32,128]{1,0:T(8,128)S(1)} collective-permute-done((f32[32,128]{1,0:T(8,128)S(1)}, f32[32,128]{1,0:T(8,128)S(1)}, u32[]{:S(2)}, u32[]{:S(2)}) %collective-permute-start.11) | collective-permute-done | bytes 16416 | tf_op jit(solution)/shard_map/ppermute | solution.py:331
  112.6 4.1 %collective-permute-done.10.left = f32[32,128]{1,0:T(8,128)S(1)} collective-permute-done((f32[32,128]{1,0:T(8,128)S(1)}, f32[32,128]{1,0:T(8,128)S(1)}, u32[]{:S(2)}, u32[]{:S(2)}) %collective-permute-start.10) | collective-permute-done | bytes 16416 | tf_op jit(solution)/shard_map/ppermute | solution.py:331
  117.7 1.0 split.1
  (43 shorter events, 7.3 us)
Async XLA Ops:
  0.6 0.7 copy-start.6
  1.4 0.8 copy-start.1
  2.2 0.9 copy-start.3
  3.1 0.9 copy-start.4
  4.0 25.9 %copy-start.5 = (bf16[9,128,128]{2,1,0:T(8,128)(2,1)S(1)}, bf16[9,128,128]{2,1,0:T(8,128)(2,1)}, u32[]{:S(2)}) copy-start(bf16[9,128,128]{2,1,0:T(8,128)(2,1)} %param.11) | copy-start | bytes 884740
  5.0 29.4 %collective-permute-start = (bf16[5,64,256]{2,1,0:T(8,128)(2,1)S(1)}, bf16[5,64,256]{2,1,0:T(8,128)(2,1)S(1)}, u32[]{:S(2)}, u32[]{:S(2)}) collective-permute-start(bf16[5,64,256]{2,1,0:T(8,128)(2,1)S(1)} %get-tuple-element.19), channel_id=1, source_target_pairs={{0,4},{1,5},{2,6},{3,7},{4,8},{5,9},{6,10},{7,11},{8,12},{9,13},{1... | collective-permute-start | bytes 491528 | tf_op jit(solution)/shard_map/ppermute | solution.py:331
  7.5 26.8 %collective-permute-start.1 = (bf16[5,64,256]{2,1,0:T(8,128)(2,1)S(1)}, bf16[5,64,256]{2,1,0:T(8,128)(2,1)S(1)}, u32[]{:S(2)}, u32[]{:S(2)}) collective-permute-start(bf16[5,64,256]{2,1,0:T(8,128)(2,1)S(1)} %get-tuple-element.20), channel_id=1, source_target_pairs={{4,0},{5,1},{6,2},{7,3},{8,4},{9,5},{10,6},{11,7},{12,8},{13,9},{1... | collective-permute-start | bytes 491528 | tf_op jit(solution)/shard_map/ppermute | solution.py:331
  8.8 12.1 %collective-permute-start.7 = (bf16[96,128]{1,0:T(8,128)(2,1)S(1)}, bf16[96,128]{1,0:T(8,128)(2,1)S(1)}, u32[]{:S(2)}, u32[]{:S(2)}) collective-permute-start(bf16[96,128]{1,0:T(8,128)(2,1)S(1)} %get-tuple-element.21), channel_id=1, source_target_pairs={{4,3},{5,0},{6,1},{7,2},{8,7},{9,4},{10,5},{11,6},{12,11},{13,8},{... | collective-permute-start | bytes 73736 | tf_op jit(solution)/shard_map/ppermute | solution.py:331
  10.1 15.4 %collective-permute-start.6 = (bf16[96,128]{1,0:T(8,128)(2,1)S(1)}, bf16[96,128]{1,0:T(8,128)(2,1)S(1)}, u32[]{:S(2)}, u32[]{:S(2)}) collective-permute-start(bf16[96,128]{1,0:T(8,128)(2,1)S(1)} %get-tuple-element.21), channel_id=1, source_target_pairs={{4,1},{5,2},{6,3},{7,0},{8,5},{9,6},{10,7},{11,4},{12,9},{13,10},{... | collective-permute-start | bytes 73736 | tf_op jit(solution)/shard_map/ppermute | solution.py:331
  11.4 17.3 %collective-permute-start.5 = (bf16[96,128]{1,0:T(8,128)(2,1)S(1)}, bf16[96,128]{1,0:T(8,128)(2,1)S(1)}, u32[]{:S(2)}, u32[]{:S(2)}) collective-permute-start(bf16[96,128]{1,0:T(8,128)(2,1)S(1)} %get-tuple-element.21), channel_id=1, source_target_pairs={{0,7},{1,4},{2,5},{3,6},{4,11},{5,8},{6,9},{7,10},{8,15},{9,12},{1... | collective-permute-start | bytes 73736 | tf_op jit(solution)/shard_map/ppermute | solution.py:331
  20.9 9.6 %collective-permute-start.4 = (bf16[96,128]{1,0:T(8,128)(2,1)S(1)}, bf16[96,128]{1,0:T(8,128)(2,1)S(1)}, u32[]{:S(2)}, u32[]{:S(2)}) collective-permute-start(bf16[96,128]{1,0:T(8,128)(2,1)S(1)} %get-tuple-element.21), channel_id=1, source_target_pairs={{0,5},{1,6},{2,7},{3,4},{4,9},{5,10},{6,11},{7,8},{8,13},{9,14},{1... | collective-permute-start | bytes 73736 | tf_op jit(solution)/shard_map/ppermute | solution.py:331
  25.5 5.1 %collective-permute-start.3 = (bf16[96,128]{1,0:T(8,128)(2,1)S(1)}, bf16[96,128]{1,0:T(8,128)(2,1)S(1)}, u32[]{:S(2)}, u32[]{:S(2)}) collective-permute-start(bf16[96,128]{1,0:T(8,128)(2,1)S(1)} %get-tuple-element.21), channel_id=1, source_target_pairs={{0,3},{1,0},{2,1},{3,2},{4,7},{5,4},{6,5},{7,6},{8,11},{9,8},{10,9... | collective-permute-start | bytes 73736 | tf_op jit(solution)/shard_map/ppermute | solution.py:331
  28.7 5.6 %collective-permute-start.2 = (bf16[96,128]{1,0:T(8,128)(2,1)S(1)}, bf16[96,128]{1,0:T(8,128)(2,1)S(1)}, u32[]{:S(2)}, u32[]{:S(2)}) collective-permute-start(bf16[96,128]{1,0:T(8,128)(2,1)S(1)} %get-tuple-element.21), channel_id=1, source_target_pairs={{0,1},{1,2},{2,3},{3,0},{4,5},{5,6},{6,7},{7,4},{8,9},{9,10},{10,1... | collective-permute-start | bytes 73736 | tf_op jit(solution)/shard_map/ppermute | solution.py:331
  28.7 1.0 copy-start
  30.4 4.0 %copy-start.2 = (s32[4,8,256]{2,1,0:T(8,128)S(1)}, s32[4,8,256]{2,1,0:T(8,128)}, u32[]{:S(2)}) copy-start(s32[4,8,256]{2,1,0:T(8,128)} %weights.3) | copy-start | bytes 98308
  86.2 31.5 %all-to-all-start.3 = ((bf16[8,224,128]{2,1,0:T(8,128)(2,1)}), bf16[8,224,128]{2,1,0:T(8,128)(2,1)S(1)}, u32[]{:S(2)}, u32[]{:S(2)}) async-start(bf16[8,224,128]{2,1,0:T(8,128)(2,1)} %broadcast_in_dim.15), calls=%async_computation.3 | async-start | bytes 917504 | tf_op jit(solution)/shard_map/all_to_all | solution.py:359
  89.7 27.0 %collective-permute-start.8 = (f32[4,32,256]{2,1,0:T(8,128)S(1)}, f32[4,32,256]{2,1,0:T(8,128)S(1)}, u32[]{:S(2)}, u32[]{:S(2)}) collective-permute-start(f32[4,32,256]{2,1,0:T(8,128)S(1)} %get-tuple-element.24), channel_id=1, source_target_pairs={{0,4},{1,5},{2,6},{3,7},{4,8},{5,9},{6,10},{7,11},{8,12},{9,13},{1... | collective-permute-start | bytes 393224 | tf_op jit(solution)/shard_map/ppermute | solution.py:331
  92.0 24.7 %collective-permute-start.9 = (f32[4,32,256]{2,1,0:T(8,128)S(1)}, f32[4,32,256]{2,1,0:T(8,128)S(1)}, u32[]{:S(2)}, u32[]{:S(2)}) collective-permute-start(f32[4,32,256]{2,1,0:T(8,128)S(1)} %get-tuple-element.25), channel_id=1, source_target_pairs={{4,0},{5,1},{6,2},{7,3},{8,4},{9,5},{10,6},{11,7},{12,8},{13,9},{1... | collective-permute-start | bytes 393224 | tf_op jit(solution)/shard_map/ppermute | solution.py:331
  93.3 8.7 %collective-permute-start.15 = (f32[32,128]{1,0:T(8,128)S(1)}, f32[32,128]{1,0:T(8,128)S(1)}, u32[]{:S(2)}, u32[]{:S(2)}) collective-permute-start(f32[32,128]{1,0:T(8,128)S(1)} %get-tuple-element.26), channel_id=1, source_target_pairs={{4,3},{5,0},{6,1},{7,2},{8,7},{9,4},{10,5},{11,6},{12,11},{13,8},{... | collective-permute-start | bytes 49160 | tf_op jit(solution)/shard_map/ppermute | solution.py:331
  94.6 11.8 %collective-permute-start.14 = (f32[32,128]{1,0:T(8,128)S(1)}, f32[32,128]{1,0:T(8,128)S(1)}, u32[]{:S(2)}, u32[]{:S(2)}) collective-permute-start(f32[32,128]{1,0:T(8,128)S(1)} %get-tuple-element.26), channel_id=1, source_target_pairs={{4,1},{5,2},{6,3},{7,0},{8,5},{9,6},{10,7},{11,4},{12,9},{13,10},{... | collective-permute-start | bytes 49160 | tf_op jit(solution)/shard_map/ppermute | solution.py:331
  95.9 15.3 %collective-permute-start.13 = (f32[32,128]{1,0:T(8,128)S(1)}, f32[32,128]{1,0:T(8,128)S(1)}, u32[]{:S(2)}, u32[]{:S(2)}) collective-permute-start(f32[32,128]{1,0:T(8,128)S(1)} %get-tuple-element.26), channel_id=1, source_target_pairs={{0,7},{1,4},{2,5},{3,6},{4,11},{5,8},{6,9},{7,10},{8,15},{9,12},{1... | collective-permute-start | bytes 49160 | tf_op jit(solution)/shard_map/ppermute | solution.py:331
  102.0 9.2 %collective-permute-start.12 = (f32[32,128]{1,0:T(8,128)S(1)}, f32[32,128]{1,0:T(8,128)S(1)}, u32[]{:S(2)}, u32[]{:S(2)}) collective-permute-start(f32[32,128]{1,0:T(8,128)S(1)} %get-tuple-element.26), channel_id=1, source_target_pairs={{0,5},{1,6},{2,7},{3,4},{4,9},{5,10},{6,11},{7,8},{8,13},{9,14},{1... | collective-permute-start | bytes 49160 | tf_op jit(solution)/shard_map/ppermute | solution.py:331
  106.4 6.2 %collective-permute-start.11 = (f32[32,128]{1,0:T(8,128)S(1)}, f32[32,128]{1,0:T(8,128)S(1)}, u32[]{:S(2)}, u32[]{:S(2)}) collective-permute-start(f32[32,128]{1,0:T(8,128)S(1)} %get-tuple-element.26), channel_id=1, source_target_pairs={{0,3},{1,0},{2,1},{3,2},{4,7},{5,4},{6,5},{7,6},{8,11},{9,8},{10,9... | collective-permute-start | bytes 49160 | tf_op jit(solution)/shard_map/ppermute | solution.py:331
  111.2 5.5 %collective-permute-start.10 = (f32[32,128]{1,0:T(8,128)S(1)}, f32[32,128]{1,0:T(8,128)S(1)}, u32[]{:S(2)}, u32[]{:S(2)}) collective-permute-start(f32[32,128]{1,0:T(8,128)S(1)} %get-tuple-element.26), channel_id=1, source_target_pairs={{0,1},{1,2},{2,3},{3,0},{4,5},{5,6},{6,7},{7,4},{8,9},{9,10},{10,1... | collective-permute-start | bytes 49160 | tf_op jit(solution)/shard_map/ppermute | solution.py:331

commit v2 on v1

--- a/solution.py
+++ b/solution.py
@@ -36,10 +36,26 @@
     return pltpu.roll(value, shift, axis)
 
 
-def pack_kernel(anchors, counts, fields, cotangent, weights, center, to_up, to_down, edges, canvas, spread):
+def choose(odd, when_odd, when_even):
+    return jnp.where(odd, when_odd, when_even)
+
+
+def pack_kernel(
+    anchors, counts, fields_in, cotangent_in, weights_in, center, first_out, second_out, canvas,
+    fields, cotangent, weights, spread, sems,
+):
+    copies = []
+    for index, (source, target) in enumerate(
+        ((weights_in, weights), (fields_in, fields), (cotangent_in, cotangent))
+    ):
+        copy = pltpu.make_async_copy(source, target, sems.at[index])
+        copy.start()
+        copies.append(copy)
     channels, rows, cols = fields.shape
     wide = cols + LANES
+    odd = lax.rem(lax.axis_index("lat"), 2) == 1
     spread[...] = jnp.zeros_like(spread)
+    copies[0].wait()
     for slot in range(SLOTS):
 
         @pl.when(slot < counts[0, 0])
@@ -55,35 +71,62 @@
 
     total = spread[...]
     canvas[...] = total
+    copies[1].wait()
+    copies[2].wait()
     both = []
     for source in (fields, cotangent):
         both.append(jnp.swapaxes(source[...].astype(F32), 0, 1))
-    tile = jnp.concatenate(both, axis=1)
-    center[...] = tile.astype(BF16)
-    to_up[0:MARGIN] = tile[:MARGIN].astype(BF16)
-    to_down[0:MARGIN] = tile[rows - MARGIN :].astype(BF16)
+    tile = jnp.concatenate(both, axis=1).astype(BF16)
+    center[...] = tile
+    half = total.shape[0] // 2
+    pad = jnp.zeros((2 * channels - 2 * half, cols), F32)
+    extras = []
+    for part in (total[:half], total[half:]):
+        beside = jnp.concatenate([part[:, cols:], jnp.zeros((half, cols - LANES), F32)], axis=1)
+        extras.append(jnp.concatenate([part[:, :cols], beside, pad], axis=0).astype(BF16))
+    top, bottom = tile[:MARGIN], tile[rows - MARGIN :]
+    first_out[0:MARGIN] = choose(odd, top, bottom)
+    first_out[MARGIN] = choose(odd, extras[0], extras[1])
+    second_out[0:MARGIN] = choose(odd, bottom, top)
+    second_out[MARGIN] = choose(odd, extras[1], extras[0])
+
+
+def edge_kernel(center, first, second, canvas, edges, total_out):
+    rows = center.shape[0]
+    channels = center.shape[1] // 2
+    cols = center.shape[2]
+    height = rows + 2 * MARGIN
+    half = height // 2
+    odd = lax.rem(lax.axis_index("lat"), 2) == 1
+
+    def stretch(block):
+        block = block.astype(F32)
+        return jnp.concatenate([block[:half], block[half:height, :LANES]], axis=1)
+
+    upper = stretch(choose(odd, first[MARGIN], second[MARGIN]))
+    lower = stretch(choose(odd, second[MARGIN], first[MARGIN]))
+    total = canvas[...] + jnp.concatenate([upper, lower], axis=0)
+    total_out[...] = total
     lanes = lane_ids((2 * channels, LANES))
     packed = jnp.zeros((2 * channels, LANES), F32)
-    for row in range(rows):
-        first = jnp.where(lanes < MARGIN, tile[row, :, :LANES], 0.0)
-        last = jnp.where(lanes >= LANES - MARGIN, tile[row, :, cols - LANES :], 0.0)
-        packed = packed + roll(first, MARGIN * row, 1) + roll(last, -MARGIN * row, 1)
+    for row in range(height):
+        if row < MARGIN:
+            line = choose(odd, first[row], second[row])
+        elif row < MARGIN + rows:
+            line = center[row - MARGIN]
+        else:
+            line = choose(odd, second[row - MARGIN - rows], first[row - MARGIN - rows])
+        line = line.astype(F32)
+        low = jnp.where(lanes < MARGIN, line[:, :LANES], 0.0)
+        high = jnp.where(lanes >= LANES - MARGIN, line[:, cols - LANES :], 0.0)
+        packed = packed + roll(low, MARGIN * row, 1) + roll(high, -MARGIN * row, 1)
     edges[0 : 2 * channels] = packed.astype(BF16)
-    first = total[:, :LANES]
-    last = total[:, cols - LANES : cols]
     margin = total[:, cols:]
     lanes = lane_ids(margin.shape)
-    height = margin.shape[0]
-    to_left = jnp.where(lanes < LANES // 2, first, margin)
-    to_right = jnp.where(lanes < LANES // 2, margin, last)
+    to_left = jnp.where(lanes < LANES // 2, total[:, :LANES], margin)
+    to_right = jnp.where(lanes < LANES // 2, margin, total[:, cols - LANES : cols])
     edges[2 * channels : 2 * channels + height] = to_left.astype(BF16)
     edges[2 * channels + height : 2 * channels + 2 * height] = to_right.astype(BF16)
-    half = height // 2
-    pad = jnp.zeros((2 * channels - height, cols), F32)
-    for target, part in ((to_up, total[:half]), (to_down, total[half:])):
-        beside = jnp.concatenate([part[:, cols:], jnp.zeros((half, cols - LANES), F32)], axis=1)
-        extra = jnp.concatenate([part[:, :cols], beside, pad], axis=0)
-        target[MARGIN] = extra.astype(BF16)
 
 
 def dot(left, right):
@@ -95,10 +138,10 @@
 
 
 def patch_kernel(
-    anchors, counts, center, up, down, left, right, up_left, up_right, down_left, down_right, canvas, weights,
+    anchors, counts, center, first, second, third, fourth, total_in, weights,
     w_in, w_mid, w_mid_back, w_out, w_out_back,
-    grads, inner, to_up, to_down, edges, den_out,
-    window, numer, x_s, d_s, h_s, z_s, slope_s, dh_s, h2_s, dz_s, y_s,
+    grads, numer, edges, den_out,
+    window, x_s, d_s, h_s, z_s, slope_s, dh_s, h2_s, dz_s, y_s,
 ):
     rows = center.shape[0]
     channels = center.shape[1] // 2
@@ -107,34 +150,15 @@
     width = w_mid.shape[0]
     full = rows * cols
     height = rows + 2 * MARGIN
-    half = height // 2
     lanes = lane_ids((2 * channels, LANES))
-
-    total = canvas[...]
-    upper = up[MARGIN].astype(F32)
-    lower = down[MARGIN].astype(F32)
-
-    def stretch(block):
-        return jnp.concatenate([block[:half], block[half:height, :LANES]], axis=1)
-
-    total = total + jnp.concatenate([stretch(upper), stretch(lower)], axis=0)
+    lat_odd = lax.rem(lax.axis_index("lat"), 2) == 1
+    lon_odd = lax.rem(lax.axis_index("lon"), 2) == 1
+
+    left = choose(lon_odd, third[...], fourth[...]).astype(F32)
+    right = choose(lon_odd, fourth[...], third[...]).astype(F32)
     base = 2 * channels
-    left_part = left[base + height : base + 2 * height].astype(F32)
-    left_part = left_part + jnp.concatenate(
-        [
-            up_left[base + height : base + 2 * height].astype(F32)[half:],
-            down_left[base + height : base + 2 * height].astype(F32)[:half],
-        ],
-        axis=0,
-    )
-    right_part = right[base : base + height].astype(F32)
-    right_part = right_part + jnp.concatenate(
-        [
-            up_right[base : base + height].astype(F32)[half:],
-            down_right[base : base + height].astype(F32)[:half],
-        ],
-        axis=0,
-    )
+    left_part = left[base + height : base + 2 * height]
+    right_part = right[base : base + height]
     edge_lanes = lane_ids((height, LANES))
     low = edge_lanes < MARGIN
     high = edge_lanes >= LANES - MARGIN
@@ -144,25 +168,21 @@
         pieces.append(zero)
     pieces.append(jnp.where(high, right_part, zero))
     pieces.append(jnp.where(high, left_part, zero) + jnp.where(low, right_part, zero))
-    den = jnp.maximum(total + jnp.concatenate(pieces, axis=1), 1.0)
+    den = jnp.maximum(total_in[...] + jnp.concatenate(pieces, axis=1), 1.0)
     den_out[...] = den[MARGIN : MARGIN + rows, :cols]
     inverse = 1.0 / den
 
-    left_e = left[0:base].astype(F32)
-    right_e = right[0:base].astype(F32)
-    up_left_e = up_left[0:base].astype(F32)
-    up_right_e = up_right[0:base].astype(F32)
-    down_left_e = down_left[0:base].astype(F32)
-    down_right_e = down_right[0:base].astype(F32)
+    left = left[:base]
+    right = right[:base]
     for row in range(height):
         if row < MARGIN:
-            body, from_left, from_right, at = up[row], up_left_e, up_right_e, rows - MARGIN + row
+            body = choose(lat_odd, first[row], second[row])
         elif row < MARGIN + rows:
-            body, from_left, from_right, at = center[row - MARGIN], left_e, right_e, row - MARGIN
+            body = center[row - MARGIN]
         else:
-            body, from_left, from_right, at = down[row - MARGIN - rows], down_left_e, down_right_e, row - MARGIN - rows
+            body = choose(lat_odd, second[row - MARGIN - rows], first[row - MARGIN - rows])
         beside = jnp.where(
-            lanes < LANES // 2, roll(from_right, -MARGIN * at, 1), roll(from_left, MARGIN * at, 1)
+            lanes < LANES // 2, roll(right, -MARGIN * row, 1), roll(left, MARGIN * row, 1)
         )
         line = jnp.concatenate([body.astype(F32), beside], axis=1)
         scaled = line[channels:] * inverse[row : row + 1]
@@ -271,38 +291,46 @@
         last = jnp.where(lanes >= LANES - MARGIN, beside, 0.0)
         packed = packed + roll(first, MARGIN * row, 1) + roll(last, -MARGIN * row, 1)
     edges[...] = packed
-    to_up[...] = numer[0:MARGIN, :, :cols]
-    inner[...] = numer[MARGIN : MARGIN + rows, :, :cols]
-    to_down[...] = numer[MARGIN + rows :, :, :cols]
-
-
-def fold_kernel(
-    inner, up, down, left, right, up_left, up_right, down_left, down_right, den, blended
-):
-    rows, channels, cols = inner.shape
+
+
+def beside_kernel(numer, third, fourth, inner, first_out, second_out):
+    height, channels, wide = numer.shape
+    cols = wide - LANES
+    rows = height - 2 * MARGIN
     lanes = lane_ids((channels, LANES))
-    inverse = 1.0 / den[...]
+    lat_odd = lax.rem(lax.axis_index("lat"), 2) == 1
+    lon_odd = lax.rem(lax.axis_index("lon"), 2) == 1
+    left = choose(lon_odd, third[...], fourth[...])
+    right = choose(lon_odd, fourth[...], third[...])
     lines = []
-    for row in range(rows):
-        line = inner[row]
-        from_left = jnp.where(lanes < MARGIN, roll(left[...], -MARGIN * (row + MARGIN), 1), 0.0)
-        from_right = jnp.where(lanes >= LANES - MARGIN, roll(right[...], MARGIN * (row + MARGIN), 1), 0.0)
-        if row < MARGIN:
-            line = line + up[row]
-            at = MARGIN * (row + MARGIN + rows)
-            more_left, more_right = up_left, up_right
-        else:
-            line = line + down[row - (rows - MARGIN)]
-            at = MARGIN * (row - (rows - MARGIN))
-            more_left, more_right = down_left, down_right
-        from_left = from_left + jnp.where(lanes < MARGIN, roll(more_left[...], -at, 1), 0.0)
-        from_right = from_right + jnp.where(lanes >= LANES - MARGIN, roll(more_right[...], at, 1), 0.0)
+    for row in range(height):
+        from_left = jnp.where(lanes < MARGIN, roll(left, -MARGIN * row, 1), 0.0)
+        from_right = jnp.where(lanes >= LANES - MARGIN, roll(right, MARGIN * row, 1), 0.0)
         beside = [from_left]
         for _ in range(cols // LANES - 2):
             beside.append(jnp.zeros((channels, LANES), F32))
         beside.append(from_right)
-        line = line + jnp.concatenate(beside, axis=1)
-        lines.append((line * inverse[row : row + 1])[None])
+        lines.append(numer[row, :, :cols] + jnp.concatenate(beside, axis=1))
+    for row in range(MARGIN):
+        upper, lower = lines[row], lines[MARGIN + rows + row]
+        first_out[row] = choose(lat_odd, upper, lower)
+        second_out[row] = choose(lat_odd, lower, upper)
+    for row in range(rows):
+        inner[row] = lines[MARGIN + row]
+
+
+def fold_kernel(inner, first, second, den, blended):
+    rows = inner.shape[0]
+    lat_odd = lax.rem(lax.axis_index("lat"), 2) == 1
+    inverse = 1.0 / den[...]
+    lines = []
+    for row in range(rows):
+        if row < MARGIN:
+            other = choose(lat_odd, first[row], second[row])
+        else:
+            at = row - (rows - MARGIN)
+            other = choose(lat_odd, second[at], first[at])
+        lines.append(((inner[row] + other) * inverse[row : row + 1])[None])
     blended[...] = jnp.swapaxes(jnp.concatenate(lines, axis=0), 0, 1)
 
 
@@ -320,27 +348,22 @@
     return pltpu.CompilerParams(vmem_limit_bytes=VMEM_LIMIT)
 
 
-def shift(value, lat_step, lon_step):
-    lat_size, lon_size = lax.axis_size("lat"), lax.axis_size("lon")
+def swap(value, axis, first, wrap):
+    size = lax.axis_size(axis)
     pairs = []
-    for lat in range(lat_size):
-        for lon in range(lon_size):
-            if 0 <= lat + lat_step < lat_size:
-                target = (lat + lat_step) * lon_size + (lon + lon_step) % lon_size
-                pairs.append((lat * lon_size + lon, target))
-    return lax.ppermute(value, ("lat", "lon"), pairs)
-
-
-def neighbours(to_up, to_down, edges):
-    up = shift(to_down, 1, 0)
-    down = shift(to_up, -1, 0)
-    left = shift(edges, 0, 1)
-    right = shift(edges, 0, -1)
-    up_left = shift(edges, 1, 1)
-    down_right = shift(edges, -1, -1)
-    up_right = shift(edges, 1, -1)
-    down_left = shift(edges, -1, 1)
-    return up, down, left, right, up_left, up_right, down_left, down_right
+    for index in range(first, size, 2):
+        other = (index + 1) % size
+        if other > index or wrap:
+            pairs.extend([(index, other), (other, index)])
+    return lax.ppermute(value, axis, pairs)
+
+
+def swap_lat(first, second):
+    return swap(first, "lat", 0, False), swap(second, "lat", 1, False)
+
+
+def swap_lon(edges):
+    return swap(edges, "lon", 0, True), swap(edges, "lon", 1, True)
 
 
 def reduce_all(grads):
@@ -370,22 +393,36 @@
     full = rows * cols
     padded = full + 2 * cols
     shape = jax.ShapeDtypeStruct
-    center, to_up, to_down, edges, canvas = pl.pallas_call(
+    center, first, second, canvas = pl.pallas_call(
         pack_kernel,
         out_shape=(
             shape((rows, 2 * channels, cols), BF16),
             shape((MARGIN + 1, 2 * channels, cols), BF16),
             shape((MARGIN + 1, 2 * channels, cols), BF16),
-            shape((2 * channels + 2 * height, LANES), BF16),
             shape((height, wide), F32),
         ),
-        in_specs=[smem(), smem(), vmem(), vmem(), vmem()],
-        out_specs=(vmem(),) * 5,
-        scratch_shapes=[pltpu.VMEM((height, wide), F32)],
+        in_specs=[smem(), smem()] + [pl.BlockSpec(memory_space=pl.ANY)] * 3,
+        out_specs=(vmem(),) * 4,
+        scratch_shapes=[
+            pltpu.VMEM(fields.shape, BF16),
+            pltpu.VMEM(cotangent.shape, BF16),
+            pltpu.VMEM(blend_weights.shape, jnp.int32),
+            pltpu.VMEM((height, wide), F32),
+            pltpu.SemaphoreType.DMA((3,)),
+        ],
         compiler_params=params(),
         name="pack",
     )(patch_anchors, tile_counts, fields, cotangent, blend_weights)
-    received = neighbours(to_up, to_down, edges)
+    first, second = swap_lat(first, second)
+    edges, total = pl.pallas_call(
+        edge_kernel,
+        out_shape=(shape((2 * channels + 2 * height, LANES), BF16), shape((height, wide), F32)),
+        in_specs=[vmem()] * 4,
+        out_specs=(vmem(),) * 2,
+        compiler_params=params(),
+        name="edges",
+    )(center, first, second, canvas)
+    third, fourth = swap_lon(edges)
 
     w_in = jnp.transpose(kernel_in, (1, 0, 2)).reshape(width, taps * channels)
     w_mid = jnp.transpose(kernel_mid, (1, 0, 2)).reshape(width, taps * width)
@@ -396,21 +433,18 @@
     length = taps * (2 * channels + width)
     unit = 8 * lax.axis_size("lat") * lax.axis_size("lon")
     length = (length + unit - 1) // unit * unit
-    grads, inner, out_up, out_down, out_edges, den = pl.pallas_call(
+    grads, numer, edges, den = pl.pallas_call(
         patch_kernel,
         out_shape=(
             shape((length, LANES), F32),
-            shape((rows, channels, cols), F32),
-            shape((MARGIN, channels, cols), F32),
-            shape((MARGIN, channels, cols), F32),
+            shape((height, channels, wide), F32),
             shape((channels, LANES), F32),
             shape((rows, cols), F32),
         ),
-        in_specs=[smem(), smem()] + [vmem()] * 16,
-        out_specs=(vmem(),) * 6,
+        in_specs=[smem(), smem()] + [vmem()] * 12,
+        out_specs=(vmem(),) * 4,
         scratch_shapes=[
             pltpu.VMEM((height, 2 * channels, wide), F32),
-            pltpu.VMEM((height, channels, wide), F32),
             pltpu.VMEM((3 * channels, padded), BF16),
             pltpu.VMEM((3 * channels, padded), BF16),
             pltpu.VMEM((3 * width, padded), BF16),
@@ -424,19 +458,32 @@
         compiler_params=params(),
         name="patches",
     )(
-        patch_anchors, tile_counts, center, *received, canvas, blend_weights,
+        patch_anchors, tile_counts, center, first, second, third, fourth, total, blend_weights,
         w_in, w_mid, w_mid_back, w_out, w_out_back,
     )
-    summed = reduce_all(grads)
-    returned = neighbours(out_up, out_down, out_edges)
+    third, fourth = swap_lon(edges)
+    inner, first, second = pl.pallas_call(
+        beside_kernel,
+        out_shape=(
+            shape((rows, channels, cols), F32),
+            shape((MARGIN, channels, cols), F32),
+            shape((MARGIN, channels, cols), F32),
+        ),
+        in_specs=[vmem()] * 3,
+        out_specs=(vmem(),) * 3,
+        compiler_params=params(),
+        name="beside",
+    )(numer, third, fourth)
+    first, second = swap_lat(first, second)
     blended = pl.pallas_call(
         fold_kernel,
         out_shape=shape((channels, rows, cols), F32),
-        in_specs=[vmem()] * 10,
+        in_specs=[vmem()] * 4,
         out_specs=vmem(),
         compiler_params=params(),
         name="fold",
-    )(inner, *returned, den)
+    )(inner, first, second, den)
+    summed = reduce_all(grads)
     grad_in, grad_mid, grad_out = pl.pallas_call(
         split_kernel,
         out_shape=(

time: 121 us -> 92.4 us (0.76)
  the two profiles are of different devices: /device:TPU:0 before, /device:TPU:3 now
where the time goes in v2:
time: 92.4 us; the launch traced here: 91.9 us
  blocking collectives  29 us (31%)
  Pallas kernels  21.3 us (23%)
  starting transfers between devices  18.9 us (20%)
  waiting for transfers between devices  15.1 us (16%)
  local copies, waits for them, and re-layouts  6.03 us (7%)
  between operations  1.43 us (2%)
    pallas_call x1, Pallas kernels, shards(): pl.pallas_call(patch_kernel, out_shape=(shape((length, LANES), F32), shap...  17.7 us
    ppermute x8, waiting for transfers between devices, swap(): return lax.ppermute(value, axis, pairs)  15.1 us
    all_to_all x2, blocking collectives, reduce_all(): parts = lax.all_to_all(parts, 'lon', 0, 0)  14.9 us
    all_to_all x1, blocking collectives, reduce_all(): parts = lax.all_to_all(parts, 'lat', 0, 0)  14.1 us
    ppermute x8, starting transfers between devices, swap(): return lax.ppermute(value, axis, pairs)  12.4 us
    all_to_all x1, starting transfers between devices, reduce_all(): parts = lax.all_to_all(parts, 'lat', 0, 0)  6.5 us
    unnamed x19, local copies, waits for them, and re-layouts  4.53 us
  transfers between devices with their start and end apart: 9, of which 4 were waited for; matrix products, arithmetic and copies ran while one was open for 1% of the time, Pallas kernels for 1%

profile of v2, /device:TPU:3, one launch (start us, length us, event | category | flops | bytes accessed | tf_op | source)
XLA Modules:
  0.0 91.9 jit_solution(5416713769827806822)
XLA Ops:
  1.4 0.8 copy-done.1
  2.2 0.9 copy-done.3
  3.1 0.9 copy-done.4
  4.0 1.4 %pack.1 = (bf16[8,64,256]{2,1,0:T(8,128)(2,1)S(1)}, bf16[5,64,256]{2,1,0:T(8,128)(2,1)S(1)}, bf16[5,64,256]{2,1,0:T(8,128)(2,1)S(1)}, f32[16,384]{1,0:T(8,128)S(1)}) custom-call(s32[1,1,4,2]{3,2,1,0:T(4,128)S(1)} %copy.29.anchors, s32[1,1]{1,0:T(1,128)S(6)} %copy.35.counts, bf16[32,8,256]{2,1,0:T(8,128)(2,1)S(1)} %copy-done.3, ...), custom_call_target="tpu_custom_call" | custom-call | tf_op jit(solution)/shard_map/pack/pallas_call | solution.py:396
  5.4 0.7 collective-permute-start
  6.1 3.1 %collective-permute-start.1 = (bf16[5,64,256]{2,1,0:T(8,128)(2,1)S(1)}, bf16[5,64,256]{2,1,0:T(8,128)(2,1)S(1)}, u32[]{:S(2)}, u32[]{:S(2)}) collective-permute-start(bf16[5,64,256]{2,1,0:T(8,128)(2,1)S(1)} %get-tuple-element.22), channel_id=1, source_target_pairs={{4,8},{8,4},{12,16},{16,12},{20,24},{24,20},{5,9},{9,5},{13,17},{1... | collective-permute-start | bytes 491528 | tf_op jit(solution)/shard_map/ppermute | solution.py:358
  9.2 5.6 %collective-permute-done.1.second = bf16[5,64,256]{2,1,0:T(8,128)(2,1)S(1)} collective-permute-done((bf16[5,64,256]{2,1,0:T(8,128)(2,1)S(1)}, bf16[5,64,256]{2,1,0:T(8,128)(2,1)S(1)}, u32[]{:S(2)}, u32[]{:S(2)}) %collective-permute-start.1) | collective-permute-done | bytes 163872 | tf_op jit(solution)/shard_map/ppermute | solution.py:358
  14.9 3.3 %collective-permute-start.3 = (bf16[96,128]{1,0:T(8,128)(2,1)S(1)}, bf16[96,128]{1,0:T(8,128)(2,1)S(1)}, u32[]{:S(2)}, u32[]{:S(2)}) collective-permute-start(bf16[96,128]{1,0:T(8,128)(2,1)S(1)} %get-tuple-element.24), channel_id=1, source_target_pairs={{1,2},{2,1},{3,0},{0,3},{5,6},{6,5},{7,4},{4,7},{9,10},{10,9},{11,... | collective-permute-start | bytes 73736 | tf_op jit(solution)/shard_map/ppermute | solution.py:358
  18.4 0.8 copy-done
  19.9 1.0 %collective-permute-done.2.third = bf16[96,128]{1,0:T(8,128)(2,1)S(1)} collective-permute-done((bf16[96,128]{1,0:T(8,128)(2,1)S(1)}, bf16[96,128]{1,0:T(8,128)(2,1)S(1)}, u32[]{:S(2)}, u32[]{:S(2)}) %collective-permute-start.2) | collective-permute-done | bytes 24608 | tf_op jit(solution)/shard_map/ppermute | solution.py:358
  20.9 17.7 %patches.1 = (f32[1792,128]{1,0:T(8,128)S(1)}, f32[16,32,384]{2,1,0:T(8,128)S(1)}, f32[32,128]{1,0:T(8,128)S(1)}, f32[8,256]{1,0:T(8,128)S(1)}) custom-call(s32[1,1,4,2]{3,2,1,0:T(4,128)S(1)} %copy.29.anchors, s32[1,1]{1,0:T(1,128)S(6)} %copy.35.counts, bf16[8,64,256]{2,1,0:T(8,128)(2,1)S(1)} %get-tuple-element.20.center, ...), custom_call_target="tpu_custom_call" | custom-call | tf_op jit(solution)/shard_map/patches/pallas_call | solution.py:436
  38.6 14.1 %all_to_all.20 = bf16[8,224,128]{2,1,0:T(8,128)(2,1)S(1)} all-to-all(bf16[8,224,128]{2,1,0:T(8,128)(2,1)S(1)} %bitcast.20), channel_id=1, replica_groups=mesh['lat'=8,'lon'=4] {'lat'}, dimensions={0} | all-to-all | bytes 917504 | tf_op jit(solution)/shard_map/all_to_all | solution.py:373
  52.8 7.1 %all_to_all.21 = f32[4,56,128]{2,1,0:T(8,128)S(1)} all-to-all(f32[4,56,128]{2,1,0:T(8,128)S(1)} %bitcast.23), channel_id=1, replica_groups=mesh['lat'=8,'lon'=4] {'lon'}, dimensions={0} | all-to-all | bytes 229376 | tf_op jit(solution)/shard_map/all_to_all | solution.py:376
  60.0 7.8 %all_to_all.22 = bf16[4,56,128]{2,1,0:T(8,128)(2,1)S(1)} all-to-all(bf16[4,56,128]{2,1,0:T(8,128)(2,1)S(1)} %broadcast_in_dim.6), channel_id=1, replica_groups=mesh['lat'=8,'lon'=4] {'lon'}, dimensions={0} | all-to-all | bytes 114688 | tf_op jit(solution)/shard_map/all_to_all | solution.py:379
  67.8 0.8 broadcast_in_dim.15
  68.6 6.5 %all-to-all-start.3 = ((bf16[8,224,128]{2,1,0:T(8,128)(2,1)}), bf16[8,224,128]{2,1,0:T(8,128)(2,1)S(1)}, u32[]{:S(2)}, u32[]{:S(2)}) async-start(bf16[8,224,128]{2,1,0:T(8,128)(2,1)} %broadcast_in_dim.15), calls=%async_computation.3 | async-start | bytes 917504 | tf_op jit(solution)/shard_map/all_to_all | solution.py:382
  75.1 0.4 collective-permute-start.5
  75.8 3.7 %collective-permute-done.5.fourth = f32[32,128]{1,0:T(8,128)S(1)} collective-permute-done((f32[32,128]{1,0:T(8,128)S(1)}, f32[32,128]{1,0:T(8,128)S(1)}, u32[]{:S(2)}, u32[]{:S(2)}) %collective-permute-start.5) | collective-permute-done | bytes 16416 | tf_op jit(solution)/shard_map/ppermute | solution.py:358
  79.7 1.6 %collective-permute-start.6 = (f32[4,32,256]{2,1,0:T(8,128)S(1)}, f32[4,32,256]{2,1,0:T(8,128)S(1)}, u32[]{:S(2)}, u32[]{:S(2)}) collective-permute-start(f32[4,32,256]{2,1,0:T(8,128)S(1)} %get-tuple-element.29), channel_id=1, source_target_pairs={{0,4},{4,0},{8,12},{12,8},{16,20},{20,16},{24,28},{28,24},{1,5},{5... | collective-permute-start | bytes 393224 | tf_op jit(solution)/shard_map/ppermute | solution.py:358
  81.3 3.0 %collective-permute-start.7 = (f32[4,32,256]{2,1,0:T(8,128)S(1)}, f32[4,32,256]{2,1,0:T(8,128)S(1)}, u32[]{:S(2)}, u32[]{:S(2)}) collective-permute-start(f32[4,32,256]{2,1,0:T(8,128)S(1)} %get-tuple-element.30), channel_id=1, source_target_pairs={{4,8},{8,4},{12,16},{16,12},{20,24},{24,20},{5,9},{9,5},{13,17},{1... | collective-permute-start | bytes 393224 | tf_op jit(solution)/shard_map/ppermute | solution.py:358
  84.3 4.9 %collective-permute-done.7.second = f32[4,32,256]{2,1,0:T(8,128)S(1)} collective-permute-done((f32[4,32,256]{2,1,0:T(8,128)S(1)}, f32[4,32,256]{2,1,0:T(8,128)S(1)}, u32[]{:S(2)}, u32[]{:S(2)}) %collective-permute-start.7) | collective-permute-done | bytes 131104 | tf_op jit(solution)/shard_map/ppermute | solution.py:358
  89.2 0.8 fold.1
  90.0 1.0 %split.1 = (f32[9,128,32]{2,1,0:T(8,128)S(1)}, f32[9,128,128]{2,1,0:T(8,128)}, f32[9,32,128]{2,1,0:T(8,128)}) custom-call(bf16[1792,128]{1,0:T(8,128)(2,1)S(1)} %bitcast.17), custom_call_target="tpu_custom_call" | custom-call | tf_op jit(solution)/shard_map/split/pallas_call | solution.py:487
  91.0 0.9 copy.34
  (31 shorter events, 1.8 us)
Async XLA Ops:
  0.6 0.7 copy-start.7
  1.4 0.8 copy-start.1
  2.2 0.9 copy-start.3
  3.1 0.9 copy-start.4
  5.4 3.8 %collective-permute-start = (bf16[5,64,256]{2,1,0:T(8,128)(2,1)S(1)}, bf16[5,64,256]{2,1,0:T(8,128)(2,1)S(1)}, u32[]{:S(2)}, u32[]{:S(2)}) collective-permute-start(bf16[5,64,256]{2,1,0:T(8,128)(2,1)S(1)} %get-tuple-element.21), channel_id=1, source_target_pairs={{0,4},{4,0},{8,12},{12,8},{16,20},{20,16},{24,28},{28,24},{1,5},{5... | collective-permute-start | bytes 491528 | tf_op jit(solution)/shard_map/ppermute | solution.py:358
  6.1 8.7 %collective-permute-start.1 = (bf16[5,64,256]{2,1,0:T(8,128)(2,1)S(1)}, bf16[5,64,256]{2,1,0:T(8,128)(2,1)S(1)}, u32[]{:S(2)}, u32[]{:S(2)}) collective-permute-start(bf16[5,64,256]{2,1,0:T(8,128)(2,1)S(1)} %get-tuple-element.22), channel_id=1, source_target_pairs={{4,8},{8,4},{12,16},{16,12},{20,24},{24,20},{5,9},{9,5},{13,17},{1... | collective-permute-start | bytes 491528 | tf_op jit(solution)/shard_map/ppermute | solution.py:358
  14.7 3.5 %copy-start.6 = (bf16[9,128,32]{1,2,0:T(8,128)(2,1)S(1)}, bf16[9,128,32]{1,2,0:T(8,128)(2,1)}, u32[]{:S(2)}) copy-start(bf16[9,128,32]{1,2,0:T(8,128)(2,1)} %param.10) | copy-start | bytes 221188
  14.7 4.5 %copy-start.5 = (bf16[9,128,128]{2,1,0:T(8,128)(2,1)S(1)}, bf16[9,128,128]{2,1,0:T(8,128)(2,1)}, u32[]{:S(2)}) copy-start(bf16[9,128,128]{2,1,0:T(8,128)(2,1)} %param.11) | copy-start | bytes 884740
  14.9 5.0 %collective-permute-start.3 = (bf16[96,128]{1,0:T(8,128)(2,1)S(1)}, bf16[96,128]{1,0:T(8,128)(2,1)S(1)}, u32[]{:S(2)}, u32[]{:S(2)}) collective-permute-start(bf16[96,128]{1,0:T(8,128)(2,1)S(1)} %get-tuple-element.24), channel_id=1, source_target_pairs={{1,2},{2,1},{3,0},{0,3},{5,6},{6,5},{7,4},{4,7},{9,10},{10,9},{11,... | collective-permute-start | bytes 73736 | tf_op jit(solution)/shard_map/ppermute | solution.py:358
  18.2 2.7 %collective-permute-start.2 = (bf16[96,128]{1,0:T(8,128)(2,1)S(1)}, bf16[96,128]{1,0:T(8,128)(2,1)S(1)}, u32[]{:S(2)}, u32[]{:S(2)}) collective-permute-start(bf16[96,128]{1,0:T(8,128)(2,1)S(1)} %get-tuple-element.24), channel_id=1, source_target_pairs={{0,1},{1,0},{2,3},{3,2},{4,5},{5,4},{6,7},{7,6},{8,9},{9,8},{10,11... | collective-permute-start | bytes 73736 | tf_op jit(solution)/shard_map/ppermute | solution.py:358
  18.3 0.9 copy-start
  19.7 1.2 %copy-start.2 = (s32[4,8,256]{2,1,0:T(8,128)S(1)}, s32[4,8,256]{2,1,0:T(8,128)}, u32[]{:S(2)}) copy-start(s32[4,8,256]{2,1,0:T(8,128)} %weights.1) | copy-start | bytes 98308
  68.6 21.4 %all-to-all-start.3 = ((bf16[8,224,128]{2,1,0:T(8,128)(2,1)}), bf16[8,224,128]{2,1,0:T(8,128)(2,1)S(1)}, u32[]{:S(2)}, u32[]{:S(2)}) async-start(bf16[8,224,128]{2,1,0:T(8,128)(2,1)} %broadcast_in_dim.15), calls=%async_computation.3 | async-start | bytes 917504 | tf_op jit(solution)/shard_map/all_to_all | solution.py:382
  75.1 4.4 %collective-permute-start.5 = (f32[32,128]{1,0:T(8,128)S(1)}, f32[32,128]{1,0:T(8,128)S(1)}, u32[]{:S(2)}, u32[]{:S(2)}) collective-permute-start(f32[32,128]{1,0:T(8,128)S(1)} %get-tuple-element.27), channel_id=1, source_target_pairs={{1,2},{2,1},{3,0},{0,3},{5,6},{6,5},{7,4},{4,7},{9,10},{10,9},{11,... | collective-permute-start | bytes 49160 | tf_op jit(solution)/shard_map/ppermute | solution.py:358
  75.6 4.0 %collective-permute-start.4 = (f32[32,128]{1,0:T(8,128)S(1)}, f32[32,128]{1,0:T(8,128)S(1)}, u32[]{:S(2)}, u32[]{:S(2)}) collective-permute-start(f32[32,128]{1,0:T(8,128)S(1)} %get-tuple-element.27), channel_id=1, source_target_pairs={{0,1},{1,0},{2,3},{3,2},{4,5},{5,4},{6,7},{7,6},{8,9},{9,8},{10,11... | collective-permute-start | bytes 49160 | tf_op jit(solution)/shard_map/ppermute | solution.py:358
  79.7 4.6 %collective-permute-start.6 = (f32[4,32,256]{2,1,0:T(8,128)S(1)}, f32[4,32,256]{2,1,0:T(8,128)S(1)}, u32[]{:S(2)}, u32[]{:S(2)}) collective-permute-start(f32[4,32,256]{2,1,0:T(8,128)S(1)} %get-tuple-element.29), channel_id=1, source_target_pairs={{0,4},{4,0},{8,12},{12,8},{16,20},{20,16},{24,28},{28,24},{1,5},{5... | collective-permute-start | bytes 393224 | tf_op jit(solution)/shard_map/ppermute | solution.py:358
  81.3 7.9 %collective-permute-start.7 = (f32[4,32,256]{2,1,0:T(8,128)S(1)}, f32[4,32,256]{2,1,0:T(8,128)S(1)}, u32[]{:S(2)}, u32[]{:S(2)}) collective-permute-start(f32[4,32,256]{2,1,0:T(8,128)S(1)} %get-tuple-element.30), channel_id=1, source_target_pairs={{4,8},{8,4},{12,16},{16,12},{20,24},{24,20},{5,9},{9,5},{13,17},{1... | collective-permute-start | bytes 393224 | tf_op jit(solution)/shard_map/ppermute | solution.py:358

commit v3 on v2

--- a/solution.py
+++ b/solution.py
@@ -140,8 +140,8 @@
 def patch_kernel(
     anchors, counts, center, first, second, third, fourth, total_in, weights,
     w_in, w_mid, w_mid_back, w_out, w_out_back,
-    grads, numer, edges, den_out,
-    window, x_s, d_s, h_s, z_s, slope_s, dh_s, h2_s, dz_s, y_s,
+    send, keep, second_out, numer, den_out,
+    grads, window, x_s, d_s, h_s, z_s, slope_s, dh_s, h2_s, dz_s, y_s,
 ):
     rows = center.shape[0]
     channels = center.shape[1] // 2
@@ -199,11 +199,11 @@
 
     def before(value):
         ids = lane_ids(value.shape)
-        return jnp.where(ids == 0, 0.0, roll(value, 1, 1))
+        return jnp.where(ids == 0, jnp.zeros_like(value), roll(value, 1, 1))
 
     def after(value):
         ids = lane_ids(value.shape)
-        return jnp.where(ids == cols - 1, 0.0, roll(value, cols - 1, 1))
+        return jnp.where(ids == cols - 1, jnp.zeros_like(value), roll(value, cols - 1, 1))
 
     def spread(ref, value, row, flip):
         count = value.shape[0]
@@ -211,9 +211,9 @@
         first, last = before(value), after(value)
         if flip:
             first, last = last, first
-        ref[0:count, at] = first.astype(BF16)
-        ref[count : 2 * count, at] = value.astype(BF16)
-        ref[2 * count : 3 * count, at] = last.astype(BF16)
+        ref[0:count, at] = first
+        ref[count : 2 * count, at] = value
+        ref[2 * count : 3 * count, at] = last
 
     def stack(ref, row, flip):
         starts = [(row + (2 - tap if flip else tap)) * cols for tap in range(3)]
@@ -226,14 +226,14 @@
         back_shift = lax.rem(wide + MARGIN - col0, wide)
         for row in range(rows):
             line = roll(window[row0 + row], back_shift, 1)[:, :cols]
-            spread(x_s, line[:channels], row, False)
+            spread(x_s, line[:channels].astype(BF16), row, False)
             grad = line[channels:] * patch_weights[row : row + 1]
-            spread(d_s, grad.astype(BF16).astype(F32), row, True)
+            spread(d_s, grad.astype(BF16), row, True)
         for row in range(rows):
             at = slice(row * cols, (row + 1) * cols)
             z1 = dot(w_in[...], stack(x_s, row, False))
             sig = 0.5 * jnp.tanh(0.5 * z1) + 0.5
-            h1 = (z1 * sig).astype(BF16).astype(F32)
+            h1 = (z1 * sig).astype(BF16)
             slope_s[:, at] = sig * (1.0 + z1 * (1.0 - sig))
             spread(h_s, h1, row, False)
         for row in range(rows):
@@ -244,7 +244,7 @@
             h1 = h_s[width : 2 * width, (row + 1) * cols : (row + 2) * cols].astype(F32)
             h2 = (h1 + z2 * sig).astype(BF16)
             h2_s[:, at] = h2
-            dz2 = (dh2 * (sig * (1.0 + z2 * (1.0 - sig)))).astype(BF16).astype(F32)
+            dz2 = (dh2 * (sig * (1.0 + z2 * (1.0 - sig)))).astype(BF16)
             dh_s[:, at] = dh2
             spread(z_s, dz2, row, True)
             y_s[:, (row + 1) * cols : (row + 2) * cols] = dot(w_out[...], h2)
@@ -283,65 +283,85 @@
 
     lax.fori_loop(0, counts[0, 0], one_patch, 0)
 
-    lanes = lane_ids((channels, LANES))
-    packed = jnp.zeros((channels, LANES), F32)
-    for row in range(height):
-        beside = numer[row, :, cols:]
-        first = jnp.where(lanes < MARGIN, beside, 0.0)
-        last = jnp.where(lanes >= LANES - MARGIN, beside, 0.0)
-        packed = packed + roll(first, MARGIN * row, 1) + roll(last, -MARGIN * row, 1)
-    edges[...] = packed
-
-
-def beside_kernel(numer, third, fourth, inner, first_out, second_out):
+    half = grads.shape[0] // 2
+    odd_index = lax.rem(lax.axis_index("lat"), 2)
+    send[0:half] = grads[pl.ds(pl.multiple_of((1 - odd_index) * half, half), half)].astype(BF16)
+    keep[...] = grads[pl.ds(pl.multiple_of(odd_index * half, half), half)]
+    blocks = wide // LANES
+    for row in range(MARGIN):
+        upper, lower = numer[row], numer[MARGIN + rows + row]
+        near = choose(lat_odd, upper, lower).astype(BF16)
+        far = choose(lat_odd, lower, upper).astype(BF16)
+        for block in range(blocks):
+            at = (row * blocks + block) * channels
+            send[half + at : half + at + channels] = near[:, block * LANES : (block + 1) * LANES]
+            second_out[at : at + channels] = far[:, block * LANES : (block + 1) * LANES]
+
+
+def beside_kernel(numer, first, second, inner, edges):
     height, channels, wide = numer.shape
     cols = wide - LANES
     rows = height - 2 * MARGIN
+    blocks = wide // LANES
+    base = first.shape[0] - second.shape[0]
     lanes = lane_ids((channels, LANES))
     lat_odd = lax.rem(lax.axis_index("lat"), 2) == 1
+    packed = jnp.zeros((channels, LANES), F32)
+    for row in range(rows):
+        parts = []
+        for block in range(blocks):
+            at = ((row % MARGIN) * blocks + block) * channels
+            near = first[base + at : base + at + channels].astype(F32)
+            far = second[at : at + channels].astype(F32)
+            other = choose(lat_odd, near, far) if row < MARGIN else choose(lat_odd, far, near)
+            parts.append(numer[MARGIN + row, :, block * LANES : (block + 1) * LANES] + other)
+        inner[row] = jnp.concatenate(parts[:-1], axis=1)
+        low = jnp.where(lanes < MARGIN, parts[-1], 0.0)
+        high = jnp.where(lanes >= LANES - MARGIN, parts[-1], 0.0)
+        packed = packed + roll(low, MARGIN * row, 1) + roll(high, -MARGIN * row, 1)
+    edges[...] = packed.astype(BF16)
+
+
+def fold_kernel(inner, third, fourth, den, blended):
+    rows, channels, cols = inner.shape
+    lanes = lane_ids((channels, LANES))
     lon_odd = lax.rem(lax.axis_index("lon"), 2) == 1
-    left = choose(lon_odd, third[...], fourth[...])
-    right = choose(lon_odd, fourth[...], third[...])
+    left = choose(lon_odd, third[...], fourth[...]).astype(F32)
+    right = choose(lon_odd, fourth[...], third[...]).astype(F32)
+    inverse = 1.0 / den[...]
     lines = []
-    for row in range(height):
+    for row in range(rows):
         from_left = jnp.where(lanes < MARGIN, roll(left, -MARGIN * row, 1), 0.0)
         from_right = jnp.where(lanes >= LANES - MARGIN, roll(right, MARGIN * row, 1), 0.0)
         beside = [from_left]
         for _ in range(cols // LANES - 2):
             beside.append(jnp.zeros((channels, LANES), F32))
         beside.append(from_right)
-        lines.append(numer[row, :, :cols] + jnp.concatenate(beside, axis=1))
-    for row in range(MARGIN):
-        upper, lower = lines[row], lines[MARGIN + rows + row]
-        first_out[row] = choose(lat_odd, upper, lower)
-        second_out[row] = choose(lat_odd, lower, upper)
-    for row in range(rows):
-        inner[row] = lines[MARGIN + row]
-
-
-def fold_kernel(inner, first, second, den, blended):
-    rows = inner.shape[0]
-    lat_odd = lax.rem(lax.axis_index("lat"), 2) == 1
-    inverse = 1.0 / den[...]
-    lines = []
-    for row in range(rows):
-        if row < MARGIN:
-            other = choose(lat_odd, first[row], second[row])
-        else:
-            at = row - (rows - MARGIN)
-            other = choose(lat_odd, second[at], first[at])
-        lines.append(((inner[row] + other) * inverse[row : row + 1])[None])
+        line = inner[row] + jnp.concatenate(beside, axis=1)
+        lines.append((line * inverse[row : row + 1])[None])
     blended[...] = jnp.swapaxes(jnp.concatenate(lines, axis=0), 0, 1)
 
 
-def split_kernel(summed, grad_in, grad_mid, grad_out):
-    taps, width, channels = grad_in.shape
+def split_kernel(own, other, grad_in, grad_mid, grad_out):
+    taps, channels, width = grad_in.shape
+    half = own.shape[0]
+    odd = lax.rem(lax.axis_index("lat"), 2) == 1
+    own, other = own[...], other[...]
+    summed = (choose(odd, other, own), choose(odd, own, other))
+
+    def rows_of(start, count):
+        pieces = []
+        stop = start + count
+        if start < half:
+            pieces.append(summed[0][start : min(stop, half)])
+        if stop > half:
+            pieces.append(summed[1][max(start, half) - half : stop - half])
+        return jnp.concatenate(pieces, axis=0).astype(F32) if len(pieces) > 1 else pieces[0].astype(F32)
+
     for tap in range(taps):
-        grad_in[tap] = summed[tap * channels : (tap + 1) * channels].astype(F32).T
-        start = taps * channels + tap * width
-        grad_mid[tap] = summed[start : start + width].astype(F32)
-        start = taps * (channels + width) + tap * channels
-        grad_out[tap] = summed[start : start + channels].astype(F32)
+        grad_in[tap] = rows_of(tap * channels, channels)
+        grad_mid[tap] = rows_of(taps * channels + tap * width, width)
+        grad_out[tap] = rows_of(taps * (channels + width) + tap * channels, channels)
 
 
 def params():
@@ -366,21 +386,20 @@
     return swap(edges, "lon", 0, True), swap(edges, "lon", 1, True)
 
 
-def reduce_all(grads):
-    lat_size, lon_size = lax.axis_size("lat"), lax.axis_size("lon")
-    length = grads.shape[0]
-    parts = grads.astype(BF16).reshape(lat_size, length // lat_size, LANES)
-    parts = lax.all_to_all(parts, "lat", 0, 0)
-    mine = jnp.sum(parts.astype(F32), axis=0)
-    parts = mine.reshape(lon_size, length // (lat_size * lon_size), LANES)
-    parts = lax.all_to_all(parts, "lon", 0, 0)
-    mine = jnp.sum(parts, axis=0).astype(BF16)
-    parts = jnp.broadcast_to(mine[None], (lon_size,) + mine.shape)
-    parts = lax.all_to_all(parts, "lon", 0, 0)
-    mine = parts.reshape(length // lat_size, LANES)
-    parts = jnp.broadcast_to(mine[None], (lat_size,) + mine.shape)
-    parts = lax.all_to_all(parts, "lat", 0, 0)
-    return parts.reshape(length, LANES)
+def exchange(value, axis, step):
+    pairs = [(index, index ^ step) for index in range(lax.axis_size(axis))]
+    return lax.ppermute(value, axis, pairs)
+
+
+def halves(value, bit):
+    half = value.shape[0] // 2
+    own = lax.dynamic_slice_in_dim(value, bit * half, half, 0)
+    other = lax.dynamic_slice_in_dim(value, (1 - bit) * half, half, 0)
+    return own, other
+
+
+def ordered(own, other, bit):
+    return jnp.concatenate([jnp.where(bit == 0, own, other), jnp.where(bit == 0, other, own)], axis=0)
 
 
 def shards(
@@ -401,7 +420,7 @@
             shape((MARGIN + 1, 2 * channels, cols), BF16),
             shape((height, wide), F32),
         ),
-        in_specs=[smem(), smem()] + [pl.BlockSpec(memory_space=pl.ANY)] * 3,
+        in_specs=[smem(), smem()] + [pl.BlockSpec(memory_space=pltpu.HBM)] * 3,
         out_specs=(vmem(),) * 4,
         scratch_shapes=[
             pltpu.VMEM(fields.shape, BF16),
@@ -430,20 +449,25 @@
     w_out = kernel_out.reshape(taps * channels, width)
     w_out_back = jnp.transpose(kernel_out, (2, 0, 1)).reshape(width, taps * channels)
 
+    lat_size, lon_size = lax.axis_size("lat"), lax.axis_size("lon")
     length = taps * (2 * channels + width)
-    unit = 8 * lax.axis_size("lat") * lax.axis_size("lon")
+    unit = 16 * lat_size
     length = (length + unit - 1) // unit * unit
-    grads, numer, edges, den = pl.pallas_call(
+    half = length // 2
+    edge_rows = MARGIN * channels * (wide // LANES)
+    send, keep, second, numer, den = pl.pallas_call(
         patch_kernel,
         out_shape=(
-            shape((length, LANES), F32),
+            shape((half + edge_rows, LANES), BF16),
+            shape((half, LANES), F32),
+            shape((edge_rows, LANES), BF16),
             shape((height, channels, wide), F32),
-            shape((channels, LANES), F32),
             shape((rows, cols), F32),
         ),
         in_specs=[smem(), smem()] + [vmem()] * 12,
-        out_specs=(vmem(),) * 4,
+        out_specs=(vmem(),) * 5,
         scratch_shapes=[
+            pltpu.VMEM((length, LANES), F32),
             pltpu.VMEM((height, 2 * channels, wide), F32),
             pltpu.VMEM((3 * channels, padded), BF16),
             pltpu.VMEM((3 * channels, padded), BF16),
@@ -461,20 +485,39 @@
         patch_anchors, tile_counts, center, first, second, third, fourth, total, blend_weights,
         w_in, w_mid, w_mid_back, w_out, w_out_back,
     )
-    third, fourth = swap_lon(edges)
-    inner, first, second = pl.pallas_call(
+
+    lat = lax.axis_index("lat")
+    first = exchange(send, "lat", 1)
+    second = swap(second, "lat", 1, False)
+    mine = keep + first[:half].astype(F32)
+    step = 2
+    while step < lat_size:
+        own, other = halves(mine, (lat // step) % 2)
+        mine = own + exchange(other.astype(BF16), "lat", step).astype(F32)
+        step *= 2
+    inner, edges = pl.pallas_call(
         beside_kernel,
-        out_shape=(
-            shape((rows, channels, cols), F32),
-            shape((MARGIN, channels, cols), F32),
-            shape((MARGIN, channels, cols), F32),
-        ),
+        out_shape=(shape((rows, channels, cols), F32), shape((channels, LANES), BF16)),
         in_specs=[vmem()] * 3,
-        out_specs=(vmem(),) * 3,
+        out_specs=(vmem(),) * 2,
         compiler_params=params(),
         name="beside",
-    )(numer, third, fourth)
-    first, second = swap_lat(first, second)
+    )(numer, first, second)
+    count = mine.shape[0]
+    mine = mine.astype(BF16)
+    if lon_size == 4:
+        received = []
+        for start in (0, 1):
+            other = swap(jnp.concatenate([mine, edges], axis=0), "lon", start, True)
+            received.append(other[count:])
+            mine = (mine.astype(F32) + other[:count].astype(F32)).astype(BF16)
+        third, fourth = received
+    else:
+        third, fourth = swap_lon(edges)
+        step = 1
+        while step < lon_size:
+            mine = (mine.astype(F32) + exchange(mine, "lon", step).astype(F32)).astype(BF16)
+            step *= 2
     blended = pl.pallas_call(
         fold_kernel,
         out_shape=shape((channels, rows, cols), F32),
@@ -482,21 +525,24 @@
         out_specs=vmem(),
         compiler_params=params(),
         name="fold",
-    )(inner, first, second, den)
-    summed = reduce_all(grads)
+    )(inner, third, fourth, den)
+    step = lat_size // 2
+    while step > 1:
+        mine = ordered(mine, exchange(mine, "lat", step), (lat // step) % 2)
+        step //= 2
     grad_in, grad_mid, grad_out = pl.pallas_call(
         split_kernel,
         out_shape=(
-            shape((taps, width, channels), F32),
+            shape((taps, channels, width), F32),
             shape((taps, width, width), F32),
             shape((taps, channels, width), F32),
         ),
-        in_specs=[vmem()],
+        in_specs=[vmem()] * 2,
         out_specs=(vmem(),) * 3,
         compiler_params=params(),
         name="split",
-    )(summed)
-    return blended, grad_in, grad_mid, grad_out
+    )(mine, exchange(mine, "lat", 1))
+    return blended, jnp.transpose(grad_in, (0, 2, 1)), grad_mid, grad_out
 
 
 def solution(mesh):

time: 92.4 us -> 79.6 us (0.86)
  the two profiles are of different devices: /device:TPU:3 before, /device:TPU:0 now
where the time goes in v3:
time: 79.6 us; the launch traced here: 79.2 us
  waiting for transfers between devices  32.3 us (41%)
  starting transfers between devices  24.8 us (31%)
  Pallas kernels  15.4 us (19%)
  local copies, waits for them, and re-layouts  4.93 us (6%)
  between operations  1.58 us (2%)
    ppermute x6, waiting for transfers between devices, exchange(): return lax.ppermute(value, axis, pairs)  20 us
    ppermute x6, starting transfers between devices, exchange(): return lax.ppermute(value, axis, pairs)  17.3 us
    ppermute x7, waiting for transfers between devices, swap(): return lax.ppermute(value, axis, pairs)  12.3 us
    pallas_call x1, Pallas kernels, shards(): pl.pallas_call(patch_kernel, out_shape=(shape((half + edge_rows, LANES),...  11.9 us
    ppermute x7, starting transfers between devices, swap(): return lax.ppermute(value, axis, pairs)  7.46 us
    unnamed x16, local copies, waits for them, and re-layouts  4.23 us
  transfers between devices with their start and end apart: 13, of which 10 were waited for; matrix products, arithmetic and copies ran while one was open for 1% of the time, Pallas kernels for 1%

profile of v3, /device:TPU:0, one launch (start us, length us, event | category | flops | bytes accessed | tf_op | source)
XLA Modules:
  0.0 79.2 jit_solution(10870402326409929617)
XLA Ops:
  0.6 0.8 copy.20.anchors
  2.1 0.7 copy-done.1
  2.8 0.9 %copy-done.3 = bf16[32,8,256]{2,1,0:T(8,128)(2,1)S(1)} copy-done((bf16[32,8,256]{2,1,0:T(8,128)(2,1)S(1)}, bf16[32,8,256]{2,1,0:T(8,128)(2,1)}, u32[]{:S(2)}) %copy-start.3) | copy-done | bytes 131096
  3.7 0.9 %copy-done.4 = bf16[32,8,256]{2,1,0:T(8,128)(2,1)S(1)} copy-done((bf16[32,8,256]{2,1,0:T(8,128)(2,1)S(1)}, bf16[32,8,256]{2,1,0:T(8,128)(2,1)}, u32[]{:S(2)}) %copy-start.4) | copy-done | bytes 131096
  4.6 1.3 %pack.1 = (bf16[8,64,256]{2,1,0:T(8,128)(2,1)S(1)}, bf16[5,64,256]{2,1,0:T(8,128)(2,1)S(1)}, bf16[5,64,256]{2,1,0:T(8,128)(2,1)S(1)}, f32[16,384]{1,0:T(8,128)S(1)}) custom-call(s32[1,1,4,2]{3,2,1,0:T(4,128)S(1)} %copy.20.anchors, s32[1,1]{1,0:T(1,128)S(6)} %copy.25.counts, bf16[32,8,256]{2,1,0:T(8,128)(2,1)S(1)} %copy-done.3, ...), custom_call_target="tpu_custom_call" | custom-call | tf_op jit(solution)/shard_map/pack/pallas_call | solution.py:415
  6.0 0.7 collective-permute-start
  6.6 0.7 collective-permute-start.1
  7.9 2.9 %collective-permute-start.2 = (bf16[96,128]{1,0:T(8,128)(2,1)S(1)}, bf16[96,128]{1,0:T(8,128)(2,1)S(1)}, u32[]{:S(2)}, u32[]{:S(2)}) collective-permute-start(bf16[96,128]{1,0:T(8,128)(2,1)S(1)} %get-tuple-element.24), channel_id=1, source_target_pairs={{0,1},{1,0},{2,3},{3,2},{4,5},{5,4},{6,7},{7,6},{8,9},{9,8},{10,11... | collective-permute-start | bytes 73736 | tf_op jit(solution)/shard_map/ppermute | solution.py:378
  10.8 2.4 %collective-permute-start.3 = (bf16[96,128]{1,0:T(8,128)(2,1)S(1)}, bf16[96,128]{1,0:T(8,128)(2,1)S(1)}, u32[]{:S(2)}, u32[]{:S(2)}) collective-permute-start(bf16[96,128]{1,0:T(8,128)(2,1)S(1)} %get-tuple-element.24), channel_id=1, source_target_pairs={{1,2},{2,1},{3,0},{0,3},{5,6},{6,5},{7,4},{4,7},{9,10},{10,9},{11,... | collective-permute-start | bytes 73736 | tf_op jit(solution)/shard_map/ppermute | solution.py:378
  14.0 0.7 copy-done
  14.8 1.6 %collective-permute-done.3.fourth = bf16[96,128]{1,0:T(8,128)(2,1)S(1)} collective-permute-done((bf16[96,128]{1,0:T(8,128)(2,1)S(1)}, bf16[96,128]{1,0:T(8,128)(2,1)S(1)}, u32[]{:S(2)}, u32[]{:S(2)}) %collective-permute-start.3) | collective-permute-done | bytes 24608 | tf_op jit(solution)/shard_map/ppermute | solution.py:378
  16.4 11.9 %patches.1 = (bf16[1280,128]{1,0:T(8,128)(2,1)S(1)}, f32[896,128]{1,0:T(8,128)S(1)}, bf16[384,128]{1,0:T(8,128)(2,1)S(1)}, f32[16,32,384]{2,1,0:T(8,128)S(1)}, f32[8,256]{1,0:T(8,128)S(1)}) custom-call(s32[1,1,4,2]{3,2,1,0:T(4,128)S(1)} %copy.20.anchors, s32[1,1]{1,0:T(1,128)S(6)} %copy.25.counts, bf16[8,64,256]{2,1,0:T(8,128)(2,1)S(1)} %get-tuple-element.20.center, ...), custom_call_target="tpu_custom_call" | custom-call | tf_op jit(solution)/shard_map/patches/pallas_call | solution.py:458
  28.4 16.9 %collective-permute-start.4 = (bf16[1280,128]{1,0:T(8,128)(2,1)S(1)}, bf16[1280,128]{1,0:T(8,128)(2,1)S(1)}, u32[]{:S(2)}, u32[]{:S(2)}) collective-permute-start(bf16[1280,128]{1,0:T(8,128)(2,1)S(1)} %get-tuple-element.27), channel_id=1, source_target_pairs={{0,4},{4,0},{8,12},{12,8},{16,20},{20,16},{24,28},{28,24},{1,5},{5... | collective-permute-start | bytes 983048 | tf_op jit(solution)/shard_map/ppermute | solution.py:391
  45.2 1.3 %collective-permute-done.4.first = bf16[1280,128]{1,0:T(8,128)(2,1)S(1)} collective-permute-done((bf16[1280,128]{1,0:T(8,128)(2,1)S(1)}, bf16[1280,128]{1,0:T(8,128)(2,1)S(1)}, u32[]{:S(2)}, u32[]{:S(2)}) %collective-permute-start.4) | collective-permute-done | bytes 327712 | tf_op jit(solution)/shard_map/ppermute | solution.py:391
  46.7 0.7 collective-permute-start.5
  47.4 5.2 %collective-permute-done.6 = bf16[448,128]{1,0:T(8,128)(2,1)S(1)} collective-permute-done((bf16[448,128]{1,0:T(8,128)(2,1)S(1)}, bf16[448,128]{1,0:T(8,128)(2,1)S(1)}, u32[]{:S(2)}, u32[]{:S(2)}) %collective-permute-start.6) | collective-permute-done | bytes 114720 | tf_op jit(solution)/shard_map/ppermute | solution.py:391
  52.9 4.0 %collective-permute-done.7 = bf16[224,128]{1,0:T(8,128)(2,1)S(1)} collective-permute-done((bf16[224,128]{1,0:T(8,128)(2,1)S(1)}, bf16[224,128]{1,0:T(8,128)(2,1)S(1)}, u32[]{:S(2)}, u32[]{:S(2)}) %collective-permute-start.7) | collective-permute-done | bytes 57376 | tf_op jit(solution)/shard_map/ppermute | solution.py:391
  57.0 4.3 %collective-permute-done.8 = bf16[256,128]{1,0:T(8,128)(2,1)S(1)} collective-permute-done((bf16[256,128]{1,0:T(8,128)(2,1)S(1)}, bf16[256,128]{1,0:T(8,128)(2,1)S(1)}, u32[]{:S(2)}, u32[]{:S(2)}) %collective-permute-start.8) | collective-permute-done | bytes 65568 | tf_op jit(solution)/shard_map/ppermute | solution.py:378
  61.4 6.0 %collective-permute-done.9 = bf16[256,128]{1,0:T(8,128)(2,1)S(1)} collective-permute-done((bf16[256,128]{1,0:T(8,128)(2,1)S(1)}, bf16[256,128]{1,0:T(8,128)(2,1)S(1)}, u32[]{:S(2)}, u32[]{:S(2)}) %collective-permute-start.9) | collective-permute-done | bytes 65568 | tf_op jit(solution)/shard_map/ppermute | solution.py:378
  67.5 4.2 %collective-permute-done.10 = bf16[224,128]{1,0:T(8,128)(2,1)S(1)} collective-permute-done((bf16[224,128]{1,0:T(8,128)(2,1)S(1)}, bf16[224,128]{1,0:T(8,128)(2,1)S(1)}, u32[]{:S(2)}, u32[]{:S(2)}) %collective-permute-start.10) | collective-permute-done | bytes 57376 | tf_op jit(solution)/shard_map/ppermute | solution.py:391
  71.9 4.7 %collective-permute-done.11 = bf16[448,128]{1,0:T(8,128)(2,1)S(1)} collective-permute-done((bf16[448,128]{1,0:T(8,128)(2,1)S(1)}, bf16[448,128]{1,0:T(8,128)(2,1)S(1)}, u32[]{:S(2)}, u32[]{:S(2)}) %collective-permute-start.11) | collective-permute-done | bytes 114720 | tf_op jit(solution)/shard_map/ppermute | solution.py:391
  76.8 0.9 %fold.1 = f32[32,8,256]{2,1,0:T(8,128)} custom-call(f32[8,32,256]{2,1,0:T(8,128)S(1)} %get-tuple-element.29.inner, bf16[32,128]{1,0:T(8,128)(2,1)S(1)} %slice.21.third, bf16[32,128]{1,0:T(8,128)(2,1)S(1)} %slice.23.fourth, f32[8,256]{1,0:T(8,128)S(1)} %get-tuple-element.32.den), custom_call_target="tpu_custom_call" | custom-call | tf_op jit(solution)/shard_map/fold/pallas_call | solution.py:521
  77.7 0.6 collective-permute-done.12.other
  78.2 1.0 %split.1 = (f32[9,32,128]{2,1,0:T(8,128)}, f32[9,128,128]{2,1,0:T(8,128)}, f32[9,32,128]{2,1,0:T(8,128)}) custom-call(bf16[896,128]{1,0:T(8,128)(2,1)S(1)} %pad_maximum_fusion.own, bf16[896,128]{1,0:T(8,128)(2,1)S(1)} %collective-permute-done.12.other), custom_call_target="tpu_custom_call" | custom-call | tf_op jit(solution)/shard_map/split/pallas_call | solution.py:533
  (43 shorter events, 2.5 us)
Async XLA Ops:
  2.0 0.8 copy-start.1
  2.8 0.9 %copy-start.3 = (bf16[32,8,256]{2,1,0:T(8,128)(2,1)S(1)}, bf16[32,8,256]{2,1,0:T(8,128)(2,1)}, u32[]{:S(2)}) copy-start(bf16[32,8,256]{2,1,0:T(8,128)(2,1)} %fields_in.1) | copy-start | bytes 393220
  3.7 0.9 %copy-start.4 = (bf16[32,8,256]{2,1,0:T(8,128)(2,1)S(1)}, bf16[32,8,256]{2,1,0:T(8,128)(2,1)}, u32[]{:S(2)}) copy-start(bf16[32,8,256]{2,1,0:T(8,128)(2,1)} %cotangent_in.1) | copy-start | bytes 393220
  6.0 1.7 %collective-permute-start = (bf16[5,64,256]{2,1,0:T(8,128)(2,1)S(1)}, bf16[5,64,256]{2,1,0:T(8,128)(2,1)S(1)}, u32[]{:S(2)}, u32[]{:S(2)}) collective-permute-start(bf16[5,64,256]{2,1,0:T(8,128)(2,1)S(1)} %get-tuple-element.21), channel_id=1, source_target_pairs={{0,4},{4,0},{8,12},{12,8},{16,20},{20,16},{24,28},{28,24},{1,5},{5... | collective-permute-start | bytes 491528 | tf_op jit(solution)/shard_map/ppermute | solution.py:378
  6.6 1.0 %collective-permute-start.1 = (bf16[5,64,256]{2,1,0:T(8,128)(2,1)S(1)}, bf16[5,64,256]{2,1,0:T(8,128)(2,1)S(1)}, u32[]{:S(2)}, u32[]{:S(2)}) collective-permute-start(bf16[5,64,256]{2,1,0:T(8,128)(2,1)S(1)} %get-tuple-element.22), channel_id=1, source_target_pairs={{4,8},{8,4},{12,16},{16,12},{20,24},{24,20},{5,9},{9,5},{13,17},{1... | collective-permute-start | bytes 491528 | tf_op jit(solution)/shard_map/ppermute | solution.py:378
  7.7 5.5 %copy-start.6 = (bf16[9,128,32]{1,2,0:T(8,128)(2,1)S(1)}, bf16[9,128,32]{1,2,0:T(8,128)(2,1)}, u32[]{:S(2)}) copy-start(bf16[9,128,32]{1,2,0:T(8,128)(2,1)} %param.10) | copy-start | bytes 221188
  7.7 5.7 %copy-start.5 = (bf16[9,128,128]{2,1,0:T(8,128)(2,1)S(1)}, bf16[9,128,128]{2,1,0:T(8,128)(2,1)}, u32[]{:S(2)}) copy-start(bf16[9,128,128]{2,1,0:T(8,128)(2,1)} %param.11) | copy-start | bytes 884740
  7.9 6.9 %collective-permute-start.2 = (bf16[96,128]{1,0:T(8,128)(2,1)S(1)}, bf16[96,128]{1,0:T(8,128)(2,1)S(1)}, u32[]{:S(2)}, u32[]{:S(2)}) collective-permute-start(bf16[96,128]{1,0:T(8,128)(2,1)S(1)} %get-tuple-element.24), channel_id=1, source_target_pairs={{0,1},{1,0},{2,3},{3,2},{4,5},{5,4},{6,7},{7,6},{8,9},{9,8},{10,11... | collective-permute-start | bytes 73736 | tf_op jit(solution)/shard_map/ppermute | solution.py:378
  10.8 5.6 %collective-permute-start.3 = (bf16[96,128]{1,0:T(8,128)(2,1)S(1)}, bf16[96,128]{1,0:T(8,128)(2,1)S(1)}, u32[]{:S(2)}, u32[]{:S(2)}) collective-permute-start(bf16[96,128]{1,0:T(8,128)(2,1)S(1)} %get-tuple-element.24), channel_id=1, source_target_pairs={{1,2},{2,1},{3,0},{0,3},{5,6},{6,5},{7,4},{4,7},{9,10},{10,9},{11,... | collective-permute-start | bytes 73736 | tf_op jit(solution)/shard_map/ppermute | solution.py:378
  13.8 0.9 %copy-start = (bf16[9,32,128]{2,1,0:T(8,128)(2,1)S(1)}, bf16[9,32,128]{2,1,0:T(8,128)(2,1)}, u32[]{:S(2)}) copy-start(bf16[9,32,128]{2,1,0:T(8,128)(2,1)} %param.12) | copy-start | bytes 221188
  14.7 1.8 %copy-start.2 = (s32[4,8,256]{2,1,0:T(8,128)S(1)}, s32[4,8,256]{2,1,0:T(8,128)}, u32[]{:S(2)}) copy-start(s32[4,8,256]{2,1,0:T(8,128)} %weights.1) | copy-start | bytes 98308
  28.4 18.1 %collective-permute-start.4 = (bf16[1280,128]{1,0:T(8,128)(2,1)S(1)}, bf16[1280,128]{1,0:T(8,128)(2,1)S(1)}, u32[]{:S(2)}, u32[]{:S(2)}) collective-permute-start(bf16[1280,128]{1,0:T(8,128)(2,1)S(1)} %get-tuple-element.27), channel_id=1, source_target_pairs={{0,4},{4,0},{8,12},{12,8},{16,20},{20,16},{24,28},{28,24},{1,5},{5... | collective-permute-start | bytes 983048 | tf_op jit(solution)/shard_map/ppermute | solution.py:391
  46.6 6.0 %collective-permute-start.6 = (bf16[448,128]{1,0:T(8,128)(2,1)S(1)}, bf16[448,128]{1,0:T(8,128)(2,1)S(1)}, u32[]{:S(2)}, u32[]{:S(2)}) collective-permute-start(bf16[448,128]{1,0:T(8,128)(2,1)S(1)} %dynamic-slice_convert_fusion), channel_id=1, source_target_pairs={{0,8},{4,12},{8,0},{12,4},{16,24},{20,28},{24,16},{28,20},{1,9},{5... | collective-permute-start | bytes 344072 | tf_op jit(solution)/shard_map/ppermute | solution.py:391
  46.7 6.1 %collective-permute-start.5 = (bf16[384,128]{1,0:T(8,128)(2,1)S(1)}, bf16[384,128]{1,0:T(8,128)(2,1)S(1)}, u32[]{:S(2)}, u32[]{:S(2)}) collective-permute-start(bf16[384,128]{1,0:T(8,128)(2,1)S(1)} %get-tuple-element.28), channel_id=1, source_target_pairs={{4,8},{8,4},{12,16},{16,12},{20,24},{24,20},{5,9},{9,5},{13,17},{1... | collective-permute-start | bytes 294920 | tf_op jit(solution)/shard_map/ppermute | solution.py:378
  52.7 4.2 %collective-permute-start.7 = (bf16[224,128]{1,0:T(8,128)(2,1)S(1)}, bf16[224,128]{1,0:T(8,128)(2,1)S(1)}, u32[]{:S(2)}, u32[]{:S(2)}) collective-permute-start(bf16[224,128]{1,0:T(8,128)(2,1)S(1)} %dynamic-slice_convert_fusion.1), channel_id=1, source_target_pairs={{0,16},{4,20},{8,24},{12,28},{16,0},{20,4},{24,8},{28,12},{1,17},{... | collective-permute-start | bytes 172040 | tf_op jit(solution)/shard_map/ppermute | solution.py:391
  56.9 4.3 %collective-permute-start.8 = (bf16[256,128]{1,0:T(8,128)(2,1)S(1)}, bf16[256,128]{1,0:T(8,128)(2,1)S(1)}, u32[]{:S(2)}, u32[]{:S(2)}) collective-permute-start(bf16[256,128]{1,0:T(8,128)(2,1)S(1)} %pad_maximum_fusion.3), channel_id=1, source_target_pairs={{0,1},{1,0},{2,3},{3,2},{4,5},{5,4},{6,7},{7,6},{8,9},{9,8},{10,11... | collective-permute-start | bytes 196616 | tf_op jit(solution)/shard_map/ppermute | solution.py:378
  61.3 6.1 %collective-permute-start.9 = (bf16[256,128]{1,0:T(8,128)(2,1)S(1)}, bf16[256,128]{1,0:T(8,128)(2,1)S(1)}, u32[]{:S(2)}, u32[]{:S(2)}) collective-permute-start(bf16[256,128]{1,0:T(8,128)(2,1)S(1)} %pad_maximum_fusion.2), channel_id=1, source_target_pairs={{1,2},{2,1},{3,0},{0,3},{5,6},{6,5},{7,4},{4,7},{9,10},{10,9},{11,... | collective-permute-start | bytes 196616 | tf_op jit(solution)/shard_map/ppermute | solution.py:378
  67.5 4.2 %collective-permute-start.10 = (bf16[224,128]{1,0:T(8,128)(2,1)S(1)}, bf16[224,128]{1,0:T(8,128)(2,1)S(1)}, u32[]{:S(2)}, u32[]{:S(2)}) collective-permute-start(bf16[224,128]{1,0:T(8,128)(2,1)S(1)} %add_convert_fusion), channel_id=1, source_target_pairs={{0,16},{4,20},{8,24},{12,28},{16,0},{20,4},{24,8},{28,12},{1,17},{... | collective-permute-start | bytes 172040 | tf_op jit(solution)/shard_map/ppermute | solution.py:391
  71.7 4.9 %collective-permute-start.11 = (bf16[448,128]{1,0:T(8,128)(2,1)S(1)}, bf16[448,128]{1,0:T(8,128)(2,1)S(1)}, u32[]{:S(2)}, u32[]{:S(2)}) collective-permute-start(bf16[448,128]{1,0:T(8,128)(2,1)S(1)} %pad_maximum_fusion.1), channel_id=1, source_target_pairs={{0,8},{4,12},{8,0},{12,4},{16,24},{20,28},{24,16},{28,20},{1,9},{5... | collective-permute-start | bytes 344072 | tf_op jit(solution)/shard_map/ppermute | solution.py:391
  76.7 1.6 %collective-permute-start.12 = (bf16[896,128]{1,0:T(8,128)(2,1)S(1)}, bf16[896,128]{1,0:T(8,128)(2,1)S(1)}, u32[]{:S(2)}, u32[]{:S(2)}) collective-permute-start(bf16[896,128]{1,0:T(8,128)(2,1)S(1)} %pad_maximum_fusion.own), channel_id=1, source_target_pairs={{0,4},{4,0},{8,12},{12,8},{16,20},{20,16},{24,28},{28,24},{1,5},{5... | collective-permute-start | bytes 688136 | tf_op jit(solution)/shard_map/ppermute | solution.py:391

commit v4 on v3

--- a/solution.py
+++ b/solution.py
@@ -60,8 +60,8 @@
 
         @pl.when(slot < counts[0, 0])
         def _():
-            row = anchors[0, 0, slot, 0]
-            col = anchors[0, 0, slot, 1]
+            row = anchors[0, 0, 0, slot]
+            col = anchors[0, 0, 1, slot]
             values = weights[slot].astype(F32)
             values = jnp.concatenate([values, jnp.zeros((rows, LANES), F32)], axis=1)
             values = jnp.concatenate([values, jnp.zeros((2 * MARGIN, wide), F32)], axis=0)
@@ -141,13 +141,13 @@
     anchors, counts, center, first, second, third, fourth, total_in, weights,
     w_in, w_mid, w_mid_back, w_out, w_out_back,
     send, keep, second_out, numer, den_out,
-    grads, window, x_s, d_s, h_s, z_s, slope_s, dh_s, h2_s, dz_s, y_s,
+    grads, window, x_s, d_s, h_s, z_s, h2_s, slope_s, dh_s, dz_s,
 ):
     rows = center.shape[0]
     channels = center.shape[1] // 2
     cols = center.shape[2]
     wide = cols + LANES
-    width = w_mid.shape[0]
+    width = w_in.shape[0]
     full = rows * cols
     height = rows + 2 * MARGIN
     lanes = lane_ids((2 * channels, LANES))
@@ -191,11 +191,9 @@
 
     numer[...] = jnp.zeros_like(numer)
     grads[...] = jnp.zeros_like(grads)
-    for ref in (x_s, d_s, h_s, z_s):
+    for ref in (x_s, d_s, h_s, z_s, h2_s):
         ref[:, 0:cols] = jnp.zeros((ref.shape[0], cols), BF16)
         ref[:, cols + full : 2 * cols + full] = jnp.zeros((ref.shape[0], cols), BF16)
-    y_s[:, 0:cols] = jnp.zeros((y_s.shape[0], cols), F32)
-    y_s[:, cols + full : 2 * cols + full] = jnp.zeros((y_s.shape[0], cols), F32)
 
     def before(value):
         ids = lane_ids(value.shape)
@@ -219,9 +217,20 @@
         starts = [(row + (2 - tap if flip else tap)) * cols for tap in range(3)]
         return jnp.concatenate([ref[:, start : start + cols] for start in starts], axis=0)
 
+    def across(parts, flip):
+        count = parts.shape[0] // 3
+        first, last = parts[:count], parts[2 * count :]
+        if flip:
+            first, last = last, first
+        return before(first) + parts[count : 2 * count] + after(last)
+
+    def all_rows(ref, flip):
+        starts = [(2 - tap if flip else tap) * cols for tap in range(3)]
+        return jnp.concatenate([ref[:, start : start + full] for start in starts], axis=0)
+
     def one_patch(slot, carry):
-        row0 = anchors[0, 0, slot, 0]
-        col0 = anchors[0, 0, slot, 1]
+        row0 = anchors[0, 0, 0, slot]
+        col0 = anchors[0, 0, 1, slot]
         patch_weights = weights[slot].astype(F32)
         back_shift = lax.rem(wide + MARGIN - col0, wide)
         for row in range(rows):
@@ -233,52 +242,39 @@
             at = slice(row * cols, (row + 1) * cols)
             z1 = dot(w_in[...], stack(x_s, row, False))
             sig = 0.5 * jnp.tanh(0.5 * z1) + 0.5
-            h1 = (z1 * sig).astype(BF16)
             slope_s[:, at] = sig * (1.0 + z1 * (1.0 - sig))
-            spread(h_s, h1, row, False)
+            h_s[:, (row + 1) * cols : (row + 2) * cols] = (z1 * sig).astype(BF16)
         for row in range(rows):
             at = slice(row * cols, (row + 1) * cols)
+            ahead = slice((row + 1) * cols, (row + 2) * cols)
             dh2 = dot(w_out_back[...], stack(d_s, row, True))
-            z2 = dot(w_mid[...], stack(h_s, row, False))
+            z2 = across(dot(w_mid[...], stack(h_s, row, False)), False)
             sig = 0.5 * jnp.tanh(0.5 * z2) + 0.5
-            h1 = h_s[width : 2 * width, (row + 1) * cols : (row + 2) * cols].astype(F32)
-            h2 = (h1 + z2 * sig).astype(BF16)
-            h2_s[:, at] = h2
+            h2_s[:, ahead] = (h_s[:, ahead].astype(F32) + z2 * sig).astype(BF16)
             dz2 = (dh2 * (sig * (1.0 + z2 * (1.0 - sig)))).astype(BF16)
             dh_s[:, at] = dh2
             spread(z_s, dz2, row, True)
-            y_s[:, (row + 1) * cols : (row + 2) * cols] = dot(w_out[...], h2)
         for row in range(rows):
             at = slice(row * cols, (row + 1) * cols)
-            dh1 = dh_s[:, at] + dot(w_mid_back[...], stack(z_s, row, True))
-            dz_s[:, at] = (dh1 * slope_s[:, at]).astype(BF16)
-        small = 9 * channels
-        for tap in range(3):
-            ahead = slice(tap * cols, tap * cols + full)
-            behind = slice((2 - tap) * cols, (2 - tap) * cols + full)
-            at = slice(tap * 3 * channels, (tap + 1) * 3 * channels)
-            grads[at] += dot_lanes(x_s[:, ahead], dz_s[...])
-            part = dot_lanes(z_s[width : 2 * width, cols : cols + full], h_s[:, ahead])
-            for tap_col in range(3):
-                start = small + (3 * tap + tap_col) * width
-                grads[start : start + width] += part[:, tap_col * width : (tap_col + 1) * width]
-            at = slice(small + 9 * width + tap * 3 * channels, small + 9 * width + (tap + 1) * 3 * channels)
-            grads[at] += dot_lanes(d_s[:, behind], h2_s[...])
+            back = across(dot(w_mid_back[...], stack(z_s.at[width : 2 * width], row, True)), True)
+            dz_s[:, at] = ((dh_s[:, at] + back) * slope_s[:, at]).astype(BF16)
         for row in range(rows):
-            sums = []
-            for tap_col in range(3):
-                terms = [
-                    y_s[
-                        (3 * tap + tap_col) * channels : (3 * tap + tap_col + 1) * channels,
-                        (row + tap) * cols : (row + tap + 1) * cols,
-                    ]
-                    for tap in range(3)
-                ]
-                sums.append(terms[0] + terms[1] + terms[2])
-            result = before(sums[0]) + sums[1] + after(sums[2])
+            result = across(dot(w_out[...], stack(h2_s, row, False)), False)
             result = result * patch_weights[row : row + 1]
             result = jnp.concatenate([result, jnp.zeros((channels, LANES), F32)], axis=1)
             numer[row0 + row] += roll(result, lax.rem(col0 + (wide - MARGIN), wide), 1)
+        inside = slice(cols, cols + full)
+        small = 9 * channels
+        part = dot_lanes(z_s[:, inside], all_rows(h_s, False))
+        for tap in range(3):
+            for tap_col in range(3):
+                start = small + (3 * tap + tap_col) * width
+                grads[start : start + width] += part[
+                    tap_col * width : (tap_col + 1) * width, tap * width : (tap + 1) * width
+                ]
+        grads[0:small] += dot_lanes(all_rows(x_s, False), dz_s[...])
+        start = small + 9 * width
+        grads[start : start + small] += dot_lanes(all_rows(d_s, True), h2_s[:, inside])
         return carry
 
     lax.fori_loop(0, counts[0, 0], one_patch, 0)
@@ -391,22 +387,12 @@
     return lax.ppermute(value, axis, pairs)
 
 
-def halves(value, bit):
-    half = value.shape[0] // 2
-    own = lax.dynamic_slice_in_dim(value, bit * half, half, 0)
-    other = lax.dynamic_slice_in_dim(value, (1 - bit) * half, half, 0)
-    return own, other
-
-
-def ordered(own, other, bit):
-    return jnp.concatenate([jnp.where(bit == 0, own, other), jnp.where(bit == 0, other, own)], axis=0)
-
-
 def shards(
     fields, cotangent, kernel_in, kernel_mid, kernel_out, patch_anchors, blend_weights, tile_counts
 ):
     channels, rows, cols = fields.shape
     taps, width, _ = kernel_in.shape
+    patch_anchors = jnp.transpose(patch_anchors, (0, 1, 3, 2))
     height = rows + 2 * MARGIN
     wide = cols + LANES
     full = rows * cols
@@ -444,10 +430,12 @@
     third, fourth = swap_lon(edges)
 
     w_in = jnp.transpose(kernel_in, (1, 0, 2)).reshape(width, taps * channels)
-    w_mid = jnp.transpose(kernel_mid, (1, 0, 2)).reshape(width, taps * width)
-    w_mid_back = jnp.transpose(kernel_mid, (2, 0, 1)).reshape(width, taps * width)
-    w_out = kernel_out.reshape(taps * channels, width)
-    w_out_back = jnp.transpose(kernel_out, (2, 0, 1)).reshape(width, taps * channels)
+    kernel_mid = kernel_mid.reshape(3, 3, width, width)
+    kernel_out = kernel_out.reshape(3, 3, channels, width)
+    w_mid = jnp.transpose(kernel_mid, (1, 2, 0, 3)).reshape(3 * width, 3 * width)
+    w_mid_back = jnp.transpose(kernel_mid, (1, 3, 0, 2)).reshape(3 * width, 3 * width)
+    w_out = jnp.transpose(kernel_out, (1, 2, 0, 3)).reshape(3 * channels, 3 * width)
+    w_out_back = jnp.transpose(kernel_out, (3, 0, 1, 2)).reshape(width, taps * channels)
 
     lat_size, lon_size = lax.axis_size("lat"), lax.axis_size("lon")
     length = taps * (2 * channels + width)
@@ -471,13 +459,12 @@
             pltpu.VMEM((height, 2 * channels, wide), F32),
             pltpu.VMEM((3 * channels, padded), BF16),
             pltpu.VMEM((3 * channels, padded), BF16),
+            pltpu.VMEM((width, padded), BF16),
             pltpu.VMEM((3 * width, padded), BF16),
-            pltpu.VMEM((3 * width, padded), BF16),
+            pltpu.VMEM((width, padded), BF16),
             pltpu.VMEM((width, full), F32),
             pltpu.VMEM((width, full), F32),
             pltpu.VMEM((width, full), BF16),
-            pltpu.VMEM((width, full), BF16),
-            pltpu.VMEM((taps * channels, padded), F32),
         ],
         compiler_params=params(),
         name="patches",
@@ -486,15 +473,13 @@
         w_in, w_mid, w_mid_back, w_out, w_out_back,
     )
 
-    lat = lax.axis_index("lat")
     first = exchange(send, "lat", 1)
     second = swap(second, "lat", 1, False)
     mine = keep + first[:half].astype(F32)
-    step = 2
-    while step < lat_size:
-        own, other = halves(mine, (lat // step) % 2)
-        mine = own + exchange(other.astype(BF16), "lat", step).astype(F32)
-        step *= 2
+    planes = [list(range(start, lat_size, 2)) for start in (0, 1)]
+    parts = mine.astype(BF16).reshape(lat_size // 2, length // lat_size, LANES)
+    parts = lax.all_to_all(parts, "lat", 0, 0, axis_index_groups=planes)
+    mine = jnp.sum(parts.astype(F32), axis=0)
     inner, edges = pl.pallas_call(
         beside_kernel,
         out_shape=(shape((rows, channels, cols), F32), shape((channels, LANES), BF16)),
@@ -526,10 +511,8 @@
         compiler_params=params(),
         name="fold",
     )(inner, third, fourth, den)
-    step = lat_size // 2
-    while step > 1:
-        mine = ordered(mine, exchange(mine, "lat", step), (lat // step) % 2)
-        step //= 2
+    parts = jnp.broadcast_to(mine[None], (lat_size // 2,) + mine.shape)
+    mine = lax.all_to_all(parts, "lat", 0, 0, axis_index_groups=planes).reshape(half, LANES)
     grad_in, grad_mid, grad_out = pl.pallas_call(
         split_kernel,
         out_shape=(

time: 79.6 us -> 77.3 us (0.971)
  waiting for transfers between devices: 32.3 us -> 19.6 us
  blocking collectives: 0 us -> 10.1 us
  Pallas kernels: 15.4 us -> 13.6 us
  local copies, waits for them, and re-layouts: 4.93 us -> 5.73 us
    ppermute x6 -> x2, waiting for transfers between devices: 20 us -> 1.87 us  [exchange(): return lax.ppermute(value, axis, pairs)]
    all_to_all x0 -> x1, blocking collectives: none -> 10.1 us  [shards(): lax.all_to_all(parts, 'lat', 0, 0, axis_index_groups=planes)]
    all_to_all x0 -> x1, waiting for transfers between devices: none -> 4.99 us  [shards(): parts = lax.all_to_all(parts, 'lat', 0, 0, axis_index_groups=planes)]
    all_to_all x0 -> x1, starting transfers between devices: none -> 3.39 us  [shards(): parts = lax.all_to_all(parts, 'lat', 0, 0, axis_index_groups=planes)]
    ppermute x6 -> x2, starting transfers between devices: 17.3 us -> 15.2 us  [exchange(): return lax.ppermute(value, axis, pairs)]
    pallas_call x1, Pallas kernels: 11.9 us -> 10.1 us  [shards(): pl.pallas_call(patch_kernel, out_shape=(shape((half + edge_rows, LANES),...]
    unnamed x16 -> x17, local copies, waits for them, and re-layouts: 4.23 us -> 4.8 us
  transfers between devices with their start and end apart: 13 -> 10, of which waited for: 10 -> 6; matrix products, arithmetic and copies ran while one was open for 1% -> 1% of each run, Pallas kernels for 1% -> 1%
where the time goes in v4:
time: 77.3 us; the launch traced here: 76.8 us
  starting transfers between devices  25.5 us (33%)
  waiting for transfers between devices  19.6 us (25%)
  Pallas kernels  13.6 us (18%)
  blocking collectives  10.1 us (13%)
  local copies, waits for them, and re-layouts  5.73 us (7%)
  between operations  1.49 us (2%)
  other arithmetic  0.84 us (1%)
    ppermute x2, starting transfers between devices, exchange(): return lax.ppermute(value, axis, pairs)  15.2 us
    ppermute x7, waiting for transfers between devices, swap(): return lax.ppermute(value, axis, pairs)  12.7 us
    pallas_call x1, Pallas kernels, shards(): pl.pallas_call(patch_kernel, out_shape=(shape((half + edge_rows, LANES),...  10.1 us
    all_to_all x1, blocking collectives, shards(): lax.all_to_all(parts, 'lat', 0, 0, axis_index_groups=planes)  10.1 us
    ppermute x7, starting transfers between devices, swap(): return lax.ppermute(value, axis, pairs)  6.91 us
    all_to_all x1, waiting for transfers between devices, shards(): parts = lax.all_to_all(parts, 'lat', 0, 0, axis_index_groups=planes)  4.99 us
    unnamed x17, local copies, waits for them, and re-layouts  4.8 us
    all_to_all x1, starting transfers between devices, shards(): parts = lax.all_to_all(parts, 'lat', 0, 0, axis_index_groups=planes)  3.39 us
  transfers between devices with their start and end apart: 10, of which 6 were waited for; matrix products, arithmetic and copies ran while one was open for 1% of the time, Pallas kernels for 1%

profile of v4, /device:TPU:0, one launch (start us, length us, event | category | flops | bytes accessed | tf_op | source)
XLA Modules:
  0.0 76.8 jit_solution(16656195862997857513)
XLA Ops:
  1.3 0.7 copy-done.4
  2.0 0.8 copy-done
  2.7 0.9 %copy-done.2 = bf16[32,8,256]{2,1,0:T(8,128)(2,1)S(1)} copy-done((bf16[32,8,256]{2,1,0:T(8,128)(2,1)S(1)}, bf16[32,8,256]{2,1,0:T(8,128)(2,1)}, u32[]{:S(2)}) %copy-start.2) | copy-done | bytes 131096
  3.6 0.9 %copy-done.3 = bf16[32,8,256]{2,1,0:T(8,128)(2,1)S(1)} copy-done((bf16[32,8,256]{2,1,0:T(8,128)(2,1)S(1)}, bf16[32,8,256]{2,1,0:T(8,128)(2,1)}, u32[]{:S(2)}) %copy-start.3) | copy-done | bytes 131096
  4.5 1.3 %pack.1 = (bf16[8,64,256]{2,1,0:T(8,128)(2,1)S(1)}, bf16[5,64,256]{2,1,0:T(8,128)(2,1)S(1)}, bf16[5,64,256]{2,1,0:T(8,128)(2,1)S(1)}, f32[16,384]{1,0:T(8,128)S(1)}) custom-call(s32[1,1,2,4]{3,2,1,0:T(2,128)S(1)} %bitcast.33, s32[1,1]{1,0:T(1,128)S(6)} %copy.29.counts, bf16[32,8,256]{2,1,0:T(8,128)(2,1)S(1)} %copy-done.2, bf16[32,8,256]{2,1,0:T(8,128)(2,1)S(1)} %copy-done.3, ...), custom_call_target="tpu_custom_call" | custom-call | tf_op jit(solution)/shard_map/pack/pallas_call | solution.py:401
  5.8 0.7 collective-permute-start
  6.5 0.7 collective-permute-start.1
  8.0 4.8 %collective-permute-start.3 = (bf16[96,128]{1,0:T(8,128)(2,1)S(1)}, bf16[96,128]{1,0:T(8,128)(2,1)S(1)}, u32[]{:S(2)}, u32[]{:S(2)}) collective-permute-start(bf16[96,128]{1,0:T(8,128)(2,1)S(1)} %get-tuple-element.24), channel_id=1, source_target_pairs={{1,2},{2,1},{3,0},{0,3},{5,6},{6,5},{7,4},{4,7},{9,10},{10,9},{11,... | collective-permute-start | bytes 73736 | tf_op jit(solution)/shard_map/ppermute | solution.py:374
  12.8 0.8 %copy-done.7 = bf16[9,128,32]{1,2,0:T(8,128)(2,1)S(1)} copy-done((bf16[9,128,32]{1,2,0:T(8,128)(2,1)S(1)}, bf16[9,128,32]{1,2,0:T(8,128)(2,1)}, u32[]{:S(2)}) %copy-start.7) | copy-done | bytes 73752
  13.7 0.8 copy-done.6
  14.7 1.8 %collective-permute-done.2.third = bf16[96,128]{1,0:T(8,128)(2,1)S(1)} collective-permute-done((bf16[96,128]{1,0:T(8,128)(2,1)S(1)}, bf16[96,128]{1,0:T(8,128)(2,1)S(1)}, u32[]{:S(2)}, u32[]{:S(2)}) %collective-permute-start.2) | collective-permute-done | bytes 24608 | tf_op jit(solution)/shard_map/ppermute | solution.py:374
  16.6 10.1 %patches.1 = (bf16[1280,128]{1,0:T(8,128)(2,1)S(1)}, f32[896,128]{1,0:T(8,128)S(1)}, bf16[384,128]{1,0:T(8,128)(2,1)S(1)}, f32[16,32,384]{2,1,0:T(8,128)S(1)}, f32[8,256]{1,0:T(8,128)S(1)}) custom-call(s32[1,1,2,4]{3,2,1,0:T(2,128)S(1)} %bitcast.34, s32[1,1]{1,0:T(1,128)S(6)} %copy.29.counts, bf16[8,64,256]{2,1,0:T(8,128)(2,1)S(1)} %get-tuple-element.20.center, ...), custom_call_target="tpu_custom_call" | custom-call | tf_op jit(solution)/shard_map/patches/pallas_call | solution.py:446
  26.7 15.2 %collective-permute-start.4 = (bf16[1280,128]{1,0:T(8,128)(2,1)S(1)}, bf16[1280,128]{1,0:T(8,128)(2,1)S(1)}, u32[]{:S(2)}, u32[]{:S(2)}) collective-permute-start(bf16[1280,128]{1,0:T(8,128)(2,1)S(1)} %get-tuple-element.27), channel_id=1, source_target_pairs={{0,4},{4,0},{8,12},{12,8},{16,20},{20,16},{24,28},{28,24},{1,5},{5... | collective-permute-start | bytes 983048 | tf_op jit(solution)/shard_map/ppermute | solution.py:387
  41.9 1.3 %collective-permute-done.4.first = bf16[1280,128]{1,0:T(8,128)(2,1)S(1)} collective-permute-done((bf16[1280,128]{1,0:T(8,128)(2,1)S(1)}, bf16[1280,128]{1,0:T(8,128)(2,1)S(1)}, u32[]{:S(2)}, u32[]{:S(2)}) %collective-permute-start.4) | collective-permute-done | bytes 327712 | tf_op jit(solution)/shard_map/ppermute | solution.py:387
  43.1 0.8 add_convert_fusion
  43.9 3.4 %all-to-all-start = ((bf16[4,224,128]{2,1,0:T(8,128)(2,1)}), bf16[4,224,128]{2,1,0:T(8,128)(2,1)S(1)}, u32[]{:S(2)}, u32[]{:S(2)}) async-start(bf16[4,224,128]{2,1,0:T(8,128)(2,1)} %bitcast.10), calls=%async_computation | async-start | bytes 458752 | tf_op jit(solution)/shard_map/all_to_all | solution.py:481
  47.3 0.7 collective-permute-start.5
  48.1 5.0 %all-to-all-done = bf16[4,224,128]{2,1,0:T(8,128)(2,1)S(1)} async-done(((bf16[4,224,128]{2,1,0:T(8,128)(2,1)}), bf16[4,224,128]{2,1,0:T(8,128)(2,1)S(1)}, u32[]{:S(2)}, u32[]{:S(2)}) %all-to-all-start) | async-done | bytes 229408 | tf_op jit(solution)/shard_map/all_to_all | solution.py:481
  53.2 4.8 %collective-permute-done.6 = bf16[256,128]{1,0:T(8,128)(2,1)S(1)} collective-permute-done((bf16[256,128]{1,0:T(8,128)(2,1)S(1)}, bf16[256,128]{1,0:T(8,128)(2,1)S(1)}, u32[]{:S(2)}, u32[]{:S(2)}) %collective-permute-start.6) | collective-permute-done | bytes 65568 | tf_op jit(solution)/shard_map/ppermute | solution.py:374
  58.2 6.0 %collective-permute-done.7 = bf16[256,128]{1,0:T(8,128)(2,1)S(1)} collective-permute-done((bf16[256,128]{1,0:T(8,128)(2,1)S(1)}, bf16[256,128]{1,0:T(8,128)(2,1)S(1)}, u32[]{:S(2)}, u32[]{:S(2)}) %collective-permute-start.7) | collective-permute-done | bytes 65568 | tf_op jit(solution)/shard_map/ppermute | solution.py:374
  64.3 10.1 %all_to_all.10 = bf16[4,224,128]{2,1,0:T(8,128)(2,1)S(1)} all-to-all(bf16[4,224,128]{2,1,0:T(8,128)(2,1)S(1)} %broadcast_in_dim.2), channel_id=1, replica_groups={{0,8,16,24},{4,12,20,28},{1,9,17,25},{5,13,21,29},{2,10,18,26},{6,14,22..., dimensions={0} | all-to-all | bytes 458752 | tf_op jit(solution)/shard_map/all_to_all | solution.py:515
  74.4 0.9 %fold.1 = f32[32,8,256]{2,1,0:T(8,128)} custom-call(f32[8,32,256]{2,1,0:T(8,128)S(1)} %get-tuple-element.29.inner, bf16[32,128]{1,0:T(8,128)(2,1)S(1)} %slice.21.third, bf16[32,128]{1,0:T(8,128)(2,1)S(1)} %slice.23.fourth, f32[8,256]{1,0:T(8,128)S(1)} %get-tuple-element.32.den), custom_call_target="tpu_custom_call" | custom-call | tf_op jit(solution)/shard_map/fold/pallas_call | solution.py:506
  75.2 0.6 collective-permute-done.8.other
  75.9 1.0 %split.1 = (f32[9,32,128]{2,1,0:T(8,128)}, f32[9,128,128]{2,1,0:T(8,128)}, f32[9,32,128]{2,1,0:T(8,128)}) custom-call(bf16[896,128]{1,0:T(8,128)(2,1)S(1)} %bitcast.31, bf16[896,128]{1,0:T(8,128)(2,1)S(1)} %collective-permute-done.8.other), custom_call_target="tpu_custom_call" | custom-call | tf_op jit(solution)/shard_map/split/pallas_call | solution.py:516
  (35 shorter events, 1.6 us)
Async XLA Ops:
  1.3 0.7 copy-start.4
  2.0 0.8 copy-start
  2.7 0.9 %copy-start.2 = (bf16[32,8,256]{2,1,0:T(8,128)(2,1)S(1)}, bf16[32,8,256]{2,1,0:T(8,128)(2,1)}, u32[]{:S(2)}) copy-start(bf16[32,8,256]{2,1,0:T(8,128)(2,1)} %fields_in.1) | copy-start | bytes 393220
  3.6 0.9 %copy-start.3 = (bf16[32,8,256]{2,1,0:T(8,128)(2,1)S(1)}, bf16[32,8,256]{2,1,0:T(8,128)(2,1)}, u32[]{:S(2)}) copy-start(bf16[32,8,256]{2,1,0:T(8,128)(2,1)} %cotangent_in.1) | copy-start | bytes 393220
  4.5 2.7 %copy-start.5 = (bf16[9,128,128]{2,1,0:T(8,128)(2,1)S(1)}, bf16[9,128,128]{2,1,0:T(8,128)(2,1)}, u32[]{:S(2)}) copy-start(bf16[9,128,128]{2,1,0:T(8,128)(2,1)} %param.11) | copy-start | bytes 884740
  5.8 1.9 %collective-permute-start = (bf16[5,64,256]{2,1,0:T(8,128)(2,1)S(1)}, bf16[5,64,256]{2,1,0:T(8,128)(2,1)S(1)}, u32[]{:S(2)}, u32[]{:S(2)}) collective-permute-start(bf16[5,64,256]{2,1,0:T(8,128)(2,1)S(1)} %get-tuple-element.21), channel_id=1, source_target_pairs={{0,4},{4,0},{8,12},{12,8},{16,20},{20,16},{24,28},{28,24},{1,5},{5... | collective-permute-start | bytes 491528 | tf_op jit(solution)/shard_map/ppermute | solution.py:374
  6.5 1.2 %collective-permute-start.1 = (bf16[5,64,256]{2,1,0:T(8,128)(2,1)S(1)}, bf16[5,64,256]{2,1,0:T(8,128)(2,1)S(1)}, u32[]{:S(2)}, u32[]{:S(2)}) collective-permute-start(bf16[5,64,256]{2,1,0:T(8,128)(2,1)S(1)} %get-tuple-element.22), channel_id=1, source_target_pairs={{4,8},{8,4},{12,16},{16,12},{20,24},{24,20},{5,9},{9,5},{13,17},{1... | collective-permute-start | bytes 491528 | tf_op jit(solution)/shard_map/ppermute | solution.py:374
  8.0 6.8 %collective-permute-start.3 = (bf16[96,128]{1,0:T(8,128)(2,1)S(1)}, bf16[96,128]{1,0:T(8,128)(2,1)S(1)}, u32[]{:S(2)}, u32[]{:S(2)}) collective-permute-start(bf16[96,128]{1,0:T(8,128)(2,1)S(1)} %get-tuple-element.24), channel_id=1, source_target_pairs={{1,2},{2,1},{3,0},{0,3},{5,6},{6,5},{7,4},{4,7},{9,10},{10,9},{11,... | collective-permute-start | bytes 73736 | tf_op jit(solution)/shard_map/ppermute | solution.py:374
  12.7 3.8 %collective-permute-start.2 = (bf16[96,128]{1,0:T(8,128)(2,1)S(1)}, bf16[96,128]{1,0:T(8,128)(2,1)S(1)}, u32[]{:S(2)}, u32[]{:S(2)}) collective-permute-start(bf16[96,128]{1,0:T(8,128)(2,1)S(1)} %get-tuple-element.24), channel_id=1, source_target_pairs={{0,1},{1,0},{2,3},{3,2},{4,5},{5,4},{6,7},{7,6},{8,9},{9,8},{10,11... | collective-permute-start | bytes 73736 | tf_op jit(solution)/shard_map/ppermute | solution.py:374
  12.7 0.9 %copy-start.7 = (bf16[9,128,32]{1,2,0:T(8,128)(2,1)S(1)}, bf16[9,128,32]{1,2,0:T(8,128)(2,1)}, u32[]{:S(2)}) copy-start(bf16[9,128,32]{1,2,0:T(8,128)(2,1)} %param.10) | copy-start | bytes 221188
  13.6 0.9 %copy-start.6 = (bf16[9,32,128]{2,1,0:T(8,128)(2,1)S(1)}, bf16[9,32,128]{2,1,0:T(8,128)(2,1)}, u32[]{:S(2)}) copy-start(bf16[9,32,128]{2,1,0:T(8,128)(2,1)} %param.12) | copy-start | bytes 221188
  14.7 1.9 %copy-start.1 = (s32[4,8,256]{2,1,0:T(8,128)S(1)}, s32[4,8,256]{2,1,0:T(8,128)}, u32[]{:S(2)}) copy-start(s32[4,8,256]{2,1,0:T(8,128)} %weights.1) | copy-start | bytes 98308
  26.7 16.4 %collective-permute-start.4 = (bf16[1280,128]{1,0:T(8,128)(2,1)S(1)}, bf16[1280,128]{1,0:T(8,128)(2,1)S(1)}, u32[]{:S(2)}, u32[]{:S(2)}) collective-permute-start(bf16[1280,128]{1,0:T(8,128)(2,1)S(1)} %get-tuple-element.27), channel_id=1, source_target_pairs={{0,4},{4,0},{8,12},{12,8},{16,20},{20,16},{24,28},{28,24},{1,5},{5... | collective-permute-start | bytes 983048 | tf_op jit(solution)/shard_map/ppermute | solution.py:387
  43.9 9.2 %all-to-all-start = ((bf16[4,224,128]{2,1,0:T(8,128)(2,1)}), bf16[4,224,128]{2,1,0:T(8,128)(2,1)S(1)}, u32[]{:S(2)}, u32[]{:S(2)}) async-start(bf16[4,224,128]{2,1,0:T(8,128)(2,1)} %bitcast.10), calls=%async_computation | async-start | bytes 458752 | tf_op jit(solution)/shard_map/all_to_all | solution.py:481
  47.3 0.7 collective-permute-start.5
  53.1 4.9 %collective-permute-start.6 = (bf16[256,128]{1,0:T(8,128)(2,1)S(1)}, bf16[256,128]{1,0:T(8,128)(2,1)S(1)}, u32[]{:S(2)}, u32[]{:S(2)}) collective-permute-start(bf16[256,128]{1,0:T(8,128)(2,1)S(1)} %pad_maximum_fusion.1), channel_id=1, source_target_pairs={{0,1},{1,0},{2,3},{3,2},{4,5},{5,4},{6,7},{7,6},{8,9},{9,8},{10,11... | collective-permute-start | bytes 196616 | tf_op jit(solution)/shard_map/ppermute | solution.py:374
  58.1 6.1 %collective-permute-start.7 = (bf16[256,128]{1,0:T(8,128)(2,1)S(1)}, bf16[256,128]{1,0:T(8,128)(2,1)S(1)}, u32[]{:S(2)}, u32[]{:S(2)}) collective-permute-start(bf16[256,128]{1,0:T(8,128)(2,1)S(1)} %pad_maximum_fusion), channel_id=1, source_target_pairs={{1,2},{2,1},{3,0},{0,3},{5,6},{6,5},{7,4},{4,7},{9,10},{10,9},{11,... | collective-permute-start | bytes 196616 | tf_op jit(solution)/shard_map/ppermute | solution.py:374
  74.4 1.5 %collective-permute-start.8 = (bf16[896,128]{1,0:T(8,128)(2,1)S(1)}, bf16[896,128]{1,0:T(8,128)(2,1)S(1)}, u32[]{:S(2)}, u32[]{:S(2)}) collective-permute-start(bf16[896,128]{1,0:T(8,128)(2,1)S(1)} %bitcast.30), channel_id=1, source_target_pairs={{0,4},{4,0},{8,12},{12,8},{16,20},{20,16},{24,28},{28,24},{1,5},{5... | collective-permute-start | bytes 688136 | tf_op jit(solution)/shard_map/ppermute | solution.py:387

commit v5 on v4

--- a/solution.py
+++ b/solution.py
@@ -195,13 +195,24 @@
         ref[:, 0:cols] = jnp.zeros((ref.shape[0], cols), BF16)
         ref[:, cols + full : 2 * cols + full] = jnp.zeros((ref.shape[0], cols), BF16)
 
+    def shifted(value, step):
+        blocks = [value[:, at : at + LANES] for at in range(0, cols, LANES)]
+        turned = [roll(block, step, 1) for block in blocks]
+        ids = lane_ids(blocks[0].shape)
+        zero = jnp.zeros_like(blocks[0])
+        if step > 0:
+            ends = [zero] + turned[:-1]
+            at_end = ids == 0
+        else:
+            ends = turned[1:] + [zero]
+            at_end = ids == LANES - 1
+        return jnp.concatenate([jnp.where(at_end, end, own) for end, own in zip(ends, turned)], axis=1)
+
     def before(value):
-        ids = lane_ids(value.shape)
-        return jnp.where(ids == 0, jnp.zeros_like(value), roll(value, 1, 1))
+        return shifted(value, 1)
 
     def after(value):
-        ids = lane_ids(value.shape)
-        return jnp.where(ids == cols - 1, jnp.zeros_like(value), roll(value, cols - 1, 1))
+        return shifted(value, -1)
 
     def spread(ref, value, row, flip):
         count = value.shape[0]
@@ -387,6 +398,17 @@
     return lax.ppermute(value, axis, pairs)
 
 
+def halves(value, bit):
+    half = value.shape[0] // 2
+    own = lax.dynamic_slice_in_dim(value, bit * half, half, 0)
+    other = lax.dynamic_slice_in_dim(value, (1 - bit) * half, half, 0)
+    return own, other
+
+
+def ordered(own, other, bit):
+    return jnp.concatenate([jnp.where(bit == 0, own, other), jnp.where(bit == 0, other, own)], axis=0)
+
+
 def shards(
     fields, cotangent, kernel_in, kernel_mid, kernel_out, patch_anchors, blend_weights, tile_counts
 ):
@@ -417,7 +439,11 @@
         ],
         compiler_params=params(),
         name="pack",
-    )(patch_anchors, tile_counts, fields, cotangent, blend_weights)
+    )(
+        patch_anchors,
+        tile_counts,
+        *(pltpu.with_memory_space_constraint(value, pltpu.HBM) for value in (fields, cotangent, blend_weights)),
+    )
     first, second = swap_lat(first, second)
     edges, total = pl.pallas_call(
         edge_kernel,
@@ -473,13 +499,19 @@
         w_in, w_mid, w_mid_back, w_out, w_out_back,
     )
 
+    lat = lax.axis_index("lat")
     first = exchange(send, "lat", 1)
     second = swap(second, "lat", 1, False)
     mine = keep + first[:half].astype(F32)
-    planes = [list(range(start, lat_size, 2)) for start in (0, 1)]
-    parts = mine.astype(BF16).reshape(lat_size // 2, length // lat_size, LANES)
-    parts = lax.all_to_all(parts, "lat", 0, 0, axis_index_groups=planes)
-    mine = jnp.sum(parts.astype(F32), axis=0)
+    steps = [2 << bit for bit in range(lat_size.bit_length() - 2)]
+    parts = jnp.split(mine, 2)
+    orders = (steps, steps[1:] + steps[:1])
+    for turn in range(len(steps)):
+        for index in (0, 1):
+            step = orders[index][turn]
+            own, other = halves(parts[index], (lat // step) % 2)
+            parts[index] = own + exchange(other.astype(BF16), "lat", step).astype(F32)
+    mine = jnp.concatenate(parts, axis=0)
     inner, edges = pl.pallas_call(
         beside_kernel,
         out_shape=(shape((rows, channels, cols), F32), shape((channels, LANES), BF16)),
@@ -511,8 +543,12 @@
         compiler_params=params(),
         name="fold",
     )(inner, third, fourth, den)
-    parts = jnp.broadcast_to(mine[None], (lat_size // 2,) + mine.shape)
-    mine = lax.all_to_all(parts, "lat", 0, 0, axis_index_groups=planes).reshape(half, LANES)
+    parts = jnp.split(mine, 2)
+    for turn in reversed(range(len(steps))):
+        for index in (0, 1):
+            step = orders[index][turn]
+            parts[index] = ordered(parts[index], exchange(parts[index], "lat", step), (lat // step) % 2)
+    mine = jnp.concatenate(parts, axis=0)
     grad_in, grad_mid, grad_out = pl.pallas_call(
         split_kernel,
         out_shape=(

time: 77.3 us -> 74.9 us (0.969)
  blocking collectives: 10.1 us -> 0 us
  starting transfers between devices: 25.5 us -> 31.6 us
  waiting for transfers between devices: 19.6 us -> 24.1 us
  local copies, waits for them, and re-layouts: 5.73 us -> 3.22 us
    ppermute x2 -> x10, waiting for transfers between devices: 1.87 us -> 13 us  [exchange(): return lax.ppermute(value, axis, pairs)]
    all_to_all x1 -> x0, blocking collectives: 10.1 us -> none  [shards(): lax.all_to_all(parts, 'lat', 0, 0, axis_index_groups=planes)]
    ppermute x2 -> x10, starting transfers between devices: 15.2 us -> 23.9 us  [exchange(): return lax.ppermute(value, axis, pairs)]
    all_to_all x1 -> x0, waiting for transfers between devices: 4.99 us -> none  [shards(): parts = lax.all_to_all(parts, 'lat', 0, 0, axis_index_groups=planes)]
    all_to_all x1 -> x0, starting transfers between devices: 3.39 us -> none  [shards(): parts = lax.all_to_all(parts, 'lat', 0, 0, axis_index_groups=planes)]
    unnamed x17 -> x11, local copies, waits for them, and re-layouts: 4.8 us -> 2.23 us
    ppermute x7, waiting for transfers between devices: 12.7 us -> 11 us  [swap(): return lax.ppermute(value, axis, pairs)]
    ppermute x7, starting transfers between devices: 6.91 us -> 7.69 us  [swap(): return lax.ppermute(value, axis, pairs)]
  transfers between devices with their start and end apart: 10 -> 17, of which waited for: 6 -> 12; matrix products, arithmetic and copies ran while one was open for 1% -> 1% of each run, Pallas kernels for 1% -> 1%
where the time goes in v5:
time: 74.9 us; the launch traced here: 74.5 us
  starting transfers between devices  31.6 us (42%)
  waiting for transfers between devices  24.1 us (32%)
  Pallas kernels  13.8 us (18%)
  local copies, waits for them, and re-layouts  3.22 us (4%)
  between operations  1.6 us (2%)
    ppermute x10, starting transfers between devices, exchange(): return lax.ppermute(value, axis, pairs)  23.9 us
    ppermute x10, waiting for transfers between devices, exchange(): return lax.ppermute(value, axis, pairs)  13 us
    ppermute x7, waiting for transfers between devices, swap(): return lax.ppermute(value, axis, pairs)  11 us
    pallas_call x1, Pallas kernels, shards(): pl.pallas_call(patch_kernel, out_shape=(shape((half + edge_rows, LANES),...  9.91 us
    ppermute x7, starting transfers between devices, swap(): return lax.ppermute(value, axis, pairs)  7.69 us
    unnamed x11, local copies, waits for them, and re-layouts  2.23 us
    pallas_call x1, Pallas kernels, shards(): pl.pallas_call(pack_kernel, out_shape=(shape((rows, 2 * channels, cols),...  1.72 us
  transfers between devices with their start and end apart: 17, of which 12 were waited for; matrix products, arithmetic and copies ran while one was open for 1% of the time, Pallas kernels for 1%

profile of v5, /device:TPU:0, one launch (start us, length us, event | category | flops | bytes accessed | tf_op | source)
XLA Modules:
  0.0 74.5 jit_solution(15174766514311977942)
XLA Ops:
  1.3 0.7 copy-done.1
  2.0 1.7 %pack.1 = (bf16[8,64,256]{2,1,0:T(8,128)(2,1)S(1)}, bf16[5,64,256]{2,1,0:T(8,128)(2,1)S(1)}, bf16[5,64,256]{2,1,0:T(8,128)(2,1)S(1)}, f32[16,384]{1,0:T(8,128)S(1)}) custom-call(s32[1,1,2,4]{3,2,1,0:T(2,128)S(1)} %bitcast.29, s32[1,1]{1,0:T(1,128)S(6)} %copy.29.counts, bf16[32,8,256]{2,1,0:T(8,128)(2,1)} %fields_in.1, bf16[32,8,256]{2,1,0:T(8,128)(2,1)} %cotangent_in.1, ...), custom_call_target="tpu_custom_call" | custom-call | tf_op jit(solution)/shard_map/pack/pallas_call | solution.py:423
  4.3 0.7 collective-permute-start.1
  5.7 2.7 %collective-permute-start.2 = (bf16[96,128]{1,0:T(8,128)(2,1)S(1)}, bf16[96,128]{1,0:T(8,128)(2,1)S(1)}, u32[]{:S(2)}, u32[]{:S(2)}) collective-permute-start(bf16[96,128]{1,0:T(8,128)(2,1)S(1)} %get-tuple-element.24), channel_id=1, source_target_pairs={{0,1},{1,0},{2,3},{3,2},{4,5},{5,4},{6,7},{7,6},{8,9},{9,8},{10,11... | collective-permute-start | bytes 73736 | tf_op jit(solution)/shard_map/ppermute | solution.py:385
  8.5 2.5 %collective-permute-start.3 = (bf16[96,128]{1,0:T(8,128)(2,1)S(1)}, bf16[96,128]{1,0:T(8,128)(2,1)S(1)}, u32[]{:S(2)}, u32[]{:S(2)}) collective-permute-start(bf16[96,128]{1,0:T(8,128)(2,1)S(1)} %get-tuple-element.24), channel_id=1, source_target_pairs={{1,2},{2,1},{3,0},{0,3},{5,6},{6,5},{7,4},{4,7},{9,10},{10,9},{11,... | collective-permute-start | bytes 73736 | tf_op jit(solution)/shard_map/ppermute | solution.py:385
  11.0 0.8 %copy-done.4 = bf16[9,128,32]{1,2,0:T(8,128)(2,1)S(1)} copy-done((bf16[9,128,32]{1,2,0:T(8,128)(2,1)S(1)}, bf16[9,128,32]{1,2,0:T(8,128)(2,1)}, u32[]{:S(2)}) %copy-start.4) | copy-done | bytes 73752
  11.9 0.8 %copy-done.3 = bf16[9,32,128]{2,1,0:T(8,128)(2,1)S(1)} copy-done((bf16[9,32,128]{2,1,0:T(8,128)(2,1)S(1)}, bf16[9,32,128]{2,1,0:T(8,128)(2,1)}, u32[]{:S(2)}) %copy-start.3) | copy-done | bytes 73752
  12.9 1.2 %collective-permute-done.3.fourth = bf16[96,128]{1,0:T(8,128)(2,1)S(1)} collective-permute-done((bf16[96,128]{1,0:T(8,128)(2,1)S(1)}, bf16[96,128]{1,0:T(8,128)(2,1)S(1)}, u32[]{:S(2)}, u32[]{:S(2)}) %collective-permute-start.3) | collective-permute-done | bytes 24608 | tf_op jit(solution)/shard_map/ppermute | solution.py:385
  14.1 9.9 %patches.1 = (bf16[1280,128]{1,0:T(8,128)(2,1)S(1)}, f32[896,128]{1,0:T(8,128)S(1)}, bf16[384,128]{1,0:T(8,128)(2,1)S(1)}, f32[16,32,384]{2,1,0:T(8,128)S(1)}, f32[8,256]{1,0:T(8,128)S(1)}) custom-call(s32[1,1,2,4]{3,2,1,0:T(2,128)S(1)} %bitcast.30, s32[1,1]{1,0:T(1,128)S(6)} %copy.29.counts, bf16[8,64,256]{2,1,0:T(8,128)(2,1)S(1)} %get-tuple-element.20.center, ...), custom_call_target="tpu_custom_call" | custom-call | tf_op jit(solution)/shard_map/patches/pallas_call | solution.py:472
  24.0 15.0 %collective-permute-start.4 = (bf16[1280,128]{1,0:T(8,128)(2,1)S(1)}, bf16[1280,128]{1,0:T(8,128)(2,1)S(1)}, u32[]{:S(2)}, u32[]{:S(2)}) collective-permute-start(bf16[1280,128]{1,0:T(8,128)(2,1)S(1)} %get-tuple-element.27), channel_id=1, source_target_pairs={{0,4},{4,0},{8,12},{12,8},{16,20},{20,16},{24,28},{28,24},{1,5},{5... | collective-permute-start | bytes 983048 | tf_op jit(solution)/shard_map/ppermute | solution.py:398
  40.5 2.5 %collective-permute-start.6 = (bf16[224,128]{1,0:T(8,128)(2,1)S(1)}, bf16[224,128]{1,0:T(8,128)(2,1)S(1)}, u32[]{:S(2)}, u32[]{:S(2)}) collective-permute-start(bf16[224,128]{1,0:T(8,128)(2,1)S(1)} %dynamic-slice_convert_fusion.1), channel_id=1, source_target_pairs={{0,8},{4,12},{8,0},{12,4},{16,24},{20,28},{24,16},{28,20},{1,9},{5... | collective-permute-start | bytes 172040 | tf_op jit(solution)/shard_map/ppermute | solution.py:398
  43.1 2.0 %collective-permute-done.8 = bf16[224,128]{1,0:T(8,128)(2,1)S(1)} collective-permute-done((bf16[224,128]{1,0:T(8,128)(2,1)S(1)}, bf16[224,128]{1,0:T(8,128)(2,1)S(1)}, u32[]{:S(2)}, u32[]{:S(2)}) %collective-permute-start.8) | collective-permute-done | bytes 57376 | tf_op jit(solution)/shard_map/ppermute | solution.py:398
  45.1 2.0 %collective-permute-start.9 = (bf16[112,128]{1,0:T(8,128)(2,1)S(1)}, bf16[112,128]{1,0:T(8,128)(2,1)S(1)}, u32[]{:S(2)}, u32[]{:S(2)}) collective-permute-start(bf16[112,128]{1,0:T(8,128)(2,1)S(1)} %dynamic-slice_convert_fusion.2), channel_id=1, source_target_pairs={{0,8},{4,12},{8,0},{12,4},{16,24},{20,28},{24,16},{28,20},{1,9},{5... | collective-permute-start | bytes 86024 | tf_op jit(solution)/shard_map/ppermute | solution.py:398
  47.3 1.8 %collective-permute-done.9 = bf16[112,128]{1,0:T(8,128)(2,1)S(1)} collective-permute-done((bf16[112,128]{1,0:T(8,128)(2,1)S(1)}, bf16[112,128]{1,0:T(8,128)(2,1)S(1)}, u32[]{:S(2)}, u32[]{:S(2)}) %collective-permute-start.9) | collective-permute-done | bytes 28704 | tf_op jit(solution)/shard_map/ppermute | solution.py:398
  49.1 2.1 %collective-permute-done.7 = bf16[112,128]{1,0:T(8,128)(2,1)S(1)} collective-permute-done((bf16[112,128]{1,0:T(8,128)(2,1)S(1)}, bf16[112,128]{1,0:T(8,128)(2,1)S(1)}, u32[]{:S(2)}, u32[]{:S(2)}) %collective-permute-start.7) | collective-permute-done | bytes 28704 | tf_op jit(solution)/shard_map/ppermute | solution.py:398
  51.3 4.3 %collective-permute-done.10 = bf16[256,128]{1,0:T(8,128)(2,1)S(1)} collective-permute-done((bf16[256,128]{1,0:T(8,128)(2,1)S(1)}, bf16[256,128]{1,0:T(8,128)(2,1)S(1)}, u32[]{:S(2)}, u32[]{:S(2)}) %collective-permute-start.10) | collective-permute-done | bytes 65568 | tf_op jit(solution)/shard_map/ppermute | solution.py:385
  56.0 5.6 %collective-permute-done.11 = bf16[256,128]{1,0:T(8,128)(2,1)S(1)} collective-permute-done((bf16[256,128]{1,0:T(8,128)(2,1)S(1)}, bf16[256,128]{1,0:T(8,128)(2,1)S(1)}, u32[]{:S(2)}, u32[]{:S(2)}) %collective-permute-start.11) | collective-permute-done | bytes 65568 | tf_op jit(solution)/shard_map/ppermute | solution.py:385
  61.8 2.0 %collective-permute-start.14 = (bf16[112,128]{1,0:T(8,128)(2,1)S(1)}, bf16[112,128]{1,0:T(8,128)(2,1)S(1)}, u32[]{:S(2)}, u32[]{:S(2)}) collective-permute-start(bf16[112,128]{1,0:T(8,128)(2,1)S(1)} %get-tuple-element.49), channel_id=1, source_target_pairs={{0,8},{4,12},{8,0},{12,4},{16,24},{20,28},{24,16},{28,20},{1,9},{5... | collective-permute-start | bytes 86024 | tf_op jit(solution)/shard_map/ppermute | solution.py:398
  63.8 1.9 %collective-permute-done.12 = bf16[112,128]{1,0:T(8,128)(2,1)S(1)} collective-permute-done((bf16[112,128]{1,0:T(8,128)(2,1)S(1)}, bf16[112,128]{1,0:T(8,128)(2,1)S(1)}, u32[]{:S(2)}, u32[]{:S(2)}) %collective-permute-start.12) | collective-permute-done | bytes 28704 | tf_op jit(solution)/shard_map/ppermute | solution.py:398
  65.8 2.0 %collective-permute-start.15 = (bf16[224,128]{1,0:T(8,128)(2,1)S(1)}, bf16[224,128]{1,0:T(8,128)(2,1)S(1)}, u32[]{:S(2)}, u32[]{:S(2)}) collective-permute-start(bf16[224,128]{1,0:T(8,128)(2,1)S(1)} %pad_maximum_fusion.4), channel_id=1, source_target_pairs={{0,16},{4,20},{8,24},{12,28},{16,0},{20,4},{24,8},{28,12},{1,17},{... | collective-permute-start | bytes 172040 | tf_op jit(solution)/shard_map/ppermute | solution.py:398
  67.8 2.2 %collective-permute-done.15 = bf16[224,128]{1,0:T(8,128)(2,1)S(1)} collective-permute-done((bf16[224,128]{1,0:T(8,128)(2,1)S(1)}, bf16[224,128]{1,0:T(8,128)(2,1)S(1)}, u32[]{:S(2)}, u32[]{:S(2)}) %collective-permute-start.15) | collective-permute-done | bytes 57376 | tf_op jit(solution)/shard_map/ppermute | solution.py:398
  70.0 1.9 %collective-permute-done.13 = bf16[224,128]{1,0:T(8,128)(2,1)S(1)} collective-permute-done((bf16[224,128]{1,0:T(8,128)(2,1)S(1)}, bf16[224,128]{1,0:T(8,128)(2,1)S(1)}, u32[]{:S(2)}, u32[]{:S(2)}) %collective-permute-start.13) | collective-permute-done | bytes 57376 | tf_op jit(solution)/shard_map/ppermute | solution.py:398
  72.1 0.9 %fold.1 = f32[32,8,256]{2,1,0:T(8,128)} custom-call(f32[8,32,256]{2,1,0:T(8,128)S(1)} %get-tuple-element.29.inner, bf16[32,128]{1,0:T(8,128)(2,1)S(1)} %slice.21.third, bf16[32,128]{1,0:T(8,128)(2,1)S(1)} %slice.23.fourth, f32[8,256]{1,0:T(8,128)S(1)} %get-tuple-element.32.den), custom_call_target="tpu_custom_call" | custom-call | tf_op jit(solution)/shard_map/fold/pallas_call | solution.py:538
  73.6 1.0 %split.29 = (f32[9,32,128]{2,1,0:T(8,128)}, f32[9,128,128]{2,1,0:T(8,128)}, f32[9,32,128]{2,1,0:T(8,128)}) custom-call(bf16[896,128]{1,0:T(8,128)(2,1)S(1)} %pad_maximum_fusion.own, bf16[896,128]{1,0:T(8,128)(2,1)S(1)} %collective-permute-done.16.other), custom_call_target="tpu_custom_call" | custom-call | tf_op jit(solution)/shard_map/split/pallas_call | solution.py:552
  (56 shorter events, 5.1 us)
Async XLA Ops:
  1.3 0.7 copy-start.1
  1.3 3.7 %copy-start.2 = (bf16[9,128,128]{2,1,0:T(8,128)(2,1)S(1)}, bf16[9,128,128]{2,1,0:T(8,128)(2,1)}, u32[]{:S(2)}) copy-start(bf16[9,128,128]{2,1,0:T(8,128)(2,1)} %param.11) | copy-start | bytes 884740
  3.7 1.8 %collective-permute-start = (bf16[5,64,256]{2,1,0:T(8,128)(2,1)S(1)}, bf16[5,64,256]{2,1,0:T(8,128)(2,1)S(1)}, u32[]{:S(2)}, u32[]{:S(2)}) collective-permute-start(bf16[5,64,256]{2,1,0:T(8,128)(2,1)S(1)} %get-tuple-element.21), channel_id=1, source_target_pairs={{0,4},{4,0},{8,12},{12,8},{16,20},{20,16},{24,28},{28,24},{1,5},{5... | collective-permute-start | bytes 491528 | tf_op jit(solution)/shard_map/ppermute | solution.py:385
  4.3 1.2 %collective-permute-start.1 = (bf16[5,64,256]{2,1,0:T(8,128)(2,1)S(1)}, bf16[5,64,256]{2,1,0:T(8,128)(2,1)S(1)}, u32[]{:S(2)}, u32[]{:S(2)}) collective-permute-start(bf16[5,64,256]{2,1,0:T(8,128)(2,1)S(1)} %get-tuple-element.22), channel_id=1, source_target_pairs={{4,8},{8,4},{12,16},{16,12},{20,24},{24,20},{5,9},{9,5},{13,17},{1... | collective-permute-start | bytes 491528 | tf_op jit(solution)/shard_map/ppermute | solution.py:385
  5.7 7.2 %collective-permute-start.2 = (bf16[96,128]{1,0:T(8,128)(2,1)S(1)}, bf16[96,128]{1,0:T(8,128)(2,1)S(1)}, u32[]{:S(2)}, u32[]{:S(2)}) collective-permute-start(bf16[96,128]{1,0:T(8,128)(2,1)S(1)} %get-tuple-element.24), channel_id=1, source_target_pairs={{0,1},{1,0},{2,3},{3,2},{4,5},{5,4},{6,7},{7,6},{8,9},{9,8},{10,11... | collective-permute-start | bytes 73736 | tf_op jit(solution)/shard_map/ppermute | solution.py:385
  8.5 5.6 %collective-permute-start.3 = (bf16[96,128]{1,0:T(8,128)(2,1)S(1)}, bf16[96,128]{1,0:T(8,128)(2,1)S(1)}, u32[]{:S(2)}, u32[]{:S(2)}) collective-permute-start(bf16[96,128]{1,0:T(8,128)(2,1)S(1)} %get-tuple-element.24), channel_id=1, source_target_pairs={{1,2},{2,1},{3,0},{0,3},{5,6},{6,5},{7,4},{4,7},{9,10},{10,9},{11,... | collective-permute-start | bytes 73736 | tf_op jit(solution)/shard_map/ppermute | solution.py:385
  10.9 0.9 %copy-start.4 = (bf16[9,128,32]{1,2,0:T(8,128)(2,1)S(1)}, bf16[9,128,32]{1,2,0:T(8,128)(2,1)}, u32[]{:S(2)}) copy-start(bf16[9,128,32]{1,2,0:T(8,128)(2,1)} %param.10) | copy-start | bytes 221188
  11.8 0.9 %copy-start.3 = (bf16[9,32,128]{2,1,0:T(8,128)(2,1)S(1)}, bf16[9,32,128]{2,1,0:T(8,128)(2,1)}, u32[]{:S(2)}) copy-start(bf16[9,32,128]{2,1,0:T(8,128)(2,1)} %param.12) | copy-start | bytes 221188
  12.8 1.3 %copy-start = (s32[4,8,256]{2,1,0:T(8,128)S(1)}, s32[4,8,256]{2,1,0:T(8,128)}, u32[]{:S(2)}) copy-start(s32[4,8,256]{2,1,0:T(8,128)} %weights.1) | copy-start | bytes 98308
  24.0 16.3 %collective-permute-start.4 = (bf16[1280,128]{1,0:T(8,128)(2,1)S(1)}, bf16[1280,128]{1,0:T(8,128)(2,1)S(1)}, u32[]{:S(2)}, u32[]{:S(2)}) collective-permute-start(bf16[1280,128]{1,0:T(8,128)(2,1)S(1)} %get-tuple-element.27), channel_id=1, source_target_pairs={{0,4},{4,0},{8,12},{12,8},{16,20},{20,16},{24,28},{28,24},{1,5},{5... | collective-permute-start | bytes 983048 | tf_op jit(solution)/shard_map/ppermute | solution.py:398
  39.0 4.0 %collective-permute-start.5 = (bf16[384,128]{1,0:T(8,128)(2,1)S(1)}, bf16[384,128]{1,0:T(8,128)(2,1)S(1)}, u32[]{:S(2)}, u32[]{:S(2)}) collective-permute-start(bf16[384,128]{1,0:T(8,128)(2,1)S(1)} %get-tuple-element.28), channel_id=1, source_target_pairs={{4,8},{8,4},{12,16},{16,12},{20,24},{24,20},{5,9},{9,5},{13,17},{1... | collective-permute-start | bytes 294920 | tf_op jit(solution)/shard_map/ppermute | solution.py:385
  40.4 4.7 %collective-permute-start.8 = (bf16[224,128]{1,0:T(8,128)(2,1)S(1)}, bf16[224,128]{1,0:T(8,128)(2,1)S(1)}, u32[]{:S(2)}, u32[]{:S(2)}) collective-permute-start(bf16[224,128]{1,0:T(8,128)(2,1)S(1)} %dynamic-slice_convert_fusion), channel_id=1, source_target_pairs={{0,16},{4,20},{8,24},{12,28},{16,0},{20,4},{24,8},{28,12},{1,17},{... | collective-permute-start | bytes 172040 | tf_op jit(solution)/shard_map/ppermute | solution.py:398
  40.5 6.7 %collective-permute-start.6 = (bf16[224,128]{1,0:T(8,128)(2,1)S(1)}, bf16[224,128]{1,0:T(8,128)(2,1)S(1)}, u32[]{:S(2)}, u32[]{:S(2)}) collective-permute-start(bf16[224,128]{1,0:T(8,128)(2,1)S(1)} %dynamic-slice_convert_fusion.1), channel_id=1, source_target_pairs={{0,8},{4,12},{8,0},{12,4},{16,24},{20,28},{24,16},{28,20},{1,9},{5... | collective-permute-start | bytes 172040 | tf_op jit(solution)/shard_map/ppermute | solution.py:398
  45.1 3.9 %collective-permute-start.9 = (bf16[112,128]{1,0:T(8,128)(2,1)S(1)}, bf16[112,128]{1,0:T(8,128)(2,1)S(1)}, u32[]{:S(2)}, u32[]{:S(2)}) collective-permute-start(bf16[112,128]{1,0:T(8,128)(2,1)S(1)} %dynamic-slice_convert_fusion.2), channel_id=1, source_target_pairs={{0,8},{4,12},{8,0},{12,4},{16,24},{20,28},{24,16},{28,20},{1,9},{5... | collective-permute-start | bytes 86024 | tf_op jit(solution)/shard_map/ppermute | solution.py:398
  47.2 3.9 %collective-permute-start.7 = (bf16[112,128]{1,0:T(8,128)(2,1)S(1)}, bf16[112,128]{1,0:T(8,128)(2,1)S(1)}, u32[]{:S(2)}, u32[]{:S(2)}) collective-permute-start(bf16[112,128]{1,0:T(8,128)(2,1)S(1)} %dynamic-slice_convert_fusion.3), channel_id=1, source_target_pairs={{0,16},{4,20},{8,24},{12,28},{16,0},{20,4},{24,8},{28,12},{1,17},{... | collective-permute-start | bytes 86024 | tf_op jit(solution)/shard_map/ppermute | solution.py:398
  51.2 4.3 %collective-permute-start.10 = (bf16[256,128]{1,0:T(8,128)(2,1)S(1)}, bf16[256,128]{1,0:T(8,128)(2,1)S(1)}, u32[]{:S(2)}, u32[]{:S(2)}) collective-permute-start(bf16[256,128]{1,0:T(8,128)(2,1)S(1)} %pad_maximum_fusion.2), channel_id=1, source_target_pairs={{0,1},{1,0},{2,3},{3,2},{4,5},{5,4},{6,7},{7,6},{8,9},{9,8},{10,11... | collective-permute-start | bytes 196616 | tf_op jit(solution)/shard_map/ppermute | solution.py:385
  55.5 6.1 %collective-permute-start.11 = (bf16[256,128]{1,0:T(8,128)(2,1)S(1)}, bf16[256,128]{1,0:T(8,128)(2,1)S(1)}, u32[]{:S(2)}, u32[]{:S(2)}) collective-permute-start(bf16[256,128]{1,0:T(8,128)(2,1)S(1)} %pad_maximum_fusion.1), channel_id=1, source_target_pairs={{1,2},{2,1},{3,0},{0,3},{5,6},{6,5},{7,4},{4,7},{9,10},{10,9},{11,... | collective-permute-start | bytes 196616 | tf_op jit(solution)/shard_map/ppermute | solution.py:385
  61.7 3.9 %collective-permute-start.12 = (bf16[112,128]{1,0:T(8,128)(2,1)S(1)}, bf16[112,128]{1,0:T(8,128)(2,1)S(1)}, u32[]{:S(2)}, u32[]{:S(2)}) collective-permute-start(bf16[112,128]{1,0:T(8,128)(2,1)S(1)} %get-tuple-element.48), channel_id=1, source_target_pairs={{0,16},{4,20},{8,24},{12,28},{16,0},{20,4},{24,8},{28,12},{1,17},{... | collective-permute-start | bytes 86024 | tf_op jit(solution)/shard_map/ppermute | solution.py:398
  61.8 3.9 %collective-permute-start.14 = (bf16[112,128]{1,0:T(8,128)(2,1)S(1)}, bf16[112,128]{1,0:T(8,128)(2,1)S(1)}, u32[]{:S(2)}, u32[]{:S(2)}) collective-permute-start(bf16[112,128]{1,0:T(8,128)(2,1)S(1)} %get-tuple-element.49), channel_id=1, source_target_pairs={{0,8},{4,12},{8,0},{12,4},{16,24},{20,28},{24,16},{28,20},{1,9},{5... | collective-permute-start | bytes 86024 | tf_op jit(solution)/shard_map/ppermute | solution.py:398
  65.8 4.2 %collective-permute-start.15 = (bf16[224,128]{1,0:T(8,128)(2,1)S(1)}, bf16[224,128]{1,0:T(8,128)(2,1)S(1)}, u32[]{:S(2)}, u32[]{:S(2)}) collective-permute-start(bf16[224,128]{1,0:T(8,128)(2,1)S(1)} %pad_maximum_fusion.4), channel_id=1, source_target_pairs={{0,16},{4,20},{8,24},{12,28},{16,0},{20,4},{24,8},{28,12},{1,17},{... | collective-permute-start | bytes 172040 | tf_op jit(solution)/shard_map/ppermute | solution.py:398
  67.8 4.2 %collective-permute-start.13 = (bf16[224,128]{1,0:T(8,128)(2,1)S(1)}, bf16[224,128]{1,0:T(8,128)(2,1)S(1)}, u32[]{:S(2)}, u32[]{:S(2)}) collective-permute-start(bf16[224,128]{1,0:T(8,128)(2,1)S(1)} %pad_maximum_fusion.3), channel_id=1, source_target_pairs={{0,8},{4,12},{8,0},{12,4},{16,24},{20,28},{24,16},{28,20},{1,9},{5... | collective-permute-start | bytes 172040 | tf_op jit(solution)/shard_map/ppermute | solution.py:398
  72.0 1.6 %collective-permute-start.16 = (bf16[896,128]{1,0:T(8,128)(2,1)S(1)}, bf16[896,128]{1,0:T(8,128)(2,1)S(1)}, u32[]{:S(2)}, u32[]{:S(2)}) collective-permute-start(bf16[896,128]{1,0:T(8,128)(2,1)S(1)} %pad_maximum_fusion.own), channel_id=1, source_target_pairs={{0,4},{4,0},{8,12},{12,8},{16,20},{20,16},{24,28},{28,24},{1,5},{5... | collective-permute-start | bytes 688136 | tf_op jit(solution)/shard_map/ppermute | solution.py:398

commit v6 on v5

--- a/solution.py
+++ b/solution.py
@@ -253,16 +253,18 @@
             at = slice(row * cols, (row + 1) * cols)
             z1 = dot(w_in[...], stack(x_s, row, False))
             sig = 0.5 * jnp.tanh(0.5 * z1) + 0.5
-            slope_s[:, at] = sig * (1.0 + z1 * (1.0 - sig))
-            h_s[:, (row + 1) * cols : (row + 2) * cols] = (z1 * sig).astype(BF16)
+            h1 = z1 * sig
+            slope_s[:, at] = sig + h1 * (1.0 - sig)
+            h_s[:, (row + 1) * cols : (row + 2) * cols] = h1.astype(BF16)
         for row in range(rows):
             at = slice(row * cols, (row + 1) * cols)
             ahead = slice((row + 1) * cols, (row + 2) * cols)
             dh2 = dot(w_out_back[...], stack(d_s, row, True))
             z2 = across(dot(w_mid[...], stack(h_s, row, False)), False)
             sig = 0.5 * jnp.tanh(0.5 * z2) + 0.5
-            h2_s[:, ahead] = (h_s[:, ahead].astype(F32) + z2 * sig).astype(BF16)
-            dz2 = (dh2 * (sig * (1.0 + z2 * (1.0 - sig)))).astype(BF16)
+            added = z2 * sig
+            h2_s[:, ahead] = (h_s[:, ahead].astype(F32) + added).astype(BF16)
+            dz2 = (dh2 * (sig + added * (1.0 - sig))).astype(BF16)
             dh_s[:, at] = dh2
             spread(z_s, dz2, row, True)
         for row in range(rows):
@@ -393,9 +395,14 @@
     return swap(edges, "lon", 0, True), swap(edges, "lon", 1, True)
 
 
-def exchange(value, axis, step):
-    pairs = [(index, index ^ step) for index in range(lax.axis_size(axis))]
+def exchange(value, axis, order):
+    pairs = [(index, index ^ order[index % 2]) for index in range(lax.axis_size(axis))]
     return lax.ppermute(value, axis, pairs)
+
+
+def order_bit(lat, order):
+    step = jnp.where(lat % 2 == 0, order[0], order[1])
+    return (lat // step) % 2
 
 
 def halves(value, bit):
@@ -445,6 +452,16 @@
         *(pltpu.with_memory_space_constraint(value, pltpu.HBM) for value in (fields, cotangent, blend_weights)),
     )
     first, second = swap_lat(first, second)
+    w_in = jnp.transpose(kernel_in, (1, 0, 2)).reshape(width, taps * channels)
+    kernel_mid = kernel_mid.reshape(3, 3, width, width)
+    kernel_out = kernel_out.reshape(3, 3, channels, width)
+    w_mid = jnp.transpose(kernel_mid, (1, 2, 0, 3)).reshape(3 * width, 3 * width)
+    w_mid_back = jnp.transpose(kernel_mid, (1, 3, 0, 2)).reshape(3 * width, 3 * width)
+    w_out = jnp.transpose(kernel_out, (1, 2, 0, 3)).reshape(3 * channels, 3 * width)
+    w_out_back = jnp.transpose(kernel_out, (3, 0, 1, 2)).reshape(width, taps * channels)
+    first, second, w_in, w_mid, w_mid_back, w_out, w_out_back = lax.optimization_barrier(
+        (first, second, w_in, w_mid, w_mid_back, w_out, w_out_back)
+    )
     edges, total = pl.pallas_call(
         edge_kernel,
         out_shape=(shape((2 * channels + 2 * height, LANES), BF16), shape((height, wide), F32)),
@@ -454,14 +471,6 @@
         name="edges",
     )(center, first, second, canvas)
     third, fourth = swap_lon(edges)
-
-    w_in = jnp.transpose(kernel_in, (1, 0, 2)).reshape(width, taps * channels)
-    kernel_mid = kernel_mid.reshape(3, 3, width, width)
-    kernel_out = kernel_out.reshape(3, 3, channels, width)
-    w_mid = jnp.transpose(kernel_mid, (1, 2, 0, 3)).reshape(3 * width, 3 * width)
-    w_mid_back = jnp.transpose(kernel_mid, (1, 3, 0, 2)).reshape(3 * width, 3 * width)
-    w_out = jnp.transpose(kernel_out, (1, 2, 0, 3)).reshape(3 * channels, 3 * width)
-    w_out_back = jnp.transpose(kernel_out, (3, 0, 1, 2)).reshape(width, taps * channels)
 
     lat_size, lon_size = lax.axis_size("lat"), lax.axis_size("lon")
     length = taps * (2 * channels + width)
@@ -500,18 +509,16 @@
     )
 
     lat = lax.axis_index("lat")
-    first = exchange(send, "lat", 1)
+    first = exchange(send, "lat", (1, 1))
     second = swap(second, "lat", 1, False)
     mine = keep + first[:half].astype(F32)
     steps = [2 << bit for bit in range(lat_size.bit_length() - 2)]
-    parts = jnp.split(mine, 2)
-    orders = (steps, steps[1:] + steps[:1])
-    for turn in range(len(steps)):
-        for index in (0, 1):
-            step = orders[index][turn]
-            own, other = halves(parts[index], (lat // step) % 2)
-            parts[index] = own + exchange(other.astype(BF16), "lat", step).astype(F32)
-    mine = jnp.concatenate(parts, axis=0)
+    orders = list(zip(steps, steps[1:] + steps[:1]))
+    for order in orders:
+        own, other = halves(mine, order_bit(lat, order))
+        mine = own + exchange(other.astype(BF16), "lat", order).astype(F32)
+    mine = mine.astype(BF16)
+    second, mine = lax.optimization_barrier((second, mine))
     inner, edges = pl.pallas_call(
         beside_kernel,
         out_shape=(shape((rows, channels, cols), F32), shape((channels, LANES), BF16)),
@@ -521,7 +528,6 @@
         name="beside",
     )(numer, first, second)
     count = mine.shape[0]
-    mine = mine.astype(BF16)
     if lon_size == 4:
         received = []
         for start in (0, 1):
@@ -533,7 +539,7 @@
         third, fourth = swap_lon(edges)
         step = 1
         while step < lon_size:
-            mine = (mine.astype(F32) + exchange(mine, "lon", step).astype(F32)).astype(BF16)
+            mine = (mine.astype(F32) + exchange(mine, "lon", (step, step)).astype(F32)).astype(BF16)
             step *= 2
     blended = pl.pallas_call(
         fold_kernel,
@@ -543,12 +549,8 @@
         compiler_params=params(),
         name="fold",
     )(inner, third, fourth, den)
-    parts = jnp.split(mine, 2)
-    for turn in reversed(range(len(steps))):
-        for index in (0, 1):
-            step = orders[index][turn]
-            parts[index] = ordered(parts[index], exchange(parts[index], "lat", step), (lat // step) % 2)
-    mine = jnp.concatenate(parts, axis=0)
+    for order in reversed(orders):
+        mine = ordered(mine, exchange(mine, "lat", order), order_bit(lat, order))
     grad_in, grad_mid, grad_out = pl.pallas_call(
         split_kernel,
         out_shape=(
@@ -560,7 +562,7 @@
         out_specs=(vmem(),) * 3,
         compiler_params=params(),
         name="split",
-    )(mine, exchange(mine, "lat", 1))
+    )(mine, exchange(mine, "lat", (1, 1)))
     return blended, jnp.transpose(grad_in, (0, 2, 1)), grad_mid, grad_out
 
 

time: 74.9 us -> 74.9 us (level)
  waiting for transfers between devices: 24.1 us -> 31 us
  starting transfers between devices: 31.6 us -> 25.8 us
  local copies, waits for them, and re-layouts: 3.22 us -> 2.24 us
    ppermute x10 -> x6, starting transfers between devices: 23.9 us -> 18.6 us  [exchange(): return lax.ppermute(value, axis, pairs)]
    ppermute x10 -> x6, waiting for transfers between devices: 13 us -> 17.4 us  [exchange(): return lax.ppermute(value, axis, pairs)]
    ppermute x7, waiting for transfers between devices: 11 us -> 13.6 us  [swap(): return lax.ppermute(value, axis, pairs)]
    unnamed x11, local copies, waits for them, and re-layouts: 2.23 us -> 1.31 us
  transfers between devices with their start and end apart: 17 -> 13, of which waited for: 12 -> 9; matrix products, arithmetic and copies ran while one was open for 1% -> 1% of each run, Pallas kernels for 1% -> 1%
where the time goes in v6:
time: 74.9 us; the launch traced here: 74.7 us
  waiting for transfers between devices  31 us (41%)
  starting transfers between devices  25.8 us (34%)
  Pallas kernels  13.8 us (18%)
  local copies, waits for them, and re-layouts  2.24 us (3%)
  between operations  1.67 us (2%)
    ppermute x6, starting transfers between devices, exchange(): return lax.ppermute(value, axis, pairs)  18.6 us
    ppermute x6, waiting for transfers between devices, exchange(): return lax.ppermute(value, axis, pairs)  17.4 us
    ppermute x7, waiting for transfers between devices, swap(): return lax.ppermute(value, axis, pairs)  13.6 us
    pallas_call x1, Pallas kernels, shards(): pl.pallas_call(patch_kernel, out_shape=(shape((half + edge_rows, LANES),...  9.9 us
    ppermute x7, starting transfers between devices, swap(): return lax.ppermute(value, axis, pairs)  7.12 us
    pallas_call x1, Pallas kernels, shards(): pl.pallas_call(pack_kernel, out_shape=(shape((rows, 2 * channels, cols),...  1.72 us
  transfers between devices with their start and end apart: 13, of which 9 were waited for; matrix products, arithmetic and copies ran while one was open for 1% of the time, Pallas kernels for 1%

profile of v6, /device:TPU:0, one launch (start us, length us, event | category | flops | bytes accessed | tf_op | source)
XLA Modules:
  0.0 74.7 jit_solution(4214604509083487084)
XLA Ops:
  1.3 0.7 copy-done.1
  2.0 1.7 %pack.1 = (bf16[8,64,256]{2,1,0:T(8,128)(2,1)S(1)}, bf16[5,64,256]{2,1,0:T(8,128)(2,1)S(1)}, bf16[5,64,256]{2,1,0:T(8,128)(2,1)S(1)}, f32[16,384]{1,0:T(8,128)S(1)}) custom-call(s32[1,1,2,4]{3,2,1,0:T(2,128)S(1)} %bitcast.29, s32[1,1]{1,0:T(1,128)S(6)} %copy.29.counts, bf16[32,8,256]{2,1,0:T(8,128)(2,1)} %fields_in.1, bf16[32,8,256]{2,1,0:T(8,128)(2,1)} %cotangent_in.1, ...), custom_call_target="tpu_custom_call" | custom-call | tf_op jit(solution)/shard_map/pack/pallas_call | solution.py:430
  3.7 0.6 collective-permute-start
  4.3 0.7 collective-permute-start.1
  5.0 0.3 copy.18
  5.3 0.3 copy.17
  5.5 0.6 copy-done.3
  6.6 2.6 %collective-permute-start.2 = (bf16[96,128]{1,0:T(8,128)(2,1)S(1)}, bf16[96,128]{1,0:T(8,128)(2,1)S(1)}, u32[]{:S(2)}, u32[]{:S(2)}) collective-permute-start(bf16[96,128]{1,0:T(8,128)(2,1)S(1)} %get-tuple-element.35), channel_id=1, source_target_pairs={{0,1},{1,0},{2,3},{3,2},{4,5},{5,4},{6,7},{7,6},{8,9},{9,8},{10,11... | collective-permute-start | bytes 73736 | tf_op jit(solution)/shard_map/ppermute | solution.py:387
  9.1 2.5 %collective-permute-start.3 = (bf16[96,128]{1,0:T(8,128)(2,1)S(1)}, bf16[96,128]{1,0:T(8,128)(2,1)S(1)}, u32[]{:S(2)}, u32[]{:S(2)}) collective-permute-start(bf16[96,128]{1,0:T(8,128)(2,1)S(1)} %get-tuple-element.35), channel_id=1, source_target_pairs={{1,2},{2,1},{3,0},{0,3},{5,6},{6,5},{7,4},{4,7},{9,10},{10,9},{11,... | collective-permute-start | bytes 73736 | tf_op jit(solution)/shard_map/ppermute | solution.py:387
  11.9 2.9 %collective-permute-done.3.fourth = bf16[96,128]{1,0:T(8,128)(2,1)S(1)} collective-permute-done((bf16[96,128]{1,0:T(8,128)(2,1)S(1)}, bf16[96,128]{1,0:T(8,128)(2,1)S(1)}, u32[]{:S(2)}, u32[]{:S(2)}) %collective-permute-start.3) | collective-permute-done | bytes 24608 | tf_op jit(solution)/shard_map/ppermute | solution.py:387
  14.7 9.9 %patches.1 = (bf16[1280,128]{1,0:T(8,128)(2,1)S(1)}, f32[896,128]{1,0:T(8,128)S(1)}, bf16[384,128]{1,0:T(8,128)(2,1)S(1)}, f32[16,32,384]{2,1,0:T(8,128)S(1)}, f32[8,256]{1,0:T(8,128)S(1)}) custom-call(s32[1,1,2,4]{3,2,1,0:T(2,128)S(1)} %bitcast.30, s32[1,1]{1,0:T(1,128)S(6)} %copy.29.counts, bf16[8,64,256]{2,1,0:T(8,128)(2,1)S(1)} %get-tuple-element.29.center, ...), custom_call_target="tpu_custom_call" | custom-call | tf_op jit(solution)/shard_map/patches/pallas_call | solution.py:481
  24.6 14.1 %collective-permute-start.4 = (bf16[1280,128]{1,0:T(8,128)(2,1)S(1)}, bf16[1280,128]{1,0:T(8,128)(2,1)S(1)}, u32[]{:S(2)}, u32[]{:S(2)}) collective-permute-start(bf16[1280,128]{1,0:T(8,128)(2,1)S(1)} %get-tuple-element.43), channel_id=1, source_target_pairs={{0,4},{4,0},{8,12},{12,8},{16,20},{20,16},{24,28},{28,24},{1,5},{5... | collective-permute-start | bytes 983048 | tf_op jit(solution)/shard_map/ppermute | solution.py:400
  38.7 1.3 %collective-permute-done.4.first = bf16[1280,128]{1,0:T(8,128)(2,1)S(1)} collective-permute-done((bf16[1280,128]{1,0:T(8,128)(2,1)S(1)}, bf16[1280,128]{1,0:T(8,128)(2,1)S(1)}, u32[]{:S(2)}, u32[]{:S(2)}) %collective-permute-start.4) | collective-permute-done | bytes 327712 | tf_op jit(solution)/shard_map/ppermute | solution.py:400
  40.2 4.7 %collective-permute-done.6 = bf16[448,128]{1,0:T(8,128)(2,1)S(1)} collective-permute-done((bf16[448,128]{1,0:T(8,128)(2,1)S(1)}, bf16[448,128]{1,0:T(8,128)(2,1)S(1)}, u32[]{:S(2)}, u32[]{:S(2)}) %collective-permute-start.6) | collective-permute-done | bytes 114720 | tf_op jit(solution)/shard_map/ppermute | solution.py:400
  45.0 0.7 collective-permute-start.5
  45.7 3.5 %collective-permute-done.7 = bf16[224,128]{1,0:T(8,128)(2,1)S(1)} collective-permute-done((bf16[224,128]{1,0:T(8,128)(2,1)S(1)}, bf16[224,128]{1,0:T(8,128)(2,1)S(1)}, u32[]{:S(2)}, u32[]{:S(2)}) %collective-permute-start.7) | collective-permute-done | bytes 57376 | tf_op jit(solution)/shard_map/ppermute | solution.py:400
  49.5 4.7 %collective-permute-done.8 = bf16[256,128]{1,0:T(8,128)(2,1)S(1)} collective-permute-done((bf16[256,128]{1,0:T(8,128)(2,1)S(1)}, bf16[256,128]{1,0:T(8,128)(2,1)S(1)}, u32[]{:S(2)}, u32[]{:S(2)}) %collective-permute-start.8) | collective-permute-done | bytes 65568 | tf_op jit(solution)/shard_map/ppermute | solution.py:387
  54.3 6.0 %collective-permute-done.9 = bf16[256,128]{1,0:T(8,128)(2,1)S(1)} collective-permute-done((bf16[256,128]{1,0:T(8,128)(2,1)S(1)}, bf16[256,128]{1,0:T(8,128)(2,1)S(1)}, u32[]{:S(2)}, u32[]{:S(2)}) %collective-permute-start.9) | collective-permute-done | bytes 65568 | tf_op jit(solution)/shard_map/ppermute | solution.py:387
  60.3 4.3 %collective-permute-start.10 = (bf16[224,128]{1,0:T(8,128)(2,1)S(1)}, bf16[224,128]{1,0:T(8,128)(2,1)S(1)}, u32[]{:S(2)}, u32[]{:S(2)}) collective-permute-start(bf16[224,128]{1,0:T(8,128)(2,1)S(1)} %add_convert_fusion), channel_id=1, source_target_pairs={{0,16},{4,12},{8,24},{12,4},{16,0},{20,28},{24,8},{28,20},{1,17},{... | collective-permute-start | bytes 172040 | tf_op jit(solution)/shard_map/ppermute | solution.py:400
  64.6 2.6 %collective-permute-done.10 = bf16[224,128]{1,0:T(8,128)(2,1)S(1)} collective-permute-done((bf16[224,128]{1,0:T(8,128)(2,1)S(1)}, bf16[224,128]{1,0:T(8,128)(2,1)S(1)}, u32[]{:S(2)}, u32[]{:S(2)}) %collective-permute-start.10) | collective-permute-done | bytes 57376 | tf_op jit(solution)/shard_map/ppermute | solution.py:400
  67.3 4.8 %collective-permute-done.11 = bf16[448,128]{1,0:T(8,128)(2,1)S(1)} collective-permute-done((bf16[448,128]{1,0:T(8,128)(2,1)S(1)}, bf16[448,128]{1,0:T(8,128)(2,1)S(1)}, u32[]{:S(2)}, u32[]{:S(2)}) %collective-permute-start.11) | collective-permute-done | bytes 114720 | tf_op jit(solution)/shard_map/ppermute | solution.py:400
  72.3 0.9 %fold.1 = f32[32,8,256]{2,1,0:T(8,128)} custom-call(f32[8,32,256]{2,1,0:T(8,128)S(1)} %get-tuple-element.47.inner, bf16[32,128]{1,0:T(8,128)(2,1)S(1)} %slice.21.third, bf16[32,128]{1,0:T(8,128)(2,1)S(1)} %slice.23.fourth, f32[8,256]{1,0:T(8,128)S(1)} %get-tuple-element.50.den), custom_call_target="tpu_custom_call" | custom-call | tf_op jit(solution)/shard_map/fold/pallas_call | solution.py:544
  73.1 0.6 collective-permute-done.12.other
  73.7 1.0 %split.1 = (f32[9,32,128]{2,1,0:T(8,128)}, f32[9,128,128]{2,1,0:T(8,128)}, f32[9,32,128]{2,1,0:T(8,128)}) custom-call(bf16[896,128]{1,0:T(8,128)(2,1)S(1)} %pad_maximum_fusion.own, bf16[896,128]{1,0:T(8,128)(2,1)S(1)} %collective-permute-done.12.other), custom_call_target="tpu_custom_call" | custom-call | tf_op jit(solution)/shard_map/split/pallas_call | solution.py:554
  (40 shorter events, 1.5 us)
Async XLA Ops:
  1.3 0.7 copy-start.1
  1.3 3.7 %copy-start.2 = (bf16[9,128,128]{2,1,0:T(8,128)(2,1)S(1)}, bf16[9,128,128]{2,1,0:T(8,128)(2,1)}, u32[]{:S(2)}) copy-start(bf16[9,128,128]{2,1,0:T(8,128)(2,1)} %param.11) | copy-start | bytes 884740
  3.7 2.6 %collective-permute-start = (bf16[5,64,256]{2,1,0:T(8,128)(2,1)S(1)}, bf16[5,64,256]{2,1,0:T(8,128)(2,1)S(1)}, u32[]{:S(2)}, u32[]{:S(2)}) collective-permute-start(bf16[5,64,256]{2,1,0:T(8,128)(2,1)S(1)} %get-tuple-element.30), channel_id=1, source_target_pairs={{0,4},{4,0},{8,12},{12,8},{16,20},{20,16},{24,28},{28,24},{1,5},{5... | collective-permute-start | bytes 491528 | tf_op jit(solution)/shard_map/ppermute | solution.py:387
  4.3 2.0 %collective-permute-start.1 = (bf16[5,64,256]{2,1,0:T(8,128)(2,1)S(1)}, bf16[5,64,256]{2,1,0:T(8,128)(2,1)S(1)}, u32[]{:S(2)}, u32[]{:S(2)}) collective-permute-start(bf16[5,64,256]{2,1,0:T(8,128)(2,1)S(1)} %get-tuple-element.31), channel_id=1, source_target_pairs={{4,8},{8,4},{12,16},{16,12},{20,24},{24,20},{5,9},{9,5},{13,17},{1... | collective-permute-start | bytes 491528 | tf_op jit(solution)/shard_map/ppermute | solution.py:387
  5.2 0.9 %copy-start.3 = (bf16[9,32,128]{2,1,0:T(8,128)(2,1)S(1)}, bf16[9,32,128]{2,1,0:T(8,128)(2,1)}, u32[]{:S(2)}) copy-start(bf16[9,32,128]{2,1,0:T(8,128)(2,1)} %param.12) | copy-start | bytes 221188
  6.3 5.3 %copy-start.4 = (bf16[9,128,32]{1,2,0:T(8,128)(2,1)S(1)}, bf16[9,128,32]{1,2,0:T(8,128)(2,1)}, u32[]{:S(2)}) copy-start(bf16[9,128,32]{1,2,0:T(8,128)(2,1)} %param.10) | copy-start | bytes 221188
  6.6 5.3 %collective-permute-start.2 = (bf16[96,128]{1,0:T(8,128)(2,1)S(1)}, bf16[96,128]{1,0:T(8,128)(2,1)S(1)}, u32[]{:S(2)}, u32[]{:S(2)}) collective-permute-start(bf16[96,128]{1,0:T(8,128)(2,1)S(1)} %get-tuple-element.35), channel_id=1, source_target_pairs={{0,1},{1,0},{2,3},{3,2},{4,5},{5,4},{6,7},{7,6},{8,9},{9,8},{10,11... | collective-permute-start | bytes 73736 | tf_op jit(solution)/shard_map/ppermute | solution.py:387
  9.1 5.6 %collective-permute-start.3 = (bf16[96,128]{1,0:T(8,128)(2,1)S(1)}, bf16[96,128]{1,0:T(8,128)(2,1)S(1)}, u32[]{:S(2)}, u32[]{:S(2)}) collective-permute-start(bf16[96,128]{1,0:T(8,128)(2,1)S(1)} %get-tuple-element.35), channel_id=1, source_target_pairs={{1,2},{2,1},{3,0},{0,3},{5,6},{6,5},{7,4},{4,7},{9,10},{10,9},{11,... | collective-permute-start | bytes 73736 | tf_op jit(solution)/shard_map/ppermute | solution.py:387
  11.7 3.0 %copy-start = (s32[4,8,256]{2,1,0:T(8,128)S(1)}, s32[4,8,256]{2,1,0:T(8,128)}, u32[]{:S(2)}) copy-start(s32[4,8,256]{2,1,0:T(8,128)} %weights.1) | copy-start | bytes 98308
  24.6 15.3 %collective-permute-start.4 = (bf16[1280,128]{1,0:T(8,128)(2,1)S(1)}, bf16[1280,128]{1,0:T(8,128)(2,1)S(1)}, u32[]{:S(2)}, u32[]{:S(2)}) collective-permute-start(bf16[1280,128]{1,0:T(8,128)(2,1)S(1)} %get-tuple-element.43), channel_id=1, source_target_pairs={{0,4},{4,0},{8,12},{12,8},{16,20},{20,16},{24,28},{28,24},{1,5},{5... | collective-permute-start | bytes 983048 | tf_op jit(solution)/shard_map/ppermute | solution.py:400
  40.1 4.9 %collective-permute-start.6 = (bf16[448,128]{1,0:T(8,128)(2,1)S(1)}, bf16[448,128]{1,0:T(8,128)(2,1)S(1)}, u32[]{:S(2)}, u32[]{:S(2)}) collective-permute-start(bf16[448,128]{1,0:T(8,128)(2,1)S(1)} %dynamic-slice_convert_fusion), channel_id=1, source_target_pairs={{0,8},{4,20},{8,0},{12,28},{16,24},{20,4},{24,16},{28,12},{1,9},{5... | collective-permute-start | bytes 344072 | tf_op jit(solution)/shard_map/ppermute | solution.py:400
  45.0 4.2 %collective-permute-start.7 = (bf16[224,128]{1,0:T(8,128)(2,1)S(1)}, bf16[224,128]{1,0:T(8,128)(2,1)S(1)}, u32[]{:S(2)}, u32[]{:S(2)}) collective-permute-start(bf16[224,128]{1,0:T(8,128)(2,1)S(1)} %dynamic-slice_convert_fusion.1), channel_id=1, source_target_pairs={{0,16},{4,12},{8,24},{12,4},{16,0},{20,28},{24,8},{28,20},{1,17},{... | collective-permute-start | bytes 172040 | tf_op jit(solution)/shard_map/ppermute | solution.py:400
  45.0 4.2 %collective-permute-start.5 = (bf16[384,128]{1,0:T(8,128)(2,1)S(1)}, bf16[384,128]{1,0:T(8,128)(2,1)S(1)}, u32[]{:S(2)}, u32[]{:S(2)}) collective-permute-start(bf16[384,128]{1,0:T(8,128)(2,1)S(1)} %get-tuple-element.44), channel_id=1, source_target_pairs={{4,8},{8,4},{12,16},{16,12},{20,24},{24,20},{5,9},{9,5},{13,17},{1... | collective-permute-start | bytes 294920 | tf_op jit(solution)/shard_map/ppermute | solution.py:387
  49.4 4.7 %collective-permute-start.8 = (bf16[256,128]{1,0:T(8,128)(2,1)S(1)}, bf16[256,128]{1,0:T(8,128)(2,1)S(1)}, u32[]{:S(2)}, u32[]{:S(2)}) collective-permute-start(bf16[256,128]{1,0:T(8,128)(2,1)S(1)} %pad_maximum_fusion.3), channel_id=1, source_target_pairs={{0,1},{1,0},{2,3},{3,2},{4,5},{5,4},{6,7},{7,6},{8,9},{9,8},{10,11... | collective-permute-start | bytes 196616 | tf_op jit(solution)/shard_map/ppermute | solution.py:387
  54.2 6.1 %collective-permute-start.9 = (bf16[256,128]{1,0:T(8,128)(2,1)S(1)}, bf16[256,128]{1,0:T(8,128)(2,1)S(1)}, u32[]{:S(2)}, u32[]{:S(2)}) collective-permute-start(bf16[256,128]{1,0:T(8,128)(2,1)S(1)} %pad_maximum_fusion.2), channel_id=1, source_target_pairs={{1,2},{2,1},{3,0},{0,3},{5,6},{6,5},{7,4},{4,7},{9,10},{10,9},{11,... | collective-permute-start | bytes 196616 | tf_op jit(solution)/shard_map/ppermute | solution.py:387
  60.3 6.9 %collective-permute-start.10 = (bf16[224,128]{1,0:T(8,128)(2,1)S(1)}, bf16[224,128]{1,0:T(8,128)(2,1)S(1)}, u32[]{:S(2)}, u32[]{:S(2)}) collective-permute-start(bf16[224,128]{1,0:T(8,128)(2,1)S(1)} %add_convert_fusion), channel_id=1, source_target_pairs={{0,16},{4,12},{8,24},{12,4},{16,0},{20,28},{24,8},{28,20},{1,17},{... | collective-permute-start | bytes 172040 | tf_op jit(solution)/shard_map/ppermute | solution.py:400
  67.2 4.9 %collective-permute-start.11 = (bf16[448,128]{1,0:T(8,128)(2,1)S(1)}, bf16[448,128]{1,0:T(8,128)(2,1)S(1)}, u32[]{:S(2)}, u32[]{:S(2)}) collective-permute-start(bf16[448,128]{1,0:T(8,128)(2,1)S(1)} %pad_maximum_fusion.1), channel_id=1, source_target_pairs={{0,8},{4,20},{8,0},{12,28},{16,24},{20,4},{24,16},{28,12},{1,9},{5... | collective-permute-start | bytes 344072 | tf_op jit(solution)/shard_map/ppermute | solution.py:400
  72.2 1.6 %collective-permute-start.12 = (bf16[896,128]{1,0:T(8,128)(2,1)S(1)}, bf16[896,128]{1,0:T(8,128)(2,1)S(1)}, u32[]{:S(2)}, u32[]{:S(2)}) collective-permute-start(bf16[896,128]{1,0:T(8,128)(2,1)S(1)} %pad_maximum_fusion.own), channel_id=1, source_target_pairs={{0,4},{4,0},{8,12},{12,8},{16,20},{20,16},{24,28},{28,24},{1,5},{5... | collective-permute-start | bytes 688136 | tf_op jit(solution)/shard_map/ppermute | solution.py:400

commit v7 on v6

--- a/solution.py
+++ b/solution.py
@@ -140,7 +140,7 @@
 def patch_kernel(
     anchors, counts, center, first, second, third, fourth, total_in, weights,
     w_in, w_mid, w_mid_back, w_out, w_out_back,
-    send, keep, second_out, numer, den_out,
+    send, keep, numer, den_out,
     grads, window, x_s, d_s, h_s, z_s, h2_s, slope_s, dh_s, dz_s,
 ):
     rows = center.shape[0]
@@ -296,33 +296,48 @@
     odd_index = lax.rem(lax.axis_index("lat"), 2)
     send[0:half] = grads[pl.ds(pl.multiple_of((1 - odd_index) * half, half), half)].astype(BF16)
     keep[...] = grads[pl.ds(pl.multiple_of(odd_index * half, half), half)]
-    blocks = wide // LANES
-    for row in range(MARGIN):
-        upper, lower = numer[row], numer[MARGIN + rows + row]
-        near = choose(lat_odd, upper, lower).astype(BF16)
-        far = choose(lat_odd, lower, upper).astype(BF16)
-        for block in range(blocks):
-            at = (row * blocks + block) * channels
-            send[half + at : half + at + channels] = near[:, block * LANES : (block + 1) * LANES]
-            second_out[at : at + channels] = far[:, block * LANES : (block + 1) * LANES]
-
-
-def beside_kernel(numer, first, second, inner, edges):
+    lanes = lane_ids((channels, LANES))
+    blocks = cols // LANES
+    base = half
+    upper = [numer[row] for row in range(MARGIN)]
+    lower = [numer[MARGIN + rows + row] for row in range(MARGIN)]
+    for when_odd, when_even in ((upper, lower), (lower, upper)):
+        packed = jnp.zeros((channels, LANES), F32)
+        for row in range(MARGIN):
+            line = choose(lat_odd, when_odd[row], when_even[row])
+            for block in range(blocks):
+                send[base : base + channels] = line[:, block * LANES : (block + 1) * LANES].astype(BF16)
+                base += channels
+            low = jnp.where(lanes < MARGIN, line[:, cols:], 0.0)
+            high = jnp.where(lanes >= LANES - MARGIN, line[:, cols:], 0.0)
+            packed = packed + roll(low, MARGIN * row, 1) + roll(high, -MARGIN * row, 1)
+        send[base : base + channels] = packed.astype(BF16)
+        base += channels
+
+
+def beside_kernel(numer, first, held, inner, edges):
     height, channels, wide = numer.shape
     cols = wide - LANES
     rows = height - 2 * MARGIN
-    blocks = wide // LANES
-    base = first.shape[0] - second.shape[0]
+    blocks = cols // LANES
+    edge_rows = held.shape[0]
+    base = first.shape[0] - 2 * edge_rows
     lanes = lane_ids((channels, LANES))
-    lat_odd = lax.rem(lax.axis_index("lat"), 2) == 1
+    lat = lax.axis_index("lat")
+    odd = lax.rem(lat, 2) == 1
+    inside = jnp.logical_and(lat > 0, lat < lax.axis_size("lat") - 1)
     packed = jnp.zeros((channels, LANES), F32)
     for row in range(rows):
+        at = row % MARGIN
         parts = []
-        for block in range(blocks):
-            at = ((row % MARGIN) * blocks + block) * channels
-            near = first[base + at : base + at + channels].astype(F32)
-            far = second[at : at + channels].astype(F32)
-            other = choose(lat_odd, near, far) if row < MARGIN else choose(lat_odd, far, near)
+        for block in range(blocks + 1):
+            start = (at * blocks + block if block < blocks else MARGIN * blocks) * channels
+            near = first[base + start : base + start + channels].astype(F32)
+            far = choose(inside, held[start : start + channels].astype(F32), 0.0)
+            other = choose(odd, near, far) if row < MARGIN else choose(odd, far, near)
+            if block == blocks:
+                low = jnp.where(lanes < MARGIN, roll(other, -MARGIN * at, 1), 0.0)
+                other = low + jnp.where(lanes >= LANES - MARGIN, roll(other, MARGIN * at, 1), 0.0)
             parts.append(numer[MARGIN + row, :, block * LANES : (block + 1) * LANES] + other)
         inner[row] = jnp.concatenate(parts[:-1], axis=1)
         low = jnp.where(lanes < MARGIN, parts[-1], 0.0)
@@ -331,12 +346,13 @@
     edges[...] = packed.astype(BF16)
 
 
-def fold_kernel(inner, third, fourth, den, blended):
+def fold_kernel(inner, parts, den, blended):
     rows, channels, cols = inner.shape
     lanes = lane_ids((channels, LANES))
-    lon_odd = lax.rem(lax.axis_index("lon"), 2) == 1
-    left = choose(lon_odd, third[...], fourth[...]).astype(F32)
-    right = choose(lon_odd, fourth[...], third[...]).astype(F32)
+    lon, lon_size = lax.axis_index("lon"), lax.axis_size("lon")
+    base = parts.shape[1] - channels
+    left = parts[lax.rem(lon + lon_size - 1, lon_size), base : base + channels].astype(F32)
+    right = parts[lax.rem(lon + 1, lon_size), base : base + channels].astype(F32)
     inverse = 1.0 / den[...]
     lines = []
     for row in range(rows):
@@ -477,18 +493,17 @@
     unit = 16 * lat_size
     length = (length + unit - 1) // unit * unit
     half = length // 2
-    edge_rows = MARGIN * channels * (wide // LANES)
-    send, keep, second, numer, den = pl.pallas_call(
+    edge_rows = channels * (MARGIN * (cols // LANES) + 1)
+    send, keep, numer, den = pl.pallas_call(
         patch_kernel,
         out_shape=(
-            shape((half + edge_rows, LANES), BF16),
+            shape((half + 2 * edge_rows, LANES), BF16),
             shape((half, LANES), F32),
-            shape((edge_rows, LANES), BF16),
             shape((height, channels, wide), F32),
             shape((rows, cols), F32),
         ),
         in_specs=[smem(), smem()] + [vmem()] * 12,
-        out_specs=(vmem(),) * 5,
+        out_specs=(vmem(),) * 4,
         scratch_shapes=[
             pltpu.VMEM((length, LANES), F32),
             pltpu.VMEM((height, 2 * channels, wide), F32),
@@ -509,16 +524,28 @@
     )
 
     lat = lax.axis_index("lat")
+    even = lat % 2 == 0
     first = exchange(send, "lat", (1, 1))
-    second = swap(second, "lat", 1, False)
     mine = keep + first[:half].astype(F32)
+    held = first[half + edge_rows :]
     steps = [2 << bit for bit in range(lat_size.bit_length() - 2)]
     orders = list(zip(steps, steps[1:] + steps[:1]))
-    for order in orders:
+    for turn, order in enumerate(orders):
         own, other = halves(mine, order_bit(lat, order))
-        mine = own + exchange(other.astype(BF16), "lat", order).astype(F32)
-    mine = mine.astype(BF16)
-    second, mine = lax.optimization_barrier((second, mine))
+        payload = jnp.concatenate([other.astype(BF16), held], axis=0)
+        payload = exchange(payload, "lat", order)
+        count = own.shape[0]
+        mine = own + payload[:count].astype(F32)
+        moves = []
+        for side in (0, 1):
+            done = [orders[before][side] for before in range(turn)]
+            move = jnp.bool_(True)
+            for step in steps:
+                if step < order[side]:
+                    carries = 1 if (step in done) == (side == 1) else 0
+                    move = jnp.logical_and(move, (lat // step) % 2 == carries)
+            moves.append(move)
+        held = jnp.where(jnp.where(even, moves[0], moves[1]), payload[count:], held)
     inner, edges = pl.pallas_call(
         beside_kernel,
         out_shape=(shape((rows, channels, cols), F32), shape((channels, LANES), BF16)),
@@ -526,29 +553,20 @@
         out_specs=(vmem(),) * 2,
         compiler_params=params(),
         name="beside",
-    )(numer, first, second)
+    )(numer, first, held)
     count = mine.shape[0]
-    if lon_size == 4:
-        received = []
-        for start in (0, 1):
-            other = swap(jnp.concatenate([mine, edges], axis=0), "lon", start, True)
-            received.append(other[count:])
-            mine = (mine.astype(F32) + other[:count].astype(F32)).astype(BF16)
-        third, fourth = received
-    else:
-        third, fourth = swap_lon(edges)
-        step = 1
-        while step < lon_size:
-            mine = (mine.astype(F32) + exchange(mine, "lon", (step, step)).astype(F32)).astype(BF16)
-            step *= 2
+    payload = jnp.concatenate([mine.astype(BF16), edges], axis=0)
+    payload = jnp.broadcast_to(payload[None], (lon_size,) + payload.shape)
+    payload = lax.all_to_all(payload, "lon", 0, 0)
+    mine = jnp.sum(payload[:, :count].astype(F32), axis=0).astype(BF16)
     blended = pl.pallas_call(
         fold_kernel,
         out_shape=shape((channels, rows, cols), F32),
-        in_specs=[vmem()] * 4,
+        in_specs=[vmem()] * 3,
         out_specs=vmem(),
         compiler_params=params(),
         name="fold",
-    )(inner, third, fourth, den)
+    )(inner, payload, den)
     for order in reversed(orders):
         mine = ordered(mine, exchange(mine, "lat", order), order_bit(lat, order))
     grad_in, grad_mid, grad_out = pl.pallas_call(

time: 74.9 us -> 73.9 us (0.987)
  blocking collectives: 0 us -> 10.2 us
  waiting for transfers between devices: 31 us -> 24 us
  starting transfers between devices: 25.8 us -> 21.3 us
    ppermute x7 -> x4, waiting for transfers between devices: 13.6 us -> 2.91 us  [swap(): return lax.ppermute(value, axis, pairs)]
    all_to_all x0 -> x1, blocking collectives: none -> 10.2 us  [shards(): payload = lax.all_to_all(payload, 'lon', 0, 0)]
    ppermute x6, waiting for transfers between devices: 17.4 us -> 21.1 us  [exchange(): return lax.ppermute(value, axis, pairs)]
    ppermute x6, starting transfers between devices: 18.6 us -> 15 us  [exchange(): return lax.ppermute(value, axis, pairs)]
    ppermute x7 -> x4, starting transfers between devices: 7.12 us -> 6.31 us  [swap(): return lax.ppermute(value, axis, pairs)]
  transfers between devices with their start and end apart: 13 -> 10, of which waited for: 9 -> 7; matrix products, arithmetic and copies ran while one was open for 1% -> 1% of each run, Pallas kernels for 1% -> 1%
where the time goes in v7:
time: 73.9 us; the launch traced here: 73.7 us
  waiting for transfers between devices  24 us (32%)
  starting transfers between devices  21.3 us (29%)
  Pallas kernels  13.9 us (19%)
  blocking collectives  10.2 us (14%)
  local copies, waits for them, and re-layouts  2.28 us (3%)
  between operations  1.68 us (2%)
    ppermute x6, waiting for transfers between devices, exchange(): return lax.ppermute(value, axis, pairs)  21.1 us
    ppermute x6, starting transfers between devices, exchange(): return lax.ppermute(value, axis, pairs)  15 us
    all_to_all x1, blocking collectives, shards(): payload = lax.all_to_all(payload, 'lon', 0, 0)  10.2 us
    pallas_call x1, Pallas kernels, shards(): pl.pallas_call(patch_kernel, out_shape=(shape((half + 2 * edge_rows, LANE...  9.96 us
    ppermute x4, starting transfers between devices, swap(): return lax.ppermute(value, axis, pairs)  6.31 us
    ppermute x4, waiting for transfers between devices, swap(): return lax.ppermute(value, axis, pairs)  2.91 us
    pallas_call x1, Pallas kernels, shards(): pl.pallas_call(pack_kernel, out_shape=(shape((rows, 2 * channels, cols),...  1.72 us
  transfers between devices with their start and end apart: 10, of which 7 were waited for; matrix products, arithmetic and copies ran while one was open for 1% of the time, Pallas kernels for 1%

profile of v7, /device:TPU:0, one launch (start us, length us, event | category | flops | bytes accessed | tf_op | source)
XLA Modules:
  0.0 73.7 jit_solution(2185471356851147507)
XLA Ops:
  1.3 0.7 copy-done.1
  2.0 1.7 %pack.1 = (bf16[8,64,256]{2,1,0:T(8,128)(2,1)S(1)}, bf16[5,64,256]{2,1,0:T(8,128)(2,1)S(1)}, bf16[5,64,256]{2,1,0:T(8,128)(2,1)S(1)}, f32[16,384]{1,0:T(8,128)S(1)}) custom-call(s32[1,1,2,4]{3,2,1,0:T(2,128)S(1)} %bitcast.29, s32[1,1]{1,0:T(1,128)S(6)} %copy.29.counts, bf16[32,8,256]{2,1,0:T(8,128)(2,1)} %fields_in.1, bf16[32,8,256]{2,1,0:T(8,128)(2,1)} %cotangent_in.1, ...), custom_call_target="tpu_custom_call" | custom-call | tf_op jit(solution)/shard_map/pack/pallas_call | solution.py:446
  3.7 0.6 collective-permute-start
  4.3 0.7 collective-permute-start.1
  5.0 0.3 copy.18
  5.3 0.3 copy.17
  5.5 0.6 copy-done.3
  6.3 0.2 edges.1
  6.6 2.6 %collective-permute-start.2 = (bf16[96,128]{1,0:T(8,128)(2,1)S(1)}, bf16[96,128]{1,0:T(8,128)(2,1)S(1)}, u32[]{:S(2)}, u32[]{:S(2)}) collective-permute-start(bf16[96,128]{1,0:T(8,128)(2,1)S(1)} %get-tuple-element.32), channel_id=1, source_target_pairs={{0,1},{1,0},{2,3},{3,2},{4,5},{5,4},{6,7},{7,6},{8,9},{9,8},{10,11... | collective-permute-start | bytes 73736 | tf_op jit(solution)/shard_map/ppermute | solution.py:403
  9.1 2.4 %collective-permute-start.3 = (bf16[96,128]{1,0:T(8,128)(2,1)S(1)}, bf16[96,128]{1,0:T(8,128)(2,1)S(1)}, u32[]{:S(2)}, u32[]{:S(2)}) collective-permute-start(bf16[96,128]{1,0:T(8,128)(2,1)S(1)} %get-tuple-element.32), channel_id=1, source_target_pairs={{1,2},{2,1},{3,0},{0,3},{5,6},{6,5},{7,4},{4,7},{9,10},{10,9},{11,... | collective-permute-start | bytes 73736 | tf_op jit(solution)/shard_map/ppermute | solution.py:403
  11.9 2.9 %collective-permute-done.3.fourth = bf16[96,128]{1,0:T(8,128)(2,1)S(1)} collective-permute-done((bf16[96,128]{1,0:T(8,128)(2,1)S(1)}, bf16[96,128]{1,0:T(8,128)(2,1)S(1)}, u32[]{:S(2)}, u32[]{:S(2)}) %collective-permute-start.3) | collective-permute-done | bytes 24608 | tf_op jit(solution)/shard_map/ppermute | solution.py:403
  14.8 10.0 %patches.1 = (bf16[1472,128]{1,0:T(8,128)(2,1)S(1)}, f32[896,128]{1,0:T(8,128)S(1)}, f32[16,32,384]{2,1,0:T(8,128)S(1)}, f32[8,256]{1,0:T(8,128)S(1)}) custom-call(s32[1,1,2,4]{3,2,1,0:T(2,128)S(1)} %bitcast.30, s32[1,1]{1,0:T(1,128)S(6)} %copy.29.counts, bf16[8,64,256]{2,1,0:T(8,128)(2,1)S(1)} %get-tuple-element.26.center, ...), custom_call_target="tpu_custom_call" | custom-call | tf_op jit(solution)/shard_map/patches/pallas_call | solution.py:497
  24.7 14.1 %collective-permute-start.4 = (bf16[1472,128]{1,0:T(8,128)(2,1)S(1)}, bf16[1472,128]{1,0:T(8,128)(2,1)S(1)}, u32[]{:S(2)}, u32[]{:S(2)}) collective-permute-start(bf16[1472,128]{1,0:T(8,128)(2,1)S(1)} %get-tuple-element.40), channel_id=1, source_target_pairs={{0,4},{4,0},{8,12},{12,8},{16,20},{20,16},{24,28},{28,24},{1,5},{5... | collective-permute-start | bytes 1130504 | tf_op jit(solution)/shard_map/ppermute | solution.py:416
  38.8 1.3 %collective-permute-done.4.first = bf16[1472,128]{1,0:T(8,128)(2,1)S(1)} collective-permute-done((bf16[1472,128]{1,0:T(8,128)(2,1)S(1)}, bf16[1472,128]{1,0:T(8,128)(2,1)S(1)}, u32[]{:S(2)}, u32[]{:S(2)}) %collective-permute-start.4) | collective-permute-done | bytes 376864 | tf_op jit(solution)/shard_map/ppermute | solution.py:416
  40.5 5.5 %collective-permute-done.5 = bf16[736,128]{1,0:T(8,128)(2,1)S(1)} collective-permute-done((bf16[736,128]{1,0:T(8,128)(2,1)S(1)}, bf16[736,128]{1,0:T(8,128)(2,1)S(1)}, u32[]{:S(2)}, u32[]{:S(2)}) %collective-permute-start.5) | collective-permute-done | bytes 188448 | tf_op jit(solution)/shard_map/ppermute | solution.py:416
  46.1 4.9 %collective-permute-done.6 = bf16[512,128]{1,0:T(8,128)(2,1)S(1)} collective-permute-done((bf16[512,128]{1,0:T(8,128)(2,1)S(1)}, bf16[512,128]{1,0:T(8,128)(2,1)S(1)}, u32[]{:S(2)}, u32[]{:S(2)}) %collective-permute-start.6) | collective-permute-done | bytes 131104 | tf_op jit(solution)/shard_map/ppermute | solution.py:416
  51.1 0.2 beside.1
  51.4 10.2 %all_to_all.5.parts = bf16[4,256,128]{2,1,0:T(8,128)(2,1)S(1)} all-to-all(bf16[4,256,128]{2,1,0:T(8,128)(2,1)S(1)} %broadcast_in_dim.2), channel_id=1, replica_groups=mesh['lat'=8,'lon'=4] {'lon'}, dimensions={0} | all-to-all | bytes 524288 | tf_op jit(solution)/shard_map/all_to_all | solution.py:560
  61.7 4.5 %collective-permute-done.7 = bf16[224,128]{1,0:T(8,128)(2,1)S(1)} collective-permute-done((bf16[224,128]{1,0:T(8,128)(2,1)S(1)}, bf16[224,128]{1,0:T(8,128)(2,1)S(1)}, u32[]{:S(2)}, u32[]{:S(2)}) %collective-permute-start.7) | collective-permute-done | bytes 57376 | tf_op jit(solution)/shard_map/ppermute | solution.py:416
  66.2 0.6 collective-permute-start.8
  66.8 4.3 %collective-permute-done.8 = bf16[448,128]{1,0:T(8,128)(2,1)S(1)} collective-permute-done((bf16[448,128]{1,0:T(8,128)(2,1)S(1)}, bf16[448,128]{1,0:T(8,128)(2,1)S(1)}, u32[]{:S(2)}, u32[]{:S(2)}) %collective-permute-start.8) | collective-permute-done | bytes 114720 | tf_op jit(solution)/shard_map/ppermute | solution.py:416
  71.2 0.9 %fold.1 = f32[32,8,256]{2,1,0:T(8,128)} custom-call(f32[8,32,256]{2,1,0:T(8,128)S(1)} %get-tuple-element.42.inner, bf16[4,256,128]{2,1,0:T(8,128)(2,1)S(1)} %all_to_all.5.parts, f32[8,256]{1,0:T(8,128)S(1)} %get-tuple-element.44.den), custom_call_target="tpu_custom_call" | custom-call | tf_op jit(solution)/shard_map/fold/pallas_call | solution.py:562
  72.1 0.6 collective-permute-done.9.other
  72.7 1.0 %split.1 = (f32[9,32,128]{2,1,0:T(8,128)}, f32[9,128,128]{2,1,0:T(8,128)}, f32[9,32,128]{2,1,0:T(8,128)}) custom-call(bf16[896,128]{1,0:T(8,128)(2,1)S(1)} %pad_maximum_fusion.own, bf16[896,128]{1,0:T(8,128)(2,1)S(1)} %collective-permute-done.9.other), custom_call_target="tpu_custom_call" | custom-call | tf_op jit(solution)/shard_map/split/pallas_call | solution.py:572
  (37 shorter events, 1.1 us)
Async XLA Ops:
  1.3 0.7 copy-start.1
  1.3 3.7 %copy-start.2 = (bf16[9,128,128]{2,1,0:T(8,128)(2,1)S(1)}, bf16[9,128,128]{2,1,0:T(8,128)(2,1)}, u32[]{:S(2)}) copy-start(bf16[9,128,128]{2,1,0:T(8,128)(2,1)} %param.11) | copy-start | bytes 884740
  3.7 2.6 %collective-permute-start = (bf16[5,64,256]{2,1,0:T(8,128)(2,1)S(1)}, bf16[5,64,256]{2,1,0:T(8,128)(2,1)S(1)}, u32[]{:S(2)}, u32[]{:S(2)}) collective-permute-start(bf16[5,64,256]{2,1,0:T(8,128)(2,1)S(1)} %get-tuple-element.27), channel_id=1, source_target_pairs={{0,4},{4,0},{8,12},{12,8},{16,20},{20,16},{24,28},{28,24},{1,5},{5... | collective-permute-start | bytes 491528 | tf_op jit(solution)/shard_map/ppermute | solution.py:403
  4.3 2.0 %collective-permute-start.1 = (bf16[5,64,256]{2,1,0:T(8,128)(2,1)S(1)}, bf16[5,64,256]{2,1,0:T(8,128)(2,1)S(1)}, u32[]{:S(2)}, u32[]{:S(2)}) collective-permute-start(bf16[5,64,256]{2,1,0:T(8,128)(2,1)S(1)} %get-tuple-element.28), channel_id=1, source_target_pairs={{4,8},{8,4},{12,16},{16,12},{20,24},{24,20},{5,9},{9,5},{13,17},{1... | collective-permute-start | bytes 491528 | tf_op jit(solution)/shard_map/ppermute | solution.py:403
  5.2 0.9 %copy-start.3 = (bf16[9,32,128]{2,1,0:T(8,128)(2,1)S(1)}, bf16[9,32,128]{2,1,0:T(8,128)(2,1)}, u32[]{:S(2)}) copy-start(bf16[9,32,128]{2,1,0:T(8,128)(2,1)} %param.12) | copy-start | bytes 221188
  6.3 5.3 %copy-start.4 = (bf16[9,128,32]{1,2,0:T(8,128)(2,1)S(1)}, bf16[9,128,32]{1,2,0:T(8,128)(2,1)}, u32[]{:S(2)}) copy-start(bf16[9,128,32]{1,2,0:T(8,128)(2,1)} %param.10) | copy-start | bytes 221188
  6.6 5.3 %collective-permute-start.2 = (bf16[96,128]{1,0:T(8,128)(2,1)S(1)}, bf16[96,128]{1,0:T(8,128)(2,1)S(1)}, u32[]{:S(2)}, u32[]{:S(2)}) collective-permute-start(bf16[96,128]{1,0:T(8,128)(2,1)S(1)} %get-tuple-element.32), channel_id=1, source_target_pairs={{0,1},{1,0},{2,3},{3,2},{4,5},{5,4},{6,7},{7,6},{8,9},{9,8},{10,11... | collective-permute-start | bytes 73736 | tf_op jit(solution)/shard_map/ppermute | solution.py:403
  9.1 5.6 %collective-permute-start.3 = (bf16[96,128]{1,0:T(8,128)(2,1)S(1)}, bf16[96,128]{1,0:T(8,128)(2,1)S(1)}, u32[]{:S(2)}, u32[]{:S(2)}) collective-permute-start(bf16[96,128]{1,0:T(8,128)(2,1)S(1)} %get-tuple-element.32), channel_id=1, source_target_pairs={{1,2},{2,1},{3,0},{0,3},{5,6},{6,5},{7,4},{4,7},{9,10},{10,9},{11,... | collective-permute-start | bytes 73736 | tf_op jit(solution)/shard_map/ppermute | solution.py:403
  11.7 3.0 %copy-start = (s32[4,8,256]{2,1,0:T(8,128)S(1)}, s32[4,8,256]{2,1,0:T(8,128)}, u32[]{:S(2)}) copy-start(s32[4,8,256]{2,1,0:T(8,128)} %weights.1) | copy-start | bytes 98308
  24.7 15.4 %collective-permute-start.4 = (bf16[1472,128]{1,0:T(8,128)(2,1)S(1)}, bf16[1472,128]{1,0:T(8,128)(2,1)S(1)}, u32[]{:S(2)}, u32[]{:S(2)}) collective-permute-start(bf16[1472,128]{1,0:T(8,128)(2,1)S(1)} %get-tuple-element.40), channel_id=1, source_target_pairs={{0,4},{4,0},{8,12},{12,8},{16,20},{20,16},{24,28},{28,24},{1,5},{5... | collective-permute-start | bytes 1130504 | tf_op jit(solution)/shard_map/ppermute | solution.py:416
  40.3 5.6 %collective-permute-start.5 = (bf16[736,128]{1,0:T(8,128)(2,1)S(1)}, bf16[736,128]{1,0:T(8,128)(2,1)S(1)}, u32[]{:S(2)}, u32[]{:S(2)}) collective-permute-start(bf16[736,128]{1,0:T(8,128)(2,1)S(1)} %pad_maximum_fusion.1), channel_id=1, source_target_pairs={{0,8},{4,20},{8,0},{12,28},{16,24},{20,4},{24,16},{28,12},{1,9},{5... | collective-permute-start | bytes 565256 | tf_op jit(solution)/shard_map/ppermute | solution.py:416
  46.0 5.0 %collective-permute-start.6 = (bf16[512,128]{1,0:T(8,128)(2,1)S(1)}, bf16[512,128]{1,0:T(8,128)(2,1)S(1)}, u32[]{:S(2)}, u32[]{:S(2)}) collective-permute-start(bf16[512,128]{1,0:T(8,128)(2,1)S(1)} %pad_maximum_fusion.2), channel_id=1, source_target_pairs={{0,16},{4,12},{8,24},{12,4},{16,0},{20,28},{24,8},{28,20},{1,17},{... | collective-permute-start | bytes 393224 | tf_op jit(solution)/shard_map/ppermute | solution.py:416
  61.6 4.6 %collective-permute-start.7 = (bf16[224,128]{1,0:T(8,128)(2,1)S(1)}, bf16[224,128]{1,0:T(8,128)(2,1)S(1)}, u32[]{:S(2)}, u32[]{:S(2)}) collective-permute-start(bf16[224,128]{1,0:T(8,128)(2,1)S(1)} %slice_reduce_fusion), channel_id=1, source_target_pairs={{0,16},{4,12},{8,24},{12,4},{16,0},{20,28},{24,8},{28,20},{1,17},{... | collective-permute-start | bytes 172040 | tf_op jit(solution)/shard_map/ppermute | solution.py:416
  66.2 4.9 %collective-permute-start.8 = (bf16[448,128]{1,0:T(8,128)(2,1)S(1)}, bf16[448,128]{1,0:T(8,128)(2,1)S(1)}, u32[]{:S(2)}, u32[]{:S(2)}) collective-permute-start(bf16[448,128]{1,0:T(8,128)(2,1)S(1)} %pad_maximum_fusion.3), channel_id=1, source_target_pairs={{0,8},{4,20},{8,0},{12,28},{16,24},{20,4},{24,16},{28,12},{1,9},{5... | collective-permute-start | bytes 344072 | tf_op jit(solution)/shard_map/ppermute | solution.py:416
  71.1 1.6 %collective-permute-start.9 = (bf16[896,128]{1,0:T(8,128)(2,1)S(1)}, bf16[896,128]{1,0:T(8,128)(2,1)S(1)}, u32[]{:S(2)}, u32[]{:S(2)}) collective-permute-start(bf16[896,128]{1,0:T(8,128)(2,1)S(1)} %pad_maximum_fusion.own), channel_id=1, source_target_pairs={{0,4},{4,0},{8,12},{12,8},{16,20},{20,16},{24,28},{28,24},{1,5},{5... | collective-permute-start | bytes 688136 | tf_op jit(solution)/shard_map/ppermute | solution.py:416

commit v8 on v7

--- a/solution.py
+++ b/solution.py
@@ -269,7 +269,7 @@
             spread(z_s, dz2, row, True)
         for row in range(rows):
             at = slice(row * cols, (row + 1) * cols)
-            back = across(dot(w_mid_back[...], stack(z_s.at[width : 2 * width], row, True)), True)
+            back = dot(w_mid_back[...], stack(z_s, row, True))
             dz_s[:, at] = ((dh_s[:, at] + back) * slope_s[:, at]).astype(BF16)
         for row in range(rows):
             result = across(dot(w_out[...], stack(h2_s, row, False)), False)
@@ -472,7 +472,7 @@
     kernel_mid = kernel_mid.reshape(3, 3, width, width)
     kernel_out = kernel_out.reshape(3, 3, channels, width)
     w_mid = jnp.transpose(kernel_mid, (1, 2, 0, 3)).reshape(3 * width, 3 * width)
-    w_mid_back = jnp.transpose(kernel_mid, (1, 3, 0, 2)).reshape(3 * width, 3 * width)
+    w_mid_back = jnp.transpose(kernel_mid, (3, 0, 1, 2)).reshape(width, taps * width)
     w_out = jnp.transpose(kernel_out, (1, 2, 0, 3)).reshape(3 * channels, 3 * width)
     w_out_back = jnp.transpose(kernel_out, (3, 0, 1, 2)).reshape(width, taps * channels)
     first, second, w_in, w_mid, w_mid_back, w_out, w_out_back = lax.optimization_barrier(
@@ -556,8 +556,7 @@
     )(numer, first, held)
     count = mine.shape[0]
     payload = jnp.concatenate([mine.astype(BF16), edges], axis=0)
-    payload = jnp.broadcast_to(payload[None], (lon_size,) + payload.shape)
-    payload = lax.all_to_all(payload, "lon", 0, 0)
+    payload = lax.all_gather(payload, "lon")
     mine = jnp.sum(payload[:, :count].astype(F32), axis=0).astype(BF16)
     blended = pl.pallas_call(
         fold_kernel,

time: 73.9 us -> 77.3 us (1.046)
  blocking collectives: 10.2 us -> 13.9 us
    all_gather x0 -> x1, blocking collectives: none -> 13.9 us  [shards(): payload = lax.all_gather(payload, 'lon')]
    all_to_all x1 -> x0, blocking collectives: 10.2 us -> none  [shards(): payload = lax.all_to_all(payload, 'lon', 0, 0)]
    unnamed x11 -> x12, local copies, waits for them, and re-layouts: 1.31 us -> 1.56 us
where the time goes in v8:
time: 77.3 us; the launch traced here: 77.1 us
  waiting for transfers between devices  24 us (31%)
  starting transfers between devices  20.9 us (27%)
  Pallas kernels  14 us (18%)
  blocking collectives  13.9 us (18%)
  local copies, waits for them, and re-layouts  2.37 us (3%)
  between operations  1.68 us (2%)
    ppermute x6, waiting for transfers between devices, exchange(): return lax.ppermute(value, axis, pairs)  21.3 us
    ppermute x6, starting transfers between devices, exchange(): return lax.ppermute(value, axis, pairs)  14.6 us
    all_gather x1, blocking collectives, shards(): payload = lax.all_gather(payload, 'lon')  13.9 us
    pallas_call x1, Pallas kernels, shards(): pl.pallas_call(patch_kernel, out_shape=(shape((half + 2 * edge_rows, LANE...  10 us
    ppermute x4, starting transfers between devices, swap(): return lax.ppermute(value, axis, pairs)  6.31 us
    ppermute x4, waiting for transfers between devices, swap(): return lax.ppermute(value, axis, pairs)  2.67 us
    pallas_call x1, Pallas kernels, shards(): pl.pallas_call(pack_kernel, out_shape=(shape((rows, 2 * channels, cols),...  1.72 us
    unnamed x12, local copies, waits for them, and re-layouts  1.56 us
  transfers between devices with their start and end apart: 10, of which 7 were waited for; matrix products, arithmetic and copies ran while one was open for 1% of the time, Pallas kernels for 1%

profile of v8, /device:TPU:0, one launch (start us, length us, event | category | flops | bytes accessed | tf_op | source)
XLA Modules:
  0.0 77.1 jit_solution(649141882627219963)
XLA Ops:
  1.3 0.7 copy-done.1
  2.0 1.7 %pack.1 = (bf16[8,64,256]{2,1,0:T(8,128)(2,1)S(1)}, bf16[5,64,256]{2,1,0:T(8,128)(2,1)S(1)}, bf16[5,64,256]{2,1,0:T(8,128)(2,1)S(1)}, f32[16,384]{1,0:T(8,128)S(1)}) custom-call(s32[1,1,2,4]{3,2,1,0:T(2,128)S(1)} %bitcast.34, s32[1,1]{1,0:T(1,128)S(6)} %copy.28.counts, bf16[32,8,256]{2,1,0:T(8,128)(2,1)} %fields_in.1, bf16[32,8,256]{2,1,0:T(8,128)(2,1)} %cotangent_in.1, ...), custom_call_target="tpu_custom_call" | custom-call | tf_op jit(solution)/shard_map/pack/pallas_call | solution.py:446
  3.7 0.6 collective-permute-start
  4.3 0.7 collective-permute-start.1
  5.0 0.3 copy.17
  5.3 0.8 %copy-done.3 = bf16[9,32,128]{2,1,0:T(8,128)(2,1)S(1)} copy-done((bf16[9,32,128]{2,1,0:T(8,128)(2,1)S(1)}, bf16[9,32,128]{2,1,0:T(8,128)(2,1)}, u32[]{:S(2)}) %copy-start.3) | copy-done | bytes 73752
  6.3 0.2 edges.1
  6.5 2.6 %collective-permute-start.2 = (bf16[96,128]{1,0:T(8,128)(2,1)S(1)}, bf16[96,128]{1,0:T(8,128)(2,1)S(1)}, u32[]{:S(2)}, u32[]{:S(2)}) collective-permute-start(bf16[96,128]{1,0:T(8,128)(2,1)S(1)} %get-tuple-element.32), channel_id=1, source_target_pairs={{0,1},{1,0},{2,3},{3,2},{4,5},{5,4},{6,7},{7,6},{8,9},{9,8},{10,11... | collective-permute-start | bytes 73736 | tf_op jit(solution)/shard_map/ppermute | solution.py:403
  9.0 2.5 %collective-permute-start.3 = (bf16[96,128]{1,0:T(8,128)(2,1)S(1)}, bf16[96,128]{1,0:T(8,128)(2,1)S(1)}, u32[]{:S(2)}, u32[]{:S(2)}) collective-permute-start(bf16[96,128]{1,0:T(8,128)(2,1)S(1)} %get-tuple-element.32), channel_id=1, source_target_pairs={{1,2},{2,1},{3,0},{0,3},{5,6},{6,5},{7,4},{4,7},{9,10},{10,9},{11,... | collective-permute-start | bytes 73736 | tf_op jit(solution)/shard_map/ppermute | solution.py:403
  11.6 0.2 copy.20.w_mid_back
  11.9 0.1 copy.21.w_out_back
  12.0 2.7 %collective-permute-done.3.fourth = bf16[96,128]{1,0:T(8,128)(2,1)S(1)} collective-permute-done((bf16[96,128]{1,0:T(8,128)(2,1)S(1)}, bf16[96,128]{1,0:T(8,128)(2,1)S(1)}, u32[]{:S(2)}, u32[]{:S(2)}) %collective-permute-start.3) | collective-permute-done | bytes 24608 | tf_op jit(solution)/shard_map/ppermute | solution.py:403
  14.7 10.0 %patches.1 = (bf16[1472,128]{1,0:T(8,128)(2,1)S(1)}, f32[896,128]{1,0:T(8,128)S(1)}, f32[16,32,384]{2,1,0:T(8,128)S(1)}, f32[8,256]{1,0:T(8,128)S(1)}) custom-call(s32[1,1,2,4]{3,2,1,0:T(2,128)S(1)} %bitcast.35, s32[1,1]{1,0:T(1,128)S(6)} %copy.28.counts, bf16[8,64,256]{2,1,0:T(8,128)(2,1)S(1)} %get-tuple-element.26.center, ...), custom_call_target="tpu_custom_call" | custom-call | tf_op jit(solution)/shard_map/patches/pallas_call | solution.py:497
  24.7 14.2 %collective-permute-start.4 = (bf16[1472,128]{1,0:T(8,128)(2,1)S(1)}, bf16[1472,128]{1,0:T(8,128)(2,1)S(1)}, u32[]{:S(2)}, u32[]{:S(2)}) collective-permute-start(bf16[1472,128]{1,0:T(8,128)(2,1)S(1)} %get-tuple-element.40), channel_id=1, source_target_pairs={{0,4},{4,0},{8,12},{12,8},{16,20},{20,16},{24,28},{28,24},{1,5},{5... | collective-permute-start | bytes 1130504 | tf_op jit(solution)/shard_map/ppermute | solution.py:416
  38.9 1.3 %collective-permute-done.4.first = bf16[1472,128]{1,0:T(8,128)(2,1)S(1)} collective-permute-done((bf16[1472,128]{1,0:T(8,128)(2,1)S(1)}, bf16[1472,128]{1,0:T(8,128)(2,1)S(1)}, u32[]{:S(2)}, u32[]{:S(2)}) %collective-permute-start.4) | collective-permute-done | bytes 376864 | tf_op jit(solution)/shard_map/ppermute | solution.py:416
  40.5 5.5 %collective-permute-done.5 = bf16[736,128]{1,0:T(8,128)(2,1)S(1)} collective-permute-done((bf16[736,128]{1,0:T(8,128)(2,1)S(1)}, bf16[736,128]{1,0:T(8,128)(2,1)S(1)}, u32[]{:S(2)}, u32[]{:S(2)}) %collective-permute-start.5) | collective-permute-done | bytes 188448 | tf_op jit(solution)/shard_map/ppermute | solution.py:416
  46.2 4.9 %collective-permute-done.6 = bf16[512,128]{1,0:T(8,128)(2,1)S(1)} collective-permute-done((bf16[512,128]{1,0:T(8,128)(2,1)S(1)}, bf16[512,128]{1,0:T(8,128)(2,1)S(1)}, u32[]{:S(2)}, u32[]{:S(2)}) %collective-permute-start.6) | collective-permute-done | bytes 131104 | tf_op jit(solution)/shard_map/ppermute | solution.py:416
  51.2 0.2 beside.1
  51.4 13.9 %all-gather = bf16[1024,128]{1,0:T(8,128)(2,1)S(1)} all-gather(bf16[256,128]{1,0:T(8,128)(2,1)S(1)} %pad_maximum_fusion.4), channel_id=2, replica_groups=mesh['lat'=8,'lon'=4] {'lon'}, dimensions={0}, use_global_device_ids=true | all-gather | bytes 327680 | tf_op jit(solution)/shard_map/all_gather | solution.py:559
  65.4 4.2 %collective-permute-done.7 = bf16[224,128]{1,0:T(8,128)(2,1)S(1)} collective-permute-done((bf16[224,128]{1,0:T(8,128)(2,1)S(1)}, bf16[224,128]{1,0:T(8,128)(2,1)S(1)}, u32[]{:S(2)}, u32[]{:S(2)}) %collective-permute-start.7) | collective-permute-done | bytes 57376 | tf_op jit(solution)/shard_map/ppermute | solution.py:416
  69.7 4.8 %collective-permute-done.8 = bf16[448,128]{1,0:T(8,128)(2,1)S(1)} collective-permute-done((bf16[448,128]{1,0:T(8,128)(2,1)S(1)}, bf16[448,128]{1,0:T(8,128)(2,1)S(1)}, u32[]{:S(2)}, u32[]{:S(2)}) %collective-permute-start.8) | collective-permute-done | bytes 114720 | tf_op jit(solution)/shard_map/ppermute | solution.py:416
  74.6 0.9 %fold.1 = f32[32,8,256]{2,1,0:T(8,128)} custom-call(f32[8,32,256]{2,1,0:T(8,128)S(1)} %get-tuple-element.42.inner, bf16[4,256,128]{2,1,0:T(8,128)(2,1)S(1)} %bitcast.31, f32[8,256]{1,0:T(8,128)S(1)} %get-tuple-element.44.den), custom_call_target="tpu_custom_call" | custom-call | tf_op jit(solution)/shard_map/fold/pallas_call | solution.py:561
  75.5 0.6 collective-permute-done.9.other
  76.1 1.0 %split.1 = (f32[9,32,128]{2,1,0:T(8,128)}, f32[9,128,128]{2,1,0:T(8,128)}, f32[9,32,128]{2,1,0:T(8,128)}) custom-call(bf16[896,128]{1,0:T(8,128)(2,1)S(1)} %pad_maximum_fusion.own, bf16[896,128]{1,0:T(8,128)(2,1)S(1)} %collective-permute-done.9.other), custom_call_target="tpu_custom_call" | custom-call | tf_op jit(solution)/shard_map/split/pallas_call | solution.py:571
  (36 shorter events, 0.9 us)
Async XLA Ops:
  1.3 0.7 copy-start.1
  1.3 3.7 %copy-start.2 = (bf16[9,128,128]{2,1,0:T(8,128)(2,1)S(1)}, bf16[9,128,128]{2,1,0:T(8,128)(2,1)}, u32[]{:S(2)}) copy-start(bf16[9,128,128]{2,1,0:T(8,128)(2,1)} %param.11) | copy-start | bytes 884740
  3.7 2.5 %collective-permute-start = (bf16[5,64,256]{2,1,0:T(8,128)(2,1)S(1)}, bf16[5,64,256]{2,1,0:T(8,128)(2,1)S(1)}, u32[]{:S(2)}, u32[]{:S(2)}) collective-permute-start(bf16[5,64,256]{2,1,0:T(8,128)(2,1)S(1)} %get-tuple-element.27), channel_id=1, source_target_pairs={{0,4},{4,0},{8,12},{12,8},{16,20},{20,16},{24,28},{28,24},{1,5},{5... | collective-permute-start | bytes 491528 | tf_op jit(solution)/shard_map/ppermute | solution.py:403
  4.3 1.9 %collective-permute-start.1 = (bf16[5,64,256]{2,1,0:T(8,128)(2,1)S(1)}, bf16[5,64,256]{2,1,0:T(8,128)(2,1)S(1)}, u32[]{:S(2)}, u32[]{:S(2)}) collective-permute-start(bf16[5,64,256]{2,1,0:T(8,128)(2,1)S(1)} %get-tuple-element.28), channel_id=1, source_target_pairs={{4,8},{8,4},{12,16},{16,12},{20,24},{24,20},{5,9},{9,5},{13,17},{1... | collective-permute-start | bytes 491528 | tf_op jit(solution)/shard_map/ppermute | solution.py:403
  5.3 0.9 %copy-start.3 = (bf16[9,32,128]{2,1,0:T(8,128)(2,1)S(1)}, bf16[9,32,128]{2,1,0:T(8,128)(2,1)}, u32[]{:S(2)}) copy-start(bf16[9,32,128]{2,1,0:T(8,128)(2,1)} %param.12) | copy-start | bytes 221188
  6.2 5.3 %copy-start.4 = (bf16[9,128,32]{1,2,0:T(8,128)(2,1)S(1)}, bf16[9,128,32]{1,2,0:T(8,128)(2,1)}, u32[]{:S(2)}) copy-start(bf16[9,128,32]{1,2,0:T(8,128)(2,1)} %param.10) | copy-start | bytes 221188
  6.5 5.5 %collective-permute-start.2 = (bf16[96,128]{1,0:T(8,128)(2,1)S(1)}, bf16[96,128]{1,0:T(8,128)(2,1)S(1)}, u32[]{:S(2)}, u32[]{:S(2)}) collective-permute-start(bf16[96,128]{1,0:T(8,128)(2,1)S(1)} %get-tuple-element.32), channel_id=1, source_target_pairs={{0,1},{1,0},{2,3},{3,2},{4,5},{5,4},{6,7},{7,6},{8,9},{9,8},{10,11... | collective-permute-start | bytes 73736 | tf_op jit(solution)/shard_map/ppermute | solution.py:403
  9.0 5.6 %collective-permute-start.3 = (bf16[96,128]{1,0:T(8,128)(2,1)S(1)}, bf16[96,128]{1,0:T(8,128)(2,1)S(1)}, u32[]{:S(2)}, u32[]{:S(2)}) collective-permute-start(bf16[96,128]{1,0:T(8,128)(2,1)S(1)} %get-tuple-element.32), channel_id=1, source_target_pairs={{1,2},{2,1},{3,0},{0,3},{5,6},{6,5},{7,4},{4,7},{9,10},{10,9},{11,... | collective-permute-start | bytes 73736 | tf_op jit(solution)/shard_map/ppermute | solution.py:403
  11.8 2.8 %copy-start = (s32[4,8,256]{2,1,0:T(8,128)S(1)}, s32[4,8,256]{2,1,0:T(8,128)}, u32[]{:S(2)}) copy-start(s32[4,8,256]{2,1,0:T(8,128)} %weights.1) | copy-start | bytes 98308
  24.7 15.5 %collective-permute-start.4 = (bf16[1472,128]{1,0:T(8,128)(2,1)S(1)}, bf16[1472,128]{1,0:T(8,128)(2,1)S(1)}, u32[]{:S(2)}, u32[]{:S(2)}) collective-permute-start(bf16[1472,128]{1,0:T(8,128)(2,1)S(1)} %get-tuple-element.40), channel_id=1, source_target_pairs={{0,4},{4,0},{8,12},{12,8},{16,20},{20,16},{24,28},{28,24},{1,5},{5... | collective-permute-start | bytes 1130504 | tf_op jit(solution)/shard_map/ppermute | solution.py:416
  40.3 5.6 %collective-permute-start.5 = (bf16[736,128]{1,0:T(8,128)(2,1)S(1)}, bf16[736,128]{1,0:T(8,128)(2,1)S(1)}, u32[]{:S(2)}, u32[]{:S(2)}) collective-permute-start(bf16[736,128]{1,0:T(8,128)(2,1)S(1)} %pad_maximum_fusion.1), channel_id=1, source_target_pairs={{0,8},{4,20},{8,0},{12,28},{16,24},{20,4},{24,16},{28,12},{1,9},{5... | collective-permute-start | bytes 565256 | tf_op jit(solution)/shard_map/ppermute | solution.py:416
  46.1 5.0 %collective-permute-start.6 = (bf16[512,128]{1,0:T(8,128)(2,1)S(1)}, bf16[512,128]{1,0:T(8,128)(2,1)S(1)}, u32[]{:S(2)}, u32[]{:S(2)}) collective-permute-start(bf16[512,128]{1,0:T(8,128)(2,1)S(1)} %pad_maximum_fusion.2), channel_id=1, source_target_pairs={{0,16},{4,12},{8,24},{12,4},{16,0},{20,28},{24,8},{28,20},{1,17},{... | collective-permute-start | bytes 393224 | tf_op jit(solution)/shard_map/ppermute | solution.py:416
  65.3 4.2 %collective-permute-start.7 = (bf16[224,128]{1,0:T(8,128)(2,1)S(1)}, bf16[224,128]{1,0:T(8,128)(2,1)S(1)}, u32[]{:S(2)}, u32[]{:S(2)}) collective-permute-start(bf16[224,128]{1,0:T(8,128)(2,1)S(1)} %slice_reduce_fusion), channel_id=1, source_target_pairs={{0,16},{4,12},{8,24},{12,4},{16,0},{20,28},{24,8},{28,20},{1,17},{... | collective-permute-start | bytes 172040 | tf_op jit(solution)/shard_map/ppermute | solution.py:416
  69.6 4.9 %collective-permute-start.8 = (bf16[448,128]{1,0:T(8,128)(2,1)S(1)}, bf16[448,128]{1,0:T(8,128)(2,1)S(1)}, u32[]{:S(2)}, u32[]{:S(2)}) collective-permute-start(bf16[448,128]{1,0:T(8,128)(2,1)S(1)} %pad_maximum_fusion.3), channel_id=1, source_target_pairs={{0,8},{4,20},{8,0},{12,28},{16,24},{20,4},{24,16},{28,12},{1,9},{5... | collective-permute-start | bytes 344072 | tf_op jit(solution)/shard_map/ppermute | solution.py:416
  74.5 1.6 %collective-permute-start.9 = (bf16[896,128]{1,0:T(8,128)(2,1)S(1)}, bf16[896,128]{1,0:T(8,128)(2,1)S(1)}, u32[]{:S(2)}, u32[]{:S(2)}) collective-permute-start(bf16[896,128]{1,0:T(8,128)(2,1)S(1)} %pad_maximum_fusion.own), channel_id=1, source_target_pairs={{0,4},{4,0},{8,12},{12,8},{16,20},{20,16},{24,28},{28,24},{1,5},{5... | collective-permute-start | bytes 688136 | tf_op jit(solution)/shard_map/ppermute | solution.py:416

commit v9 on v8

--- a/solution.py
+++ b/solution.py
@@ -41,12 +41,12 @@
 
 
 def pack_kernel(
-    anchors, counts, fields_in, cotangent_in, weights_in, center, first_out, second_out, canvas,
-    fields, cotangent, weights, spread, sems,
+    counts, anchors_in, fields_in, cotangent_in, weights_in, center, first_out, second_out, canvas,
+    fields, cotangent, weights, anchors, spread, sems,
 ):
     copies = []
     for index, (source, target) in enumerate(
-        ((weights_in, weights), (fields_in, fields), (cotangent_in, cotangent))
+        ((weights_in, weights), (fields_in, fields), (cotangent_in, cotangent), (anchors_in, anchors))
     ):
         copy = pltpu.make_async_copy(source, target, sems.at[index])
         copy.start()
@@ -56,6 +56,7 @@
     odd = lax.rem(lax.axis_index("lat"), 2) == 1
     spread[...] = jnp.zeros_like(spread)
     copies[0].wait()
+    copies[3].wait()
     for slot in range(SLOTS):
 
         @pl.when(slot < counts[0, 0])
@@ -141,7 +142,7 @@
     anchors, counts, center, first, second, third, fourth, total_in, weights,
     w_in, w_mid, w_mid_back, w_out, w_out_back,
     send, keep, numer, den_out,
-    grads, window, x_s, d_s, h_s, z_s, h2_s, slope_s, dh_s, dz_s,
+    grads, window, *sets,
 ):
     rows = center.shape[0]
     channels = center.shape[1] // 2
@@ -191,7 +192,8 @@
 
     numer[...] = jnp.zeros_like(numer)
     grads[...] = jnp.zeros_like(grads)
-    for ref in (x_s, d_s, h_s, z_s, h2_s):
+    sets = (sets[: len(sets) // 2], sets[len(sets) // 2 :])
+    for ref in sets[0][:5] + sets[1][:5]:
         ref[:, 0:cols] = jnp.zeros((ref.shape[0], cols), BF16)
         ref[:, cols + full : 2 * cols + full] = jnp.zeros((ref.shape[0], cols), BF16)
 
@@ -239,24 +241,30 @@
         starts = [(2 - tap if flip else tap) * cols for tap in range(3)]
         return jnp.concatenate([ref[:, start : start + full] for start in starts], axis=0)
 
-    def one_patch(slot, carry):
+    def weights_of(slot):
+        return weights[slot].astype(F32) * (slot < counts[0, 0]).astype(F32)
+
+    def first_part(slot, x_s, d_s, h_s, z_s, h2_s, slope_s, dh_s, dz_s):
         row0 = anchors[0, 0, 0, slot]
         col0 = anchors[0, 0, 1, slot]
-        patch_weights = weights[slot].astype(F32)
+        patch_weights = weights_of(slot)
         back_shift = lax.rem(wide + MARGIN - col0, wide)
-        for row in range(rows):
+
+        def cut(row):
             line = roll(window[row0 + row], back_shift, 1)[:, :cols]
             spread(x_s, line[:channels].astype(BF16), row, False)
             grad = line[channels:] * patch_weights[row : row + 1]
             spread(d_s, grad.astype(BF16), row, True)
-        for row in range(rows):
+
+        def conv_in(row):
             at = slice(row * cols, (row + 1) * cols)
             z1 = dot(w_in[...], stack(x_s, row, False))
             sig = 0.5 * jnp.tanh(0.5 * z1) + 0.5
             h1 = z1 * sig
             slope_s[:, at] = sig + h1 * (1.0 - sig)
             h_s[:, (row + 1) * cols : (row + 2) * cols] = h1.astype(BF16)
-        for row in range(rows):
+
+        def conv_mid(row):
             at = slice(row * cols, (row + 1) * cols)
             ahead = slice((row + 1) * cols, (row + 2) * cols)
             dh2 = dot(w_out_back[...], stack(d_s, row, True))
@@ -267,30 +275,57 @@
             dz2 = (dh2 * (sig + added * (1.0 - sig))).astype(BF16)
             dh_s[:, at] = dh2
             spread(z_s, dz2, row, True)
-        for row in range(rows):
+
+        return [functools.partial(step, row) for step in (cut, conv_in, conv_mid) for row in range(rows)]
+
+    def second_part(slot, x_s, d_s, h_s, z_s, h2_s, slope_s, dh_s, dz_s):
+        row0 = anchors[0, 0, 0, slot]
+        col0 = anchors[0, 0, 1, slot]
+        patch_weights = weights_of(slot)
+        inside = slice(cols, cols + full)
+        small = 9 * channels
+
+        def conv_back(row):
             at = slice(row * cols, (row + 1) * cols)
             back = dot(w_mid_back[...], stack(z_s, row, True))
             dz_s[:, at] = ((dh_s[:, at] + back) * slope_s[:, at]).astype(BF16)
-        for row in range(rows):
+
+        def conv_out(row):
             result = across(dot(w_out[...], stack(h2_s, row, False)), False)
             result = result * patch_weights[row : row + 1]
             result = jnp.concatenate([result, jnp.zeros((channels, LANES), F32)], axis=1)
             numer[row0 + row] += roll(result, lax.rem(col0 + (wide - MARGIN), wide), 1)
-        inside = slice(cols, cols + full)
-        small = 9 * channels
-        part = dot_lanes(z_s[:, inside], all_rows(h_s, False))
-        for tap in range(3):
-            for tap_col in range(3):
-                start = small + (3 * tap + tap_col) * width
-                grads[start : start + width] += part[
-                    tap_col * width : (tap_col + 1) * width, tap * width : (tap + 1) * width
-                ]
-        grads[0:small] += dot_lanes(all_rows(x_s, False), dz_s[...])
-        start = small + 9 * width
-        grads[start : start + small] += dot_lanes(all_rows(d_s, True), h2_s[:, inside])
-        return carry
-
-    lax.fori_loop(0, counts[0, 0], one_patch, 0)
+
+        def grad_mid():
+            part = dot_lanes(z_s[:, inside], all_rows(h_s, False))
+            for tap in range(3):
+                for tap_col in range(3):
+                    start = small + (3 * tap + tap_col) * width
+                    grads[start : start + width] += part[
+                        tap_col * width : (tap_col + 1) * width, tap * width : (tap + 1) * width
+                    ]
+
+        def grad_out():
+            start = small + 9 * width
+            grads[start : start + small] += dot_lanes(all_rows(d_s, True), h2_s[:, inside])
+
+        def grad_in():
+            grads[0:small] += dot_lanes(all_rows(x_s, False), dz_s[...])
+
+        backs = [functools.partial(conv_back, row) for row in range(rows)]
+        outs = [functools.partial(conv_out, row) for row in range(rows)]
+        return [grad_mid, grad_out] + backs + [grad_in] + outs
+
+    def merged(left, right):
+        left = [((at + 0.5) / len(left), step) for at, step in enumerate(left)]
+        right = [((at + 0.5) / len(right), step) for at, step in enumerate(right)]
+        for _, step in sorted(left + right, key=lambda pair: pair[0]):
+            step()
+
+    for slot in range(SLOTS + 1):
+        ahead = first_part(slot, *sets[slot % 2]) if slot < SLOTS else []
+        behind = second_part(slot - 1, *sets[(slot - 1) % 2]) if slot > 0 else []
+        merged(behind, ahead)
 
     half = grads.shape[0] // 2
     odd_index = lax.rem(lax.axis_index("lat"), 2)
@@ -451,21 +486,24 @@
             shape((MARGIN + 1, 2 * channels, cols), BF16),
             shape((height, wide), F32),
         ),
-        in_specs=[smem(), smem()] + [pl.BlockSpec(memory_space=pltpu.HBM)] * 3,
+        in_specs=[smem()] + [pl.BlockSpec(memory_space=pltpu.HBM)] * 4,
         out_specs=(vmem(),) * 4,
         scratch_shapes=[
             pltpu.VMEM(fields.shape, BF16),
             pltpu.VMEM(cotangent.shape, BF16),
             pltpu.VMEM(blend_weights.shape, jnp.int32),
+            pltpu.SMEM(patch_anchors.shape, jnp.int32),
             pltpu.VMEM((height, wide), F32),
-            pltpu.SemaphoreType.DMA((3,)),
+            pltpu.SemaphoreType.DMA((4,)),
         ],
         compiler_params=params(),
         name="pack",
     )(
-        patch_anchors,
         tile_counts,
-        *(pltpu.with_memory_space_constraint(value, pltpu.HBM) for value in (fields, cotangent, blend_weights)),
+        *(
+            pltpu.with_memory_space_constraint(value, pltpu.HBM)
+            for value in (patch_anchors, fields, cotangent, blend_weights)
+        ),
     )
     first, second = swap_lat(first, second)
     w_in = jnp.transpose(kernel_in, (1, 0, 2)).reshape(width, taps * channels)
@@ -507,6 +545,9 @@
         scratch_shapes=[
             pltpu.VMEM((length, LANES), F32),
             pltpu.VMEM((height, 2 * channels, wide), F32),
+        ]
+        + 2
+        * [
             pltpu.VMEM((3 * channels, padded), BF16),
             pltpu.VMEM((3 * channels, padded), BF16),
             pltpu.VMEM((width, padded), BF16),
@@ -556,7 +597,8 @@
     )(numer, first, held)
     count = mine.shape[0]
     payload = jnp.concatenate([mine.astype(BF16), edges], axis=0)
-    payload = lax.all_gather(payload, "lon")
+    payload = jnp.broadcast_to(payload[None], (lon_size,) + payload.shape)
+    payload = lax.all_to_all(payload, "lon", 0, 0)
     mine = jnp.sum(payload[:, :count].astype(F32), axis=0).astype(BF16)
     blended = pl.pallas_call(
         fold_kernel,

time: 77.3 us -> 73.7 us (0.953)
  Pallas kernels: 14 us -> 20.9 us
  waiting for transfers between devices: 24 us -> 18.1 us
  blocking collectives: 13.9 us -> 10.8 us
  starting transfers between devices: 20.9 us -> 20.1 us
    all_gather x1 -> x0, blocking collectives: 13.9 us -> none  [shards(): payload = lax.all_gather(payload, 'lon')]
    all_to_all x0 -> x1, blocking collectives: none -> 10.8 us  [shards(): payload = lax.all_to_all(payload, 'lon', 0, 0)]
    pallas_call x1, Pallas kernels: 10 us -> 17.4 us  [shards(): pl.pallas_call(patch_kernel, out_shape=(shape((half + 2 * edge_rows, LANE...]
    ppermute x6, waiting for transfers between devices: 21.3 us -> 15.6 us  [exchange(): return lax.ppermute(value, axis, pairs)]
    ppermute x6, starting transfers between devices: 14.6 us -> 13.7 us  [exchange(): return lax.ppermute(value, axis, pairs)]
where the time goes in v9:
time: 73.7 us; the launch traced here: 73.5 us
  Pallas kernels  20.9 us (28%)
  starting transfers between devices  20.1 us (27%)
  waiting for transfers between devices  18.1 us (25%)
  blocking collectives  10.8 us (15%)
  local copies, waits for them, and re-layouts  1.75 us (2%)
  between operations  1.58 us (2%)
    pallas_call x1, Pallas kernels, shards(): pl.pallas_call(patch_kernel, out_shape=(shape((half + 2 * edge_rows, LANE...  17.4 us
    ppermute x6, waiting for transfers between devices, exchange(): return lax.ppermute(value, axis, pairs)  15.6 us
    ppermute x6, starting transfers between devices, exchange(): return lax.ppermute(value, axis, pairs)  13.7 us
    all_to_all x1, blocking collectives, shards(): payload = lax.all_to_all(payload, 'lon', 0, 0)  10.8 us
    ppermute x4, starting transfers between devices, swap(): return lax.ppermute(value, axis, pairs)  6.4 us
    ppermute x4, waiting for transfers between devices, swap(): return lax.ppermute(value, axis, pairs)  2.55 us
  transfers between devices with their start and end apart: 10, of which 7 were waited for; matrix products, arithmetic and copies ran while one was open for 1% of the time, Pallas kernels for 1%

profile of v9, /device:TPU:0, one launch (start us, length us, event | category | flops | bytes accessed | tf_op | source)
XLA Modules:
  0.0 73.5 jit_solution(1766744890053941456)
XLA Ops:
  1.3 1.2 %pack.1 = (bf16[8,64,256]{2,1,0:T(8,128)(2,1)S(1)}, bf16[5,64,256]{2,1,0:T(8,128)(2,1)S(1)}, bf16[5,64,256]{2,1,0:T(8,128)(2,1)S(1)}, f32[16,384]{1,0:T(8,128)S(1)}) custom-call(s32[1,1]{1,0:T(1,128)S(6)} %copy.28.counts, s32[1,1,2,4]{3,2,1,0:T(2,128)} %bitcast.31, bf16[32,8,256]{2,1,0:T(8,128)(2,1)} %fields_in.1, bf16[32,8,256]{2,1,0:T(8,128)(2,1)} %cotangent_in.1, ...), custom_call_target="tpu_custom_call" | custom-call | tf_op jit(solution)/shard_map/pack/pallas_call | solution.py:481
  2.5 0.7 collective-permute-start
  3.2 0.7 collective-permute-start.1
  3.9 0.3 copy.17
  4.2 0.8 %copy-done.3 = bf16[9,32,128]{2,1,0:T(8,128)(2,1)S(1)} copy-done((bf16[9,32,128]{2,1,0:T(8,128)(2,1)S(1)}, bf16[9,32,128]{2,1,0:T(8,128)(2,1)}, u32[]{:S(2)}) %copy-start.3) | copy-done | bytes 73752
  5.2 0.2 edges.1
  5.4 2.5 %collective-permute-start.2 = (bf16[96,128]{1,0:T(8,128)(2,1)S(1)}, bf16[96,128]{1,0:T(8,128)(2,1)S(1)}, u32[]{:S(2)}, u32[]{:S(2)}) collective-permute-start(bf16[96,128]{1,0:T(8,128)(2,1)S(1)} %get-tuple-element.32), channel_id=1, source_target_pairs={{0,1},{1,0},{2,3},{3,2},{4,5},{5,4},{6,7},{7,6},{8,9},{9,8},{10,11... | collective-permute-start | bytes 73736 | tf_op jit(solution)/shard_map/ppermute | solution.py:438
  7.9 2.6 %collective-permute-start.3 = (bf16[96,128]{1,0:T(8,128)(2,1)S(1)}, bf16[96,128]{1,0:T(8,128)(2,1)S(1)}, u32[]{:S(2)}, u32[]{:S(2)}) collective-permute-start(bf16[96,128]{1,0:T(8,128)(2,1)S(1)} %get-tuple-element.32), channel_id=1, source_target_pairs={{1,2},{2,1},{3,0},{0,3},{5,6},{6,5},{7,4},{4,7},{9,10},{10,9},{11,... | collective-permute-start | bytes 73736 | tf_op jit(solution)/shard_map/ppermute | solution.py:438
  10.9 2.5 %collective-permute-done.3.fourth = bf16[96,128]{1,0:T(8,128)(2,1)S(1)} collective-permute-done((bf16[96,128]{1,0:T(8,128)(2,1)S(1)}, bf16[96,128]{1,0:T(8,128)(2,1)S(1)}, u32[]{:S(2)}, u32[]{:S(2)}) %collective-permute-start.3) | collective-permute-done | bytes 24608 | tf_op jit(solution)/shard_map/ppermute | solution.py:438
  13.5 17.4 %patches.1 = (bf16[1472,128]{1,0:T(8,128)(2,1)S(1)}, f32[896,128]{1,0:T(8,128)S(1)}, f32[16,32,384]{2,1,0:T(8,128)S(1)}, f32[8,256]{1,0:T(8,128)S(1)}) custom-call(s32[1,1,2,4]{3,2,1,0:T(2,128)S(1)} %bitcast.32, s32[1,1]{1,0:T(1,128)S(6)} %copy.28.counts, bf16[8,64,256]{2,1,0:T(8,128)(2,1)S(1)} %get-tuple-element.26.center, ...), custom_call_target="tpu_custom_call" | custom-call | tf_op jit(solution)/shard_map/patches/pallas_call | solution.py:535
  30.9 5.2 %collective-permute-start.4 = (bf16[1472,128]{1,0:T(8,128)(2,1)S(1)}, bf16[1472,128]{1,0:T(8,128)(2,1)S(1)}, u32[]{:S(2)}, u32[]{:S(2)}) collective-permute-start(bf16[1472,128]{1,0:T(8,128)(2,1)S(1)} %get-tuple-element.40), channel_id=1, source_target_pairs={{0,4},{4,0},{8,12},{12,8},{16,20},{20,16},{24,28},{28,24},{1,5},{5... | collective-permute-start | bytes 1130504 | tf_op jit(solution)/shard_map/ppermute | solution.py:451
  36.2 1.3 %collective-permute-done.4.first = bf16[1472,128]{1,0:T(8,128)(2,1)S(1)} collective-permute-done((bf16[1472,128]{1,0:T(8,128)(2,1)S(1)}, bf16[1472,128]{1,0:T(8,128)(2,1)S(1)}, u32[]{:S(2)}, u32[]{:S(2)}) %collective-permute-start.4) | collective-permute-done | bytes 376864 | tf_op jit(solution)/shard_map/ppermute | solution.py:451
  37.6 2.2 %collective-permute-start.5 = (bf16[736,128]{1,0:T(8,128)(2,1)S(1)}, bf16[736,128]{1,0:T(8,128)(2,1)S(1)}, u32[]{:S(2)}, u32[]{:S(2)}) collective-permute-start(bf16[736,128]{1,0:T(8,128)(2,1)S(1)} %pad_maximum_fusion.1), channel_id=1, source_target_pairs={{0,8},{4,20},{8,0},{12,28},{16,24},{20,4},{24,16},{28,12},{1,9},{5... | collective-permute-start | bytes 565256 | tf_op jit(solution)/shard_map/ppermute | solution.py:451
  39.8 3.6 %collective-permute-done.5 = bf16[736,128]{1,0:T(8,128)(2,1)S(1)} collective-permute-done((bf16[736,128]{1,0:T(8,128)(2,1)S(1)}, bf16[736,128]{1,0:T(8,128)(2,1)S(1)}, u32[]{:S(2)}, u32[]{:S(2)}) %collective-permute-start.5) | collective-permute-done | bytes 188448 | tf_op jit(solution)/shard_map/ppermute | solution.py:451
  43.5 3.7 %collective-permute-start.6 = (bf16[512,128]{1,0:T(8,128)(2,1)S(1)}, bf16[512,128]{1,0:T(8,128)(2,1)S(1)}, u32[]{:S(2)}, u32[]{:S(2)}) collective-permute-start(bf16[512,128]{1,0:T(8,128)(2,1)S(1)} %pad_maximum_fusion.2), channel_id=1, source_target_pairs={{0,16},{4,12},{8,24},{12,4},{16,0},{20,28},{24,8},{28,20},{1,17},{... | collective-permute-start | bytes 393224 | tf_op jit(solution)/shard_map/ppermute | solution.py:451
  47.2 2.9 %collective-permute-done.6 = bf16[512,128]{1,0:T(8,128)(2,1)S(1)} collective-permute-done((bf16[512,128]{1,0:T(8,128)(2,1)S(1)}, bf16[512,128]{1,0:T(8,128)(2,1)S(1)}, u32[]{:S(2)}, u32[]{:S(2)}) %collective-permute-start.6) | collective-permute-done | bytes 131104 | tf_op jit(solution)/shard_map/ppermute | solution.py:451
  50.4 10.8 %all_to_all.5.parts = bf16[4,256,128]{2,1,0:T(8,128)(2,1)S(1)} all-to-all(bf16[4,256,128]{2,1,0:T(8,128)(2,1)S(1)} %broadcast_in_dim.2), channel_id=1, replica_groups=mesh['lat'=8,'lon'=4] {'lon'}, dimensions={0} | all-to-all | bytes 524288 | tf_op jit(solution)/shard_map/all_to_all | solution.py:601
  61.2 2.1 %collective-permute-start.7 = (bf16[224,128]{1,0:T(8,128)(2,1)S(1)}, bf16[224,128]{1,0:T(8,128)(2,1)S(1)}, u32[]{:S(2)}, u32[]{:S(2)}) collective-permute-start(bf16[224,128]{1,0:T(8,128)(2,1)S(1)} %slice_reduce_fusion), channel_id=1, source_target_pairs={{0,16},{4,12},{8,24},{12,4},{16,0},{20,28},{24,8},{28,20},{1,17},{... | collective-permute-start | bytes 172040 | tf_op jit(solution)/shard_map/ppermute | solution.py:451
  63.3 2.7 %collective-permute-done.7 = bf16[224,128]{1,0:T(8,128)(2,1)S(1)} collective-permute-done((bf16[224,128]{1,0:T(8,128)(2,1)S(1)}, bf16[224,128]{1,0:T(8,128)(2,1)S(1)}, u32[]{:S(2)}, u32[]{:S(2)}) %collective-permute-start.7) | collective-permute-done | bytes 57376 | tf_op jit(solution)/shard_map/ppermute | solution.py:451
  66.1 0.4 collective-permute-start.8
  66.5 4.4 %collective-permute-done.8 = bf16[448,128]{1,0:T(8,128)(2,1)S(1)} collective-permute-done((bf16[448,128]{1,0:T(8,128)(2,1)S(1)}, bf16[448,128]{1,0:T(8,128)(2,1)S(1)}, u32[]{:S(2)}, u32[]{:S(2)}) %collective-permute-start.8) | collective-permute-done | bytes 114720 | tf_op jit(solution)/shard_map/ppermute | solution.py:451
  71.1 0.9 %fold.1 = f32[32,8,256]{2,1,0:T(8,128)} custom-call(f32[8,32,256]{2,1,0:T(8,128)S(1)} %get-tuple-element.42.inner, bf16[4,256,128]{2,1,0:T(8,128)(2,1)S(1)} %all_to_all.5.parts, f32[8,256]{1,0:T(8,128)S(1)} %get-tuple-element.44.den), custom_call_target="tpu_custom_call" | custom-call | tf_op jit(solution)/shard_map/fold/pallas_call | solution.py:603
  71.9 0.6 collective-permute-done.9.other
  72.6 1.0 %split.1 = (f32[9,32,128]{2,1,0:T(8,128)}, f32[9,128,128]{2,1,0:T(8,128)}, f32[9,32,128]{2,1,0:T(8,128)}) custom-call(bf16[896,128]{1,0:T(8,128)(2,1)S(1)} %pad_maximum_fusion.own, bf16[896,128]{1,0:T(8,128)(2,1)S(1)} %collective-permute-done.9.other), custom_call_target="tpu_custom_call" | custom-call | tf_op jit(solution)/shard_map/split/pallas_call | solution.py:613
  (37 shorter events, 1.2 us)
Async XLA Ops:
  0.6 3.3 %copy-start.2 = (bf16[9,128,128]{2,1,0:T(8,128)(2,1)S(1)}, bf16[9,128,128]{2,1,0:T(8,128)(2,1)}, u32[]{:S(2)}) copy-start(bf16[9,128,128]{2,1,0:T(8,128)(2,1)} %param.11) | copy-start | bytes 884740
  2.5 2.6 %collective-permute-start = (bf16[5,64,256]{2,1,0:T(8,128)(2,1)S(1)}, bf16[5,64,256]{2,1,0:T(8,128)(2,1)S(1)}, u32[]{:S(2)}, u32[]{:S(2)}) collective-permute-start(bf16[5,64,256]{2,1,0:T(8,128)(2,1)S(1)} %get-tuple-element.27), channel_id=1, source_target_pairs={{0,4},{4,0},{8,12},{12,8},{16,20},{20,16},{24,28},{28,24},{1,5},{5... | collective-permute-start | bytes 491528 | tf_op jit(solution)/shard_map/ppermute | solution.py:438
  3.2 1.9 %collective-permute-start.1 = (bf16[5,64,256]{2,1,0:T(8,128)(2,1)S(1)}, bf16[5,64,256]{2,1,0:T(8,128)(2,1)S(1)}, u32[]{:S(2)}, u32[]{:S(2)}) collective-permute-start(bf16[5,64,256]{2,1,0:T(8,128)(2,1)S(1)} %get-tuple-element.28), channel_id=1, source_target_pairs={{4,8},{8,4},{12,16},{16,12},{20,24},{24,20},{5,9},{9,5},{13,17},{1... | collective-permute-start | bytes 491528 | tf_op jit(solution)/shard_map/ppermute | solution.py:438
  4.2 0.9 %copy-start.3 = (bf16[9,32,128]{2,1,0:T(8,128)(2,1)S(1)}, bf16[9,32,128]{2,1,0:T(8,128)(2,1)}, u32[]{:S(2)}) copy-start(bf16[9,32,128]{2,1,0:T(8,128)(2,1)} %param.12) | copy-start | bytes 221188
  5.2 5.3 %copy-start.4 = (bf16[9,128,32]{1,2,0:T(8,128)(2,1)S(1)}, bf16[9,128,32]{1,2,0:T(8,128)(2,1)}, u32[]{:S(2)}) copy-start(bf16[9,128,32]{1,2,0:T(8,128)(2,1)} %param.10) | copy-start | bytes 221188
  5.4 5.5 %collective-permute-start.2 = (bf16[96,128]{1,0:T(8,128)(2,1)S(1)}, bf16[96,128]{1,0:T(8,128)(2,1)S(1)}, u32[]{:S(2)}, u32[]{:S(2)}) collective-permute-start(bf16[96,128]{1,0:T(8,128)(2,1)S(1)} %get-tuple-element.32), channel_id=1, source_target_pairs={{0,1},{1,0},{2,3},{3,2},{4,5},{5,4},{6,7},{7,6},{8,9},{9,8},{10,11... | collective-permute-start | bytes 73736 | tf_op jit(solution)/shard_map/ppermute | solution.py:438
  7.9 5.6 %collective-permute-start.3 = (bf16[96,128]{1,0:T(8,128)(2,1)S(1)}, bf16[96,128]{1,0:T(8,128)(2,1)S(1)}, u32[]{:S(2)}, u32[]{:S(2)}) collective-permute-start(bf16[96,128]{1,0:T(8,128)(2,1)S(1)} %get-tuple-element.32), channel_id=1, source_target_pairs={{1,2},{2,1},{3,0},{0,3},{5,6},{6,5},{7,4},{4,7},{9,10},{10,9},{11,... | collective-permute-start | bytes 73736 | tf_op jit(solution)/shard_map/ppermute | solution.py:438
  10.8 2.7 %copy-start = (s32[4,8,256]{2,1,0:T(8,128)S(1)}, s32[4,8,256]{2,1,0:T(8,128)}, u32[]{:S(2)}) copy-start(s32[4,8,256]{2,1,0:T(8,128)} %weights.1) | copy-start | bytes 98308
  10.9 2.6 %copy-start.1 = (s32[1,1,4,2]{2,3,1,0:T(2,128)S(1)}, s32[1,1,4,2]{2,3,1,0:T(2,128)}, u32[]{:S(2)}) copy-start(s32[1,1,4,2]{2,3,1,0:T(2,128)} %param.13) | copy-start | bytes 100
  30.9 6.6 %collective-permute-start.4 = (bf16[1472,128]{1,0:T(8,128)(2,1)S(1)}, bf16[1472,128]{1,0:T(8,128)(2,1)S(1)}, u32[]{:S(2)}, u32[]{:S(2)}) collective-permute-start(bf16[1472,128]{1,0:T(8,128)(2,1)S(1)} %get-tuple-element.40), channel_id=1, source_target_pairs={{0,4},{4,0},{8,12},{12,8},{16,20},{20,16},{24,28},{28,24},{1,5},{5... | collective-permute-start | bytes 1130504 | tf_op jit(solution)/shard_map/ppermute | solution.py:451
  37.6 5.7 %collective-permute-start.5 = (bf16[736,128]{1,0:T(8,128)(2,1)S(1)}, bf16[736,128]{1,0:T(8,128)(2,1)S(1)}, u32[]{:S(2)}, u32[]{:S(2)}) collective-permute-start(bf16[736,128]{1,0:T(8,128)(2,1)S(1)} %pad_maximum_fusion.1), channel_id=1, source_target_pairs={{0,8},{4,20},{8,0},{12,28},{16,24},{20,4},{24,16},{28,12},{1,9},{5... | collective-permute-start | bytes 565256 | tf_op jit(solution)/shard_map/ppermute | solution.py:451
  43.5 6.7 %collective-permute-start.6 = (bf16[512,128]{1,0:T(8,128)(2,1)S(1)}, bf16[512,128]{1,0:T(8,128)(2,1)S(1)}, u32[]{:S(2)}, u32[]{:S(2)}) collective-permute-start(bf16[512,128]{1,0:T(8,128)(2,1)S(1)} %pad_maximum_fusion.2), channel_id=1, source_target_pairs={{0,16},{4,12},{8,24},{12,4},{16,0},{20,28},{24,8},{28,20},{1,17},{... | collective-permute-start | bytes 393224 | tf_op jit(solution)/shard_map/ppermute | solution.py:451
  61.2 4.8 %collective-permute-start.7 = (bf16[224,128]{1,0:T(8,128)(2,1)S(1)}, bf16[224,128]{1,0:T(8,128)(2,1)S(1)}, u32[]{:S(2)}, u32[]{:S(2)}) collective-permute-start(bf16[224,128]{1,0:T(8,128)(2,1)S(1)} %slice_reduce_fusion), channel_id=1, source_target_pairs={{0,16},{4,12},{8,24},{12,4},{16,0},{20,28},{24,8},{28,20},{1,17},{... | collective-permute-start | bytes 172040 | tf_op jit(solution)/shard_map/ppermute | solution.py:451
  66.1 4.9 %collective-permute-start.8 = (bf16[448,128]{1,0:T(8,128)(2,1)S(1)}, bf16[448,128]{1,0:T(8,128)(2,1)S(1)}, u32[]{:S(2)}, u32[]{:S(2)}) collective-permute-start(bf16[448,128]{1,0:T(8,128)(2,1)S(1)} %pad_maximum_fusion.3), channel_id=1, source_target_pairs={{0,8},{4,20},{8,0},{12,28},{16,24},{20,4},{24,16},{28,12},{1,9},{5... | collective-permute-start | bytes 344072 | tf_op jit(solution)/shard_map/ppermute | solution.py:451
  71.0 1.6 %collective-permute-start.9 = (bf16[896,128]{1,0:T(8,128)(2,1)S(1)}, bf16[896,128]{1,0:T(8,128)(2,1)S(1)}, u32[]{:S(2)}, u32[]{:S(2)}) collective-permute-start(bf16[896,128]{1,0:T(8,128)(2,1)S(1)} %pad_maximum_fusion.own), channel_id=1, source_target_pairs={{0,4},{4,0},{8,12},{12,8},{16,20},{20,16},{24,28},{28,24},{1,5},{5... | collective-permute-start | bytes 688136 | tf_op jit(solution)/shard_map/ppermute | solution.py:451

commit v10 on v9

--- a/solution.py
+++ b/solution.py
@@ -142,13 +142,13 @@
     anchors, counts, center, first, second, third, fourth, total_in, weights,
     w_in, w_mid, w_mid_back, w_out, w_out_back,
     send, keep, numer, den_out,
-    grads, window, *sets,
+    grads, window, y_s, *sets,
 ):
     rows = center.shape[0]
     channels = center.shape[1] // 2
     cols = center.shape[2]
     wide = cols + LANES
-    width = w_in.shape[0]
+    width = w_mid.shape[0] // 3
     full = rows * cols
     height = rows + 2 * MARGIN
     lanes = lane_ids((2 * channels, LANES))
@@ -258,7 +258,8 @@
 
         def conv_in(row):
             at = slice(row * cols, (row + 1) * cols)
-            z1 = dot(w_in[...], stack(x_s, row, False))
+            parts = dot(w_in[...], stack(x_s.at[0 : 2 * channels], row, False))
+            z1 = parts[:width] + after(parts[width:])
             sig = 0.5 * jnp.tanh(0.5 * z1) + 0.5
             h1 = z1 * sig
             slope_s[:, at] = sig + h1 * (1.0 - sig)
@@ -267,7 +268,8 @@
         def conv_mid(row):
             at = slice(row * cols, (row + 1) * cols)
             ahead = slice((row + 1) * cols, (row + 2) * cols)
-            dh2 = dot(w_out_back[...], stack(d_s, row, True))
+            parts = dot(w_out_back[...], stack(d_s.at[0 : 2 * channels], row, True))
+            dh2 = parts[:width] + before(parts[width:])
             z2 = across(dot(w_mid[...], stack(h_s, row, False)), False)
             sig = 0.5 * jnp.tanh(0.5 * z2) + 0.5
             added = z2 * sig
@@ -287,11 +289,20 @@
 
         def conv_back(row):
             at = slice(row * cols, (row + 1) * cols)
-            back = dot(w_mid_back[...], stack(z_s, row, True))
+            back = across(dot(w_mid_back[...], stack(z_s.at[width : 2 * width], row, True)), True)
             dz_s[:, at] = ((dh_s[:, at] + back) * slope_s[:, at]).astype(BF16)
 
+        def pair_out(pair):
+            starts = [(2 * pair + 1 + at) * cols for at in range(2)]
+            both = jnp.concatenate([h2_s[:, start : start + cols] for start in starts], axis=0)
+            y_s[pair] = dot(w_out[...], both)
+
         def conv_out(row):
-            result = across(dot(w_out[...], stack(h2_s, row, False)), False)
+            terms = []
+            for pair, at in ((row // 2, 1 + row % 2), (row // 2 + 2 * (row % 2) - 1, 3 - 3 * (row % 2))):
+                if 0 <= pair < rows // 2:
+                    terms.append(y_s[pair, at * 3 * channels : (at + 1) * 3 * channels])
+            result = across(terms[0] + terms[1] if len(terms) > 1 else terms[0], False)
             result = result * patch_weights[row : row + 1]
             result = jnp.concatenate([result, jnp.zeros((channels, LANES), F32)], axis=1)
             numer[row0 + row] += roll(result, lax.rem(col0 + (wide - MARGIN), wide), 1)
@@ -313,7 +324,8 @@
             grads[0:small] += dot_lanes(all_rows(x_s, False), dz_s[...])
 
         backs = [functools.partial(conv_back, row) for row in range(rows)]
-        outs = [functools.partial(conv_out, row) for row in range(rows)]
+        outs = [functools.partial(pair_out, pair) for pair in range(rows // 2)]
+        outs += [functools.partial(conv_out, row) for row in range(rows)]
         return [grad_mid, grad_out] + backs + [grad_in] + outs
 
     def merged(left, right):
@@ -323,9 +335,12 @@
             step()
 
     for slot in range(SLOTS + 1):
-        ahead = first_part(slot, *sets[slot % 2]) if slot < SLOTS else []
-        behind = second_part(slot - 1, *sets[(slot - 1) % 2]) if slot > 0 else []
-        merged(behind, ahead)
+
+        @pl.when(max(slot, 1) <= counts[0, 0])
+        def _():
+            ahead = first_part(slot, *sets[slot % 2]) if slot < SLOTS else []
+            behind = second_part(slot - 1, *sets[(slot - 1) % 2]) if slot > 0 else []
+            merged(behind, ahead)
 
     half = grads.shape[0] // 2
     odd_index = lax.rem(lax.axis_index("lat"), 2)
@@ -465,6 +480,11 @@
 
 def ordered(own, other, bit):
     return jnp.concatenate([jnp.where(bit == 0, own, other), jnp.where(bit == 0, other, own)], axis=0)
+
+
+def two_taps(kernel):
+    last = jnp.stack([jnp.zeros_like(kernel[:, :, 2]), kernel[:, :, 2]], axis=2)
+    return jnp.concatenate([kernel[:, :, :2], last], axis=0).reshape(2 * kernel.shape[0], -1)
 
 
 def shards(
@@ -506,13 +526,22 @@
         ),
     )
     first, second = swap_lat(first, second)
-    w_in = jnp.transpose(kernel_in, (1, 0, 2)).reshape(width, taps * channels)
+    kernel_in = kernel_in.reshape(3, 3, width, channels)
     kernel_mid = kernel_mid.reshape(3, 3, width, width)
     kernel_out = kernel_out.reshape(3, 3, channels, width)
+    w_in = two_taps(jnp.transpose(kernel_in, (2, 0, 1, 3)))
     w_mid = jnp.transpose(kernel_mid, (1, 2, 0, 3)).reshape(3 * width, 3 * width)
-    w_mid_back = jnp.transpose(kernel_mid, (3, 0, 1, 2)).reshape(width, taps * width)
-    w_out = jnp.transpose(kernel_out, (1, 2, 0, 3)).reshape(3 * channels, 3 * width)
-    w_out_back = jnp.transpose(kernel_out, (3, 0, 1, 2)).reshape(width, taps * channels)
+    w_mid_back = jnp.transpose(kernel_mid, (1, 3, 0, 2)).reshape(3 * width, 3 * width)
+    by_col = kernel_out.reshape(3, 3 * channels, width)
+    none = jnp.zeros_like(by_col[0])
+    w_out = jnp.concatenate(
+        [
+            jnp.concatenate([by_col[at - out + 2] if 0 <= at - out + 2 < 3 else none for at in range(2)], axis=1)
+            for out in range(4)
+        ],
+        axis=0,
+    )
+    w_out_back = two_taps(jnp.transpose(kernel_out, (3, 0, 1, 2)))
     first, second, w_in, w_mid, w_mid_back, w_out, w_out_back = lax.optimization_barrier(
         (first, second, w_in, w_mid, w_mid_back, w_out, w_out_back)
     )
@@ -545,6 +574,7 @@
         scratch_shapes=[
             pltpu.VMEM((length, LANES), F32),
             pltpu.VMEM((height, 2 * channels, wide), F32),
+            pltpu.VMEM((rows // 2, 12 * channels, cols), F32),
         ]
         + 2
         * [

time: 73.7 us -> 75 us (1.018)
  Pallas kernels: 20.9 us -> 12.3 us
  starting transfers between devices: 20.1 us -> 25.3 us
  waiting for transfers between devices: 18.1 us -> 22.6 us
    pallas_call x1, Pallas kernels: 17.4 us -> 8.88 us  [shards(): pl.pallas_call(patch_kernel, out_shape=(shape((half + 2 * edge_rows, LANE...]
    ppermute x6, starting transfers between devices: 13.7 us -> 18.9 us  [exchange(): return lax.ppermute(value, axis, pairs)]
    ppermute x6, waiting for transfers between devices: 15.6 us -> 19.8 us  [exchange(): return lax.ppermute(value, axis, pairs)]
    slice x0 -> x5, local copies, waits for them, and re-layouts: none -> 0.76 us  [the longest x2 0.75 us: two_taps(): last = jnp.stack([jnp.zeros_like(kernel[:, :, 2]), kernel[:, :, 2]], axis=2)]
  transfers between devices with their start and end apart: 10 -> 10, of which waited for: 7 -> 7; matrix products, arithmetic and copies ran while one was open for 1% -> 2% of each run, Pallas kernels for 1% -> 1%
where the time goes in v10:
time: 75 us; the launch traced here: 74.7 us
  starting transfers between devices  25.3 us (34%)
  waiting for transfers between devices  22.6 us (30%)
  Pallas kernels  12.3 us (16%)
  blocking collectives  10.2 us (14%)
  local copies, waits for them, and re-layouts  2.28 us (3%)
  between operations  1.72 us (2%)
    ppermute x6, waiting for transfers between devices, exchange(): return lax.ppermute(value, axis, pairs)  19.8 us
    ppermute x6, starting transfers between devices, exchange(): return lax.ppermute(value, axis, pairs)  18.9 us
    all_to_all x1, blocking collectives, shards(): payload = lax.all_to_all(payload, 'lon', 0, 0)  10.2 us
    pallas_call x1, Pallas kernels, shards(): pl.pallas_call(patch_kernel, out_shape=(shape((half + 2 * edge_rows, LANE...  8.88 us
    ppermute x4, starting transfers between devices, swap(): return lax.ppermute(value, axis, pairs)  6.42 us
    ppermute x4, waiting for transfers between devices, swap(): return lax.ppermute(value, axis, pairs)  2.83 us
  transfers between devices with their start and end apart: 10, of which 7 were waited for; matrix products, arithmetic and copies ran while one was open for 2% of the time, Pallas kernels for 1%

profile of v10, /device:TPU:0, one launch (start us, length us, event | category | flops | bytes accessed | tf_op | source)
XLA Modules:
  0.0 74.7 jit_solution(7140334202061117248)
XLA Ops:
  1.3 1.2 %pack.1 = (bf16[8,64,256]{2,1,0:T(8,128)(2,1)S(1)}, bf16[5,64,256]{2,1,0:T(8,128)(2,1)S(1)}, bf16[5,64,256]{2,1,0:T(8,128)(2,1)S(1)}, f32[16,384]{1,0:T(8,128)S(1)}) custom-call(s32[1,1]{1,0:T(1,128)S(6)} %copy.24.counts, s32[1,1,2,4]{3,2,1,0:T(2,128)} %bitcast.24, bf16[32,8,256]{2,1,0:T(8,128)(2,1)} %fields_in.1, bf16[32,8,256]{2,1,0:T(8,128)(2,1)} %cotangent_in.1, ...), custom_call_target="tpu_custom_call" | custom-call | tf_op jit(solution)/shard_map/pack/pallas_call | solution.py:501
  2.5 0.7 collective-permute-start
  3.2 0.7 collective-permute-start.1
  3.9 0.7 slice.63
  4.7 0.2 copy.17
  4.9 0.3 copy.16
  5.2 0.6 copy-done.3
  6.3 2.5 %collective-permute-start.2 = (bf16[96,128]{1,0:T(8,128)(2,1)S(1)}, bf16[96,128]{1,0:T(8,128)(2,1)S(1)}, u32[]{:S(2)}, u32[]{:S(2)}) collective-permute-start(bf16[96,128]{1,0:T(8,128)(2,1)S(1)} %get-tuple-element.32), channel_id=1, source_target_pairs={{0,1},{1,0},{2,3},{3,2},{4,5},{5,4},{6,7},{7,6},{8,9},{9,8},{10,11... | collective-permute-start | bytes 73736 | tf_op jit(solution)/shard_map/ppermute | solution.py:453
  8.7 2.6 %collective-permute-start.3 = (bf16[96,128]{1,0:T(8,128)(2,1)S(1)}, bf16[96,128]{1,0:T(8,128)(2,1)S(1)}, u32[]{:S(2)}, u32[]{:S(2)}) collective-permute-start(bf16[96,128]{1,0:T(8,128)(2,1)S(1)} %get-tuple-element.32), channel_id=1, source_target_pairs={{1,2},{2,1},{3,0},{0,3},{5,6},{6,5},{7,4},{4,7},{9,10},{10,9},{11,... | collective-permute-start | bytes 73736 | tf_op jit(solution)/shard_map/ppermute | solution.py:453
  11.6 2.8 %collective-permute-done.3.fourth = bf16[96,128]{1,0:T(8,128)(2,1)S(1)} collective-permute-done((bf16[96,128]{1,0:T(8,128)(2,1)S(1)}, bf16[96,128]{1,0:T(8,128)(2,1)S(1)}, u32[]{:S(2)}, u32[]{:S(2)}) %collective-permute-start.3) | collective-permute-done | bytes 24608 | tf_op jit(solution)/shard_map/ppermute | solution.py:453
  14.4 8.9 %patches.1 = (bf16[1472,128]{1,0:T(8,128)(2,1)S(1)}, f32[896,128]{1,0:T(8,128)S(1)}, f32[16,32,384]{2,1,0:T(8,128)S(1)}, f32[8,256]{1,0:T(8,128)S(1)}) custom-call(s32[1,1,2,4]{3,2,1,0:T(2,128)S(1)} %bitcast.25, s32[1,1]{1,0:T(1,128)S(6)} %copy.24.counts, bf16[8,64,256]{2,1,0:T(8,128)(2,1)S(1)} %get-tuple-element.26.center, ...), custom_call_target="tpu_custom_call" | custom-call | tf_op jit(solution)/shard_map/patches/pallas_call | solution.py:564
  23.3 16.6 %collective-permute-start.4 = (bf16[1472,128]{1,0:T(8,128)(2,1)S(1)}, bf16[1472,128]{1,0:T(8,128)(2,1)S(1)}, u32[]{:S(2)}, u32[]{:S(2)}) collective-permute-start(bf16[1472,128]{1,0:T(8,128)(2,1)S(1)} %get-tuple-element.40), channel_id=1, source_target_pairs={{0,4},{4,0},{8,12},{12,8},{16,20},{20,16},{24,28},{28,24},{1,5},{5... | collective-permute-start | bytes 1130504 | tf_op jit(solution)/shard_map/ppermute | solution.py:466
  39.9 1.3 %collective-permute-done.4.first = bf16[1472,128]{1,0:T(8,128)(2,1)S(1)} collective-permute-done((bf16[1472,128]{1,0:T(8,128)(2,1)S(1)}, bf16[1472,128]{1,0:T(8,128)(2,1)S(1)}, u32[]{:S(2)}, u32[]{:S(2)}) %collective-permute-start.4) | collective-permute-done | bytes 376864 | tf_op jit(solution)/shard_map/ppermute | solution.py:466
  41.5 5.5 %collective-permute-done.5 = bf16[736,128]{1,0:T(8,128)(2,1)S(1)} collective-permute-done((bf16[736,128]{1,0:T(8,128)(2,1)S(1)}, bf16[736,128]{1,0:T(8,128)(2,1)S(1)}, u32[]{:S(2)}, u32[]{:S(2)}) %collective-permute-start.5) | collective-permute-done | bytes 188448 | tf_op jit(solution)/shard_map/ppermute | solution.py:466
  47.1 1.0 %collective-permute-start.6 = (bf16[512,128]{1,0:T(8,128)(2,1)S(1)}, bf16[512,128]{1,0:T(8,128)(2,1)S(1)}, u32[]{:S(2)}, u32[]{:S(2)}) collective-permute-start(bf16[512,128]{1,0:T(8,128)(2,1)S(1)} %pad_maximum_fusion.2), channel_id=1, source_target_pairs={{0,16},{4,12},{8,24},{12,4},{16,0},{20,28},{24,8},{28,20},{1,17},{... | collective-permute-start | bytes 393224 | tf_op jit(solution)/shard_map/ppermute | solution.py:466
  48.1 4.0 %collective-permute-done.6 = bf16[512,128]{1,0:T(8,128)(2,1)S(1)} collective-permute-done((bf16[512,128]{1,0:T(8,128)(2,1)S(1)}, bf16[512,128]{1,0:T(8,128)(2,1)S(1)}, u32[]{:S(2)}, u32[]{:S(2)}) %collective-permute-start.6) | collective-permute-done | bytes 131104 | tf_op jit(solution)/shard_map/ppermute | solution.py:466
  52.4 10.2 %all_to_all.5.parts = bf16[4,256,128]{2,1,0:T(8,128)(2,1)S(1)} all-to-all(bf16[4,256,128]{2,1,0:T(8,128)(2,1)S(1)} %broadcast_in_dim.2), channel_id=1, replica_groups=mesh['lat'=8,'lon'=4] {'lon'}, dimensions={0} | all-to-all | bytes 524288 | tf_op jit(solution)/shard_map/all_to_all | solution.py:631
  62.7 0.5 collective-permute-start.7
  63.2 4.1 %collective-permute-done.7 = bf16[224,128]{1,0:T(8,128)(2,1)S(1)} collective-permute-done((bf16[224,128]{1,0:T(8,128)(2,1)S(1)}, bf16[224,128]{1,0:T(8,128)(2,1)S(1)}, u32[]{:S(2)}, u32[]{:S(2)}) %collective-permute-start.7) | collective-permute-done | bytes 57376 | tf_op jit(solution)/shard_map/ppermute | solution.py:466
  67.3 0.6 collective-permute-start.8
  67.8 4.3 %collective-permute-done.8 = bf16[448,128]{1,0:T(8,128)(2,1)S(1)} collective-permute-done((bf16[448,128]{1,0:T(8,128)(2,1)S(1)}, bf16[448,128]{1,0:T(8,128)(2,1)S(1)}, u32[]{:S(2)}, u32[]{:S(2)}) %collective-permute-start.8) | collective-permute-done | bytes 114720 | tf_op jit(solution)/shard_map/ppermute | solution.py:466
  72.3 0.9 %fold.1 = f32[32,8,256]{2,1,0:T(8,128)} custom-call(f32[8,32,256]{2,1,0:T(8,128)S(1)} %get-tuple-element.42.inner, bf16[4,256,128]{2,1,0:T(8,128)(2,1)S(1)} %all_to_all.5.parts, f32[8,256]{1,0:T(8,128)S(1)} %get-tuple-element.44.den), custom_call_target="tpu_custom_call" | custom-call | tf_op jit(solution)/shard_map/fold/pallas_call | solution.py:633
  73.1 0.6 collective-permute-done.9.other
  73.7 1.0 %split.1 = (f32[9,32,128]{2,1,0:T(8,128)}, f32[9,128,128]{2,1,0:T(8,128)}, f32[9,32,128]{2,1,0:T(8,128)}) custom-call(bf16[896,128]{1,0:T(8,128)(2,1)S(1)} %pad_maximum_fusion.own, bf16[896,128]{1,0:T(8,128)(2,1)S(1)} %collective-permute-done.9.other), custom_call_target="tpu_custom_call" | custom-call | tf_op jit(solution)/shard_map/split/pallas_call | solution.py:643
  (43 shorter events, 1.3 us)
Async XLA Ops:
  0.6 4.0 %copy-start.4 = (bf16[9,128,32]{1,2,0:T(8,128)(2,1)S(1)}, bf16[9,128,32]{1,2,0:T(8,128)(2,1)}, u32[]{:S(2)}) copy-start(bf16[9,128,32]{1,2,0:T(8,128)(2,1)} %param.10) | copy-start | bytes 221188
  0.6 4.0 %copy-start.2 = (bf16[9,128,128]{2,1,0:T(8,128)(2,1)S(1)}, bf16[9,128,128]{2,1,0:T(8,128)(2,1)}, u32[]{:S(2)}) copy-start(bf16[9,128,128]{2,1,0:T(8,128)(2,1)} %param.11) | copy-start | bytes 884740
  2.5 3.5 %collective-permute-start = (bf16[5,64,256]{2,1,0:T(8,128)(2,1)S(1)}, bf16[5,64,256]{2,1,0:T(8,128)(2,1)S(1)}, u32[]{:S(2)}, u32[]{:S(2)}) collective-permute-start(bf16[5,64,256]{2,1,0:T(8,128)(2,1)S(1)} %get-tuple-element.27), channel_id=1, source_target_pairs={{0,4},{4,0},{8,12},{12,8},{16,20},{20,16},{24,28},{28,24},{1,5},{5... | collective-permute-start | bytes 491528 | tf_op jit(solution)/shard_map/ppermute | solution.py:453
  3.2 2.8 %collective-permute-start.1 = (bf16[5,64,256]{2,1,0:T(8,128)(2,1)S(1)}, bf16[5,64,256]{2,1,0:T(8,128)(2,1)S(1)}, u32[]{:S(2)}, u32[]{:S(2)}) collective-permute-start(bf16[5,64,256]{2,1,0:T(8,128)(2,1)S(1)} %get-tuple-element.28), channel_id=1, source_target_pairs={{4,8},{8,4},{12,16},{16,12},{20,24},{24,20},{5,9},{9,5},{13,17},{1... | collective-permute-start | bytes 491528 | tf_op jit(solution)/shard_map/ppermute | solution.py:453
  4.9 0.9 %copy-start.3 = (bf16[9,32,128]{2,1,0:T(8,128)(2,1)S(1)}, bf16[9,32,128]{2,1,0:T(8,128)(2,1)}, u32[]{:S(2)}) copy-start(bf16[9,32,128]{2,1,0:T(8,128)(2,1)} %param.12) | copy-start | bytes 221188
  6.3 5.3 %collective-permute-start.2 = (bf16[96,128]{1,0:T(8,128)(2,1)S(1)}, bf16[96,128]{1,0:T(8,128)(2,1)S(1)}, u32[]{:S(2)}, u32[]{:S(2)}) collective-permute-start(bf16[96,128]{1,0:T(8,128)(2,1)S(1)} %get-tuple-element.32), channel_id=1, source_target_pairs={{0,1},{1,0},{2,3},{3,2},{4,5},{5,4},{6,7},{7,6},{8,9},{9,8},{10,11... | collective-permute-start | bytes 73736 | tf_op jit(solution)/shard_map/ppermute | solution.py:453
  8.7 5.6 %collective-permute-start.3 = (bf16[96,128]{1,0:T(8,128)(2,1)S(1)}, bf16[96,128]{1,0:T(8,128)(2,1)S(1)}, u32[]{:S(2)}, u32[]{:S(2)}) collective-permute-start(bf16[96,128]{1,0:T(8,128)(2,1)S(1)} %get-tuple-element.32), channel_id=1, source_target_pairs={{1,2},{2,1},{3,0},{0,3},{5,6},{6,5},{7,4},{4,7},{9,10},{10,9},{11,... | collective-permute-start | bytes 73736 | tf_op jit(solution)/shard_map/ppermute | solution.py:453
  11.4 3.0 %copy-start = (s32[4,8,256]{2,1,0:T(8,128)S(1)}, s32[4,8,256]{2,1,0:T(8,128)}, u32[]{:S(2)}) copy-start(s32[4,8,256]{2,1,0:T(8,128)} %weights.1) | copy-start | bytes 98308
  11.5 2.8 %copy-start.1 = (s32[1,1,4,2]{2,3,1,0:T(2,128)S(1)}, s32[1,1,4,2]{2,3,1,0:T(2,128)}, u32[]{:S(2)}) copy-start(s32[1,1,4,2]{2,3,1,0:T(2,128)} %param.13) | copy-start | bytes 100
  23.3 18.0 %collective-permute-start.4 = (bf16[1472,128]{1,0:T(8,128)(2,1)S(1)}, bf16[1472,128]{1,0:T(8,128)(2,1)S(1)}, u32[]{:S(2)}, u32[]{:S(2)}) collective-permute-start(bf16[1472,128]{1,0:T(8,128)(2,1)S(1)} %get-tuple-element.40), channel_id=1, source_target_pairs={{0,4},{4,0},{8,12},{12,8},{16,20},{20,16},{24,28},{28,24},{1,5},{5... | collective-permute-start | bytes 1130504 | tf_op jit(solution)/shard_map/ppermute | solution.py:466
  41.3 5.6 %collective-permute-start.5 = (bf16[736,128]{1,0:T(8,128)(2,1)S(1)}, bf16[736,128]{1,0:T(8,128)(2,1)S(1)}, u32[]{:S(2)}, u32[]{:S(2)}) collective-permute-start(bf16[736,128]{1,0:T(8,128)(2,1)S(1)} %pad_maximum_fusion.1), channel_id=1, source_target_pairs={{0,8},{4,20},{8,0},{12,28},{16,24},{20,4},{24,16},{28,12},{1,9},{5... | collective-permute-start | bytes 565256 | tf_op jit(solution)/shard_map/ppermute | solution.py:466
  47.1 5.0 %collective-permute-start.6 = (bf16[512,128]{1,0:T(8,128)(2,1)S(1)}, bf16[512,128]{1,0:T(8,128)(2,1)S(1)}, u32[]{:S(2)}, u32[]{:S(2)}) collective-permute-start(bf16[512,128]{1,0:T(8,128)(2,1)S(1)} %pad_maximum_fusion.2), channel_id=1, source_target_pairs={{0,16},{4,12},{8,24},{12,4},{16,0},{20,28},{24,8},{28,20},{1,17},{... | collective-permute-start | bytes 393224 | tf_op jit(solution)/shard_map/ppermute | solution.py:466
  62.7 4.6 %collective-permute-start.7 = (bf16[224,128]{1,0:T(8,128)(2,1)S(1)}, bf16[224,128]{1,0:T(8,128)(2,1)S(1)}, u32[]{:S(2)}, u32[]{:S(2)}) collective-permute-start(bf16[224,128]{1,0:T(8,128)(2,1)S(1)} %slice_reduce_fusion), channel_id=1, source_target_pairs={{0,16},{4,12},{8,24},{12,4},{16,0},{20,28},{24,8},{28,20},{1,17},{... | collective-permute-start | bytes 172040 | tf_op jit(solution)/shard_map/ppermute | solution.py:466
  67.3 4.9 %collective-permute-start.8 = (bf16[448,128]{1,0:T(8,128)(2,1)S(1)}, bf16[448,128]{1,0:T(8,128)(2,1)S(1)}, u32[]{:S(2)}, u32[]{:S(2)}) collective-permute-start(bf16[448,128]{1,0:T(8,128)(2,1)S(1)} %pad_maximum_fusion.3), channel_id=1, source_target_pairs={{0,8},{4,20},{8,0},{12,28},{16,24},{20,4},{24,16},{28,12},{1,9},{5... | collective-permute-start | bytes 344072 | tf_op jit(solution)/shard_map/ppermute | solution.py:466
  72.2 1.6 %collective-permute-start.9 = (bf16[896,128]{1,0:T(8,128)(2,1)S(1)}, bf16[896,128]{1,0:T(8,128)(2,1)S(1)}, u32[]{:S(2)}, u32[]{:S(2)}) collective-permute-start(bf16[896,128]{1,0:T(8,128)(2,1)S(1)} %pad_maximum_fusion.own), channel_id=1, source_target_pairs={{0,4},{4,0},{8,12},{12,8},{16,20},{20,16},{24,28},{28,24},{1,5},{5... | collective-permute-start | bytes 688136 | tf_op jit(solution)/shard_map/ppermute | solution.py:466

commit v11 on v9

--- a/solution.py
+++ b/solution.py
@@ -187,8 +187,8 @@
         )
         line = jnp.concatenate([body.astype(F32), beside], axis=1)
         scaled = line[channels:] * inverse[row : row + 1]
-        window[row, 0:channels] = line[:channels]
-        window[row, channels : 2 * channels] = scaled.astype(BF16).astype(F32)
+        window[row, 0:channels] = line[:channels].astype(BF16)
+        window[row, channels : 2 * channels] = scaled.astype(BF16)
 
     numer[...] = jnp.zeros_like(numer)
     grads[...] = jnp.zeros_like(grads)
@@ -252,8 +252,8 @@
 
         def cut(row):
             line = roll(window[row0 + row], back_shift, 1)[:, :cols]
-            spread(x_s, line[:channels].astype(BF16), row, False)
-            grad = line[channels:] * patch_weights[row : row + 1]
+            spread(x_s, line[:channels], row, False)
+            grad = line[channels:].astype(F32) * patch_weights[row : row + 1]
             spread(d_s, grad.astype(BF16), row, True)
 
         def conv_in(row):
@@ -262,16 +262,16 @@
             sig = 0.5 * jnp.tanh(0.5 * z1) + 0.5
             h1 = z1 * sig
             slope_s[:, at] = sig + h1 * (1.0 - sig)
-            h_s[:, (row + 1) * cols : (row + 2) * cols] = h1.astype(BF16)
+            spread(h_s, h1.astype(BF16), row, False)
 
         def conv_mid(row):
             at = slice(row * cols, (row + 1) * cols)
             ahead = slice((row + 1) * cols, (row + 2) * cols)
             dh2 = dot(w_out_back[...], stack(d_s, row, True))
-            z2 = across(dot(w_mid[...], stack(h_s, row, False)), False)
+            z2 = dot(w_mid[...], stack(h_s, row, False))
             sig = 0.5 * jnp.tanh(0.5 * z2) + 0.5
             added = z2 * sig
-            h2_s[:, ahead] = (h_s[:, ahead].astype(F32) + added).astype(BF16)
+            h2_s[:, ahead] = (h_s[width : 2 * width, ahead].astype(F32) + added).astype(BF16)
             dz2 = (dh2 * (sig + added * (1.0 - sig))).astype(BF16)
             dh_s[:, at] = dh2
             spread(z_s, dz2, row, True)
@@ -297,7 +297,7 @@
             numer[row0 + row] += roll(result, lax.rem(col0 + (wide - MARGIN), wide), 1)
 
         def grad_mid():
-            part = dot_lanes(z_s[:, inside], all_rows(h_s, False))
+            part = dot_lanes(z_s[:, inside], all_rows(h_s.at[width : 2 * width], False))
             for tap in range(3):
                 for tap_col in range(3):
                     start = small + (3 * tap + tap_col) * width
@@ -323,9 +323,12 @@
             step()
 
     for slot in range(SLOTS + 1):
-        ahead = first_part(slot, *sets[slot % 2]) if slot < SLOTS else []
-        behind = second_part(slot - 1, *sets[(slot - 1) % 2]) if slot > 0 else []
-        merged(behind, ahead)
+
+        @pl.when(max(slot, 1) <= counts[0, 0])
+        def _():
+            ahead = first_part(slot, *sets[slot % 2]) if slot < SLOTS else []
+            behind = second_part(slot - 1, *sets[(slot - 1) % 2]) if slot > 0 else []
+            merged(behind, ahead)
 
     half = grads.shape[0] // 2
     odd_index = lax.rem(lax.axis_index("lat"), 2)
@@ -509,7 +512,7 @@
     w_in = jnp.transpose(kernel_in, (1, 0, 2)).reshape(width, taps * channels)
     kernel_mid = kernel_mid.reshape(3, 3, width, width)
     kernel_out = kernel_out.reshape(3, 3, channels, width)
-    w_mid = jnp.transpose(kernel_mid, (1, 2, 0, 3)).reshape(3 * width, 3 * width)
+    w_mid = jnp.transpose(kernel_mid, (2, 0, 1, 3)).reshape(width, taps * width)
     w_mid_back = jnp.transpose(kernel_mid, (3, 0, 1, 2)).reshape(width, taps * width)
     w_out = jnp.transpose(kernel_out, (1, 2, 0, 3)).reshape(3 * channels, 3 * width)
     w_out_back = jnp.transpose(kernel_out, (3, 0, 1, 2)).reshape(width, taps * channels)
@@ -544,13 +547,13 @@
         out_specs=(vmem(),) * 4,
         scratch_shapes=[
             pltpu.VMEM((length, LANES), F32),
-            pltpu.VMEM((height, 2 * channels, wide), F32),
+            pltpu.VMEM((height, 2 * channels, wide), BF16),
         ]
         + 2
         * [
             pltpu.VMEM((3 * channels, padded), BF16),
             pltpu.VMEM((3 * channels, padded), BF16),
-            pltpu.VMEM((width, padded), BF16),
+            pltpu.VMEM((3 * width, padded), BF16),
             pltpu.VMEM((3 * width, padded), BF16),
             pltpu.VMEM((width, padded), BF16),
             pltpu.VMEM((width, full), F32),

time: 73.7 us -> 72 us (0.977)
  Pallas kernels: 20.9 us -> 10.6 us
  starting transfers between devices: 20.1 us -> 26.5 us
  waiting for transfers between devices: 18.1 us -> 21.5 us
    pallas_call x1, Pallas kernels: 17.4 us -> 7.17 us  [shards(): pl.pallas_call(patch_kernel, out_shape=(shape((half + 2 * edge_rows, LANE...]
    ppermute x6, starting transfers between devices: 13.7 us -> 19.9 us  [exchange(): return lax.ppermute(value, axis, pairs)]
    ppermute x6, waiting for transfers between devices: 15.6 us -> 18.9 us  [exchange(): return lax.ppermute(value, axis, pairs)]
where the time goes in v11:
time: 72 us; the launch traced here: 71.8 us
  starting transfers between devices  26.5 us (37%)
  waiting for transfers between devices  21.5 us (30%)
  Pallas kernels  10.6 us (15%)
  blocking collectives  10.2 us (14%)
  between operations  1.68 us (2%)
  local copies, waits for them, and re-layouts  1.06 us (1%)
    ppermute x6, starting transfers between devices, exchange(): return lax.ppermute(value, axis, pairs)  19.9 us
    ppermute x6, waiting for transfers between devices, exchange(): return lax.ppermute(value, axis, pairs)  18.9 us
    all_to_all x1, blocking collectives, shards(): payload = lax.all_to_all(payload, 'lon', 0, 0)  10.2 us
    pallas_call x1, Pallas kernels, shards(): pl.pallas_call(patch_kernel, out_shape=(shape((half + 2 * edge_rows, LANE...  7.17 us
    ppermute x4, starting transfers between devices, swap(): return lax.ppermute(value, axis, pairs)  6.66 us
    ppermute x4, waiting for transfers between devices, swap(): return lax.ppermute(value, axis, pairs)  2.55 us
  transfers between devices with their start and end apart: 10, of which 7 were waited for; matrix products, arithmetic and copies ran while one was open for 1% of the time, Pallas kernels for 1%

profile of v11, /device:TPU:0, one launch (start us, length us, event | category | flops | bytes accessed | tf_op | source)
XLA Modules:
  0.0 71.8 jit_solution(6561863468860503494)
XLA Ops:
  1.3 1.2 %pack.1 = (bf16[8,64,256]{2,1,0:T(8,128)(2,1)S(1)}, bf16[5,64,256]{2,1,0:T(8,128)(2,1)S(1)}, bf16[5,64,256]{2,1,0:T(8,128)(2,1)S(1)}, f32[16,384]{1,0:T(8,128)S(1)}) custom-call(s32[1,1]{1,0:T(1,128)S(6)} %copy.28.counts, s32[1,1,2,4]{3,2,1,0:T(2,128)} %bitcast.27, bf16[32,8,256]{2,1,0:T(8,128)(2,1)} %fields_in.1, bf16[32,8,256]{2,1,0:T(8,128)(2,1)} %cotangent_in.1, ...), custom_call_target="tpu_custom_call" | custom-call | tf_op jit(solution)/shard_map/pack/pallas_call | solution.py:484
  2.5 0.7 collective-permute-start
  3.2 0.8 %collective-permute-start.1 = (bf16[5,64,256]{2,1,0:T(8,128)(2,1)S(1)}, bf16[5,64,256]{2,1,0:T(8,128)(2,1)S(1)}, u32[]{:S(2)}, u32[]{:S(2)}) collective-permute-start(bf16[5,64,256]{2,1,0:T(8,128)(2,1)S(1)} %get-tuple-element.28), channel_id=1, source_target_pairs={{4,8},{8,4},{12,16},{16,12},{20,24},{24,20},{5,9},{9,5},{13,17},{1... | collective-permute-start | bytes 491528 | tf_op jit(solution)/shard_map/ppermute | solution.py:441
  4.0 0.2 copy.17
  4.4 0.2 edges.1
  4.6 2.8 %collective-permute-start.2 = (bf16[96,128]{1,0:T(8,128)(2,1)S(1)}, bf16[96,128]{1,0:T(8,128)(2,1)S(1)}, u32[]{:S(2)}, u32[]{:S(2)}) collective-permute-start(bf16[96,128]{1,0:T(8,128)(2,1)S(1)} %get-tuple-element.32), channel_id=1, source_target_pairs={{0,1},{1,0},{2,3},{3,2},{4,5},{5,4},{6,7},{7,6},{8,9},{9,8},{10,11... | collective-permute-start | bytes 73736 | tf_op jit(solution)/shard_map/ppermute | solution.py:441
  7.4 2.4 %collective-permute-start.3 = (bf16[96,128]{1,0:T(8,128)(2,1)S(1)}, bf16[96,128]{1,0:T(8,128)(2,1)S(1)}, u32[]{:S(2)}, u32[]{:S(2)}) collective-permute-start(bf16[96,128]{1,0:T(8,128)(2,1)S(1)} %get-tuple-element.32), channel_id=1, source_target_pairs={{1,2},{2,1},{3,0},{0,3},{5,6},{6,5},{7,4},{4,7},{9,10},{10,9},{11,... | collective-permute-start | bytes 73736 | tf_op jit(solution)/shard_map/ppermute | solution.py:441
  9.9 0.2 copy.21.w_mid
  10.1 0.2 copy.22.w_mid_back
  10.5 2.5 %collective-permute-done.3.fourth = bf16[96,128]{1,0:T(8,128)(2,1)S(1)} collective-permute-done((bf16[96,128]{1,0:T(8,128)(2,1)S(1)}, bf16[96,128]{1,0:T(8,128)(2,1)S(1)}, u32[]{:S(2)}, u32[]{:S(2)}) %collective-permute-start.3) | collective-permute-done | bytes 24608 | tf_op jit(solution)/shard_map/ppermute | solution.py:441
  13.0 7.2 %patches.1 = (bf16[1472,128]{1,0:T(8,128)(2,1)S(1)}, f32[896,128]{1,0:T(8,128)S(1)}, f32[16,32,384]{2,1,0:T(8,128)S(1)}, f32[8,256]{1,0:T(8,128)S(1)}) custom-call(s32[1,1,2,4]{3,2,1,0:T(2,128)S(1)} %bitcast.28, s32[1,1]{1,0:T(1,128)S(6)} %copy.28.counts, bf16[8,64,256]{2,1,0:T(8,128)(2,1)S(1)} %get-tuple-element.26.center, ...), custom_call_target="tpu_custom_call" | custom-call | tf_op jit(solution)/shard_map/patches/pallas_call | solution.py:538
  20.2 16.8 %collective-permute-start.4 = (bf16[1472,128]{1,0:T(8,128)(2,1)S(1)}, bf16[1472,128]{1,0:T(8,128)(2,1)S(1)}, u32[]{:S(2)}, u32[]{:S(2)}) collective-permute-start(bf16[1472,128]{1,0:T(8,128)(2,1)S(1)} %get-tuple-element.40), channel_id=1, source_target_pairs={{0,4},{4,0},{8,12},{12,8},{16,20},{20,16},{24,28},{28,24},{1,5},{5... | collective-permute-start | bytes 1130504 | tf_op jit(solution)/shard_map/ppermute | solution.py:454
  37.0 1.3 %collective-permute-done.4.first = bf16[1472,128]{1,0:T(8,128)(2,1)S(1)} collective-permute-done((bf16[1472,128]{1,0:T(8,128)(2,1)S(1)}, bf16[1472,128]{1,0:T(8,128)(2,1)S(1)}, u32[]{:S(2)}, u32[]{:S(2)}) %collective-permute-start.4) | collective-permute-done | bytes 376864 | tf_op jit(solution)/shard_map/ppermute | solution.py:454
  38.6 5.5 %collective-permute-done.5 = bf16[736,128]{1,0:T(8,128)(2,1)S(1)} collective-permute-done((bf16[736,128]{1,0:T(8,128)(2,1)S(1)}, bf16[736,128]{1,0:T(8,128)(2,1)S(1)}, u32[]{:S(2)}, u32[]{:S(2)}) %collective-permute-start.5) | collective-permute-done | bytes 188448 | tf_op jit(solution)/shard_map/ppermute | solution.py:454
  44.2 1.0 %collective-permute-start.6 = (bf16[512,128]{1,0:T(8,128)(2,1)S(1)}, bf16[512,128]{1,0:T(8,128)(2,1)S(1)}, u32[]{:S(2)}, u32[]{:S(2)}) collective-permute-start(bf16[512,128]{1,0:T(8,128)(2,1)S(1)} %pad_maximum_fusion.2), channel_id=1, source_target_pairs={{0,16},{4,12},{8,24},{12,4},{16,0},{20,28},{24,8},{28,20},{1,17},{... | collective-permute-start | bytes 393224 | tf_op jit(solution)/shard_map/ppermute | solution.py:454
  45.2 4.0 %collective-permute-done.6 = bf16[512,128]{1,0:T(8,128)(2,1)S(1)} collective-permute-done((bf16[512,128]{1,0:T(8,128)(2,1)S(1)}, bf16[512,128]{1,0:T(8,128)(2,1)S(1)}, u32[]{:S(2)}, u32[]{:S(2)}) %collective-permute-start.6) | collective-permute-done | bytes 131104 | tf_op jit(solution)/shard_map/ppermute | solution.py:454
  49.5 10.2 %all_to_all.5.parts = bf16[4,256,128]{2,1,0:T(8,128)(2,1)S(1)} all-to-all(bf16[4,256,128]{2,1,0:T(8,128)(2,1)S(1)} %broadcast_in_dim.2), channel_id=1, replica_groups=mesh['lat'=8,'lon'=4] {'lon'}, dimensions={0} | all-to-all | bytes 524288 | tf_op jit(solution)/shard_map/all_to_all | solution.py:604
  59.7 1.4 %collective-permute-start.7 = (bf16[224,128]{1,0:T(8,128)(2,1)S(1)}, bf16[224,128]{1,0:T(8,128)(2,1)S(1)}, u32[]{:S(2)}, u32[]{:S(2)}) collective-permute-start(bf16[224,128]{1,0:T(8,128)(2,1)S(1)} %slice_reduce_fusion), channel_id=1, source_target_pairs={{0,16},{4,12},{8,24},{12,4},{16,0},{20,28},{24,8},{28,20},{1,17},{... | collective-permute-start | bytes 172040 | tf_op jit(solution)/shard_map/ppermute | solution.py:454
  61.1 3.2 %collective-permute-done.7 = bf16[224,128]{1,0:T(8,128)(2,1)S(1)} collective-permute-done((bf16[224,128]{1,0:T(8,128)(2,1)S(1)}, bf16[224,128]{1,0:T(8,128)(2,1)S(1)}, u32[]{:S(2)}, u32[]{:S(2)}) %collective-permute-start.7) | collective-permute-done | bytes 57376 | tf_op jit(solution)/shard_map/ppermute | solution.py:454
  64.3 0.6 collective-permute-start.8
  64.9 4.3 %collective-permute-done.8 = bf16[448,128]{1,0:T(8,128)(2,1)S(1)} collective-permute-done((bf16[448,128]{1,0:T(8,128)(2,1)S(1)}, bf16[448,128]{1,0:T(8,128)(2,1)S(1)}, u32[]{:S(2)}, u32[]{:S(2)}) %collective-permute-start.8) | collective-permute-done | bytes 114720 | tf_op jit(solution)/shard_map/ppermute | solution.py:454
  69.3 0.9 %fold.1 = f32[32,8,256]{2,1,0:T(8,128)} custom-call(f32[8,32,256]{2,1,0:T(8,128)S(1)} %get-tuple-element.42.inner, bf16[4,256,128]{2,1,0:T(8,128)(2,1)S(1)} %all_to_all.5.parts, f32[8,256]{1,0:T(8,128)S(1)} %get-tuple-element.44.den), custom_call_target="tpu_custom_call" | custom-call | tf_op jit(solution)/shard_map/fold/pallas_call | solution.py:606
  70.2 0.6 collective-permute-done.9.other
  70.8 1.0 %split.1 = (f32[9,32,128]{2,1,0:T(8,128)}, f32[9,128,128]{2,1,0:T(8,128)}, f32[9,32,128]{2,1,0:T(8,128)}) custom-call(bf16[896,128]{1,0:T(8,128)(2,1)S(1)} %pad_maximum_fusion.own, bf16[896,128]{1,0:T(8,128)(2,1)S(1)} %collective-permute-done.9.other), custom_call_target="tpu_custom_call" | custom-call | tf_op jit(solution)/shard_map/split/pallas_call | solution.py:616
  (37 shorter events, 1.0 us)
Async XLA Ops:
  0.6 3.4 %copy-start.2 = (bf16[9,128,128]{2,1,0:T(8,128)(2,1)S(1)}, bf16[9,128,128]{2,1,0:T(8,128)(2,1)}, u32[]{:S(2)}) copy-start(bf16[9,128,128]{2,1,0:T(8,128)(2,1)} %param.11) | copy-start | bytes 884740
  2.5 1.8 %collective-permute-start = (bf16[5,64,256]{2,1,0:T(8,128)(2,1)S(1)}, bf16[5,64,256]{2,1,0:T(8,128)(2,1)S(1)}, u32[]{:S(2)}, u32[]{:S(2)}) collective-permute-start(bf16[5,64,256]{2,1,0:T(8,128)(2,1)S(1)} %get-tuple-element.27), channel_id=1, source_target_pairs={{0,4},{4,0},{8,12},{12,8},{16,20},{20,16},{24,28},{28,24},{1,5},{5... | collective-permute-start | bytes 491528 | tf_op jit(solution)/shard_map/ppermute | solution.py:441
  3.2 1.0 %copy-start.3 = (bf16[9,32,128]{2,1,0:T(8,128)(2,1)S(1)}, bf16[9,32,128]{2,1,0:T(8,128)(2,1)}, u32[]{:S(2)}) copy-start(bf16[9,32,128]{2,1,0:T(8,128)(2,1)} %param.12) | copy-start | bytes 221188
  3.2 1.1 %collective-permute-start.1 = (bf16[5,64,256]{2,1,0:T(8,128)(2,1)S(1)}, bf16[5,64,256]{2,1,0:T(8,128)(2,1)S(1)}, u32[]{:S(2)}, u32[]{:S(2)}) collective-permute-start(bf16[5,64,256]{2,1,0:T(8,128)(2,1)S(1)} %get-tuple-element.28), channel_id=1, source_target_pairs={{4,8},{8,4},{12,16},{16,12},{20,24},{24,20},{5,9},{9,5},{13,17},{1... | collective-permute-start | bytes 491528 | tf_op jit(solution)/shard_map/ppermute | solution.py:441
  4.4 5.4 %copy-start.4 = (bf16[9,128,32]{1,2,0:T(8,128)(2,1)S(1)}, bf16[9,128,32]{1,2,0:T(8,128)(2,1)}, u32[]{:S(2)}) copy-start(bf16[9,128,32]{1,2,0:T(8,128)(2,1)} %param.10) | copy-start | bytes 221188
  4.6 5.9 %collective-permute-start.2 = (bf16[96,128]{1,0:T(8,128)(2,1)S(1)}, bf16[96,128]{1,0:T(8,128)(2,1)S(1)}, u32[]{:S(2)}, u32[]{:S(2)}) collective-permute-start(bf16[96,128]{1,0:T(8,128)(2,1)S(1)} %get-tuple-element.32), channel_id=1, source_target_pairs={{0,1},{1,0},{2,3},{3,2},{4,5},{5,4},{6,7},{7,6},{8,9},{9,8},{10,11... | collective-permute-start | bytes 73736 | tf_op jit(solution)/shard_map/ppermute | solution.py:441
  7.4 5.6 %collective-permute-start.3 = (bf16[96,128]{1,0:T(8,128)(2,1)S(1)}, bf16[96,128]{1,0:T(8,128)(2,1)S(1)}, u32[]{:S(2)}, u32[]{:S(2)}) collective-permute-start(bf16[96,128]{1,0:T(8,128)(2,1)S(1)} %get-tuple-element.32), channel_id=1, source_target_pairs={{1,2},{2,1},{3,0},{0,3},{5,6},{6,5},{7,4},{4,7},{9,10},{10,9},{11,... | collective-permute-start | bytes 73736 | tf_op jit(solution)/shard_map/ppermute | solution.py:441
  10.3 2.7 %copy-start = (s32[4,8,256]{2,1,0:T(8,128)S(1)}, s32[4,8,256]{2,1,0:T(8,128)}, u32[]{:S(2)}) copy-start(s32[4,8,256]{2,1,0:T(8,128)} %weights.1) | copy-start | bytes 98308
  10.5 2.6 %copy-start.1 = (s32[1,1,4,2]{2,3,1,0:T(2,128)S(1)}, s32[1,1,4,2]{2,3,1,0:T(2,128)}, u32[]{:S(2)}) copy-start(s32[1,1,4,2]{2,3,1,0:T(2,128)} %param.13) | copy-start | bytes 100
  20.2 18.1 %collective-permute-start.4 = (bf16[1472,128]{1,0:T(8,128)(2,1)S(1)}, bf16[1472,128]{1,0:T(8,128)(2,1)S(1)}, u32[]{:S(2)}, u32[]{:S(2)}) collective-permute-start(bf16[1472,128]{1,0:T(8,128)(2,1)S(1)} %get-tuple-element.40), channel_id=1, source_target_pairs={{0,4},{4,0},{8,12},{12,8},{16,20},{20,16},{24,28},{28,24},{1,5},{5... | collective-permute-start | bytes 1130504 | tf_op jit(solution)/shard_map/ppermute | solution.py:454
  38.4 5.6 %collective-permute-start.5 = (bf16[736,128]{1,0:T(8,128)(2,1)S(1)}, bf16[736,128]{1,0:T(8,128)(2,1)S(1)}, u32[]{:S(2)}, u32[]{:S(2)}) collective-permute-start(bf16[736,128]{1,0:T(8,128)(2,1)S(1)} %pad_maximum_fusion.1), channel_id=1, source_target_pairs={{0,8},{4,20},{8,0},{12,28},{16,24},{20,4},{24,16},{28,12},{1,9},{5... | collective-permute-start | bytes 565256 | tf_op jit(solution)/shard_map/ppermute | solution.py:454
  44.2 5.0 %collective-permute-start.6 = (bf16[512,128]{1,0:T(8,128)(2,1)S(1)}, bf16[512,128]{1,0:T(8,128)(2,1)S(1)}, u32[]{:S(2)}, u32[]{:S(2)}) collective-permute-start(bf16[512,128]{1,0:T(8,128)(2,1)S(1)} %pad_maximum_fusion.2), channel_id=1, source_target_pairs={{0,16},{4,12},{8,24},{12,4},{16,0},{20,28},{24,8},{28,20},{1,17},{... | collective-permute-start | bytes 393224 | tf_op jit(solution)/shard_map/ppermute | solution.py:454
  59.7 4.6 %collective-permute-start.7 = (bf16[224,128]{1,0:T(8,128)(2,1)S(1)}, bf16[224,128]{1,0:T(8,128)(2,1)S(1)}, u32[]{:S(2)}, u32[]{:S(2)}) collective-permute-start(bf16[224,128]{1,0:T(8,128)(2,1)S(1)} %slice_reduce_fusion), channel_id=1, source_target_pairs={{0,16},{4,12},{8,24},{12,4},{16,0},{20,28},{24,8},{28,20},{1,17},{... | collective-permute-start | bytes 172040 | tf_op jit(solution)/shard_map/ppermute | solution.py:454
  64.3 4.9 %collective-permute-start.8 = (bf16[448,128]{1,0:T(8,128)(2,1)S(1)}, bf16[448,128]{1,0:T(8,128)(2,1)S(1)}, u32[]{:S(2)}, u32[]{:S(2)}) collective-permute-start(bf16[448,128]{1,0:T(8,128)(2,1)S(1)} %pad_maximum_fusion.3), channel_id=1, source_target_pairs={{0,8},{4,20},{8,0},{12,28},{16,24},{20,4},{24,16},{28,12},{1,9},{5... | collective-permute-start | bytes 344072 | tf_op jit(solution)/shard_map/ppermute | solution.py:454
  69.3 1.6 %collective-permute-start.9 = (bf16[896,128]{1,0:T(8,128)(2,1)S(1)}, bf16[896,128]{1,0:T(8,128)(2,1)S(1)}, u32[]{:S(2)}, u32[]{:S(2)}) collective-permute-start(bf16[896,128]{1,0:T(8,128)(2,1)S(1)} %pad_maximum_fusion.own), channel_id=1, source_target_pairs={{0,4},{4,0},{8,12},{12,8},{16,20},{20,16},{24,28},{28,24},{1,5},{5... | collective-permute-start | bytes 688136 | tf_op jit(solution)/shard_map/ppermute | solution.py:454

commit v12 on v11

--- a/solution.py
+++ b/solution.py
@@ -80,16 +80,16 @@
     tile = jnp.concatenate(both, axis=1).astype(BF16)
     center[...] = tile
     half = total.shape[0] // 2
-    pad = jnp.zeros((2 * channels - 2 * half, cols), F32)
     extras = []
     for part in (total[:half], total[half:]):
         beside = jnp.concatenate([part[:, cols:], jnp.zeros((half, cols - LANES), F32)], axis=1)
-        extras.append(jnp.concatenate([part[:, :cols], beside, pad], axis=0).astype(BF16))
-    top, bottom = tile[:MARGIN], tile[rows - MARGIN :]
-    first_out[0:MARGIN] = choose(odd, top, bottom)
-    first_out[MARGIN] = choose(odd, extras[0], extras[1])
-    second_out[0:MARGIN] = choose(odd, bottom, top)
-    second_out[MARGIN] = choose(odd, extras[1], extras[0])
+        extras.append(jnp.concatenate([part[:, :cols], beside], axis=0).astype(BF16))
+    flat = (MARGIN * 2 * channels, cols)
+    top, bottom = tile[:MARGIN].reshape(flat), tile[rows - MARGIN :].reshape(flat)
+    first_out[0 : flat[0]] = choose(odd, top, bottom)
+    first_out[flat[0] :] = choose(odd, extras[0], extras[1])
+    second_out[0 : flat[0]] = choose(odd, bottom, top)
+    second_out[flat[0] :] = choose(odd, extras[1], extras[0])
 
 
 def edge_kernel(center, first, second, canvas, edges, total_out):
@@ -104,19 +104,21 @@
         block = block.astype(F32)
         return jnp.concatenate([block[:half], block[half:height, :LANES]], axis=1)
 
-    upper = stretch(choose(odd, first[MARGIN], second[MARGIN]))
-    lower = stretch(choose(odd, second[MARGIN], first[MARGIN]))
+    base = MARGIN * 2 * channels
+    upper = stretch(choose(odd, first[base:], second[base:]))
+    lower = stretch(choose(odd, second[base:], first[base:]))
     total = canvas[...] + jnp.concatenate([upper, lower], axis=0)
     total_out[...] = total
     lanes = lane_ids((2 * channels, LANES))
     packed = jnp.zeros((2 * channels, LANES), F32)
     for row in range(height):
+        at = slice(row % MARGIN * 2 * channels, (row % MARGIN + 1) * 2 * channels)
         if row < MARGIN:
-            line = choose(odd, first[row], second[row])
+            line = choose(odd, first[at], second[at])
         elif row < MARGIN + rows:
             line = center[row - MARGIN]
         else:
-            line = choose(odd, second[row - MARGIN - rows], first[row - MARGIN - rows])
+            line = choose(odd, second[at], first[at])
         line = line.astype(F32)
         low = jnp.where(lanes < MARGIN, line[:, :LANES], 0.0)
         high = jnp.where(lanes >= LANES - MARGIN, line[:, cols - LANES :], 0.0)
@@ -176,12 +178,13 @@
     left = left[:base]
     right = right[:base]
     for row in range(height):
+        at = slice(row % MARGIN * base, (row % MARGIN + 1) * base)
         if row < MARGIN:
-            body = choose(lat_odd, first[row], second[row])
+            body = choose(lat_odd, first[at], second[at])
         elif row < MARGIN + rows:
             body = center[row - MARGIN]
         else:
-            body = choose(lat_odd, second[row - MARGIN - rows], first[row - MARGIN - rows])
+            body = choose(lat_odd, second[at], first[at])
         beside = jnp.where(
             lanes < LANES // 2, roll(right, -MARGIN * row, 1), roll(left, MARGIN * row, 1)
         )
@@ -262,16 +265,16 @@
             sig = 0.5 * jnp.tanh(0.5 * z1) + 0.5
             h1 = z1 * sig
             slope_s[:, at] = sig + h1 * (1.0 - sig)
-            spread(h_s, h1.astype(BF16), row, False)
+            h_s[:, (row + 1) * cols : (row + 2) * cols] = h1.astype(BF16)
 
         def conv_mid(row):
             at = slice(row * cols, (row + 1) * cols)
             ahead = slice((row + 1) * cols, (row + 2) * cols)
             dh2 = dot(w_out_back[...], stack(d_s, row, True))
-            z2 = dot(w_mid[...], stack(h_s, row, False))
+            z2 = across(dot(w_mid[...], stack(h_s, row, False)), False)
             sig = 0.5 * jnp.tanh(0.5 * z2) + 0.5
             added = z2 * sig
-            h2_s[:, ahead] = (h_s[width : 2 * width, ahead].astype(F32) + added).astype(BF16)
+            h2_s[:, ahead] = (h_s[:, ahead].astype(F32) + added).astype(BF16)
             dz2 = (dh2 * (sig + added * (1.0 - sig))).astype(BF16)
             dh_s[:, at] = dh2
             spread(z_s, dz2, row, True)
@@ -297,7 +300,7 @@
             numer[row0 + row] += roll(result, lax.rem(col0 + (wide - MARGIN), wide), 1)
 
         def grad_mid():
-            part = dot_lanes(z_s[:, inside], all_rows(h_s.at[width : 2 * width], False))
+            part = dot_lanes(z_s[:, inside], all_rows(h_s, False))
             for tap in range(3):
                 for tap_col in range(3):
                     start = small + (3 * tap + tap_col) * width
@@ -381,16 +384,29 @@
         low = jnp.where(lanes < MARGIN, parts[-1], 0.0)
         high = jnp.where(lanes >= LANES - MARGIN, parts[-1], 0.0)
         packed = packed + roll(low, MARGIN * row, 1) + roll(high, -MARGIN * row, 1)
-    edges[...] = packed.astype(BF16)
+    part = channels // 2
+    lanes = lane_ids((part, LANES))
+    quarter = LANES // 4
+    rest = packed[part:]
+    rest = jnp.where(lanes < 2 * quarter, roll(rest, quarter, 1), roll(rest, -quarter, 1))
+    middle = jnp.logical_and(lanes >= quarter, lanes < 3 * quarter)
+    edges[...] = jnp.where(middle, rest, packed[:part]).astype(BF16)
 
 
 def fold_kernel(inner, parts, den, blended):
     rows, channels, cols = inner.shape
     lanes = lane_ids((channels, LANES))
     lon, lon_size = lax.axis_index("lon"), lax.axis_size("lon")
-    base = parts.shape[1] - channels
-    left = parts[lax.rem(lon + lon_size - 1, lon_size), base : base + channels].astype(F32)
-    right = parts[lax.rem(lon + 1, lon_size), base : base + channels].astype(F32)
+    quarter = LANES // 4
+    part_lanes = lane_ids((channels // 2, LANES))
+
+    def margins(index):
+        part = parts[index, 0 : channels // 2].astype(F32)
+        rest = jnp.where(part_lanes < 2 * quarter, roll(part, -quarter, 1), roll(part, quarter, 1))
+        return jnp.concatenate([part, rest], axis=0)
+
+    left = margins(lax.rem(lon + lon_size - 1, lon_size))
+    right = margins(lax.rem(lon + 1, lon_size))
     inverse = 1.0 / den[...]
     lines = []
     for row in range(rows):
@@ -485,8 +501,8 @@
         pack_kernel,
         out_shape=(
             shape((rows, 2 * channels, cols), BF16),
-            shape((MARGIN + 1, 2 * channels, cols), BF16),
-            shape((MARGIN + 1, 2 * channels, cols), BF16),
+            shape((MARGIN * 2 * channels + height, cols), BF16),
+            shape((MARGIN * 2 * channels + height, cols), BF16),
             shape((height, wide), F32),
         ),
         in_specs=[smem()] + [pl.BlockSpec(memory_space=pltpu.HBM)] * 4,
@@ -512,7 +528,7 @@
     w_in = jnp.transpose(kernel_in, (1, 0, 2)).reshape(width, taps * channels)
     kernel_mid = kernel_mid.reshape(3, 3, width, width)
     kernel_out = kernel_out.reshape(3, 3, channels, width)
-    w_mid = jnp.transpose(kernel_mid, (2, 0, 1, 3)).reshape(width, taps * width)
+    w_mid = jnp.transpose(kernel_mid, (1, 2, 0, 3)).reshape(3 * width, 3 * width)
     w_mid_back = jnp.transpose(kernel_mid, (3, 0, 1, 2)).reshape(width, taps * width)
     w_out = jnp.transpose(kernel_out, (1, 2, 0, 3)).reshape(3 * channels, 3 * width)
     w_out_back = jnp.transpose(kernel_out, (3, 0, 1, 2)).reshape(width, taps * channels)
@@ -531,7 +547,7 @@
 
     lat_size, lon_size = lax.axis_size("lat"), lax.axis_size("lon")
     length = taps * (2 * channels + width)
-    unit = 16 * lat_size
+    unit = 8 * lat_size
     length = (length + unit - 1) // unit * unit
     half = length // 2
     edge_rows = channels * (MARGIN * (cols // LANES) + 1)
@@ -553,7 +569,7 @@
         * [
             pltpu.VMEM((3 * channels, padded), BF16),
             pltpu.VMEM((3 * channels, padded), BF16),
-            pltpu.VMEM((3 * width, padded), BF16),
+            pltpu.VMEM((width, padded), BF16),
             pltpu.VMEM((3 * width, padded), BF16),
             pltpu.VMEM((width, padded), BF16),
             pltpu.VMEM((width, full), F32),
@@ -592,17 +608,16 @@
         held = jnp.where(jnp.where(even, moves[0], moves[1]), payload[count:], held)
     inner, edges = pl.pallas_call(
         beside_kernel,
-        out_shape=(shape((rows, channels, cols), F32), shape((channels, LANES), BF16)),
+        out_shape=(shape((rows, channels, cols), F32), shape((channels // 2, LANES), BF16)),
         in_specs=[vmem()] * 3,
         out_specs=(vmem(),) * 2,
         compiler_params=params(),
         name="beside",
     )(numer, first, held)
-    count = mine.shape[0]
-    payload = jnp.concatenate([mine.astype(BF16), edges], axis=0)
+    payload = jnp.concatenate([edges, mine.astype(BF16)], axis=0)
     payload = jnp.broadcast_to(payload[None], (lon_size,) + payload.shape)
     payload = lax.all_to_all(payload, "lon", 0, 0)
-    mine = jnp.sum(payload[:, :count].astype(F32), axis=0).astype(BF16)
+    mine = jnp.sum(payload[:, channels // 2 :].astype(F32), axis=0).astype(BF16)
     blended = pl.pallas_call(
         fold_kernel,
         out_shape=shape((channels, rows, cols), F32),

time: 72 us -> 71.5 us (level)
  starting transfers between devices: 26.5 us -> 14.6 us
  Pallas kernels: 10.6 us -> 19.7 us
  waiting for transfers between devices: 21.5 us -> 23.6 us
    ppermute x6, starting transfers between devices: 19.9 us -> 8.27 us  [exchange(): return lax.ppermute(value, axis, pairs)]
    pallas_call x1, Pallas kernels: 7.17 us -> 16.1 us  [shards(): pl.pallas_call(patch_kernel, out_shape=(shape((half + 2 * edge_rows, LANE...]
    ppermute x6, waiting for transfers between devices: 18.9 us -> 21.1 us  [exchange(): return lax.ppermute(value, axis, pairs)]
where the time goes in v12:
time: 71.5 us; the launch traced here: 71.1 us
  waiting for transfers between devices  23.6 us (33%)
  Pallas kernels  19.7 us (28%)
  starting transfers between devices  14.6 us (20%)
  blocking collectives  9.52 us (13%)
  local copies, waits for them, and re-layouts  1.75 us (2%)
  between operations  1.71 us (2%)
    ppermute x6, waiting for transfers between devices, exchange(): return lax.ppermute(value, axis, pairs)  21.1 us
    pallas_call x1, Pallas kernels, shards(): pl.pallas_call(patch_kernel, out_shape=(shape((half + 2 * edge_rows, LANE...  16.1 us
    all_to_all x1, blocking collectives, shards(): payload = lax.all_to_all(payload, 'lon', 0, 0)  9.52 us
    ppermute x6, starting transfers between devices, exchange(): return lax.ppermute(value, axis, pairs)  8.27 us
    ppermute x4, starting transfers between devices, swap(): return lax.ppermute(value, axis, pairs)  6.31 us
    ppermute x4, waiting for transfers between devices, swap(): return lax.ppermute(value, axis, pairs)  2.55 us
  transfers between devices with their start and end apart: 10, of which 7 were waited for; matrix products, arithmetic and copies ran while one was open for 1% of the time, Pallas kernels for 1%

profile of v12, /device:TPU:0, one launch (start us, length us, event | category | flops | bytes accessed | tf_op | source)
XLA Modules:
  0.0 71.1 jit_solution(3500232765381858378)
XLA Ops:
  1.3 1.3 %pack.1 = (bf16[8,64,256]{2,1,0:T(8,128)(2,1)S(1)}, bf16[272,256]{1,0:T(8,128)(2,1)S(1)}, bf16[272,256]{1,0:T(8,128)(2,1)S(1)}, f32[16,384]{1,0:T(8,128)S(1)}) custom-call(s32[1,1]{1,0:T(1,128)S(6)} %copy.28.counts, s32[1,1,2,4]{3,2,1,0:T(2,128)} %bitcast.31, bf16[32,8,256]{2,1,0:T(8,128)(2,1)} %fields_in.1, bf16[32,8,256]{2,1,0:T(8,128)(2,1)} %cotangent_in.1, ...), custom_call_target="tpu_custom_call" | custom-call | tf_op jit(solution)/shard_map/pack/pallas_call | solution.py:500
  2.6 0.6 collective-permute-start
  3.2 0.7 collective-permute-start.1
  3.9 0.3 copy.17
  4.2 0.8 %copy-done.3 = bf16[9,32,128]{2,1,0:T(8,128)(2,1)S(1)} copy-done((bf16[9,32,128]{2,1,0:T(8,128)(2,1)S(1)}, bf16[9,32,128]{2,1,0:T(8,128)(2,1)}, u32[]{:S(2)}) %copy-start.3) | copy-done | bytes 73752
  5.2 0.2 edges.1
  5.4 2.5 %collective-permute-start.2 = (bf16[96,128]{1,0:T(8,128)(2,1)S(1)}, bf16[96,128]{1,0:T(8,128)(2,1)S(1)}, u32[]{:S(2)}, u32[]{:S(2)}) collective-permute-start(bf16[96,128]{1,0:T(8,128)(2,1)S(1)} %get-tuple-element.32), channel_id=1, source_target_pairs={{0,1},{1,0},{2,3},{3,2},{4,5},{5,4},{6,7},{7,6},{8,9},{9,8},{10,11... | collective-permute-start | bytes 73736 | tf_op jit(solution)/shard_map/ppermute | solution.py:457
  7.9 2.6 %collective-permute-start.3 = (bf16[96,128]{1,0:T(8,128)(2,1)S(1)}, bf16[96,128]{1,0:T(8,128)(2,1)S(1)}, u32[]{:S(2)}, u32[]{:S(2)}) collective-permute-start(bf16[96,128]{1,0:T(8,128)(2,1)S(1)} %get-tuple-element.32), channel_id=1, source_target_pairs={{1,2},{2,1},{3,0},{0,3},{5,6},{6,5},{7,4},{4,7},{9,10},{10,9},{11,... | collective-permute-start | bytes 73736 | tf_op jit(solution)/shard_map/ppermute | solution.py:457
  10.6 0.2 copy.20.w_mid_back
  10.8 0.1 copy.21.w_out_back
  10.9 2.5 %collective-permute-done.3.fourth = bf16[96,128]{1,0:T(8,128)(2,1)S(1)} collective-permute-done((bf16[96,128]{1,0:T(8,128)(2,1)S(1)}, bf16[96,128]{1,0:T(8,128)(2,1)S(1)}, u32[]{:S(2)}, u32[]{:S(2)}) %collective-permute-start.3) | collective-permute-done | bytes 24608 | tf_op jit(solution)/shard_map/ppermute | solution.py:457
  13.5 16.1 %patches.1 = (bf16[1440,128]{1,0:T(8,128)(2,1)S(1)}, f32[864,128]{1,0:T(8,128)S(1)}, f32[16,32,384]{2,1,0:T(8,128)S(1)}, f32[8,256]{1,0:T(8,128)S(1)}) custom-call(s32[1,1,2,4]{3,2,1,0:T(2,128)S(1)} %bitcast.32, s32[1,1]{1,0:T(1,128)S(6)} %copy.28.counts, bf16[8,64,256]{2,1,0:T(8,128)(2,1)S(1)} %get-tuple-element.26.center, ...), custom_call_target="tpu_custom_call" | custom-call | tf_op jit(solution)/shard_map/patches/pallas_call | solution.py:554
  29.6 7.4 %collective-permute-start.4 = (bf16[1440,128]{1,0:T(8,128)(2,1)S(1)}, bf16[1440,128]{1,0:T(8,128)(2,1)S(1)}, u32[]{:S(2)}, u32[]{:S(2)}) collective-permute-start(bf16[1440,128]{1,0:T(8,128)(2,1)S(1)} %get-tuple-element.40), channel_id=1, source_target_pairs={{0,4},{4,0},{8,12},{12,8},{16,20},{20,16},{24,28},{28,24},{1,5},{5... | collective-permute-start | bytes 1105928 | tf_op jit(solution)/shard_map/ppermute | solution.py:470
  37.0 1.3 %collective-permute-done.4.first = bf16[1440,128]{1,0:T(8,128)(2,1)S(1)} collective-permute-done((bf16[1440,128]{1,0:T(8,128)(2,1)S(1)}, bf16[1440,128]{1,0:T(8,128)(2,1)S(1)}, u32[]{:S(2)}, u32[]{:S(2)}) %collective-permute-start.4) | collective-permute-done | bytes 368672 | tf_op jit(solution)/shard_map/ppermute | solution.py:470
  38.6 5.4 %collective-permute-done.5 = bf16[720,128]{1,0:T(8,128)(2,1)S(1)} collective-permute-done((bf16[720,128]{1,0:T(8,128)(2,1)S(1)}, bf16[720,128]{1,0:T(8,128)(2,1)S(1)}, u32[]{:S(2)}, u32[]{:S(2)}) %collective-permute-start.5) | collective-permute-done | bytes 184352 | tf_op jit(solution)/shard_map/ppermute | solution.py:470
  44.2 4.9 %collective-permute-done.6 = bf16[504,128]{1,0:T(8,128)(2,1)S(1)} collective-permute-done((bf16[504,128]{1,0:T(8,128)(2,1)S(1)}, bf16[504,128]{1,0:T(8,128)(2,1)S(1)}, u32[]{:S(2)}, u32[]{:S(2)}) %collective-permute-start.6) | collective-permute-done | bytes 129056 | tf_op jit(solution)/shard_map/ppermute | solution.py:470
  49.2 0.3 beside.1
  49.5 9.5 %all_to_all.5.parts = bf16[4,232,128]{2,1,0:T(8,128)(2,1)S(1)} all-to-all(bf16[4,232,128]{2,1,0:T(8,128)(2,1)S(1)} %broadcast_in_dim.2), channel_id=1, replica_groups=mesh['lat'=8,'lon'=4] {'lon'}, dimensions={0} | all-to-all | bytes 475136 | tf_op jit(solution)/shard_map/all_to_all | solution.py:619
  59.1 4.6 %collective-permute-done.7 = bf16[216,128]{1,0:T(8,128)(2,1)S(1)} collective-permute-done((bf16[216,128]{1,0:T(8,128)(2,1)S(1)}, bf16[216,128]{1,0:T(8,128)(2,1)S(1)}, u32[]{:S(2)}, u32[]{:S(2)}) %collective-permute-start.7) | collective-permute-done | bytes 55328 | tf_op jit(solution)/shard_map/ppermute | solution.py:470
  63.7 0.6 collective-permute-start.8
  64.3 4.2 %collective-permute-done.8 = bf16[432,128]{1,0:T(8,128)(2,1)S(1)} collective-permute-done((bf16[432,128]{1,0:T(8,128)(2,1)S(1)}, bf16[432,128]{1,0:T(8,128)(2,1)S(1)}, u32[]{:S(2)}, u32[]{:S(2)}) %collective-permute-start.8) | collective-permute-done | bytes 110624 | tf_op jit(solution)/shard_map/ppermute | solution.py:470
  68.7 0.9 %fold.1 = f32[32,8,256]{2,1,0:T(8,128)} custom-call(f32[8,32,256]{2,1,0:T(8,128)S(1)} %get-tuple-element.42.inner, bf16[4,232,128]{2,1,0:T(8,128)(2,1)S(1)} %all_to_all.5.parts, f32[8,256]{1,0:T(8,128)S(1)} %get-tuple-element.44.den), custom_call_target="tpu_custom_call" | custom-call | tf_op jit(solution)/shard_map/fold/pallas_call | solution.py:621
  69.6 0.6 collective-permute-done.9.other
  70.2 1.0 %split.1 = (f32[9,32,128]{2,1,0:T(8,128)}, f32[9,128,128]{2,1,0:T(8,128)}, f32[9,32,128]{2,1,0:T(8,128)}) custom-call(bf16[864,128]{1,0:T(8,128)(2,1)S(1)} %pad_maximum_fusion.own, bf16[864,128]{1,0:T(8,128)(2,1)S(1)} %collective-permute-done.9.other), custom_call_target="tpu_custom_call" | custom-call | tf_op jit(solution)/shard_map/split/pallas_call | solution.py:631
  (37 shorter events, 0.9 us)
Async XLA Ops:
  0.6 3.3 %copy-start.2 = (bf16[9,128,128]{2,1,0:T(8,128)(2,1)S(1)}, bf16[9,128,128]{2,1,0:T(8,128)(2,1)}, u32[]{:S(2)}) copy-start(bf16[9,128,128]{2,1,0:T(8,128)(2,1)} %param.11) | copy-start | bytes 884740
  2.6 2.5 %collective-permute-start = (bf16[272,256]{1,0:T(8,128)(2,1)S(1)}, bf16[272,256]{1,0:T(8,128)(2,1)S(1)}, u32[]{:S(2)}, u32[]{:S(2)}) collective-permute-start(bf16[272,256]{1,0:T(8,128)(2,1)S(1)} %get-tuple-element.27), channel_id=1, source_target_pairs={{0,4},{4,0},{8,12},{12,8},{16,20},{20,16},{24,28},{28,24},{1,5},{5... | collective-permute-start | bytes 417800 | tf_op jit(solution)/shard_map/ppermute | solution.py:457
  3.2 1.9 %collective-permute-start.1 = (bf16[272,256]{1,0:T(8,128)(2,1)S(1)}, bf16[272,256]{1,0:T(8,128)(2,1)S(1)}, u32[]{:S(2)}, u32[]{:S(2)}) collective-permute-start(bf16[272,256]{1,0:T(8,128)(2,1)S(1)} %get-tuple-element.28), channel_id=1, source_target_pairs={{4,8},{8,4},{12,16},{16,12},{20,24},{24,20},{5,9},{9,5},{13,17},{1... | collective-permute-start | bytes 417800 | tf_op jit(solution)/shard_map/ppermute | solution.py:457
  4.2 0.9 %copy-start.3 = (bf16[9,32,128]{2,1,0:T(8,128)(2,1)S(1)}, bf16[9,32,128]{2,1,0:T(8,128)(2,1)}, u32[]{:S(2)}) copy-start(bf16[9,32,128]{2,1,0:T(8,128)(2,1)} %param.12) | copy-start | bytes 221188
  5.2 5.3 %copy-start.4 = (bf16[9,128,32]{1,2,0:T(8,128)(2,1)S(1)}, bf16[9,128,32]{1,2,0:T(8,128)(2,1)}, u32[]{:S(2)}) copy-start(bf16[9,128,32]{1,2,0:T(8,128)(2,1)} %param.10) | copy-start | bytes 221188
  5.4 5.5 %collective-permute-start.2 = (bf16[96,128]{1,0:T(8,128)(2,1)S(1)}, bf16[96,128]{1,0:T(8,128)(2,1)S(1)}, u32[]{:S(2)}, u32[]{:S(2)}) collective-permute-start(bf16[96,128]{1,0:T(8,128)(2,1)S(1)} %get-tuple-element.32), channel_id=1, source_target_pairs={{0,1},{1,0},{2,3},{3,2},{4,5},{5,4},{6,7},{7,6},{8,9},{9,8},{10,11... | collective-permute-start | bytes 73736 | tf_op jit(solution)/shard_map/ppermute | solution.py:457
  7.9 5.6 %collective-permute-start.3 = (bf16[96,128]{1,0:T(8,128)(2,1)S(1)}, bf16[96,128]{1,0:T(8,128)(2,1)S(1)}, u32[]{:S(2)}, u32[]{:S(2)}) collective-permute-start(bf16[96,128]{1,0:T(8,128)(2,1)S(1)} %get-tuple-element.32), channel_id=1, source_target_pairs={{1,2},{2,1},{3,0},{0,3},{5,6},{6,5},{7,4},{4,7},{9,10},{10,9},{11,... | collective-permute-start | bytes 73736 | tf_op jit(solution)/shard_map/ppermute | solution.py:457
  10.8 2.7 %copy-start = (s32[4,8,256]{2,1,0:T(8,128)S(1)}, s32[4,8,256]{2,1,0:T(8,128)}, u32[]{:S(2)}) copy-start(s32[4,8,256]{2,1,0:T(8,128)} %weights.1) | copy-start | bytes 98308
  10.9 2.6 %copy-start.1 = (s32[1,1,4,2]{2,3,1,0:T(2,128)S(1)}, s32[1,1,4,2]{2,3,1,0:T(2,128)}, u32[]{:S(2)}) copy-start(s32[1,1,4,2]{2,3,1,0:T(2,128)} %param.13) | copy-start | bytes 100
  29.6 8.7 %collective-permute-start.4 = (bf16[1440,128]{1,0:T(8,128)(2,1)S(1)}, bf16[1440,128]{1,0:T(8,128)(2,1)S(1)}, u32[]{:S(2)}, u32[]{:S(2)}) collective-permute-start(bf16[1440,128]{1,0:T(8,128)(2,1)S(1)} %get-tuple-element.40), channel_id=1, source_target_pairs={{0,4},{4,0},{8,12},{12,8},{16,20},{20,16},{24,28},{28,24},{1,5},{5... | collective-permute-start | bytes 1105928 | tf_op jit(solution)/shard_map/ppermute | solution.py:470
  38.4 5.6 %collective-permute-start.5 = (bf16[720,128]{1,0:T(8,128)(2,1)S(1)}, bf16[720,128]{1,0:T(8,128)(2,1)S(1)}, u32[]{:S(2)}, u32[]{:S(2)}) collective-permute-start(bf16[720,128]{1,0:T(8,128)(2,1)S(1)} %pad_maximum_fusion.1), channel_id=1, source_target_pairs={{0,8},{4,20},{8,0},{12,28},{16,24},{20,4},{24,16},{28,12},{1,9},{5... | collective-permute-start | bytes 552968 | tf_op jit(solution)/shard_map/ppermute | solution.py:470
  44.1 5.0 %collective-permute-start.6 = (bf16[504,128]{1,0:T(8,128)(2,1)S(1)}, bf16[504,128]{1,0:T(8,128)(2,1)S(1)}, u32[]{:S(2)}, u32[]{:S(2)}) collective-permute-start(bf16[504,128]{1,0:T(8,128)(2,1)S(1)} %pad_maximum_fusion.2), channel_id=1, source_target_pairs={{0,16},{4,12},{8,24},{12,4},{16,0},{20,28},{24,8},{28,20},{1,17},{... | collective-permute-start | bytes 387080 | tf_op jit(solution)/shard_map/ppermute | solution.py:470
  59.0 4.7 %collective-permute-start.7 = (bf16[216,128]{1,0:T(8,128)(2,1)S(1)}, bf16[216,128]{1,0:T(8,128)(2,1)S(1)}, u32[]{:S(2)}, u32[]{:S(2)}) collective-permute-start(bf16[216,128]{1,0:T(8,128)(2,1)S(1)} %slice_reduce_fusion), channel_id=1, source_target_pairs={{0,16},{4,12},{8,24},{12,4},{16,0},{20,28},{24,8},{28,20},{1,17},{... | collective-permute-start | bytes 165896 | tf_op jit(solution)/shard_map/ppermute | solution.py:470
  63.7 4.8 %collective-permute-start.8 = (bf16[432,128]{1,0:T(8,128)(2,1)S(1)}, bf16[432,128]{1,0:T(8,128)(2,1)S(1)}, u32[]{:S(2)}, u32[]{:S(2)}) collective-permute-start(bf16[432,128]{1,0:T(8,128)(2,1)S(1)} %pad_maximum_fusion.3), channel_id=1, source_target_pairs={{0,8},{4,20},{8,0},{12,28},{16,24},{20,4},{24,16},{28,12},{1,9},{5... | collective-permute-start | bytes 331784 | tf_op jit(solution)/shard_map/ppermute | solution.py:470
  68.6 1.5 %collective-permute-start.9 = (bf16[864,128]{1,0:T(8,128)(2,1)S(1)}, bf16[864,128]{1,0:T(8,128)(2,1)S(1)}, u32[]{:S(2)}, u32[]{:S(2)}) collective-permute-start(bf16[864,128]{1,0:T(8,128)(2,1)S(1)} %pad_maximum_fusion.own), channel_id=1, source_target_pairs={{0,4},{4,0},{8,12},{12,8},{16,20},{20,16},{24,28},{28,24},{1,5},{5... | collective-permute-start | bytes 663560 | tf_op jit(solution)/shard_map/ppermute | solution.py:470

commit v13 on v12

--- a/solution.py
+++ b/solution.py
@@ -299,13 +299,14 @@
             result = jnp.concatenate([result, jnp.zeros((channels, LANES), F32)], axis=1)
             numer[row0 + row] += roll(result, lax.rem(col0 + (wide - MARGIN), wide), 1)
 
-        def grad_mid():
-            part = dot_lanes(z_s[:, inside], all_rows(h_s, False))
-            for tap in range(3):
+        def grad_mid(taps):
+            both = jnp.concatenate([h_s[:, tap * cols : tap * cols + full] for tap in taps], axis=0)
+            part = dot_lanes(z_s[:, inside], both)
+            for at, tap in enumerate(taps):
                 for tap_col in range(3):
                     start = small + (3 * tap + tap_col) * width
                     grads[start : start + width] += part[
-                        tap_col * width : (tap_col + 1) * width, tap * width : (tap + 1) * width
+                        tap_col * width : (tap_col + 1) * width, at * width : (at + 1) * width
                     ]
 
         def grad_out():
@@ -315,23 +316,33 @@
         def grad_in():
             grads[0:small] += dot_lanes(all_rows(x_s, False), dz_s[...])
 
-        backs = [functools.partial(conv_back, row) for row in range(rows)]
-        outs = [functools.partial(conv_out, row) for row in range(rows)]
-        return [grad_mid, grad_out] + backs + [grad_in] + outs
-
-    def merged(left, right):
-        left = [((at + 0.5) / len(left), step) for at, step in enumerate(left)]
-        right = [((at + 0.5) / len(right), step) for at, step in enumerate(right)]
-        for _, step in sorted(left + right, key=lambda pair: pair[0]):
+        steps = [(0.02 + 0.04 * row, functools.partial(conv_back, row)) for row in range(rows)]
+        steps += [(0.33 + 0.08 * row, functools.partial(conv_out, row)) for row in range(rows)]
+        steps.append((0.41, functools.partial(grad_mid, (0, 1))))
+        steps.append((0.53, grad_in))
+        steps.append((0.68, functools.partial(grad_mid, (2,))))
+        steps.append((0.82, grad_out))
+        return steps
+
+    def run(slot):
+        steps = []
+        if slot < SLOTS:
+            ahead = first_part(slot, *sets[slot % 2])
+            steps += [((at + 0.5) / len(ahead), step) for at, step in enumerate(ahead)]
+        if slot > 0:
+            steps += second_part(slot - 1, *sets[(slot - 1) % 2])
+        for _, step in sorted(steps, key=lambda pair: pair[0]):
             step()
 
-    for slot in range(SLOTS + 1):
-
-        @pl.when(max(slot, 1) <= counts[0, 0])
-        def _():
-            ahead = first_part(slot, *sets[slot % 2]) if slot < SLOTS else []
-            behind = second_part(slot - 1, *sets[(slot - 1) % 2]) if slot > 0 else []
-            merged(behind, ahead)
+    @pl.when(counts[0, 0] == SLOTS)
+    def _():
+        for slot in range(SLOTS + 1):
+            run(slot)
+
+    @pl.when(counts[0, 0] < SLOTS)
+    def _():
+        for slot in range(SLOTS):
+            pl.when(max(slot, 1) <= counts[0, 0])(functools.partial(run, slot))
 
     half = grads.shape[0] // 2
     odd_index = lax.rem(lax.axis_index("lat"), 2)

time: 71.5 us -> 71.4 us (level)
  starting transfers between devices: 14.6 us -> 25.8 us
  Pallas kernels: 19.7 us -> 11.8 us
  waiting for transfers between devices: 23.6 us -> 20.3 us
    ppermute x6, starting transfers between devices: 8.27 us -> 19.5 us  [exchange(): return lax.ppermute(value, axis, pairs)]
    pallas_call x1, Pallas kernels: 16.1 us -> 8.22 us  [shards(): pl.pallas_call(patch_kernel, out_shape=(shape((half + 2 * edge_rows, LANE...]
    ppermute x6, waiting for transfers between devices: 21.1 us -> 17.6 us  [exchange(): return lax.ppermute(value, axis, pairs)]
where the time goes in v13:
time: 71.4 us; the launch traced here: 71.1 us
  starting transfers between devices  25.8 us (36%)
  waiting for transfers between devices  20.3 us (28%)
  Pallas kernels  11.8 us (17%)
  blocking collectives  9.52 us (13%)
  local copies, waits for them, and re-layouts  1.75 us (2%)
  between operations  1.67 us (2%)
    ppermute x6, starting transfers between devices, exchange(): return lax.ppermute(value, axis, pairs)  19.5 us
    ppermute x6, waiting for transfers between devices, exchange(): return lax.ppermute(value, axis, pairs)  17.6 us
    all_to_all x1, blocking collectives, shards(): payload = lax.all_to_all(payload, 'lon', 0, 0)  9.52 us
    pallas_call x1, Pallas kernels, shards(): pl.pallas_call(patch_kernel, out_shape=(shape((half + 2 * edge_rows, LANE...  8.22 us
    ppermute x4, starting transfers between devices, swap(): return lax.ppermute(value, axis, pairs)  6.31 us
    ppermute x4, waiting for transfers between devices, swap(): return lax.ppermute(value, axis, pairs)  2.68 us
  transfers between devices with their start and end apart: 10, of which 7 were waited for; matrix products, arithmetic and copies ran while one was open for 1% of the time, Pallas kernels for 1%

profile of v13, /device:TPU:0, one launch (start us, length us, event | category | flops | bytes accessed | tf_op | source)
XLA Modules:
  0.0 71.1 jit_solution(6209374888089082346)
XLA Ops:
  1.3 1.2 %pack.1 = (bf16[8,64,256]{2,1,0:T(8,128)(2,1)S(1)}, bf16[272,256]{1,0:T(8,128)(2,1)S(1)}, bf16[272,256]{1,0:T(8,128)(2,1)S(1)}, f32[16,384]{1,0:T(8,128)S(1)}) custom-call(s32[1,1]{1,0:T(1,128)S(6)} %copy.28.counts, s32[1,1,2,4]{3,2,1,0:T(2,128)} %bitcast.31, bf16[32,8,256]{2,1,0:T(8,128)(2,1)} %fields_in.1, bf16[32,8,256]{2,1,0:T(8,128)(2,1)} %cotangent_in.1, ...), custom_call_target="tpu_custom_call" | custom-call | tf_op jit(solution)/shard_map/pack/pallas_call | solution.py:511
  2.5 0.7 collective-permute-start
  3.2 0.7 collective-permute-start.1
  3.9 0.3 copy.17
  4.2 0.8 %copy-done.3 = bf16[9,32,128]{2,1,0:T(8,128)(2,1)S(1)} copy-done((bf16[9,32,128]{2,1,0:T(8,128)(2,1)S(1)}, bf16[9,32,128]{2,1,0:T(8,128)(2,1)}, u32[]{:S(2)}) %copy-start.3) | copy-done | bytes 73752
  5.2 0.2 edges.1
  5.4 2.5 %collective-permute-start.2 = (bf16[96,128]{1,0:T(8,128)(2,1)S(1)}, bf16[96,128]{1,0:T(8,128)(2,1)S(1)}, u32[]{:S(2)}, u32[]{:S(2)}) collective-permute-start(bf16[96,128]{1,0:T(8,128)(2,1)S(1)} %get-tuple-element.32), channel_id=1, source_target_pairs={{0,1},{1,0},{2,3},{3,2},{4,5},{5,4},{6,7},{7,6},{8,9},{9,8},{10,11... | collective-permute-start | bytes 73736 | tf_op jit(solution)/shard_map/ppermute | solution.py:468
  7.9 2.5 %collective-permute-start.3 = (bf16[96,128]{1,0:T(8,128)(2,1)S(1)}, bf16[96,128]{1,0:T(8,128)(2,1)S(1)}, u32[]{:S(2)}, u32[]{:S(2)}) collective-permute-start(bf16[96,128]{1,0:T(8,128)(2,1)S(1)} %get-tuple-element.32), channel_id=1, source_target_pairs={{1,2},{2,1},{3,0},{0,3},{5,6},{6,5},{7,4},{4,7},{9,10},{10,9},{11,... | collective-permute-start | bytes 73736 | tf_op jit(solution)/shard_map/ppermute | solution.py:468
  10.8 2.7 %collective-permute-done.3.fourth = bf16[96,128]{1,0:T(8,128)(2,1)S(1)} collective-permute-done((bf16[96,128]{1,0:T(8,128)(2,1)S(1)}, bf16[96,128]{1,0:T(8,128)(2,1)S(1)}, u32[]{:S(2)}, u32[]{:S(2)}) %collective-permute-start.3) | collective-permute-done | bytes 24608 | tf_op jit(solution)/shard_map/ppermute | solution.py:468
  13.5 8.2 %patches.1 = (bf16[1440,128]{1,0:T(8,128)(2,1)S(1)}, f32[864,128]{1,0:T(8,128)S(1)}, f32[16,32,384]{2,1,0:T(8,128)S(1)}, f32[8,256]{1,0:T(8,128)S(1)}) custom-call(s32[1,1,2,4]{3,2,1,0:T(2,128)S(1)} %bitcast.32, s32[1,1]{1,0:T(1,128)S(6)} %copy.28.counts, bf16[8,64,256]{2,1,0:T(8,128)(2,1)S(1)} %get-tuple-element.26.center, ...), custom_call_target="tpu_custom_call" | custom-call | tf_op jit(solution)/shard_map/patches/pallas_call | solution.py:565
  21.7 15.2 %collective-permute-start.4 = (bf16[1440,128]{1,0:T(8,128)(2,1)S(1)}, bf16[1440,128]{1,0:T(8,128)(2,1)S(1)}, u32[]{:S(2)}, u32[]{:S(2)}) collective-permute-start(bf16[1440,128]{1,0:T(8,128)(2,1)S(1)} %get-tuple-element.40), channel_id=1, source_target_pairs={{0,4},{4,0},{8,12},{12,8},{16,20},{20,16},{24,28},{28,24},{1,5},{5... | collective-permute-start | bytes 1105928 | tf_op jit(solution)/shard_map/ppermute | solution.py:481
  37.0 1.3 %collective-permute-done.4.first = bf16[1440,128]{1,0:T(8,128)(2,1)S(1)} collective-permute-done((bf16[1440,128]{1,0:T(8,128)(2,1)S(1)}, bf16[1440,128]{1,0:T(8,128)(2,1)S(1)}, u32[]{:S(2)}, u32[]{:S(2)}) %collective-permute-start.4) | collective-permute-done | bytes 368672 | tf_op jit(solution)/shard_map/ppermute | solution.py:481
  38.6 5.4 %collective-permute-done.5 = bf16[720,128]{1,0:T(8,128)(2,1)S(1)} collective-permute-done((bf16[720,128]{1,0:T(8,128)(2,1)S(1)}, bf16[720,128]{1,0:T(8,128)(2,1)S(1)}, u32[]{:S(2)}, u32[]{:S(2)}) %collective-permute-start.5) | collective-permute-done | bytes 184352 | tf_op jit(solution)/shard_map/ppermute | solution.py:481
  44.1 1.7 %collective-permute-start.6 = (bf16[504,128]{1,0:T(8,128)(2,1)S(1)}, bf16[504,128]{1,0:T(8,128)(2,1)S(1)}, u32[]{:S(2)}, u32[]{:S(2)}) collective-permute-start(bf16[504,128]{1,0:T(8,128)(2,1)S(1)} %pad_maximum_fusion.2), channel_id=1, source_target_pairs={{0,16},{4,12},{8,24},{12,4},{16,0},{20,28},{24,8},{28,20},{1,17},{... | collective-permute-start | bytes 387080 | tf_op jit(solution)/shard_map/ppermute | solution.py:481
  45.8 3.3 %collective-permute-done.6 = bf16[504,128]{1,0:T(8,128)(2,1)S(1)} collective-permute-done((bf16[504,128]{1,0:T(8,128)(2,1)S(1)}, bf16[504,128]{1,0:T(8,128)(2,1)S(1)}, u32[]{:S(2)}, u32[]{:S(2)}) %collective-permute-start.6) | collective-permute-done | bytes 129056 | tf_op jit(solution)/shard_map/ppermute | solution.py:481
  49.1 0.3 beside.1
  49.4 9.5 %all_to_all.5.parts = bf16[4,232,128]{2,1,0:T(8,128)(2,1)S(1)} all-to-all(bf16[4,232,128]{2,1,0:T(8,128)(2,1)S(1)} %broadcast_in_dim.2), channel_id=1, replica_groups=mesh['lat'=8,'lon'=4] {'lon'}, dimensions={0} | all-to-all | bytes 475136 | tf_op jit(solution)/shard_map/all_to_all | solution.py:630
  59.0 1.5 %collective-permute-start.7 = (bf16[216,128]{1,0:T(8,128)(2,1)S(1)}, bf16[216,128]{1,0:T(8,128)(2,1)S(1)}, u32[]{:S(2)}, u32[]{:S(2)}) collective-permute-start(bf16[216,128]{1,0:T(8,128)(2,1)S(1)} %slice_reduce_fusion), channel_id=1, source_target_pairs={{0,16},{4,12},{8,24},{12,4},{16,0},{20,28},{24,8},{28,20},{1,17},{... | collective-permute-start | bytes 165896 | tf_op jit(solution)/shard_map/ppermute | solution.py:481
  60.5 3.1 %collective-permute-done.7 = bf16[216,128]{1,0:T(8,128)(2,1)S(1)} collective-permute-done((bf16[216,128]{1,0:T(8,128)(2,1)S(1)}, bf16[216,128]{1,0:T(8,128)(2,1)S(1)}, u32[]{:S(2)}, u32[]{:S(2)}) %collective-permute-start.7) | collective-permute-done | bytes 55328 | tf_op jit(solution)/shard_map/ppermute | solution.py:481
  63.7 0.9 %collective-permute-start.8 = (bf16[432,128]{1,0:T(8,128)(2,1)S(1)}, bf16[432,128]{1,0:T(8,128)(2,1)S(1)}, u32[]{:S(2)}, u32[]{:S(2)}) collective-permute-start(bf16[432,128]{1,0:T(8,128)(2,1)S(1)} %pad_maximum_fusion.3), channel_id=1, source_target_pairs={{0,8},{4,20},{8,0},{12,28},{16,24},{20,4},{24,16},{28,12},{1,9},{5... | collective-permute-start | bytes 331784 | tf_op jit(solution)/shard_map/ppermute | solution.py:481
  64.6 3.9 %collective-permute-done.8 = bf16[432,128]{1,0:T(8,128)(2,1)S(1)} collective-permute-done((bf16[432,128]{1,0:T(8,128)(2,1)S(1)}, bf16[432,128]{1,0:T(8,128)(2,1)S(1)}, u32[]{:S(2)}, u32[]{:S(2)}) %collective-permute-start.8) | collective-permute-done | bytes 110624 | tf_op jit(solution)/shard_map/ppermute | solution.py:481
  68.7 0.9 %fold.1 = f32[32,8,256]{2,1,0:T(8,128)} custom-call(f32[8,32,256]{2,1,0:T(8,128)S(1)} %get-tuple-element.42.inner, bf16[4,232,128]{2,1,0:T(8,128)(2,1)S(1)} %all_to_all.5.parts, f32[8,256]{1,0:T(8,128)S(1)} %get-tuple-element.44.den), custom_call_target="tpu_custom_call" | custom-call | tf_op jit(solution)/shard_map/fold/pallas_call | solution.py:632
  69.6 0.6 collective-permute-done.9.other
  70.1 1.0 %split.1 = (f32[9,32,128]{2,1,0:T(8,128)}, f32[9,128,128]{2,1,0:T(8,128)}, f32[9,32,128]{2,1,0:T(8,128)}) custom-call(bf16[864,128]{1,0:T(8,128)(2,1)S(1)} %pad_maximum_fusion.own, bf16[864,128]{1,0:T(8,128)(2,1)S(1)} %collective-permute-done.9.other), custom_call_target="tpu_custom_call" | custom-call | tf_op jit(solution)/shard_map/split/pallas_call | solution.py:642
  (37 shorter events, 1.1 us)
Async XLA Ops:
  0.6 3.3 %copy-start.2 = (bf16[9,128,128]{2,1,0:T(8,128)(2,1)S(1)}, bf16[9,128,128]{2,1,0:T(8,128)(2,1)}, u32[]{:S(2)}) copy-start(bf16[9,128,128]{2,1,0:T(8,128)(2,1)} %param.11) | copy-start | bytes 884740
  2.5 2.6 %collective-permute-start = (bf16[272,256]{1,0:T(8,128)(2,1)S(1)}, bf16[272,256]{1,0:T(8,128)(2,1)S(1)}, u32[]{:S(2)}, u32[]{:S(2)}) collective-permute-start(bf16[272,256]{1,0:T(8,128)(2,1)S(1)} %get-tuple-element.27), channel_id=1, source_target_pairs={{0,4},{4,0},{8,12},{12,8},{16,20},{20,16},{24,28},{28,24},{1,5},{5... | collective-permute-start | bytes 417800 | tf_op jit(solution)/shard_map/ppermute | solution.py:468
  3.2 1.9 %collective-permute-start.1 = (bf16[272,256]{1,0:T(8,128)(2,1)S(1)}, bf16[272,256]{1,0:T(8,128)(2,1)S(1)}, u32[]{:S(2)}, u32[]{:S(2)}) collective-permute-start(bf16[272,256]{1,0:T(8,128)(2,1)S(1)} %get-tuple-element.28), channel_id=1, source_target_pairs={{4,8},{8,4},{12,16},{16,12},{20,24},{24,20},{5,9},{9,5},{13,17},{1... | collective-permute-start | bytes 417800 | tf_op jit(solution)/shard_map/ppermute | solution.py:468
  4.2 0.9 %copy-start.3 = (bf16[9,32,128]{2,1,0:T(8,128)(2,1)S(1)}, bf16[9,32,128]{2,1,0:T(8,128)(2,1)}, u32[]{:S(2)}) copy-start(bf16[9,32,128]{2,1,0:T(8,128)(2,1)} %param.12) | copy-start | bytes 221188
  5.2 5.2 %copy-start.4 = (bf16[9,128,32]{1,2,0:T(8,128)(2,1)S(1)}, bf16[9,128,32]{1,2,0:T(8,128)(2,1)}, u32[]{:S(2)}) copy-start(bf16[9,128,32]{1,2,0:T(8,128)(2,1)} %param.10) | copy-start | bytes 221188
  5.4 5.4 %collective-permute-start.2 = (bf16[96,128]{1,0:T(8,128)(2,1)S(1)}, bf16[96,128]{1,0:T(8,128)(2,1)S(1)}, u32[]{:S(2)}, u32[]{:S(2)}) collective-permute-start(bf16[96,128]{1,0:T(8,128)(2,1)S(1)} %get-tuple-element.32), channel_id=1, source_target_pairs={{0,1},{1,0},{2,3},{3,2},{4,5},{5,4},{6,7},{7,6},{8,9},{9,8},{10,11... | collective-permute-start | bytes 73736 | tf_op jit(solution)/shard_map/ppermute | solution.py:468
  7.9 5.6 %collective-permute-start.3 = (bf16[96,128]{1,0:T(8,128)(2,1)S(1)}, bf16[96,128]{1,0:T(8,128)(2,1)S(1)}, u32[]{:S(2)}, u32[]{:S(2)}) collective-permute-start(bf16[96,128]{1,0:T(8,128)(2,1)S(1)} %get-tuple-element.32), channel_id=1, source_target_pairs={{1,2},{2,1},{3,0},{0,3},{5,6},{6,5},{7,4},{4,7},{9,10},{10,9},{11,... | collective-permute-start | bytes 73736 | tf_op jit(solution)/shard_map/ppermute | solution.py:468
  10.7 2.8 %copy-start = (s32[4,8,256]{2,1,0:T(8,128)S(1)}, s32[4,8,256]{2,1,0:T(8,128)}, u32[]{:S(2)}) copy-start(s32[4,8,256]{2,1,0:T(8,128)} %weights.1) | copy-start | bytes 98308
  10.8 2.7 %copy-start.1 = (s32[1,1,4,2]{2,3,1,0:T(2,128)S(1)}, s32[1,1,4,2]{2,3,1,0:T(2,128)}, u32[]{:S(2)}) copy-start(s32[1,1,4,2]{2,3,1,0:T(2,128)} %param.13) | copy-start | bytes 100
  21.7 16.5 %collective-permute-start.4 = (bf16[1440,128]{1,0:T(8,128)(2,1)S(1)}, bf16[1440,128]{1,0:T(8,128)(2,1)S(1)}, u32[]{:S(2)}, u32[]{:S(2)}) collective-permute-start(bf16[1440,128]{1,0:T(8,128)(2,1)S(1)} %get-tuple-element.40), channel_id=1, source_target_pairs={{0,4},{4,0},{8,12},{12,8},{16,20},{20,16},{24,28},{28,24},{1,5},{5... | collective-permute-start | bytes 1105928 | tf_op jit(solution)/shard_map/ppermute | solution.py:481
  38.4 5.6 %collective-permute-start.5 = (bf16[720,128]{1,0:T(8,128)(2,1)S(1)}, bf16[720,128]{1,0:T(8,128)(2,1)S(1)}, u32[]{:S(2)}, u32[]{:S(2)}) collective-permute-start(bf16[720,128]{1,0:T(8,128)(2,1)S(1)} %pad_maximum_fusion.1), channel_id=1, source_target_pairs={{0,8},{4,20},{8,0},{12,28},{16,24},{20,4},{24,16},{28,12},{1,9},{5... | collective-permute-start | bytes 552968 | tf_op jit(solution)/shard_map/ppermute | solution.py:481
  44.1 5.0 %collective-permute-start.6 = (bf16[504,128]{1,0:T(8,128)(2,1)S(1)}, bf16[504,128]{1,0:T(8,128)(2,1)S(1)}, u32[]{:S(2)}, u32[]{:S(2)}) collective-permute-start(bf16[504,128]{1,0:T(8,128)(2,1)S(1)} %pad_maximum_fusion.2), channel_id=1, source_target_pairs={{0,16},{4,12},{8,24},{12,4},{16,0},{20,28},{24,8},{28,20},{1,17},{... | collective-permute-start | bytes 387080 | tf_op jit(solution)/shard_map/ppermute | solution.py:481
  59.0 4.7 %collective-permute-start.7 = (bf16[216,128]{1,0:T(8,128)(2,1)S(1)}, bf16[216,128]{1,0:T(8,128)(2,1)S(1)}, u32[]{:S(2)}, u32[]{:S(2)}) collective-permute-start(bf16[216,128]{1,0:T(8,128)(2,1)S(1)} %slice_reduce_fusion), channel_id=1, source_target_pairs={{0,16},{4,12},{8,24},{12,4},{16,0},{20,28},{24,8},{28,20},{1,17},{... | collective-permute-start | bytes 165896 | tf_op jit(solution)/shard_map/ppermute | solution.py:481
  63.7 4.8 %collective-permute-start.8 = (bf16[432,128]{1,0:T(8,128)(2,1)S(1)}, bf16[432,128]{1,0:T(8,128)(2,1)S(1)}, u32[]{:S(2)}, u32[]{:S(2)}) collective-permute-start(bf16[432,128]{1,0:T(8,128)(2,1)S(1)} %pad_maximum_fusion.3), channel_id=1, source_target_pairs={{0,8},{4,20},{8,0},{12,28},{16,24},{20,4},{24,16},{28,12},{1,9},{5... | collective-permute-start | bytes 331784 | tf_op jit(solution)/shard_map/ppermute | solution.py:481
  68.6 1.5 %collective-permute-start.9 = (bf16[864,128]{1,0:T(8,128)(2,1)S(1)}, bf16[864,128]{1,0:T(8,128)(2,1)S(1)}, u32[]{:S(2)}, u32[]{:S(2)}) collective-permute-start(bf16[864,128]{1,0:T(8,128)(2,1)S(1)} %pad_maximum_fusion.own), channel_id=1, source_target_pairs={{0,4},{4,0},{8,12},{12,8},{16,20},{20,16},{24,28},{28,24},{1,5},{5... | collective-permute-start | bytes 663560 | tf_op jit(solution)/shard_map/ppermute | solution.py:481

commit v14 on v13

--- a/solution.py
+++ b/solution.py
@@ -265,16 +265,16 @@
             sig = 0.5 * jnp.tanh(0.5 * z1) + 0.5
             h1 = z1 * sig
             slope_s[:, at] = sig + h1 * (1.0 - sig)
-            h_s[:, (row + 1) * cols : (row + 2) * cols] = h1.astype(BF16)
+            spread(h_s, h1.astype(BF16), row, False)
 
         def conv_mid(row):
             at = slice(row * cols, (row + 1) * cols)
             ahead = slice((row + 1) * cols, (row + 2) * cols)
             dh2 = dot(w_out_back[...], stack(d_s, row, True))
-            z2 = across(dot(w_mid[...], stack(h_s, row, False)), False)
+            z2 = dot(w_mid[...], stack(h_s, row, False))
             sig = 0.5 * jnp.tanh(0.5 * z2) + 0.5
             added = z2 * sig
-            h2_s[:, ahead] = (h_s[:, ahead].astype(F32) + added).astype(BF16)
+            h2_s[:, ahead] = (h_s[width : 2 * width, ahead].astype(F32) + added).astype(BF16)
             dz2 = (dh2 * (sig + added * (1.0 - sig))).astype(BF16)
             dh_s[:, at] = dh2
             spread(z_s, dz2, row, True)
@@ -299,14 +299,13 @@
             result = jnp.concatenate([result, jnp.zeros((channels, LANES), F32)], axis=1)
             numer[row0 + row] += roll(result, lax.rem(col0 + (wide - MARGIN), wide), 1)
 
-        def grad_mid(taps):
-            both = jnp.concatenate([h_s[:, tap * cols : tap * cols + full] for tap in taps], axis=0)
-            part = dot_lanes(z_s[:, inside], both)
-            for at, tap in enumerate(taps):
+        def grad_mid():
+            part = dot_lanes(z_s[:, inside], all_rows(h_s.at[width : 2 * width], False))
+            for tap in range(3):
                 for tap_col in range(3):
                     start = small + (3 * tap + tap_col) * width
                     grads[start : start + width] += part[
-                        tap_col * width : (tap_col + 1) * width, at * width : (at + 1) * width
+                        tap_col * width : (tap_col + 1) * width, tap * width : (tap + 1) * width
                     ]
 
         def grad_out():
@@ -316,21 +315,18 @@
         def grad_in():
             grads[0:small] += dot_lanes(all_rows(x_s, False), dz_s[...])
 
-        steps = [(0.02 + 0.04 * row, functools.partial(conv_back, row)) for row in range(rows)]
-        steps += [(0.33 + 0.08 * row, functools.partial(conv_out, row)) for row in range(rows)]
-        steps.append((0.41, functools.partial(grad_mid, (0, 1))))
-        steps.append((0.53, grad_in))
-        steps.append((0.68, functools.partial(grad_mid, (2,))))
-        steps.append((0.82, grad_out))
-        return steps
+        backs = [functools.partial(conv_back, row) for row in range(rows)]
+        outs = [functools.partial(conv_out, row) for row in range(rows)]
+        return [grad_mid, grad_out] + backs + [grad_in] + outs
 
     def run(slot):
         steps = []
+        if slot > 0:
+            behind = second_part(slot - 1, *sets[(slot - 1) % 2])
+            steps += [((at + 0.5) / len(behind), step) for at, step in enumerate(behind)]
         if slot < SLOTS:
             ahead = first_part(slot, *sets[slot % 2])
             steps += [((at + 0.5) / len(ahead), step) for at, step in enumerate(ahead)]
-        if slot > 0:
-            steps += second_part(slot - 1, *sets[(slot - 1) % 2])
         for _, step in sorted(steps, key=lambda pair: pair[0]):
             step()
 
@@ -539,7 +535,7 @@
     w_in = jnp.transpose(kernel_in, (1, 0, 2)).reshape(width, taps * channels)
     kernel_mid = kernel_mid.reshape(3, 3, width, width)
     kernel_out = kernel_out.reshape(3, 3, channels, width)
-    w_mid = jnp.transpose(kernel_mid, (1, 2, 0, 3)).reshape(3 * width, 3 * width)
+    w_mid = jnp.transpose(kernel_mid, (2, 0, 1, 3)).reshape(width, taps * width)
     w_mid_back = jnp.transpose(kernel_mid, (3, 0, 1, 2)).reshape(width, taps * width)
     w_out = jnp.transpose(kernel_out, (1, 2, 0, 3)).reshape(3 * channels, 3 * width)
     w_out_back = jnp.transpose(kernel_out, (3, 0, 1, 2)).reshape(width, taps * channels)
@@ -580,7 +576,7 @@
         * [
             pltpu.VMEM((3 * channels, padded), BF16),
             pltpu.VMEM((3 * channels, padded), BF16),
-            pltpu.VMEM((width, padded), BF16),
+            pltpu.VMEM((3 * width, padded), BF16),
             pltpu.VMEM((3 * width, padded), BF16),
             pltpu.VMEM((width, padded), BF16),
             pltpu.VMEM((width, full), F32),

time: 71.4 us -> 70.7 us (level)
  starting transfers between devices: 25.8 us -> 16.6 us
  Pallas kernels: 11.8 us -> 19.3 us
  waiting for transfers between devices: 20.3 us -> 21.6 us
  blocking collectives: 9.52 us -> 10.5 us
    ppermute x6, starting transfers between devices: 19.5 us -> 10.1 us  [exchange(): return lax.ppermute(value, axis, pairs)]
    pallas_call x1, Pallas kernels: 8.22 us -> 15.7 us  [shards(): pl.pallas_call(patch_kernel, out_shape=(shape((half + 2 * edge_rows, LANE...]
    ppermute x6, waiting for transfers between devices: 17.6 us -> 19.1 us  [exchange(): return lax.ppermute(value, axis, pairs)]
    all_to_all x1, blocking collectives: 9.52 us -> 10.5 us  [shards(): payload = lax.all_to_all(payload, 'lon', 0, 0)]
where the time goes in v14:
time: 70.7 us; the launch traced here: 71 us
  waiting for transfers between devices  21.6 us (31%)
  Pallas kernels  19.3 us (27%)
  starting transfers between devices  16.6 us (23%)
  blocking collectives  10.5 us (15%)
  between operations  1.57 us (2%)
  local copies, waits for them, and re-layouts  1.05 us (1%)
    ppermute x6, waiting for transfers between devices, exchange(): return lax.ppermute(value, axis, pairs)  19.1 us
    pallas_call x1, Pallas kernels, shards(): pl.pallas_call(patch_kernel, out_shape=(shape((half + 2 * edge_rows, LANE...  15.7 us
    all_to_all x1, blocking collectives, shards(): payload = lax.all_to_all(payload, 'lon', 0, 0)  10.5 us
    ppermute x6, starting transfers between devices, exchange(): return lax.ppermute(value, axis, pairs)  10.1 us
    ppermute x4, starting transfers between devices, swap(): return lax.ppermute(value, axis, pairs)  6.54 us
    ppermute x4, waiting for transfers between devices, swap(): return lax.ppermute(value, axis, pairs)  2.53 us
  transfers between devices with their start and end apart: 10, of which 7 were waited for; matrix products, arithmetic and copies ran while one was open for 1% of the time, Pallas kernels for 1%

profile of v14, /device:TPU:0, one launch (start us, length us, event | category | flops | bytes accessed | tf_op | source)
XLA Modules:
  0.0 71.0 jit_solution(17912473748106565927)
XLA Ops:
  1.3 1.3 %pack.1 = (bf16[8,64,256]{2,1,0:T(8,128)(2,1)S(1)}, bf16[272,256]{1,0:T(8,128)(2,1)S(1)}, bf16[272,256]{1,0:T(8,128)(2,1)S(1)}, f32[16,384]{1,0:T(8,128)S(1)}) custom-call(s32[1,1]{1,0:T(1,128)S(6)} %copy.28.counts, s32[1,1,2,4]{3,2,1,0:T(2,128)} %bitcast.27, bf16[32,8,256]{2,1,0:T(8,128)(2,1)} %fields_in.1, bf16[32,8,256]{2,1,0:T(8,128)(2,1)} %cotangent_in.1, ...), custom_call_target="tpu_custom_call" | custom-call | tf_op jit(solution)/shard_map/pack/pallas_call | solution.py:507
  2.6 0.6 collective-permute-start
  3.2 0.8 %collective-permute-start.1 = (bf16[272,256]{1,0:T(8,128)(2,1)S(1)}, bf16[272,256]{1,0:T(8,128)(2,1)S(1)}, u32[]{:S(2)}, u32[]{:S(2)}) collective-permute-start(bf16[272,256]{1,0:T(8,128)(2,1)S(1)} %get-tuple-element.28), channel_id=1, source_target_pairs={{4,8},{8,4},{12,16},{16,12},{20,24},{24,20},{5,9},{9,5},{13,17},{1... | collective-permute-start | bytes 417800 | tf_op jit(solution)/shard_map/ppermute | solution.py:464
  4.0 0.2 copy.17
  4.4 0.2 edges.1
  4.6 2.8 %collective-permute-start.2 = (bf16[96,128]{1,0:T(8,128)(2,1)S(1)}, bf16[96,128]{1,0:T(8,128)(2,1)S(1)}, u32[]{:S(2)}, u32[]{:S(2)}) collective-permute-start(bf16[96,128]{1,0:T(8,128)(2,1)S(1)} %get-tuple-element.32), channel_id=1, source_target_pairs={{0,1},{1,0},{2,3},{3,2},{4,5},{5,4},{6,7},{7,6},{8,9},{9,8},{10,11... | collective-permute-start | bytes 73736 | tf_op jit(solution)/shard_map/ppermute | solution.py:464
  7.4 2.4 %collective-permute-start.3 = (bf16[96,128]{1,0:T(8,128)(2,1)S(1)}, bf16[96,128]{1,0:T(8,128)(2,1)S(1)}, u32[]{:S(2)}, u32[]{:S(2)}) collective-permute-start(bf16[96,128]{1,0:T(8,128)(2,1)S(1)} %get-tuple-element.32), channel_id=1, source_target_pairs={{1,2},{2,1},{3,0},{0,3},{5,6},{6,5},{7,4},{4,7},{9,10},{10,9},{11,... | collective-permute-start | bytes 73736 | tf_op jit(solution)/shard_map/ppermute | solution.py:464
  10.1 0.2 copy.22.w_mid_back
  10.5 2.5 %collective-permute-done.3.fourth = bf16[96,128]{1,0:T(8,128)(2,1)S(1)} collective-permute-done((bf16[96,128]{1,0:T(8,128)(2,1)S(1)}, bf16[96,128]{1,0:T(8,128)(2,1)S(1)}, u32[]{:S(2)}, u32[]{:S(2)}) %collective-permute-start.3) | collective-permute-done | bytes 24608 | tf_op jit(solution)/shard_map/ppermute | solution.py:464
  13.0 15.7 %patches.1 = (bf16[1440,128]{1,0:T(8,128)(2,1)S(1)}, f32[864,128]{1,0:T(8,128)S(1)}, f32[16,32,384]{2,1,0:T(8,128)S(1)}, f32[8,256]{1,0:T(8,128)S(1)}) custom-call(s32[1,1,2,4]{3,2,1,0:T(2,128)S(1)} %bitcast.28, s32[1,1]{1,0:T(1,128)S(6)} %copy.28.counts, bf16[8,64,256]{2,1,0:T(8,128)(2,1)S(1)} %get-tuple-element.26.center, ...), custom_call_target="tpu_custom_call" | custom-call | tf_op jit(solution)/shard_map/patches/pallas_call | solution.py:561
  28.7 7.1 %collective-permute-start.4 = (bf16[1440,128]{1,0:T(8,128)(2,1)S(1)}, bf16[1440,128]{1,0:T(8,128)(2,1)S(1)}, u32[]{:S(2)}, u32[]{:S(2)}) collective-permute-start(bf16[1440,128]{1,0:T(8,128)(2,1)S(1)} %get-tuple-element.40), channel_id=1, source_target_pairs={{0,4},{4,0},{8,12},{12,8},{16,20},{20,16},{24,28},{28,24},{1,5},{5... | collective-permute-start | bytes 1105928 | tf_op jit(solution)/shard_map/ppermute | solution.py:477
  35.7 1.3 %collective-permute-done.4.first = bf16[1440,128]{1,0:T(8,128)(2,1)S(1)} collective-permute-done((bf16[1440,128]{1,0:T(8,128)(2,1)S(1)}, bf16[1440,128]{1,0:T(8,128)(2,1)S(1)}, u32[]{:S(2)}, u32[]{:S(2)}) %collective-permute-start.4) | collective-permute-done | bytes 368672 | tf_op jit(solution)/shard_map/ppermute | solution.py:477
  37.2 0.5 collective-permute-start.5
  37.6 5.1 %collective-permute-done.5 = bf16[720,128]{1,0:T(8,128)(2,1)S(1)} collective-permute-done((bf16[720,128]{1,0:T(8,128)(2,1)S(1)}, bf16[720,128]{1,0:T(8,128)(2,1)S(1)}, u32[]{:S(2)}, u32[]{:S(2)}) %collective-permute-start.5) | collective-permute-done | bytes 184352 | tf_op jit(solution)/shard_map/ppermute | solution.py:477
  42.9 0.3 collective-permute-start.6
  43.2 4.7 %collective-permute-done.6 = bf16[504,128]{1,0:T(8,128)(2,1)S(1)} collective-permute-done((bf16[504,128]{1,0:T(8,128)(2,1)S(1)}, bf16[504,128]{1,0:T(8,128)(2,1)S(1)}, u32[]{:S(2)}, u32[]{:S(2)}) %collective-permute-start.6) | collective-permute-done | bytes 129056 | tf_op jit(solution)/shard_map/ppermute | solution.py:477
  47.9 0.3 beside.1
  48.2 10.5 %all_to_all.5.parts = bf16[4,232,128]{2,1,0:T(8,128)(2,1)S(1)} all-to-all(bf16[4,232,128]{2,1,0:T(8,128)(2,1)S(1)} %broadcast_in_dim.2), channel_id=1, replica_groups=mesh['lat'=8,'lon'=4] {'lon'}, dimensions={0} | all-to-all | bytes 475136 | tf_op jit(solution)/shard_map/all_to_all | solution.py:626
  58.8 2.1 %collective-permute-start.7 = (bf16[216,128]{1,0:T(8,128)(2,1)S(1)}, bf16[216,128]{1,0:T(8,128)(2,1)S(1)}, u32[]{:S(2)}, u32[]{:S(2)}) collective-permute-start(bf16[216,128]{1,0:T(8,128)(2,1)S(1)} %slice_reduce_fusion), channel_id=1, source_target_pairs={{0,16},{4,12},{8,24},{12,4},{16,0},{20,28},{24,8},{28,20},{1,17},{... | collective-permute-start | bytes 165896 | tf_op jit(solution)/shard_map/ppermute | solution.py:477
  60.9 2.7 %collective-permute-done.7 = bf16[216,128]{1,0:T(8,128)(2,1)S(1)} collective-permute-done((bf16[216,128]{1,0:T(8,128)(2,1)S(1)}, bf16[216,128]{1,0:T(8,128)(2,1)S(1)}, u32[]{:S(2)}, u32[]{:S(2)}) %collective-permute-start.7) | collective-permute-done | bytes 55328 | tf_op jit(solution)/shard_map/ppermute | solution.py:477
  63.7 4.7 %collective-permute-done.8 = bf16[432,128]{1,0:T(8,128)(2,1)S(1)} collective-permute-done((bf16[432,128]{1,0:T(8,128)(2,1)S(1)}, bf16[432,128]{1,0:T(8,128)(2,1)S(1)}, u32[]{:S(2)}, u32[]{:S(2)}) %collective-permute-start.8) | collective-permute-done | bytes 110624 | tf_op jit(solution)/shard_map/ppermute | solution.py:477
  68.5 0.9 %fold.1 = f32[32,8,256]{2,1,0:T(8,128)} custom-call(f32[8,32,256]{2,1,0:T(8,128)S(1)} %get-tuple-element.42.inner, bf16[4,232,128]{2,1,0:T(8,128)(2,1)S(1)} %all_to_all.5.parts, f32[8,256]{1,0:T(8,128)S(1)} %get-tuple-element.44.den), custom_call_target="tpu_custom_call" | custom-call | tf_op jit(solution)/shard_map/fold/pallas_call | solution.py:628
  69.4 0.6 collective-permute-done.9.other
  70.0 1.0 %split.1 = (f32[9,32,128]{2,1,0:T(8,128)}, f32[9,128,128]{2,1,0:T(8,128)}, f32[9,32,128]{2,1,0:T(8,128)}) custom-call(bf16[864,128]{1,0:T(8,128)(2,1)S(1)} %pad_maximum_fusion.own, bf16[864,128]{1,0:T(8,128)(2,1)S(1)} %collective-permute-done.9.other), custom_call_target="tpu_custom_call" | custom-call | tf_op jit(solution)/shard_map/split/pallas_call | solution.py:638
  (37 shorter events, 1.0 us)
Async XLA Ops:
  0.6 3.4 %copy-start.2 = (bf16[9,128,128]{2,1,0:T(8,128)(2,1)S(1)}, bf16[9,128,128]{2,1,0:T(8,128)(2,1)}, u32[]{:S(2)}) copy-start(bf16[9,128,128]{2,1,0:T(8,128)(2,1)} %param.11) | copy-start | bytes 884740
  2.6 1.7 %collective-permute-start = (bf16[272,256]{1,0:T(8,128)(2,1)S(1)}, bf16[272,256]{1,0:T(8,128)(2,1)S(1)}, u32[]{:S(2)}, u32[]{:S(2)}) collective-permute-start(bf16[272,256]{1,0:T(8,128)(2,1)S(1)} %get-tuple-element.27), channel_id=1, source_target_pairs={{0,4},{4,0},{8,12},{12,8},{16,20},{20,16},{24,28},{28,24},{1,5},{5... | collective-permute-start | bytes 417800 | tf_op jit(solution)/shard_map/ppermute | solution.py:464
  3.2 1.0 %copy-start.3 = (bf16[9,32,128]{2,1,0:T(8,128)(2,1)S(1)}, bf16[9,32,128]{2,1,0:T(8,128)(2,1)}, u32[]{:S(2)}) copy-start(bf16[9,32,128]{2,1,0:T(8,128)(2,1)} %param.12) | copy-start | bytes 221188
  3.2 1.1 %collective-permute-start.1 = (bf16[272,256]{1,0:T(8,128)(2,1)S(1)}, bf16[272,256]{1,0:T(8,128)(2,1)S(1)}, u32[]{:S(2)}, u32[]{:S(2)}) collective-permute-start(bf16[272,256]{1,0:T(8,128)(2,1)S(1)} %get-tuple-element.28), channel_id=1, source_target_pairs={{4,8},{8,4},{12,16},{16,12},{20,24},{24,20},{5,9},{9,5},{13,17},{1... | collective-permute-start | bytes 417800 | tf_op jit(solution)/shard_map/ppermute | solution.py:464
  4.4 5.4 %copy-start.4 = (bf16[9,128,32]{1,2,0:T(8,128)(2,1)S(1)}, bf16[9,128,32]{1,2,0:T(8,128)(2,1)}, u32[]{:S(2)}) copy-start(bf16[9,128,32]{1,2,0:T(8,128)(2,1)} %param.10) | copy-start | bytes 221188
  4.6 5.9 %collective-permute-start.2 = (bf16[96,128]{1,0:T(8,128)(2,1)S(1)}, bf16[96,128]{1,0:T(8,128)(2,1)S(1)}, u32[]{:S(2)}, u32[]{:S(2)}) collective-permute-start(bf16[96,128]{1,0:T(8,128)(2,1)S(1)} %get-tuple-element.32), channel_id=1, source_target_pairs={{0,1},{1,0},{2,3},{3,2},{4,5},{5,4},{6,7},{7,6},{8,9},{9,8},{10,11... | collective-permute-start | bytes 73736 | tf_op jit(solution)/shard_map/ppermute | solution.py:464
  7.4 5.6 %collective-permute-start.3 = (bf16[96,128]{1,0:T(8,128)(2,1)S(1)}, bf16[96,128]{1,0:T(8,128)(2,1)S(1)}, u32[]{:S(2)}, u32[]{:S(2)}) collective-permute-start(bf16[96,128]{1,0:T(8,128)(2,1)S(1)} %get-tuple-element.32), channel_id=1, source_target_pairs={{1,2},{2,1},{3,0},{0,3},{5,6},{6,5},{7,4},{4,7},{9,10},{10,9},{11,... | collective-permute-start | bytes 73736 | tf_op jit(solution)/shard_map/ppermute | solution.py:464
  10.3 2.7 %copy-start = (s32[4,8,256]{2,1,0:T(8,128)S(1)}, s32[4,8,256]{2,1,0:T(8,128)}, u32[]{:S(2)}) copy-start(s32[4,8,256]{2,1,0:T(8,128)} %weights.1) | copy-start | bytes 98308
  10.4 2.5 %copy-start.1 = (s32[1,1,4,2]{2,3,1,0:T(2,128)S(1)}, s32[1,1,4,2]{2,3,1,0:T(2,128)}, u32[]{:S(2)}) copy-start(s32[1,1,4,2]{2,3,1,0:T(2,128)} %param.13) | copy-start | bytes 100
  28.7 8.4 %collective-permute-start.4 = (bf16[1440,128]{1,0:T(8,128)(2,1)S(1)}, bf16[1440,128]{1,0:T(8,128)(2,1)S(1)}, u32[]{:S(2)}, u32[]{:S(2)}) collective-permute-start(bf16[1440,128]{1,0:T(8,128)(2,1)S(1)} %get-tuple-element.40), channel_id=1, source_target_pairs={{0,4},{4,0},{8,12},{12,8},{16,20},{20,16},{24,28},{28,24},{1,5},{5... | collective-permute-start | bytes 1105928 | tf_op jit(solution)/shard_map/ppermute | solution.py:477
  37.2 5.6 %collective-permute-start.5 = (bf16[720,128]{1,0:T(8,128)(2,1)S(1)}, bf16[720,128]{1,0:T(8,128)(2,1)S(1)}, u32[]{:S(2)}, u32[]{:S(2)}) collective-permute-start(bf16[720,128]{1,0:T(8,128)(2,1)S(1)} %pad_maximum_fusion.1), channel_id=1, source_target_pairs={{0,8},{4,20},{8,0},{12,28},{16,24},{20,4},{24,16},{28,12},{1,9},{5... | collective-permute-start | bytes 552968 | tf_op jit(solution)/shard_map/ppermute | solution.py:477
  42.9 5.0 %collective-permute-start.6 = (bf16[504,128]{1,0:T(8,128)(2,1)S(1)}, bf16[504,128]{1,0:T(8,128)(2,1)S(1)}, u32[]{:S(2)}, u32[]{:S(2)}) collective-permute-start(bf16[504,128]{1,0:T(8,128)(2,1)S(1)} %pad_maximum_fusion.2), channel_id=1, source_target_pairs={{0,16},{4,12},{8,24},{12,4},{16,0},{20,28},{24,8},{28,20},{1,17},{... | collective-permute-start | bytes 387080 | tf_op jit(solution)/shard_map/ppermute | solution.py:477
  58.8 4.8 %collective-permute-start.7 = (bf16[216,128]{1,0:T(8,128)(2,1)S(1)}, bf16[216,128]{1,0:T(8,128)(2,1)S(1)}, u32[]{:S(2)}, u32[]{:S(2)}) collective-permute-start(bf16[216,128]{1,0:T(8,128)(2,1)S(1)} %slice_reduce_fusion), channel_id=1, source_target_pairs={{0,16},{4,12},{8,24},{12,4},{16,0},{20,28},{24,8},{28,20},{1,17},{... | collective-permute-start | bytes 165896 | tf_op jit(solution)/shard_map/ppermute | solution.py:477
  63.6 4.8 %collective-permute-start.8 = (bf16[432,128]{1,0:T(8,128)(2,1)S(1)}, bf16[432,128]{1,0:T(8,128)(2,1)S(1)}, u32[]{:S(2)}, u32[]{:S(2)}) collective-permute-start(bf16[432,128]{1,0:T(8,128)(2,1)S(1)} %pad_maximum_fusion.3), channel_id=1, source_target_pairs={{0,8},{4,20},{8,0},{12,28},{16,24},{20,4},{24,16},{28,12},{1,9},{5... | collective-permute-start | bytes 331784 | tf_op jit(solution)/shard_map/ppermute | solution.py:477
  68.5 1.5 %collective-permute-start.9 = (bf16[864,128]{1,0:T(8,128)(2,1)S(1)}, bf16[864,128]{1,0:T(8,128)(2,1)S(1)}, u32[]{:S(2)}, u32[]{:S(2)}) collective-permute-start(bf16[864,128]{1,0:T(8,128)(2,1)S(1)} %pad_maximum_fusion.own), channel_id=1, source_target_pairs={{0,4},{4,0},{8,12},{12,8},{16,20},{20,16},{24,28},{28,24},{1,5},{5... | collective-permute-start | bytes 663560 | tf_op jit(solution)/shard_map/ppermute | solution.py:477

commit v15 on v14

--- a/solution.py
+++ b/solution.py
@@ -175,30 +175,33 @@
     den_out[...] = den[MARGIN : MARGIN + rows, :cols]
     inverse = 1.0 / den
 
-    left = left[:base]
-    right = right[:base]
-    for row in range(height):
-        at = slice(row % MARGIN * base, (row % MARGIN + 1) * base)
-        if row < MARGIN:
-            body = choose(lat_odd, first[at], second[at])
-        elif row < MARGIN + rows:
-            body = center[row - MARGIN]
-        else:
-            body = choose(lat_odd, second[at], first[at])
-        beside = jnp.where(
-            lanes < LANES // 2, roll(right, -MARGIN * row, 1), roll(left, MARGIN * row, 1)
-        )
-        line = jnp.concatenate([body.astype(F32), beside], axis=1)
-        scaled = line[channels:] * inverse[row : row + 1]
-        window[row, 0:channels] = line[:channels].astype(BF16)
-        window[row, channels : 2 * channels] = scaled.astype(BF16)
-
-    numer[...] = jnp.zeros_like(numer)
-    grads[...] = jnp.zeros_like(grads)
     sets = (sets[: len(sets) // 2], sets[len(sets) // 2 :])
-    for ref in sets[0][:5] + sets[1][:5]:
-        ref[:, 0:cols] = jnp.zeros((ref.shape[0], cols), BF16)
-        ref[:, cols + full : 2 * cols + full] = jnp.zeros((ref.shape[0], cols), BF16)
+
+    def prepare():
+        left_edge = left[:base]
+        right_edge = right[:base]
+        for row in range(height):
+            at = slice(row % MARGIN * base, (row % MARGIN + 1) * base)
+            if row < MARGIN:
+                body = choose(lat_odd, first[at], second[at])
+            elif row < MARGIN + rows:
+                body = center[row - MARGIN]
+            else:
+                body = choose(lat_odd, second[at], first[at])
+            beside = jnp.where(
+                lanes < LANES // 2, roll(right_edge, -MARGIN * row, 1), roll(left_edge, MARGIN * row, 1)
+            )
+            line = jnp.concatenate([body.astype(F32), beside], axis=1)
+            scaled = line[channels:] * inverse[row : row + 1]
+            window[row, 0:channels] = line[:channels].astype(BF16)
+            window[row, channels : 2 * channels] = scaled.astype(BF16)
+        numer[...] = jnp.zeros_like(numer)
+        used = 9 * (2 * channels + width)
+        if used < grads.shape[0]:
+            grads[used:] = jnp.zeros((grads.shape[0] - used, LANES), F32)
+        for ref in sets[0][:5] + sets[1][:5]:
+            ref[:, 0:cols] = jnp.zeros((ref.shape[0], cols), BF16)
+            ref[:, cols + full : 2 * cols + full] = jnp.zeros((ref.shape[0], cols), BF16)
 
     def shifted(value, step):
         blocks = [value[:, at : at + LANES] for at in range(0, cols, LANES)]
@@ -288,6 +291,10 @@
         inside = slice(cols, cols + full)
         small = 9 * channels
 
+        def add(start, part):
+            at = slice(start, start + part.shape[0])
+            grads[at] = part if slot == 0 else grads[at] + part
+
         def conv_back(row):
             at = slice(row * cols, (row + 1) * cols)
             back = dot(w_mid_back[...], stack(z_s, row, True))
@@ -304,16 +311,14 @@
             for tap in range(3):
                 for tap_col in range(3):
                     start = small + (3 * tap + tap_col) * width
-                    grads[start : start + width] += part[
-                        tap_col * width : (tap_col + 1) * width, tap * width : (tap + 1) * width
-                    ]
+                    add(start, part[tap_col * width : (tap_col + 1) * width, tap * width : (tap + 1) * width])
 
         def grad_out():
             start = small + 9 * width
-            grads[start : start + small] += dot_lanes(all_rows(d_s, True), h2_s[:, inside])
+            add(start, dot_lanes(all_rows(d_s, True), h2_s[:, inside]))
 
         def grad_in():
-            grads[0:small] += dot_lanes(all_rows(x_s, False), dz_s[...])
+            add(0, dot_lanes(all_rows(x_s, False), dz_s[...]))
 
         backs = [functools.partial(conv_back, row) for row in range(rows)]
         outs = [functools.partial(conv_out, row) for row in range(rows)]
@@ -330,37 +335,47 @@
         for _, step in sorted(steps, key=lambda pair: pair[0]):
             step()
 
+    def finish():
+        half = grads.shape[0] // 2
+        odd_index = lax.rem(lax.axis_index("lat"), 2)
+        send[0:half] = grads[pl.ds(pl.multiple_of((1 - odd_index) * half, half), half)].astype(BF16)
+        keep[...] = grads[pl.ds(pl.multiple_of(odd_index * half, half), half)]
+        lanes = lane_ids((channels, LANES))
+        blocks = cols // LANES
+        base = half
+        upper = [numer[row] for row in range(MARGIN)]
+        lower = [numer[MARGIN + rows + row] for row in range(MARGIN)]
+        for when_odd, when_even in ((upper, lower), (lower, upper)):
+            packed = jnp.zeros((channels, LANES), F32)
+            for row in range(MARGIN):
+                line = choose(lat_odd, when_odd[row], when_even[row])
+                for block in range(blocks):
+                    send[base : base + channels] = line[:, block * LANES : (block + 1) * LANES].astype(BF16)
+                    base += channels
+                low = jnp.where(lanes < MARGIN, line[:, cols:], 0.0)
+                high = jnp.where(lanes >= LANES - MARGIN, line[:, cols:], 0.0)
+                packed = packed + roll(low, MARGIN * row, 1) + roll(high, -MARGIN * row, 1)
+            send[base : base + channels] = packed.astype(BF16)
+            base += channels
+
     @pl.when(counts[0, 0] == SLOTS)
     def _():
+        prepare()
         for slot in range(SLOTS + 1):
             run(slot)
+        finish()
 
     @pl.when(counts[0, 0] < SLOTS)
     def _():
+        prepare()
+
+        @pl.when(counts[0, 0] == 0)
+        def _():
+            grads[...] = jnp.zeros_like(grads)
+
         for slot in range(SLOTS):
             pl.when(max(slot, 1) <= counts[0, 0])(functools.partial(run, slot))
-
-    half = grads.shape[0] // 2
-    odd_index = lax.rem(lax.axis_index("lat"), 2)
-    send[0:half] = grads[pl.ds(pl.multiple_of((1 - odd_index) * half, half), half)].astype(BF16)
-    keep[...] = grads[pl.ds(pl.multiple_of(odd_index * half, half), half)]
-    lanes = lane_ids((channels, LANES))
-    blocks = cols // LANES
-    base = half
-    upper = [numer[row] for row in range(MARGIN)]
-    lower = [numer[MARGIN + rows + row] for row in range(MARGIN)]
-    for when_odd, when_even in ((upper, lower), (lower, upper)):
-        packed = jnp.zeros((channels, LANES), F32)
-        for row in range(MARGIN):
-            line = choose(lat_odd, when_odd[row], when_even[row])
-            for block in range(blocks):
-                send[base : base + channels] = line[:, block * LANES : (block + 1) * LANES].astype(BF16)
-                base += channels
-            low = jnp.where(lanes < MARGIN, line[:, cols:], 0.0)
-            high = jnp.where(lanes >= LANES - MARGIN, line[:, cols:], 0.0)
-            packed = packed + roll(low, MARGIN * row, 1) + roll(high, -MARGIN * row, 1)
-        send[base : base + channels] = packed.astype(BF16)
-        base += channels
+        finish()
 
 
 def beside_kernel(numer, first, held, inner, edges):

time: 70.7 us -> 71.3 us (level)
  no operation moved by 1% of the time
where the time goes in v15:
time: 71.3 us; the launch traced here: 71.1 us
  waiting for transfers between devices  21.5 us (30%)
  Pallas kernels  19.4 us (27%)
  starting transfers between devices  16.6 us (23%)
  blocking collectives  10.5 us (15%)
  between operations  1.68 us (2%)
  local copies, waits for them, and re-layouts  1.05 us (1%)
    ppermute x6, waiting for transfers between devices, exchange(): return lax.ppermute(value, axis, pairs)  19 us
    pallas_call x1, Pallas kernels, shards(): pl.pallas_call(patch_kernel, out_shape=(shape((half + 2 * edge_rows, LANE...  15.8 us
    all_to_all x1, blocking collectives, shards(): payload = lax.all_to_all(payload, 'lon', 0, 0)  10.5 us
    ppermute x6, starting transfers between devices, exchange(): return lax.ppermute(value, axis, pairs)  10.1 us
    ppermute x4, starting transfers between devices, swap(): return lax.ppermute(value, axis, pairs)  6.52 us
    ppermute x4, waiting for transfers between devices, swap(): return lax.ppermute(value, axis, pairs)  2.44 us
  transfers between devices with their start and end apart: 10, of which 7 were waited for; matrix products, arithmetic and copies ran while one was open for 1% of the time, Pallas kernels for 1%

profile of v15, /device:TPU:0, one launch (start us, length us, event | category | flops | bytes accessed | tf_op | source)
XLA Modules:
  0.0 71.1 jit_solution(9749930201031385462)
XLA Ops:
  1.3 1.3 %pack.1 = (bf16[8,64,256]{2,1,0:T(8,128)(2,1)S(1)}, bf16[272,256]{1,0:T(8,128)(2,1)S(1)}, bf16[272,256]{1,0:T(8,128)(2,1)S(1)}, f32[16,384]{1,0:T(8,128)S(1)}) custom-call(s32[1,1]{1,0:T(1,128)S(6)} %copy.28.counts, s32[1,1,2,4]{3,2,1,0:T(2,128)} %bitcast.27, bf16[32,8,256]{2,1,0:T(8,128)(2,1)} %fields_in.1, bf16[32,8,256]{2,1,0:T(8,128)(2,1)} %cotangent_in.1, ...), custom_call_target="tpu_custom_call" | custom-call | tf_op jit(solution)/shard_map/pack/pallas_call | solution.py:522
  2.6 0.6 collective-permute-start
  3.2 0.8 %collective-permute-start.1 = (bf16[272,256]{1,0:T(8,128)(2,1)S(1)}, bf16[272,256]{1,0:T(8,128)(2,1)S(1)}, u32[]{:S(2)}, u32[]{:S(2)}) collective-permute-start(bf16[272,256]{1,0:T(8,128)(2,1)S(1)} %get-tuple-element.28), channel_id=1, source_target_pairs={{4,8},{8,4},{12,16},{16,12},{20,24},{24,20},{5,9},{9,5},{13,17},{1... | collective-permute-start | bytes 417800 | tf_op jit(solution)/shard_map/ppermute | solution.py:479
  4.0 0.2 copy.17
  4.4 0.2 edges.1
  4.6 2.7 %collective-permute-start.2 = (bf16[96,128]{1,0:T(8,128)(2,1)S(1)}, bf16[96,128]{1,0:T(8,128)(2,1)S(1)}, u32[]{:S(2)}, u32[]{:S(2)}) collective-permute-start(bf16[96,128]{1,0:T(8,128)(2,1)S(1)} %get-tuple-element.32), channel_id=1, source_target_pairs={{0,1},{1,0},{2,3},{3,2},{4,5},{5,4},{6,7},{7,6},{8,9},{9,8},{10,11... | collective-permute-start | bytes 73736 | tf_op jit(solution)/shard_map/ppermute | solution.py:479
  7.3 2.5 %collective-permute-start.3 = (bf16[96,128]{1,0:T(8,128)(2,1)S(1)}, bf16[96,128]{1,0:T(8,128)(2,1)S(1)}, u32[]{:S(2)}, u32[]{:S(2)}) collective-permute-start(bf16[96,128]{1,0:T(8,128)(2,1)S(1)} %get-tuple-element.32), channel_id=1, source_target_pairs={{1,2},{2,1},{3,0},{0,3},{5,6},{6,5},{7,4},{4,7},{9,10},{10,9},{11,... | collective-permute-start | bytes 73736 | tf_op jit(solution)/shard_map/ppermute | solution.py:479
  9.9 0.2 copy.21.w_mid
  10.1 0.2 copy.22.w_mid_back
  10.4 2.4 %collective-permute-done.3.fourth = bf16[96,128]{1,0:T(8,128)(2,1)S(1)} collective-permute-done((bf16[96,128]{1,0:T(8,128)(2,1)S(1)}, bf16[96,128]{1,0:T(8,128)(2,1)S(1)}, u32[]{:S(2)}, u32[]{:S(2)}) %collective-permute-start.3) | collective-permute-done | bytes 24608 | tf_op jit(solution)/shard_map/ppermute | solution.py:479
  12.9 15.8 %patches.1 = (bf16[1440,128]{1,0:T(8,128)(2,1)S(1)}, f32[864,128]{1,0:T(8,128)S(1)}, f32[16,32,384]{2,1,0:T(8,128)S(1)}, f32[8,256]{1,0:T(8,128)S(1)}) custom-call(s32[1,1,2,4]{3,2,1,0:T(2,128)S(1)} %bitcast.28, s32[1,1]{1,0:T(1,128)S(6)} %copy.28.counts, bf16[8,64,256]{2,1,0:T(8,128)(2,1)S(1)} %get-tuple-element.26.center, ...), custom_call_target="tpu_custom_call" | custom-call | tf_op jit(solution)/shard_map/patches/pallas_call | solution.py:576
  28.7 7.1 %collective-permute-start.4 = (bf16[1440,128]{1,0:T(8,128)(2,1)S(1)}, bf16[1440,128]{1,0:T(8,128)(2,1)S(1)}, u32[]{:S(2)}, u32[]{:S(2)}) collective-permute-start(bf16[1440,128]{1,0:T(8,128)(2,1)S(1)} %get-tuple-element.40), channel_id=1, source_target_pairs={{0,4},{4,0},{8,12},{12,8},{16,20},{20,16},{24,28},{28,24},{1,5},{5... | collective-permute-start | bytes 1105928 | tf_op jit(solution)/shard_map/ppermute | solution.py:492
  35.8 1.3 %collective-permute-done.4.first = bf16[1440,128]{1,0:T(8,128)(2,1)S(1)} collective-permute-done((bf16[1440,128]{1,0:T(8,128)(2,1)S(1)}, bf16[1440,128]{1,0:T(8,128)(2,1)S(1)}, u32[]{:S(2)}, u32[]{:S(2)}) %collective-permute-start.4) | collective-permute-done | bytes 368672 | tf_op jit(solution)/shard_map/ppermute | solution.py:492
  37.4 5.4 %collective-permute-done.5 = bf16[720,128]{1,0:T(8,128)(2,1)S(1)} collective-permute-done((bf16[720,128]{1,0:T(8,128)(2,1)S(1)}, bf16[720,128]{1,0:T(8,128)(2,1)S(1)}, u32[]{:S(2)}, u32[]{:S(2)}) %collective-permute-start.5) | collective-permute-done | bytes 184352 | tf_op jit(solution)/shard_map/ppermute | solution.py:492
  43.0 4.9 %collective-permute-done.6 = bf16[504,128]{1,0:T(8,128)(2,1)S(1)} collective-permute-done((bf16[504,128]{1,0:T(8,128)(2,1)S(1)}, bf16[504,128]{1,0:T(8,128)(2,1)S(1)}, u32[]{:S(2)}, u32[]{:S(2)}) %collective-permute-start.6) | collective-permute-done | bytes 129056 | tf_op jit(solution)/shard_map/ppermute | solution.py:492
  48.0 0.3 beside.1
  48.3 10.5 %all_to_all.5.parts = bf16[4,232,128]{2,1,0:T(8,128)(2,1)S(1)} all-to-all(bf16[4,232,128]{2,1,0:T(8,128)(2,1)S(1)} %broadcast_in_dim.2), channel_id=1, replica_groups=mesh['lat'=8,'lon'=4] {'lon'}, dimensions={0} | all-to-all | bytes 475136 | tf_op jit(solution)/shard_map/all_to_all | solution.py:641
  58.8 2.1 %collective-permute-start.7 = (bf16[216,128]{1,0:T(8,128)(2,1)S(1)}, bf16[216,128]{1,0:T(8,128)(2,1)S(1)}, u32[]{:S(2)}, u32[]{:S(2)}) collective-permute-start(bf16[216,128]{1,0:T(8,128)(2,1)S(1)} %slice_reduce_fusion), channel_id=1, source_target_pairs={{0,16},{4,12},{8,24},{12,4},{16,0},{20,28},{24,8},{28,20},{1,17},{... | collective-permute-start | bytes 165896 | tf_op jit(solution)/shard_map/ppermute | solution.py:492
  60.9 2.7 %collective-permute-done.7 = bf16[216,128]{1,0:T(8,128)(2,1)S(1)} collective-permute-done((bf16[216,128]{1,0:T(8,128)(2,1)S(1)}, bf16[216,128]{1,0:T(8,128)(2,1)S(1)}, u32[]{:S(2)}, u32[]{:S(2)}) %collective-permute-start.7) | collective-permute-done | bytes 55328 | tf_op jit(solution)/shard_map/ppermute | solution.py:492
  63.6 0.7 collective-permute-start.8
  64.3 4.2 %collective-permute-done.8 = bf16[432,128]{1,0:T(8,128)(2,1)S(1)} collective-permute-done((bf16[432,128]{1,0:T(8,128)(2,1)S(1)}, bf16[432,128]{1,0:T(8,128)(2,1)S(1)}, u32[]{:S(2)}, u32[]{:S(2)}) %collective-permute-start.8) | collective-permute-done | bytes 110624 | tf_op jit(solution)/shard_map/ppermute | solution.py:492
  68.6 0.9 %fold.1 = f32[32,8,256]{2,1,0:T(8,128)} custom-call(f32[8,32,256]{2,1,0:T(8,128)S(1)} %get-tuple-element.42.inner, bf16[4,232,128]{2,1,0:T(8,128)(2,1)S(1)} %all_to_all.5.parts, f32[8,256]{1,0:T(8,128)S(1)} %get-tuple-element.44.den), custom_call_target="tpu_custom_call" | custom-call | tf_op jit(solution)/shard_map/fold/pallas_call | solution.py:643
  69.5 0.6 collective-permute-done.9.other
  70.1 1.0 %split.1 = (f32[9,32,128]{2,1,0:T(8,128)}, f32[9,128,128]{2,1,0:T(8,128)}, f32[9,32,128]{2,1,0:T(8,128)}) custom-call(bf16[864,128]{1,0:T(8,128)(2,1)S(1)} %pad_maximum_fusion.own, bf16[864,128]{1,0:T(8,128)(2,1)S(1)} %collective-permute-done.9.other), custom_call_target="tpu_custom_call" | custom-call | tf_op jit(solution)/shard_map/split/pallas_call | solution.py:653
  (37 shorter events, 0.9 us)
Async XLA Ops:
  0.6 3.4 %copy-start.2 = (bf16[9,128,128]{2,1,0:T(8,128)(2,1)S(1)}, bf16[9,128,128]{2,1,0:T(8,128)(2,1)}, u32[]{:S(2)}) copy-start(bf16[9,128,128]{2,1,0:T(8,128)(2,1)} %param.11) | copy-start | bytes 884740
  2.6 1.7 %collective-permute-start = (bf16[272,256]{1,0:T(8,128)(2,1)S(1)}, bf16[272,256]{1,0:T(8,128)(2,1)S(1)}, u32[]{:S(2)}, u32[]{:S(2)}) collective-permute-start(bf16[272,256]{1,0:T(8,128)(2,1)S(1)} %get-tuple-element.27), channel_id=1, source_target_pairs={{0,4},{4,0},{8,12},{12,8},{16,20},{20,16},{24,28},{28,24},{1,5},{5... | collective-permute-start | bytes 417800 | tf_op jit(solution)/shard_map/ppermute | solution.py:479
  3.2 1.0 %copy-start.3 = (bf16[9,32,128]{2,1,0:T(8,128)(2,1)S(1)}, bf16[9,32,128]{2,1,0:T(8,128)(2,1)}, u32[]{:S(2)}) copy-start(bf16[9,32,128]{2,1,0:T(8,128)(2,1)} %param.12) | copy-start | bytes 221188
  3.2 1.1 %collective-permute-start.1 = (bf16[272,256]{1,0:T(8,128)(2,1)S(1)}, bf16[272,256]{1,0:T(8,128)(2,1)S(1)}, u32[]{:S(2)}, u32[]{:S(2)}) collective-permute-start(bf16[272,256]{1,0:T(8,128)(2,1)S(1)} %get-tuple-element.28), channel_id=1, source_target_pairs={{4,8},{8,4},{12,16},{16,12},{20,24},{24,20},{5,9},{9,5},{13,17},{1... | collective-permute-start | bytes 417800 | tf_op jit(solution)/shard_map/ppermute | solution.py:479
  4.4 5.4 %copy-start.4 = (bf16[9,128,32]{1,2,0:T(8,128)(2,1)S(1)}, bf16[9,128,32]{1,2,0:T(8,128)(2,1)}, u32[]{:S(2)}) copy-start(bf16[9,128,32]{1,2,0:T(8,128)(2,1)} %param.10) | copy-start | bytes 221188
  4.6 5.8 %collective-permute-start.2 = (bf16[96,128]{1,0:T(8,128)(2,1)S(1)}, bf16[96,128]{1,0:T(8,128)(2,1)S(1)}, u32[]{:S(2)}, u32[]{:S(2)}) collective-permute-start(bf16[96,128]{1,0:T(8,128)(2,1)S(1)} %get-tuple-element.32), channel_id=1, source_target_pairs={{0,1},{1,0},{2,3},{3,2},{4,5},{5,4},{6,7},{7,6},{8,9},{9,8},{10,11... | collective-permute-start | bytes 73736 | tf_op jit(solution)/shard_map/ppermute | solution.py:479
  7.3 5.6 %collective-permute-start.3 = (bf16[96,128]{1,0:T(8,128)(2,1)S(1)}, bf16[96,128]{1,0:T(8,128)(2,1)S(1)}, u32[]{:S(2)}, u32[]{:S(2)}) collective-permute-start(bf16[96,128]{1,0:T(8,128)(2,1)S(1)} %get-tuple-element.32), channel_id=1, source_target_pairs={{1,2},{2,1},{3,0},{0,3},{5,6},{6,5},{7,4},{4,7},{9,10},{10,9},{11,... | collective-permute-start | bytes 73736 | tf_op jit(solution)/shard_map/ppermute | solution.py:479
  10.3 2.6 %copy-start = (s32[4,8,256]{2,1,0:T(8,128)S(1)}, s32[4,8,256]{2,1,0:T(8,128)}, u32[]{:S(2)}) copy-start(s32[4,8,256]{2,1,0:T(8,128)} %weights.1) | copy-start | bytes 98308
  10.4 2.5 %copy-start.1 = (s32[1,1,4,2]{2,3,1,0:T(2,128)S(1)}, s32[1,1,4,2]{2,3,1,0:T(2,128)}, u32[]{:S(2)}) copy-start(s32[1,1,4,2]{2,3,1,0:T(2,128)} %param.13) | copy-start | bytes 100
  28.7 8.5 %collective-permute-start.4 = (bf16[1440,128]{1,0:T(8,128)(2,1)S(1)}, bf16[1440,128]{1,0:T(8,128)(2,1)S(1)}, u32[]{:S(2)}, u32[]{:S(2)}) collective-permute-start(bf16[1440,128]{1,0:T(8,128)(2,1)S(1)} %get-tuple-element.40), channel_id=1, source_target_pairs={{0,4},{4,0},{8,12},{12,8},{16,20},{20,16},{24,28},{28,24},{1,5},{5... | collective-permute-start | bytes 1105928 | tf_op jit(solution)/shard_map/ppermute | solution.py:492
  37.2 5.6 %collective-permute-start.5 = (bf16[720,128]{1,0:T(8,128)(2,1)S(1)}, bf16[720,128]{1,0:T(8,128)(2,1)S(1)}, u32[]{:S(2)}, u32[]{:S(2)}) collective-permute-start(bf16[720,128]{1,0:T(8,128)(2,1)S(1)} %pad_maximum_fusion.1), channel_id=1, source_target_pairs={{0,8},{4,20},{8,0},{12,28},{16,24},{20,4},{24,16},{28,12},{1,9},{5... | collective-permute-start | bytes 552968 | tf_op jit(solution)/shard_map/ppermute | solution.py:492
  42.9 5.0 %collective-permute-start.6 = (bf16[504,128]{1,0:T(8,128)(2,1)S(1)}, bf16[504,128]{1,0:T(8,128)(2,1)S(1)}, u32[]{:S(2)}, u32[]{:S(2)}) collective-permute-start(bf16[504,128]{1,0:T(8,128)(2,1)S(1)} %pad_maximum_fusion.2), channel_id=1, source_target_pairs={{0,16},{4,12},{8,24},{12,4},{16,0},{20,28},{24,8},{28,20},{1,17},{... | collective-permute-start | bytes 387080 | tf_op jit(solution)/shard_map/ppermute | solution.py:492
  58.8 4.8 %collective-permute-start.7 = (bf16[216,128]{1,0:T(8,128)(2,1)S(1)}, bf16[216,128]{1,0:T(8,128)(2,1)S(1)}, u32[]{:S(2)}, u32[]{:S(2)}) collective-permute-start(bf16[216,128]{1,0:T(8,128)(2,1)S(1)} %slice_reduce_fusion), channel_id=1, source_target_pairs={{0,16},{4,12},{8,24},{12,4},{16,0},{20,28},{24,8},{28,20},{1,17},{... | collective-permute-start | bytes 165896 | tf_op jit(solution)/shard_map/ppermute | solution.py:492
  63.6 4.8 %collective-permute-start.8 = (bf16[432,128]{1,0:T(8,128)(2,1)S(1)}, bf16[432,128]{1,0:T(8,128)(2,1)S(1)}, u32[]{:S(2)}, u32[]{:S(2)}) collective-permute-start(bf16[432,128]{1,0:T(8,128)(2,1)S(1)} %pad_maximum_fusion.3), channel_id=1, source_target_pairs={{0,8},{4,20},{8,0},{12,28},{16,24},{20,4},{24,16},{28,12},{1,9},{5... | collective-permute-start | bytes 331784 | tf_op jit(solution)/shard_map/ppermute | solution.py:492
  68.5 1.5 %collective-permute-start.9 = (bf16[864,128]{1,0:T(8,128)(2,1)S(1)}, bf16[864,128]{1,0:T(8,128)(2,1)S(1)}, u32[]{:S(2)}, u32[]{:S(2)}) collective-permute-start(bf16[864,128]{1,0:T(8,128)(2,1)S(1)} %pad_maximum_fusion.own), channel_id=1, source_target_pairs={{0,4},{4,0},{8,12},{12,8},{16,20},{20,16},{24,28},{28,24},{1,5},{5... | collective-permute-start | bytes 663560 | tf_op jit(solution)/shard_map/ppermute | solution.py:492

commit v16 on v14

--- a/solution.py
+++ b/solution.py
@@ -337,8 +337,12 @@
 
     @pl.when(counts[0, 0] < SLOTS)
     def _():
-        for slot in range(SLOTS):
-            pl.when(max(slot, 1) <= counts[0, 0])(functools.partial(run, slot))
+        def one_slot(slot, carry):
+            for step in first_part(slot, *sets[0]) + second_part(slot, *sets[0]):
+                step()
+            return carry
+
+        lax.fori_loop(0, counts[0, 0], one_slot, 0)
 
     half = grads.shape[0] // 2
     odd_index = lax.rem(lax.axis_index("lat"), 2)

time: 70.7 us -> 70 us (0.990)
  starting transfers between devices: 16.6 us -> 27.2 us
  Pallas kernels: 19.3 us -> 9.15 us
  blocking collectives: 10.5 us -> 9.52 us
  waiting for transfers between devices: 21.6 us -> 20.8 us
    ppermute x6, starting transfers between devices: 10.1 us -> 20.5 us  [exchange(): return lax.ppermute(value, axis, pairs)]
    pallas_call x1, Pallas kernels: 15.7 us -> 5.62 us  [shards(): pl.pallas_call(patch_kernel, out_shape=(shape((half + 2 * edge_rows, LANE...]
    all_to_all x1, blocking collectives: 10.5 us -> 9.52 us  [shards(): payload = lax.all_to_all(payload, 'lon', 0, 0)]
    ppermute x6, waiting for transfers between devices: 19.1 us -> 18.4 us  [exchange(): return lax.ppermute(value, axis, pairs)]
where the time goes in v16:
time: 70 us; the launch traced here: 69.7 us
  starting transfers between devices  27.2 us (39%)
  waiting for transfers between devices  20.8 us (30%)
  blocking collectives  9.52 us (14%)
  Pallas kernels  9.15 us (13%)
  between operations  1.66 us (2%)
  local copies, waits for them, and re-layouts  1.05 us (2%)
    ppermute x6, starting transfers between devices, exchange(): return lax.ppermute(value, axis, pairs)  20.5 us
    ppermute x6, waiting for transfers between devices, exchange(): return lax.ppermute(value, axis, pairs)  18.4 us
    all_to_all x1, blocking collectives, shards(): payload = lax.all_to_all(payload, 'lon', 0, 0)  9.52 us
    ppermute x4, starting transfers between devices, swap(): return lax.ppermute(value, axis, pairs)  6.74 us
    pallas_call x1, Pallas kernels, shards(): pl.pallas_call(patch_kernel, out_shape=(shape((half + 2 * edge_rows, LANE...  5.62 us
    ppermute x4, waiting for transfers between devices, swap(): return lax.ppermute(value, axis, pairs)  2.44 us
  transfers between devices with their start and end apart: 10, of which 7 were waited for; matrix products, arithmetic and copies ran while one was open for 1% of the time, Pallas kernels for 1%

profile of v16, /device:TPU:0, one launch (start us, length us, event | category | flops | bytes accessed | tf_op | source)
XLA Modules:
  0.0 69.7 jit_solution(11810003177393844925)
XLA Ops:
  1.3 1.2 %pack.1 = (bf16[8,64,256]{2,1,0:T(8,128)(2,1)S(1)}, bf16[272,256]{1,0:T(8,128)(2,1)S(1)}, bf16[272,256]{1,0:T(8,128)(2,1)S(1)}, f32[16,384]{1,0:T(8,128)S(1)}) custom-call(s32[1,1]{1,0:T(1,128)S(6)} %copy.28.counts, s32[1,1,2,4]{3,2,1,0:T(2,128)} %bitcast.27, bf16[32,8,256]{2,1,0:T(8,128)(2,1)} %fields_in.1, bf16[32,8,256]{2,1,0:T(8,128)(2,1)} %cotangent_in.1, ...), custom_call_target="tpu_custom_call" | custom-call | tf_op jit(solution)/shard_map/pack/pallas_call | solution.py:511
  2.5 0.7 %collective-permute-start = (bf16[272,256]{1,0:T(8,128)(2,1)S(1)}, bf16[272,256]{1,0:T(8,128)(2,1)S(1)}, u32[]{:S(2)}, u32[]{:S(2)}) collective-permute-start(bf16[272,256]{1,0:T(8,128)(2,1)S(1)} %get-tuple-element.27), channel_id=1, source_target_pairs={{0,4},{4,0},{8,12},{12,8},{16,20},{20,16},{24,28},{28,24},{1,5},{5... | collective-permute-start | bytes 417800 | tf_op jit(solution)/shard_map/ppermute | solution.py:468
  3.2 0.8 %collective-permute-start.1 = (bf16[272,256]{1,0:T(8,128)(2,1)S(1)}, bf16[272,256]{1,0:T(8,128)(2,1)S(1)}, u32[]{:S(2)}, u32[]{:S(2)}) collective-permute-start(bf16[272,256]{1,0:T(8,128)(2,1)S(1)} %get-tuple-element.28), channel_id=1, source_target_pairs={{4,8},{8,4},{12,16},{16,12},{20,24},{24,20},{5,9},{9,5},{13,17},{1... | collective-permute-start | bytes 417800 | tf_op jit(solution)/shard_map/ppermute | solution.py:468
  4.0 0.2 copy.17
  4.4 0.2 edges.1
  4.6 2.8 %collective-permute-start.2 = (bf16[96,128]{1,0:T(8,128)(2,1)S(1)}, bf16[96,128]{1,0:T(8,128)(2,1)S(1)}, u32[]{:S(2)}, u32[]{:S(2)}) collective-permute-start(bf16[96,128]{1,0:T(8,128)(2,1)S(1)} %get-tuple-element.32), channel_id=1, source_target_pairs={{0,1},{1,0},{2,3},{3,2},{4,5},{5,4},{6,7},{7,6},{8,9},{9,8},{10,11... | collective-permute-start | bytes 73736 | tf_op jit(solution)/shard_map/ppermute | solution.py:468
  7.4 2.5 %collective-permute-start.3 = (bf16[96,128]{1,0:T(8,128)(2,1)S(1)}, bf16[96,128]{1,0:T(8,128)(2,1)S(1)}, u32[]{:S(2)}, u32[]{:S(2)}) collective-permute-start(bf16[96,128]{1,0:T(8,128)(2,1)S(1)} %get-tuple-element.32), channel_id=1, source_target_pairs={{1,2},{2,1},{3,0},{0,3},{5,6},{6,5},{7,4},{4,7},{9,10},{10,9},{11,... | collective-permute-start | bytes 73736 | tf_op jit(solution)/shard_map/ppermute | solution.py:468
  10.2 0.2 copy.22.w_mid_back
  10.6 2.4 %collective-permute-done.3.fourth = bf16[96,128]{1,0:T(8,128)(2,1)S(1)} collective-permute-done((bf16[96,128]{1,0:T(8,128)(2,1)S(1)}, bf16[96,128]{1,0:T(8,128)(2,1)S(1)}, u32[]{:S(2)}, u32[]{:S(2)}) %collective-permute-start.3) | collective-permute-done | bytes 24608 | tf_op jit(solution)/shard_map/ppermute | solution.py:468
  13.0 5.6 %patches.1 = (bf16[1440,128]{1,0:T(8,128)(2,1)S(1)}, f32[864,128]{1,0:T(8,128)S(1)}, f32[16,32,384]{2,1,0:T(8,128)S(1)}, f32[8,256]{1,0:T(8,128)S(1)}) custom-call(s32[1,1,2,4]{3,2,1,0:T(2,128)S(1)} %bitcast.28, s32[1,1]{1,0:T(1,128)S(6)} %copy.28.counts, bf16[8,64,256]{2,1,0:T(8,128)(2,1)S(1)} %get-tuple-element.26.center, ...), custom_call_target="tpu_custom_call" | custom-call | tf_op jit(solution)/shard_map/patches/pallas_call | solution.py:565
  18.6 16.9 %collective-permute-start.4 = (bf16[1440,128]{1,0:T(8,128)(2,1)S(1)}, bf16[1440,128]{1,0:T(8,128)(2,1)S(1)}, u32[]{:S(2)}, u32[]{:S(2)}) collective-permute-start(bf16[1440,128]{1,0:T(8,128)(2,1)S(1)} %get-tuple-element.40), channel_id=1, source_target_pairs={{0,4},{4,0},{8,12},{12,8},{16,20},{20,16},{24,28},{28,24},{1,5},{5... | collective-permute-start | bytes 1105928 | tf_op jit(solution)/shard_map/ppermute | solution.py:481
  35.5 1.3 %collective-permute-done.4.first = bf16[1440,128]{1,0:T(8,128)(2,1)S(1)} collective-permute-done((bf16[1440,128]{1,0:T(8,128)(2,1)S(1)}, bf16[1440,128]{1,0:T(8,128)(2,1)S(1)}, u32[]{:S(2)}, u32[]{:S(2)}) %collective-permute-start.4) | collective-permute-done | bytes 368672 | tf_op jit(solution)/shard_map/ppermute | solution.py:481
  37.1 5.4 %collective-permute-done.5 = bf16[720,128]{1,0:T(8,128)(2,1)S(1)} collective-permute-done((bf16[720,128]{1,0:T(8,128)(2,1)S(1)}, bf16[720,128]{1,0:T(8,128)(2,1)S(1)}, u32[]{:S(2)}, u32[]{:S(2)}) %collective-permute-start.5) | collective-permute-done | bytes 184352 | tf_op jit(solution)/shard_map/ppermute | solution.py:481
  42.7 0.9 %collective-permute-start.6 = (bf16[504,128]{1,0:T(8,128)(2,1)S(1)}, bf16[504,128]{1,0:T(8,128)(2,1)S(1)}, u32[]{:S(2)}, u32[]{:S(2)}) collective-permute-start(bf16[504,128]{1,0:T(8,128)(2,1)S(1)} %pad_maximum_fusion.2), channel_id=1, source_target_pairs={{0,16},{4,12},{8,24},{12,4},{16,0},{20,28},{24,8},{28,20},{1,17},{... | collective-permute-start | bytes 387080 | tf_op jit(solution)/shard_map/ppermute | solution.py:481
  43.6 4.1 %collective-permute-done.6 = bf16[504,128]{1,0:T(8,128)(2,1)S(1)} collective-permute-done((bf16[504,128]{1,0:T(8,128)(2,1)S(1)}, bf16[504,128]{1,0:T(8,128)(2,1)S(1)}, u32[]{:S(2)}, u32[]{:S(2)}) %collective-permute-start.6) | collective-permute-done | bytes 129056 | tf_op jit(solution)/shard_map/ppermute | solution.py:481
  47.7 0.3 beside.1
  48.0 9.5 %all_to_all.5.parts = bf16[4,232,128]{2,1,0:T(8,128)(2,1)S(1)} all-to-all(bf16[4,232,128]{2,1,0:T(8,128)(2,1)S(1)} %broadcast_in_dim.2), channel_id=1, replica_groups=mesh['lat'=8,'lon'=4] {'lon'}, dimensions={0} | all-to-all | bytes 475136 | tf_op jit(solution)/shard_map/all_to_all | solution.py:630
  57.6 1.9 %collective-permute-start.7 = (bf16[216,128]{1,0:T(8,128)(2,1)S(1)}, bf16[216,128]{1,0:T(8,128)(2,1)S(1)}, u32[]{:S(2)}, u32[]{:S(2)}) collective-permute-start(bf16[216,128]{1,0:T(8,128)(2,1)S(1)} %slice_reduce_fusion), channel_id=1, source_target_pairs={{0,16},{4,12},{8,24},{12,4},{16,0},{20,28},{24,8},{28,20},{1,17},{... | collective-permute-start | bytes 165896 | tf_op jit(solution)/shard_map/ppermute | solution.py:481
  59.4 2.8 %collective-permute-done.7 = bf16[216,128]{1,0:T(8,128)(2,1)S(1)} collective-permute-done((bf16[216,128]{1,0:T(8,128)(2,1)S(1)}, bf16[216,128]{1,0:T(8,128)(2,1)S(1)}, u32[]{:S(2)}, u32[]{:S(2)}) %collective-permute-start.7) | collective-permute-done | bytes 55328 | tf_op jit(solution)/shard_map/ppermute | solution.py:481
  62.3 0.7 collective-permute-start.8
  63.0 4.1 %collective-permute-done.8 = bf16[432,128]{1,0:T(8,128)(2,1)S(1)} collective-permute-done((bf16[432,128]{1,0:T(8,128)(2,1)S(1)}, bf16[432,128]{1,0:T(8,128)(2,1)S(1)}, u32[]{:S(2)}, u32[]{:S(2)}) %collective-permute-start.8) | collective-permute-done | bytes 110624 | tf_op jit(solution)/shard_map/ppermute | solution.py:481
  67.3 0.9 %fold.1 = f32[32,8,256]{2,1,0:T(8,128)} custom-call(f32[8,32,256]{2,1,0:T(8,128)S(1)} %get-tuple-element.42.inner, bf16[4,232,128]{2,1,0:T(8,128)(2,1)S(1)} %all_to_all.5.parts, f32[8,256]{1,0:T(8,128)S(1)} %get-tuple-element.44.den), custom_call_target="tpu_custom_call" | custom-call | tf_op jit(solution)/shard_map/fold/pallas_call | solution.py:632
  68.2 0.6 collective-permute-done.9.other
  68.7 1.0 %split.1 = (f32[9,32,128]{2,1,0:T(8,128)}, f32[9,128,128]{2,1,0:T(8,128)}, f32[9,32,128]{2,1,0:T(8,128)}) custom-call(bf16[864,128]{1,0:T(8,128)(2,1)S(1)} %pad_maximum_fusion.own, bf16[864,128]{1,0:T(8,128)(2,1)S(1)} %collective-permute-done.9.other), custom_call_target="tpu_custom_call" | custom-call | tf_op jit(solution)/shard_map/split/pallas_call | solution.py:642
  (37 shorter events, 1.0 us)
Async XLA Ops:
  0.6 3.4 %copy-start.2 = (bf16[9,128,128]{2,1,0:T(8,128)(2,1)S(1)}, bf16[9,128,128]{2,1,0:T(8,128)(2,1)}, u32[]{:S(2)}) copy-start(bf16[9,128,128]{2,1,0:T(8,128)(2,1)} %param.11) | copy-start | bytes 884740
  2.5 1.8 %collective-permute-start = (bf16[272,256]{1,0:T(8,128)(2,1)S(1)}, bf16[272,256]{1,0:T(8,128)(2,1)S(1)}, u32[]{:S(2)}, u32[]{:S(2)}) collective-permute-start(bf16[272,256]{1,0:T(8,128)(2,1)S(1)} %get-tuple-element.27), channel_id=1, source_target_pairs={{0,4},{4,0},{8,12},{12,8},{16,20},{20,16},{24,28},{28,24},{1,5},{5... | collective-permute-start | bytes 417800 | tf_op jit(solution)/shard_map/ppermute | solution.py:468
  3.2 1.0 %copy-start.3 = (bf16[9,32,128]{2,1,0:T(8,128)(2,1)S(1)}, bf16[9,32,128]{2,1,0:T(8,128)(2,1)}, u32[]{:S(2)}) copy-start(bf16[9,32,128]{2,1,0:T(8,128)(2,1)} %param.12) | copy-start | bytes 221188
  3.2 1.1 %collective-permute-start.1 = (bf16[272,256]{1,0:T(8,128)(2,1)S(1)}, bf16[272,256]{1,0:T(8,128)(2,1)S(1)}, u32[]{:S(2)}, u32[]{:S(2)}) collective-permute-start(bf16[272,256]{1,0:T(8,128)(2,1)S(1)} %get-tuple-element.28), channel_id=1, source_target_pairs={{4,8},{8,4},{12,16},{16,12},{20,24},{24,20},{5,9},{9,5},{13,17},{1... | collective-permute-start | bytes 417800 | tf_op jit(solution)/shard_map/ppermute | solution.py:468
  4.4 5.5 %copy-start.4 = (bf16[9,128,32]{1,2,0:T(8,128)(2,1)S(1)}, bf16[9,128,32]{1,2,0:T(8,128)(2,1)}, u32[]{:S(2)}) copy-start(bf16[9,128,32]{1,2,0:T(8,128)(2,1)} %param.10) | copy-start | bytes 221188
  4.6 5.9 %collective-permute-start.2 = (bf16[96,128]{1,0:T(8,128)(2,1)S(1)}, bf16[96,128]{1,0:T(8,128)(2,1)S(1)}, u32[]{:S(2)}, u32[]{:S(2)}) collective-permute-start(bf16[96,128]{1,0:T(8,128)(2,1)S(1)} %get-tuple-element.32), channel_id=1, source_target_pairs={{0,1},{1,0},{2,3},{3,2},{4,5},{5,4},{6,7},{7,6},{8,9},{9,8},{10,11... | collective-permute-start | bytes 73736 | tf_op jit(solution)/shard_map/ppermute | solution.py:468
  7.4 5.6 %collective-permute-start.3 = (bf16[96,128]{1,0:T(8,128)(2,1)S(1)}, bf16[96,128]{1,0:T(8,128)(2,1)S(1)}, u32[]{:S(2)}, u32[]{:S(2)}) collective-permute-start(bf16[96,128]{1,0:T(8,128)(2,1)S(1)} %get-tuple-element.32), channel_id=1, source_target_pairs={{1,2},{2,1},{3,0},{0,3},{5,6},{6,5},{7,4},{4,7},{9,10},{10,9},{11,... | collective-permute-start | bytes 73736 | tf_op jit(solution)/shard_map/ppermute | solution.py:468
  10.4 2.6 %copy-start = (s32[4,8,256]{2,1,0:T(8,128)S(1)}, s32[4,8,256]{2,1,0:T(8,128)}, u32[]{:S(2)}) copy-start(s32[4,8,256]{2,1,0:T(8,128)} %weights.1) | copy-start | bytes 98308
  10.5 2.5 %copy-start.1 = (s32[1,1,4,2]{2,3,1,0:T(2,128)S(1)}, s32[1,1,4,2]{2,3,1,0:T(2,128)}, u32[]{:S(2)}) copy-start(s32[1,1,4,2]{2,3,1,0:T(2,128)} %param.13) | copy-start | bytes 100
  18.6 18.2 %collective-permute-start.4 = (bf16[1440,128]{1,0:T(8,128)(2,1)S(1)}, bf16[1440,128]{1,0:T(8,128)(2,1)S(1)}, u32[]{:S(2)}, u32[]{:S(2)}) collective-permute-start(bf16[1440,128]{1,0:T(8,128)(2,1)S(1)} %get-tuple-element.40), channel_id=1, source_target_pairs={{0,4},{4,0},{8,12},{12,8},{16,20},{20,16},{24,28},{28,24},{1,5},{5... | collective-permute-start | bytes 1105928 | tf_op jit(solution)/shard_map/ppermute | solution.py:481
  37.0 5.6 %collective-permute-start.5 = (bf16[720,128]{1,0:T(8,128)(2,1)S(1)}, bf16[720,128]{1,0:T(8,128)(2,1)S(1)}, u32[]{:S(2)}, u32[]{:S(2)}) collective-permute-start(bf16[720,128]{1,0:T(8,128)(2,1)S(1)} %pad_maximum_fusion.1), channel_id=1, source_target_pairs={{0,8},{4,20},{8,0},{12,28},{16,24},{20,4},{24,16},{28,12},{1,9},{5... | collective-permute-start | bytes 552968 | tf_op jit(solution)/shard_map/ppermute | solution.py:481
  42.7 5.0 %collective-permute-start.6 = (bf16[504,128]{1,0:T(8,128)(2,1)S(1)}, bf16[504,128]{1,0:T(8,128)(2,1)S(1)}, u32[]{:S(2)}, u32[]{:S(2)}) collective-permute-start(bf16[504,128]{1,0:T(8,128)(2,1)S(1)} %pad_maximum_fusion.2), channel_id=1, source_target_pairs={{0,16},{4,12},{8,24},{12,4},{16,0},{20,28},{24,8},{28,20},{1,17},{... | collective-permute-start | bytes 387080 | tf_op jit(solution)/shard_map/ppermute | solution.py:481
  57.6 4.7 %collective-permute-start.7 = (bf16[216,128]{1,0:T(8,128)(2,1)S(1)}, bf16[216,128]{1,0:T(8,128)(2,1)S(1)}, u32[]{:S(2)}, u32[]{:S(2)}) collective-permute-start(bf16[216,128]{1,0:T(8,128)(2,1)S(1)} %slice_reduce_fusion), channel_id=1, source_target_pairs={{0,16},{4,12},{8,24},{12,4},{16,0},{20,28},{24,8},{28,20},{1,17},{... | collective-permute-start | bytes 165896 | tf_op jit(solution)/shard_map/ppermute | solution.py:481
  62.3 4.8 %collective-permute-start.8 = (bf16[432,128]{1,0:T(8,128)(2,1)S(1)}, bf16[432,128]{1,0:T(8,128)(2,1)S(1)}, u32[]{:S(2)}, u32[]{:S(2)}) collective-permute-start(bf16[432,128]{1,0:T(8,128)(2,1)S(1)} %pad_maximum_fusion.3), channel_id=1, source_target_pairs={{0,8},{4,20},{8,0},{12,28},{16,24},{20,4},{24,16},{28,12},{1,9},{5... | collective-permute-start | bytes 331784 | tf_op jit(solution)/shard_map/ppermute | solution.py:481
  67.2 1.5 %collective-permute-start.9 = (bf16[864,128]{1,0:T(8,128)(2,1)S(1)}, bf16[864,128]{1,0:T(8,128)(2,1)S(1)}, u32[]{:S(2)}, u32[]{:S(2)}) collective-permute-start(bf16[864,128]{1,0:T(8,128)(2,1)S(1)} %pad_maximum_fusion.own), channel_id=1, source_target_pairs={{0,4},{4,0},{8,12},{12,8},{16,20},{20,16},{24,28},{28,24},{1,5},{5... | collective-permute-start | bytes 663560 | tf_op jit(solution)/shard_map/ppermute | solution.py:481
